TPU v7x, 32 devices: a whole 2x2x4 slice. The times are simulated.
32 devices in a mesh: batch: 4 (over x, core), edge: 8 (over z, y).
Axes of the slice: x: 2, y: 2, z: 4, core: 2. Of those that a mesh axis runs over, the one named last changes fastest.
Arguments:
- states: bfloat16 [4, 1024, 128], P('batch', 'edge'), may hold values from -6 to 6
- edge_feats: bfloat16 [4, 16384, 16], P('batch', 'edge'), may hold values from -6 to 6
- molecule: int32 [4, 1024], P('batch', 'edge'), may hold values from 0 to 1023, as said below
- source: int32 [4, 16384], P('batch', 'edge'), may hold values from 0 to 1023, as said below
- target: int32 [4, 16384], P('batch', 'edge'), may hold values from 0 to 1023, as said below
- edge_mask: int32 [4, 16384], P('batch', 'edge'), may hold values 0 or 1
- w_edge_in: bfloat16 [16, 128], replicated, may hold values from -1.5 to 1.5
- b_edge_in: bfloat16 [128], replicated, may hold values from -3 to 3
- w_edge_out: bfloat16 [128, 16384], replicated, may hold values from -0.01171875 to 0.01171875
- b_edge_out: bfloat16 [16384], replicated, may hold values from -0.119628906 to 0.119628906
- w_input: bfloat16 [128, 384], replicated, may hold values from -0.5 to 0.5
- w_hidden: bfloat16 [128, 384], replicated, may hold values from -0.5 to 0.5
- b_input: bfloat16 [384], replicated, may hold values from -3 to 3
- b_hidden: bfloat16 [384], replicated, may hold values from -3 to 3
- cotangent: bfloat16 [4, 1024, 128], P('batch', 'edge'), may hold values from -6 to 6
Outputs:
- new_states: bfloat16 [4, 1024, 128], P('batch', 'edge')
- state_grads: float32 [4, 1024, 128], P('batch', 'edge')
- edge_grads: float32 [4, 16384, 16], P('batch', 'edge')
- grad_w_edge_in: float32 [16, 128], replicated
- grad_b_edge_in: float32 [128], replicated
- grad_w_edge_out: float32 [128, 16384], replicated
- grad_b_edge_out: float32 [16384], replicated
- grad_w_input: float32 [128, 384], replicated
- grad_w_hidden: float32 [128, 384], replicated
- grad_b_input: float32 [384], replicated
- grad_b_hidden: float32 [384], replicated
Inputs may be any that keep to these rules, and one draw needn't show every extreme that they name: The molecule number of a node is the lowest position of its molecule in a hidden packing order; nodes of one molecule share it; each graph batch holds one molecule of min(100, 512) nodes. `source`: node index within the graph batch; most edges join two nodes of one molecule. `target`: node index within the graph batch.
All inputs are finite; a program needn't handle non-finite values. No bound on the sum of `edge_mask` on one device may be relied on, other than what follows from the above.
Results may differ from a plain program's by a relative error of at most 0.011.
Values may be sent and summed in bfloat16 or wider, within the bound.
No kernel may reach another device: no remote copies, remote signals or barrier semaphores. Data moves between devices by JAX's collectives and lax.ppermute only.
A program may use at most 128 MiB of HBM per device.

v0:
```python
import jax
import jax.numpy as jnp
from jax import lax
from jax.sharding import PartitionSpec as P

HIGH = lax.Precision.HIGHEST


def gated_update(mixed, prior, w_input, w_hidden, b_input, b_hidden):
    width = prior.shape[1]
    from_input = jnp.dot(mixed, w_input, precision=HIGH) + b_input
    from_state = jnp.dot(prior, w_hidden, precision=HIGH) + b_hidden
    reset = jax.nn.sigmoid(from_input[:, :width] + from_state[:, :width])
    update = jax.nn.sigmoid(from_input[:, width : 2 * width] + from_state[:, width : 2 * width])
    candidate = jnp.tanh(from_input[:, 2 * width :] + reset * from_state[:, 2 * width :])
    return (1.0 - update) * candidate + update * prior


def edge_hidden(feats, w_edge_in, b_edge_in):
    return jax.nn.silu(jnp.dot(feats, w_edge_in, precision=HIGH) + b_edge_in)


def pick_by(index_rows, piece):
    columns = lax.broadcasted_iota(jnp.int32, (1, piece.shape[0]), 1)
    onehot = (index_rows[:, None] == columns).astype(jnp.bfloat16)
    return jnp.dot(onehot, piece, preferred_element_type=jnp.float32)


def spread_by(index_rows, values, count):
    rows = lax.broadcasted_iota(jnp.int32, (count, 1), 0)
    onehot = (rows == index_rows[None, :]).astype(jnp.bfloat16)
    return jnp.dot(onehot, values, preferred_element_type=jnp.float32)


def per_device(
    states,
    edge_feats,
    molecule,
    source,
    target,
    edge_mask,
    w_edge_in,
    b_edge_in,
    w_edge_out,
    b_edge_out,
    w_input,
    w_hidden,
    b_input,
    b_hidden,
    cotangent,
):
    states_here = states[0]
    feats = edge_feats[0]
    source_ids = source[0]
    target_ids = target[0]
    width = states_here.shape[1]
    owned = states_here.shape[0]
    edges = source_ids.shape[0]
    block = min(512, edges)
    count = edges // block
    labels = lax.all_gather(molecule[0], "edge", axis=0, tiled=True)
    same = (jnp.take(labels, source_ids) == jnp.take(labels, target_ids)).astype(jnp.float32)
    valid = edge_mask[0].astype(jnp.float32) * same
    near = pick_by(source_ids, lax.all_gather(states_here, "edge", axis=0, tiled=True)).astype(
        jnp.bfloat16
    )
    hidden, edge_pull = jax.vjp(
        edge_hidden,
        feats.astype(jnp.float32),
        w_edge_in.astype(jnp.float32),
        b_edge_in.astype(jnp.float32),
    )
    latent_blocks = hidden.astype(jnp.bfloat16).reshape(count, block, -1)
    near_blocks = near.reshape(count, block, width)
    bias_out = b_edge_out.astype(jnp.float32)

    def expand(latent):
        flat = jnp.dot(latent, w_edge_out, preferred_element_type=jnp.float32) + bias_out
        return flat.astype(jnp.bfloat16).reshape(latent.shape[0], width, width)

    def apply(mats, vectors):
        return jnp.einsum("bij,bj->bi", mats, vectors, preferred_element_type=jnp.float32)

    outgoing = lax.map(lambda item: apply(expand(item[0]), item[1]), (latent_blocks, near_blocks))
    messages = (outgoing.reshape(edges, width) * valid[:, None]).astype(jnp.bfloat16)
    summed = lax.psum_scatter(
        spread_by(target_ids, messages, lax.axis_size("edge") * owned),
        "edge",
        scatter_dimension=0,
        tiled=True,
    )
    mixed = summed.astype(jnp.bfloat16).astype(jnp.float32)
    updated, update_pull = jax.vjp(
        gated_update,
        mixed,
        states_here.astype(jnp.float32),
        w_input.astype(jnp.float32),
        w_hidden.astype(jnp.float32),
        b_input.astype(jnp.float32),
        b_hidden.astype(jnp.float32),
    )
    new_states = updated.astype(jnp.bfloat16)
    d_mixed, d_direct, grad_wi, grad_wh, grad_bi, grad_bh = update_pull(
        cotangent[0].astype(jnp.float32)
    )
    pulled = pick_by(
        target_ids, lax.all_gather(d_mixed.astype(jnp.bfloat16), "edge", axis=0, tiled=True)
    )
    d_message = (pulled * valid[:, None]).astype(jnp.bfloat16)
    d_message_blocks = d_message.reshape(count, block, width)

    def backward_core(carry, mats, latent, vectors, d_out):
        grad_weight, grad_bias = carry
        outer = (
            d_out.astype(jnp.float32)[:, :, None] * vectors.astype(jnp.float32)[:, None, :]
        ).astype(jnp.bfloat16)
        flat = outer.reshape(latent.shape[0], width * width)
        d_latent = lax.dot_general(
            flat, w_edge_out, (((1,), (1,)), ((), ())), preferred_element_type=jnp.float32
        )
        grad_weight = grad_weight + lax.dot_general(
            latent, flat, (((0,), (0,)), ((), ())), preferred_element_type=jnp.float32
        )
        grad_bias = grad_bias + jnp.sum(flat.astype(jnp.float32), axis=0)
        d_vectors = jnp.einsum(
            "bij,bi->bj", mats, d_out, preferred_element_type=jnp.float32
        ).astype(jnp.bfloat16)
        return ((grad_weight, grad_bias), (d_latent, d_vectors))

    start_carry = (
        jnp.zeros((w_edge_out.shape[0], width * width), jnp.float32),
        jnp.zeros((width * width,), jnp.float32),
    )

    def backward_block(carry, item):
        return backward_core(carry, expand(item[0]), item[0], item[1], item[2])

    sums_out, per_edge = lax.scan(
        backward_block, start_carry, (latent_blocks, near_blocks, d_message_blocks)
    )
    grad_w2, grad_b2 = sums_out
    d_latent_all = per_edge[0].reshape(edges, -1)
    d_near_all = per_edge[1].reshape(edges, width)
    d_feats, grad_w1, grad_b1 = edge_pull(d_latent_all)
    returned = lax.psum_scatter(
        spread_by(source_ids, d_near_all, owned * lax.axis_size("edge")).astype(jnp.bfloat16),
        "edge",
        scatter_dimension=0,
        tiled=True,
    ).astype(jnp.float32)
    state_grads = d_direct + returned
    grad_w1, grad_b1, grad_w2, grad_b2, grad_wi, grad_wh, grad_bi, grad_bh = lax.psum(
        (grad_w1, grad_b1, grad_w2, grad_b2, grad_wi, grad_wh, grad_bi, grad_bh), ("batch", "edge")
    )
    return (
        new_states[None],
        state_grads[None],
        d_feats[None],
        grad_w1,
        grad_b1,
        grad_w2,
        grad_b2,
        grad_wi,
        grad_wh,
        grad_bi,
        grad_bh,
    )


def solution(mesh):
    return jax.shard_map(
        per_device,
        mesh=mesh,
        in_specs=(
            P("batch", "edge", None),
            P("batch", "edge", None),
            P("batch", "edge"),
            P("batch", "edge"),
            P("batch", "edge"),
            P("batch", "edge"),
            P(),
            P(),
            P(),
            P(),
            P(),
            P(),
            P(),
            P(),
            P("batch", "edge", None),
        ),
        out_specs=(
            P("batch", "edge", None),
            P("batch", "edge", None),
            P("batch", "edge", None),
            P(),
            P(),
            P(),
            P(),
            P(),
            P(),
            P(),
            P(),
        ),
        check_vma=False,
    )
```

profile of v0, /device:TPU:0, one launch (start us, length us, event | category | flops | bytes accessed | tf_op | source)
XLA Modules:
  0.0 911.6 jit_solution(11660205351659762116)
XLA Ops:
  7.9 22.3 %all-gather.1 = s32[1,1024]{1,0:T(1,128)S(1)} all-gather(s32[1,128]{1,0:T(1,128)} %param.23), channel_id=3, replica_groups=mesh['batch'=4,'edge'=8] {'edge'}, dimensions={1}, use_global_device_ids=true | all-gather | bytes 4608 | tf_op jit(solution)/shard_map/all_gather | solution.py:61
  31.0 8.6 gather_fusion
  39.6 8.6 gather_fusion.1
  48.2 30.7 %all-gather = bf16[1,1024,128]{2,1,0:T(8,128)(2,1)S(1)} all-gather(bf16[1,128,128]{2,1,0:T(8,128)(2,1)S(1)} %copy-done.15), channel_id=2, replica_groups=mesh['batch'=4,'edge'=8] {'edge'}, dimensions={1}, use_global_device_ids=true | all-gather | bytes 294912 | tf_op jit(solution)/shard_map/all_gather | solution.py:64
  82.2 115.6 %while.27 = (s32[]{:T(128)}, f32[4,512,128]{2,1,0:T(8,128)S(1)}, bf16[4,512,128]{2,1,0:T(8,128)(2,1)S(1)}, bf16[128,16384]{1,0:T(8,128)(2,1)}, f32[16384]{0:T(10...) while((s32[]{:T(128)}, f32[4,512,128]{2,1,0:T(8,128)S(1)}, bf16[4,512,128]{2,1,0:T(8,128)(2,1)S(1)}, ...), condition=%wide.region_1.2_spmd, body=%wide.region_0.1_spmd.sunk | while | flops 2181038080 | bytes 72679504 | solution.py:84
  82.2 10.3 %fusion.120 = bf16[64,8,128,128]{3,1,2,0:T(8,128)(2,1)} fusion(f32[16384]{0:T(1024)S(1)} %get-tuple-element.354, bf16[128,16384]{1,0:T(8,128)(2,1)} %get-tuple-element.353, bf16[4,512,128]{2,1,0:T(8,128)(2,1)S(1)} %get-tuple-element.352, s32[]{:T(128)} %get-tuple-element.343), kind=kOutput, calls=%fused_computation.3.clone.1 | convolution fusion | flops 2164260864 | bytes 21168132 | tf_op jit(solution)/shard_map/while/body/eval_jaxpr/dot_general | solution.py:78
  92.6 9.8 %copy.59 = bf16[64,8,128,128]{3,2,1,0:T(8,128)(2,1)S(1)} copy(bf16[64,8,128,128]{3,1,2,0:T(8,128)(2,1)} %fusion.120) | data formatting | bytes 33554432 | tf_op jit(solution)/shard_map/while
  102.4 8.7 fusion.121
  111.2 10.3 %fusion.120 = bf16[64,8,128,128]{3,1,2,0:T(8,128)(2,1)} fusion(f32[16384]{0:T(1024)S(1)} %get-tuple-element.354, bf16[128,16384]{1,0:T(8,128)(2,1)} %get-tuple-element.353, bf16[4,512,128]{2,1,0:T(8,128)(2,1)S(1)} %get-tuple-element.352, s32[]{:T(128)} %get-tuple-element.343), kind=kOutput, calls=%fused_computation.3.clone.1 | convolution fusion | flops 2164260864 | bytes 21168132 | tf_op jit(solution)/shard_map/while/body/eval_jaxpr/dot_general | solution.py:78
  121.5 9.8 %copy.59 = bf16[64,8,128,128]{3,2,1,0:T(8,128)(2,1)S(1)} copy(bf16[64,8,128,128]{3,1,2,0:T(8,128)(2,1)} %fusion.120) | data formatting | bytes 33554432 | tf_op jit(solution)/shard_map/while
  131.3 8.7 fusion.121
  140.1 10.3 %fusion.120 = bf16[64,8,128,128]{3,1,2,0:T(8,128)(2,1)} fusion(f32[16384]{0:T(1024)S(1)} %get-tuple-element.354, bf16[128,16384]{1,0:T(8,128)(2,1)} %get-tuple-element.353, bf16[4,512,128]{2,1,0:T(8,128)(2,1)S(1)} %get-tuple-element.352, s32[]{:T(128)} %get-tuple-element.343), kind=kOutput, calls=%fused_computation.3.clone.1 | convolution fusion | flops 2164260864 | bytes 21168132 | tf_op jit(solution)/shard_map/while/body/eval_jaxpr/dot_general | solution.py:78
  150.4 9.8 %copy.59 = bf16[64,8,128,128]{3,2,1,0:T(8,128)(2,1)S(1)} copy(bf16[64,8,128,128]{3,1,2,0:T(8,128)(2,1)} %fusion.120) | data formatting | bytes 33554432 | tf_op jit(solution)/shard_map/while
  160.2 8.7 fusion.121
  169.0 10.3 %fusion.120 = bf16[64,8,128,128]{3,1,2,0:T(8,128)(2,1)} fusion(f32[16384]{0:T(1024)S(1)} %get-tuple-element.354, bf16[128,16384]{1,0:T(8,128)(2,1)} %get-tuple-element.353, bf16[4,512,128]{2,1,0:T(8,128)(2,1)S(1)} %get-tuple-element.352, s32[]{:T(128)} %get-tuple-element.343), kind=kOutput, calls=%fused_computation.3.clone.1 | convolution fusion | flops 2164260864 | bytes 21168132 | tf_op jit(solution)/shard_map/while/body/eval_jaxpr/dot_general | solution.py:78
  179.3 9.8 %copy.59 = bf16[64,8,128,128]{3,2,1,0:T(8,128)(2,1)S(1)} copy(bf16[64,8,128,128]{3,1,2,0:T(8,128)(2,1)} %fusion.120) | data formatting | bytes 33554432 | tf_op jit(solution)/shard_map/while
  189.1 8.7 fusion.121
  200.8 59.0 %reduce-scatter.3.cloned.1.call-done = f32[128,128]{1,0:T(8,128)} async-done(((f32[1024,128]{1,0:T(8,128)}), f32[128,128]{1,0:T(8,128)}) %reduce-scatter.3.cloned.1.call-update) | async-done | bytes 65552 | tf_op jit(solution)/shard_map/reduce_scatter | solution.py:86
  262.5 30.9 %all_gather.11 = bf16[1024,128]{1,0:T(8,128)(2,1)S(1)} all-gather(bf16[128,128]{1,0:T(8,128)(2,1)S(1)} %convolution_convert_fusion), channel_id=1, replica_groups=mesh['batch'=4,'edge'=8] {'edge'}, dimensions={0}, use_global_device_ids=true | all-gather | bytes 294912 | tf_op jit(solution)/shard_map/all_gather | solution.py:107
  295.3 341.3 %while.28 = (s32[]{:T(128)}, f32[128,16384]{1,0:T(8,128)}, f32[16384]{0:T(1024)S(1)}, f32[4,512,128]{2,1,0:T(8,128)S(1)}, bf16[4,512,128]{2,1,0:T(8,128)(2,1)}, ...) while((s32[]{:T(128)}, f32[128,16384]{1,0:T(8,128)}, ...), condition=%wide.region_5.7_spmd.clone, body=%wide.region_3.6_spmd.clone.sunk | while | flops 6513967104 | bytes 166658800 | solution.py:138
  313.7 12.3 %convert_reduce_fusion.2 = (f32[128,128]{1,0:T(8,128)S(1)}, bf16[512,128,128]{2,1,0:T(8,128)(2,1)}) fusion(f32[512,128]{1,0:T(8,128)S(1)} %get-tuple-element.331, f32[512,128]{1,0:T(8,128)S(1)} %get-tuple-element.332), kind=kLoop, calls=%fused_computation.12.clone.1 | loop fusion | flops 33538048 | bytes 17367040 | tf_op jit(solution)/shard_map/while/body/eval_jaxpr/reduce_sum | solution.py:124
  326.0 20.2 %convolution_add_fusion.6 = f32[128,16384]{1,0:T(8,128)} fusion(bf16[64,8,128,128]{3,2,1,0:T(8,128)(2,1)} %bitcast.166, f32[128,16384]{1,0:T(8,128)} %get-tuple-element.370, pred[]{:T(512)S(6)} %compare.7, bf16[4,512,128]{2,1,0:T(8,128)(2,1)S(1)} %get-tuple-element.386, s32[]{:T(128)} %get-tuple-element.369), kind=kOutput, calls=%fused_computation.14.clone.1 | convolution fusion | flops 2151677952 | bytes 33685508 | tf_op jit(solution)/shard_map/while/body/eval_jaxpr/dot_general | solution.py:121
  346.2 21.1 %fusion.130 = f32[4,512,128]{2,1,0:T(8,128)S(1)} fusion(f32[4,512,128]{2,1,0:T(8,128)S(1)} %get-tuple-element.372, s32[]{:T(128)} %get-tuple-element.369, bf16[128,16384]{1,0:T(8,128)(2,1)S(1)} %copy-done.2, bf16[64,8,128,128]{3,2,1,0:T(8,128)(2,1)} %bitcast.167), kind=kOutput, calls=%fused_computation.22.clone.1 | convolution fusion | flops 2147483648 | bytes 21233668 | tf_op jit(solution)/shard_map/while/body/eval_jaxpr/dot_general | solution.py:118
  367.3 10.3 %fusion.131 = bf16[64,8,128,128]{3,1,2,0:T(8,128)(2,1)} fusion(f32[16384]{0:T(1024)S(1)} %get-tuple-element.390, bf16[128,16384]{1,0:T(8,128)(2,1)} %get-tuple-element.389, bf16[4,512,128]{2,1,0:T(8,128)(2,1)S(1)} %get-tuple-element.386, s32[]{:T(128)} %get-tuple-element.369), kind=kOutput, calls=%fused_computation.20.clone.1 | convolution fusion | flops 2164260864 | bytes 21168132 | tf_op jit(solution)/shard_map/while/body/eval_jaxpr/dot_general | solution.py:78
  377.6 9.8 %copy.63 = bf16[64,8,128,128]{3,2,1,0:T(8,128)(2,1)S(1)} copy(bf16[64,8,128,128]{3,1,2,0:T(8,128)(2,1)} %fusion.131) | data formatting | bytes 33554432 | tf_op jit(solution)/shard_map/while
  387.4 4.4 fusion.132
  392.6 12.3 %convert_reduce_fusion.2 = (f32[128,128]{1,0:T(8,128)S(1)}, bf16[512,128,128]{2,1,0:T(8,128)(2,1)}) fusion(f32[512,128]{1,0:T(8,128)S(1)} %get-tuple-element.331, f32[512,128]{1,0:T(8,128)S(1)} %get-tuple-element.332), kind=kLoop, calls=%fused_computation.12.clone.1 | loop fusion | flops 33538048 | bytes 17367040 | tf_op jit(solution)/shard_map/while/body/eval_jaxpr/reduce_sum | solution.py:124
  404.9 22.6 %convolution_add_fusion.6 = f32[128,16384]{1,0:T(8,128)} fusion(bf16[64,8,128,128]{3,2,1,0:T(8,128)(2,1)} %bitcast.166, f32[128,16384]{1,0:T(8,128)} %get-tuple-element.370, pred[]{:T(512)S(6)} %compare.7, bf16[4,512,128]{2,1,0:T(8,128)(2,1)S(1)} %get-tuple-element.386, s32[]{:T(128)} %get-tuple-element.369), kind=kOutput, calls=%fused_computation.14.clone.1 | convolution fusion | flops 2151677952 | bytes 33685508 | tf_op jit(solution)/shard_map/while/body/eval_jaxpr/dot_general | solution.py:121
  427.5 21.1 %fusion.130 = f32[4,512,128]{2,1,0:T(8,128)S(1)} fusion(f32[4,512,128]{2,1,0:T(8,128)S(1)} %get-tuple-element.372, s32[]{:T(128)} %get-tuple-element.369, bf16[128,16384]{1,0:T(8,128)(2,1)S(1)} %copy-done.2, bf16[64,8,128,128]{3,2,1,0:T(8,128)(2,1)} %bitcast.167), kind=kOutput, calls=%fused_computation.22.clone.1 | convolution fusion | flops 2147483648 | bytes 21233668 | tf_op jit(solution)/shard_map/while/body/eval_jaxpr/dot_general | solution.py:118
  448.6 10.3 %fusion.131 = bf16[64,8,128,128]{3,1,2,0:T(8,128)(2,1)} fusion(f32[16384]{0:T(1024)S(1)} %get-tuple-element.390, bf16[128,16384]{1,0:T(8,128)(2,1)} %get-tuple-element.389, bf16[4,512,128]{2,1,0:T(8,128)(2,1)S(1)} %get-tuple-element.386, s32[]{:T(128)} %get-tuple-element.369), kind=kOutput, calls=%fused_computation.20.clone.1 | convolution fusion | flops 2164260864 | bytes 21168132 | tf_op jit(solution)/shard_map/while/body/eval_jaxpr/dot_general | solution.py:78
  458.9 9.8 %copy.63 = bf16[64,8,128,128]{3,2,1,0:T(8,128)(2,1)S(1)} copy(bf16[64,8,128,128]{3,1,2,0:T(8,128)(2,1)} %fusion.131) | data formatting | bytes 33554432 | tf_op jit(solution)/shard_map/while
  468.7 4.4 fusion.132
  473.9 12.3 %convert_reduce_fusion.2 = (f32[128,128]{1,0:T(8,128)S(1)}, bf16[512,128,128]{2,1,0:T(8,128)(2,1)}) fusion(f32[512,128]{1,0:T(8,128)S(1)} %get-tuple-element.331, f32[512,128]{1,0:T(8,128)S(1)} %get-tuple-element.332), kind=kLoop, calls=%fused_computation.12.clone.1 | loop fusion | flops 33538048 | bytes 17367040 | tf_op jit(solution)/shard_map/while/body/eval_jaxpr/reduce_sum | solution.py:124
  486.2 22.6 %convolution_add_fusion.6 = f32[128,16384]{1,0:T(8,128)} fusion(bf16[64,8,128,128]{3,2,1,0:T(8,128)(2,1)} %bitcast.166, f32[128,16384]{1,0:T(8,128)} %get-tuple-element.370, pred[]{:T(512)S(6)} %compare.7, bf16[4,512,128]{2,1,0:T(8,128)(2,1)S(1)} %get-tuple-element.386, s32[]{:T(128)} %get-tuple-element.369), kind=kOutput, calls=%fused_computation.14.clone.1 | convolution fusion | flops 2151677952 | bytes 33685508 | tf_op jit(solution)/shard_map/while/body/eval_jaxpr/dot_general | solution.py:121
  508.8 21.1 %fusion.130 = f32[4,512,128]{2,1,0:T(8,128)S(1)} fusion(f32[4,512,128]{2,1,0:T(8,128)S(1)} %get-tuple-element.372, s32[]{:T(128)} %get-tuple-element.369, bf16[128,16384]{1,0:T(8,128)(2,1)S(1)} %copy-done.2, bf16[64,8,128,128]{3,2,1,0:T(8,128)(2,1)} %bitcast.167), kind=kOutput, calls=%fused_computation.22.clone.1 | convolution fusion | flops 2147483648 | bytes 21233668 | tf_op jit(solution)/shard_map/while/body/eval_jaxpr/dot_general | solution.py:118
  529.9 10.3 %fusion.131 = bf16[64,8,128,128]{3,1,2,0:T(8,128)(2,1)} fusion(f32[16384]{0:T(1024)S(1)} %get-tuple-element.390, bf16[128,16384]{1,0:T(8,128)(2,1)} %get-tuple-element.389, bf16[4,512,128]{2,1,0:T(8,128)(2,1)S(1)} %get-tuple-element.386, s32[]{:T(128)} %get-tuple-element.369), kind=kOutput, calls=%fused_computation.20.clone.1 | convolution fusion | flops 2164260864 | bytes 21168132 | tf_op jit(solution)/shard_map/while/body/eval_jaxpr/dot_general | solution.py:78
  540.2 9.8 %copy.63 = bf16[64,8,128,128]{3,2,1,0:T(8,128)(2,1)S(1)} copy(bf16[64,8,128,128]{3,1,2,0:T(8,128)(2,1)} %fusion.131) | data formatting | bytes 33554432 | tf_op jit(solution)/shard_map/while
  550.0 4.4 fusion.132
  555.2 12.3 %convert_reduce_fusion.2 = (f32[128,128]{1,0:T(8,128)S(1)}, bf16[512,128,128]{2,1,0:T(8,128)(2,1)}) fusion(f32[512,128]{1,0:T(8,128)S(1)} %get-tuple-element.331, f32[512,128]{1,0:T(8,128)S(1)} %get-tuple-element.332), kind=kLoop, calls=%fused_computation.12.clone.1 | loop fusion | flops 33538048 | bytes 17367040 | tf_op jit(solution)/shard_map/while/body/eval_jaxpr/reduce_sum | solution.py:124
  567.5 22.6 %convolution_add_fusion.6 = f32[128,16384]{1,0:T(8,128)} fusion(bf16[64,8,128,128]{3,2,1,0:T(8,128)(2,1)} %bitcast.166, f32[128,16384]{1,0:T(8,128)} %get-tuple-element.370, pred[]{:T(512)S(6)} %compare.7, bf16[4,512,128]{2,1,0:T(8,128)(2,1)S(1)} %get-tuple-element.386, s32[]{:T(128)} %get-tuple-element.369), kind=kOutput, calls=%fused_computation.14.clone.1 | convolution fusion | flops 2151677952 | bytes 33685508 | tf_op jit(solution)/shard_map/while/body/eval_jaxpr/dot_general | solution.py:121
  590.1 21.1 %fusion.130 = f32[4,512,128]{2,1,0:T(8,128)S(1)} fusion(f32[4,512,128]{2,1,0:T(8,128)S(1)} %get-tuple-element.372, s32[]{:T(128)} %get-tuple-element.369, bf16[128,16384]{1,0:T(8,128)(2,1)S(1)} %copy-done.2, bf16[64,8,128,128]{3,2,1,0:T(8,128)(2,1)} %bitcast.167), kind=kOutput, calls=%fused_computation.22.clone.1 | convolution fusion | flops 2147483648 | bytes 21233668 | tf_op jit(solution)/shard_map/while/body/eval_jaxpr/dot_general | solution.py:118
  611.2 10.3 %fusion.131 = bf16[64,8,128,128]{3,1,2,0:T(8,128)(2,1)} fusion(f32[16384]{0:T(1024)S(1)} %get-tuple-element.390, bf16[128,16384]{1,0:T(8,128)(2,1)} %get-tuple-element.389, bf16[4,512,128]{2,1,0:T(8,128)(2,1)S(1)} %get-tuple-element.386, s32[]{:T(128)} %get-tuple-element.369), kind=kOutput, calls=%fused_computation.20.clone.1 | convolution fusion | flops 2164260864 | bytes 21168132 | tf_op jit(solution)/shard_map/while/body/eval_jaxpr/dot_general | solution.py:78
  621.5 9.8 %copy.63 = bf16[64,8,128,128]{3,2,1,0:T(8,128)(2,1)S(1)} copy(bf16[64,8,128,128]{3,1,2,0:T(8,128)(2,1)} %fusion.131) | data formatting | bytes 33554432 | tf_op jit(solution)/shard_map/while
  631.3 4.4 fusion.132
  646.1 38.1 %all-reduce.4 = (f32[16,128]{1,0:T(8,128)}, f32[128]{0:T(128)}, f32[384]{0:T(512)}, f32[384]{0:T(512)}) all-reduce(f32[16,128]{1,0:T(8,128)S(1)} %convolution_bitcast_fusion.2, f32[128]{0:T(128)S(1)} %get-tuple-element.212, f32[384]{0:T(512)S(1)} %get-tuple-element.171, ...), channel_id=1, replica_groups=mesh['batch'=4,'edge'=8] {'batch','edge'}, use_global_device_ids=true, to_apply=%region_7.9 | all-reduce | flops 2944 | bytes 23552 | tf_op jit(solution)/shard_map/psum | solution.py:152
  685.4 15.2 %reduce-scatter.5.cloned.1.call-done = bf16[128,128]{1,0:T(8,128)(2,1)} async-done(((bf16[1024,128]{1,0:T(8,128)(2,1)}), bf16[128,128]{1,0:T(8,128)(2,1)}) %reduce-scatter.5.cloned.1.call-update) | async-done | bytes 32784 | tf_op jit(solution)/shard_map/reduce_scatter | solution.py:145
  702.3 191.8 %all-reduce.8.cloned.1.call-done = (f32[128,16384]{1,0:T(8,128)}, f32[16384]{0:T(1024)}, f32[128,384]{1,0:T(8,128)}, f32[128,384]{0,1:T(8,128)}) async-done(((f32[128,16384]{1,0:T(8,128)}, f32[16384]{0:T(1024)}, f32[128,384]{1,0:T(8,128)}, f32[128,384]{0,1:T(8,128)}), (f32[128,16384]{1,0:T(8,128)}, f32[16384]{0:T(1024)}, f32[128,384]{1,0:T(8,128)}, f32[128,384]{0,1:T(8,128)})) %all-reduce.8.cloned.1.call-update) | async-done | bytes 8847376 | tf_op jit(solution)/shard_map/psum | solution.py:152
  895.8 7.6 copy.92
  (148 shorter events, 30.5 us)
Async XLA Ops:
  7.2 252.7 %copy-start = (bf16[128,384]{1,0:T(8,128)(2,1)S(1)}, bf16[128,384]{1,0:T(8,128)(2,1)}, u32[]{:S(2)}) copy-start(bf16[128,384]{1,0:T(8,128)(2,1)} %param.31) | copy-start | bytes 294916
  7.2 252.7 %reduce-scatter.3.cloned.1.call-start = ((), (), s32[]{:S(2)}) async-start(), calls=%async_computation.2 | async-start | bytes 589824 | tf_op jit(solution)/shard_map/reduce_scatter | solution.py:86
  31.0 17.2 %copy-start.29 = (s32[1,2048]{1,0:T(1,128)S(1)}, s32[1,2048]{1,0:T(1,128)}, u32[]{:S(2)}) copy-start(s32[1,2048]{1,0:T(1,128)} %param.26) | copy-start | bytes 24580
  31.0 17.3 %copy-start.15 = (bf16[1,128,128]{2,1,0:T(8,128)(2,1)S(1)}, bf16[1,128,128]{2,1,0:T(8,128)(2,1)}, u32[]{:S(2)}) copy-start(bf16[1,128,128]{2,1,0:T(8,128)(2,1)} %param.21) | copy-start | bytes 98308
  31.0 48.0 %copy-start.27 = (s32[1,2048]{1,0:T(1,128)S(1)}, s32[1,2048]{1,0:T(1,128)}, u32[]{:S(2)}) copy-start(s32[1,2048]{1,0:T(1,128)} %param.24) | copy-start | bytes 24580
  39.6 41.1 %copy-start.34 = (bf16[128]{0:T(256)(128)(2,1)S(1)}, bf16[128]{0:T(256)(128)(2,1)}, u32[]{:S(2)}) copy-start(bf16[128]{0:T(256)(128)(2,1)} %param.28) | copy-start | bytes 772
  39.6 41.1 %copy-start.25 = (bf16[16384]{0:T(1024)(128)(2,1)S(1)}, bf16[16384]{0:T(1024)(128)(2,1)}, u32[]{:S(2)}) copy-start(bf16[16384]{0:T(1024)(128)(2,1)} %param.30) | copy-start | bytes 98308
  39.6 41.1 %copy-start.22 = (bf16[1,2048,16]{1,2,0:T(8,128)(2,1)S(1)}, bf16[1,2048,16]{1,2,0:T(8,128)(2,1)}, u32[]{:S(2)}) copy-start(bf16[1,2048,16]{1,2,0:T(8,128)(2,1)} %param.22) | copy-start | bytes 196612
  39.6 41.1 %copy-start.30 = (bf16[16,128]{1,0:T(8,128)(2,1)S(1)}, bf16[16,128]{1,0:T(8,128)(2,1)}, u32[]{:S(2)}) copy-start(bf16[16,128]{1,0:T(8,128)(2,1)} %param.27) | copy-start | bytes 12292
  82.2 115.7 %copy-start.26 = (s32[1,2048]{1,0:T(1,128)S(1)}, s32[1,2048]{1,0:T(1,128)}, u32[]{:S(2)}) copy-start(s32[1,2048]{1,0:T(1,128)} %param.25) | copy-start | bytes 24580
  82.2 118.4 %copy-start.32 = (bf16[384]{0:T(512)(128)(2,1)S(1)}, bf16[384]{0:T(512)(128)(2,1)}, u32[]{:S(2)}) copy-start(bf16[384]{0:T(512)(128)(2,1)} %param.33) | copy-start | bytes 2308
  82.2 118.4 %copy-start.33 = (bf16[384]{0:T(512)(128)(2,1)S(1)}, bf16[384]{0:T(512)(128)(2,1)}, u32[]{:S(2)}) copy-start(bf16[384]{0:T(512)(128)(2,1)} %param.34) | copy-start | bytes 2308
  82.2 118.4 %copy-start.17 = (bf16[128,384]{1,0:T(8,128)(2,1)S(1)}, bf16[128,384]{1,0:T(8,128)(2,1)}, u32[]{:S(2)}) copy-start(bf16[128,384]{1,0:T(8,128)(2,1)} %param.32) | copy-start | bytes 294916
  197.9 63.0 %copy-start.19 = (bf16[1,128,128]{2,1,0:T(8,128)(2,1)S(1)}, bf16[1,128,128]{2,1,0:T(8,128)(2,1)}, u32[]{:S(2)}) copy-start(bf16[1,128,128]{2,1,0:T(8,128)(2,1)} %param.35) | copy-start | bytes 98308
  200.5 500.1 %reduce-scatter.5.cloned.1.call-start = ((), (), s32[]{:S(2)}) async-start(), calls=%async_computation.3 | async-start | bytes 294912 | tf_op jit(solution)/shard_map/reduce_scatter | solution.py:145
  261.6 33.5 %copy-start.8 = (f32[128,128]{1,0:T(8,128)}, f32[128,128]{1,0:T(8,128)S(1)}, u32[]{:S(2)}) copy-start(f32[128,128]{1,0:T(8,128)S(1)} %get-tuple-element.215) | copy-start | bytes 196612
  261.6 33.6 %copy-start.13 = (f32[128,128]{1,0:T(8,128)}, f32[128,128]{1,0:T(8,128)S(1)}, u32[]{:S(2)}) copy-start(f32[128,128]{1,0:T(8,128)S(1)} %get-tuple-element.217) | copy-start | bytes 196612
  262.3 33.0 %copy-start.4 = (f32[128,128]{1,0:T(8,128)}, f32[128,128]{1,0:T(8,128)S(1)}, u32[]{:S(2)}) copy-start(f32[128,128]{1,0:T(8,128)S(1)} %get-tuple-element.223) | copy-start | bytes 196612
  262.3 33.0 %copy-start.6 = (f32[128,128]{1,0:T(8,128)}, f32[128,128]{1,0:T(8,128)S(1)}, u32[]{:S(2)}) copy-start(f32[128,128]{1,0:T(8,128)S(1)} %get-tuple-element.227) | copy-start | bytes 196612
  295.2 341.4 %copy-start.28 = (s32[1,2048]{1,0:T(1,128)S(1)}, s32[1,2048]{1,0:T(1,128)}, u32[]{:S(2)}) copy-start(s32[1,2048]{1,0:T(1,128)} %param.24) | copy-start | bytes 24580
  295.2 344.8 %copy-start.16 = (bf16[1,128,128]{2,1,0:T(8,128)(2,1)S(1)}, bf16[1,128,128]{2,1,0:T(8,128)(2,1)}, u32[]{:S(2)}) copy-start(bf16[1,128,128]{2,1,0:T(8,128)(2,1)} %param.21) | copy-start | bytes 98308
  295.2 346.7 %copy-start.9 = (f32[128,128]{1,0:T(8,128)S(1)}, f32[128,128]{1,0:T(8,128)}, u32[]{:S(2)}) copy-start(f32[128,128]{1,0:T(8,128)} %copy-done.8) | copy-start | bytes 196612
  313.6 12.4 %copy-start.11 = (bf16[4,512,128]{2,1,0:T(8,128)(2,1)}, bf16[4,512,128]{2,1,0:T(8,128)(2,1)S(1)}, u32[]{:S(2)}) copy-start(bf16[4,512,128]{2,1,0:T(8,128)(2,1)S(1)} %get-tuple-element.387) | copy-start | bytes 1572868 | tf_op jit(solution)/shard_map/while
  326.0 20.2 %copy-start.2 = (bf16[128,16384]{1,0:T(8,128)(2,1)S(1)}, bf16[128,16384]{1,0:T(8,128)(2,1)}, u32[]{:S(2)}) copy-start(bf16[128,16384]{1,0:T(8,128)(2,1)} %get-tuple-element.389) | copy-start | bytes 12582916 | tf_op jit(solution)/shard_map/while
  387.4 5.1 copy-start.12
  392.5 12.4 %copy-start.11 = (bf16[4,512,128]{2,1,0:T(8,128)(2,1)}, bf16[4,512,128]{2,1,0:T(8,128)(2,1)S(1)}, u32[]{:S(2)}) copy-start(bf16[4,512,128]{2,1,0:T(8,128)(2,1)S(1)} %get-tuple-element.387) | copy-start | bytes 1572868 | tf_op jit(solution)/shard_map/while
  404.9 22.6 %copy-start.2 = (bf16[128,16384]{1,0:T(8,128)(2,1)S(1)}, bf16[128,16384]{1,0:T(8,128)(2,1)}, u32[]{:S(2)}) copy-start(bf16[128,16384]{1,0:T(8,128)(2,1)} %get-tuple-element.389) | copy-start | bytes 12582916 | tf_op jit(solution)/shard_map/while
  468.7 5.1 copy-start.12
  473.8 12.4 %copy-start.11 = (bf16[4,512,128]{2,1,0:T(8,128)(2,1)}, bf16[4,512,128]{2,1,0:T(8,128)(2,1)S(1)}, u32[]{:S(2)}) copy-start(bf16[4,512,128]{2,1,0:T(8,128)(2,1)S(1)} %get-tuple-element.387) | copy-start | bytes 1572868 | tf_op jit(solution)/shard_map/while
  486.2 22.6 %copy-start.2 = (bf16[128,16384]{1,0:T(8,128)(2,1)S(1)}, bf16[128,16384]{1,0:T(8,128)(2,1)}, u32[]{:S(2)}) copy-start(bf16[128,16384]{1,0:T(8,128)(2,1)} %get-tuple-element.389) | copy-start | bytes 12582916 | tf_op jit(solution)/shard_map/while
  550.0 5.1 copy-start.12
  555.1 12.4 %copy-start.11 = (bf16[4,512,128]{2,1,0:T(8,128)(2,1)}, bf16[4,512,128]{2,1,0:T(8,128)(2,1)S(1)}, u32[]{:S(2)}) copy-start(bf16[4,512,128]{2,1,0:T(8,128)(2,1)S(1)} %get-tuple-element.387) | copy-start | bytes 1572868 | tf_op jit(solution)/shard_map/while
  567.5 22.6 %copy-start.2 = (bf16[128,16384]{1,0:T(8,128)(2,1)S(1)}, bf16[128,16384]{1,0:T(8,128)(2,1)}, u32[]{:S(2)}) copy-start(bf16[128,16384]{1,0:T(8,128)(2,1)} %get-tuple-element.389) | copy-start | bytes 12582916 | tf_op jit(solution)/shard_map/while
  631.3 5.1 copy-start.12
  636.6 7.3 copy-start.3
  636.6 7.3 copy-start.5
  636.6 7.3 copy-start.7
  636.6 7.3 copy-start.10
  636.7 9.0 copy-start.23
  640.0 44.2 %copy-start.31 = (bf16[16,128]{1,0:T(8,128)(2,1)S(1)}, bf16[16,128]{1,0:T(8,128)(2,1)}, u32[]{:S(2)}) copy-start(bf16[16,128]{1,0:T(8,128)(2,1)} %param.27) | copy-start | bytes 12292
  640.0 60.6 %copy-start.14 = (f32[128,128]{1,0:T(8,128)S(1)}, f32[128,128]{1,0:T(8,128)}, u32[]{:S(2)}) copy-start(f32[128,128]{1,0:T(8,128)} %copy-done.13) | copy-start | bytes 196612
  640.0 60.6 %copy-start.18 = (bf16[128,384]{1,0:T(8,128)(2,1)S(1)}, bf16[128,384]{1,0:T(8,128)(2,1)}, u32[]{:S(2)}) copy-start(bf16[128,384]{1,0:T(8,128)(2,1)} %param.32) | copy-start | bytes 294916
  640.0 60.6 %copy-start.20 = (bf16[1,128,128]{2,1,0:T(8,128)(2,1)S(1)}, bf16[1,128,128]{2,1,0:T(8,128)(2,1)}, u32[]{:S(2)}) copy-start(bf16[1,128,128]{2,1,0:T(8,128)(2,1)} %param.35) | copy-start | bytes 98308
  640.0 254.0 %all-reduce.8.cloned.1.call-start = ((), (), s32[]{:S(2)}) async-start(), calls=%async_computation.4 | async-start | bytes 17694720 | tf_op jit(solution)/shard_map/psum | solution.py:152
  895.8 9.0 copy-start.1
  895.8 7.6 copy-start.24
  895.8 8.3 copy-start.21
Sparse Core Ops, SparseCore 0:
  200.6 59.1 reduce-scatter.2
  640.1 60.4 reduce-scatter.4
  709.1 184.8 all-reduce.7
where the time goes:
time: 922 us; the launch traced here: 912 us
  matrix products  326 us (35%)
  waiting for transfers between devices  266 us (29%)
  blocking collectives  122 us (13%)
  local copies, waits for them, and re-layouts  107 us (12%)
  other arithmetic  57.1 us (6%)
  loops' own time  18.9 us (2%)
  between operations  14.6 us (2%)
    psum x1, waiting for transfers between devices, per_device(): lax.psum((grad_w1, grad_b1, grad_w2, grad_b2, grad_wi, grad_wh, grad_bi,...  192 us
    dot_general x4, matrix products, backward_core(): lax.dot_general(latent, flat, (((0,), (0,)), ((), ())), preferred_element...  88 us
    dot_general x4, matrix products, backward_core(): lax.dot_general(flat, w_edge_out, (((1,), (1,)), ((), ())), preferred_ele...  84.3 us
    dot_general x8, matrix products, expand(): jnp.dot(latent, w_edge_out, preferred_element_type=jnp.float32) + bias_out  82.5 us
    while x32, local copies, waits for them, and re-layouts  78.3 us
    reduce_scatter x1, waiting for transfers between devices, per_device(): lax.psum_scatter(spread_by(target_ids, messages, lax.axis_size('edge') *...  59 us
    reduce_sum x4, other arithmetic, backward_core(): grad_bias = grad_bias + jnp.sum(flat.astype(jnp.float32), axis=0)  49.2 us
    psum x1, blocking collectives, per_device(): lax.psum((grad_w1, grad_b1, grad_w2, grad_b2, grad_wi, grad_wh, grad_bi,...  38.1 us
  transfers between devices with their start and end apart: 3, of which 3 were waited for; matrix products, arithmetic and copies ran while one was open for 1% of the time, Pallas kernels for 0%

commit v1 on v0

--- a/solution.py
+++ b/solution.py
@@ -1,7 +1,806 @@
+import functools
+
 import jax
 import jax.numpy as jnp
 from jax import lax
+from jax.experimental import pallas as pl
+from jax.experimental.pallas import tpu as pltpu
 from jax.sharding import PartitionSpec as P
+
+F32 = jnp.float32
+BF16 = jnp.bfloat16
+H = 128
+CAP = 64
+GROUP = 16
+PIECES = 32
+UNITS = H // PIECES
+EXTRA = 32
+VMEM_LIMIT = 60 * 1024 * 1024
+BACK = 4
+UNROLL = 1
+AGG = 16
+
+
+def nn(a, b):
+    return lax.dot_general(a, b, (((1,), (0,)), ((), ())), preferred_element_type=F32)
+
+
+def nt(a, b):
+    return lax.dot_general(a, b, (((1,), (1,)), ((), ())), preferred_element_type=F32)
+
+
+def eye(n):
+    rows = lax.broadcasted_iota(jnp.int32, (n, n), 0)
+    cols = lax.broadcasted_iota(jnp.int32, (n, n), 1)
+    return jnp.where(rows == cols, 1.0, 0.0).astype(BF16)
+
+
+def one_hot_rows(rel, count):
+    rel = jnp.clip(rel, -1, count).astype(F32).astype(BF16)
+    rows = lax.broadcasted_iota(jnp.int32, (count, rel.shape[1]), 0).astype(F32).astype(BF16)
+    return jnp.where(rows == rel, jnp.ones((), BF16), jnp.zeros((), BF16))
+
+
+def slot_hots(slot, count):
+    return one_hot_rows(jnp.right_shift(slot, 7), count), one_hot_rows(jnp.bitwise_and(slot, H - 1), H)
+
+
+def sort_kernel(shape, target_ref, source_ref, mask_ref, label_ref, feats_ref, states_ref, out_ref, slot_ref, data_ref):
+    holders, own, groups = shape
+    blocks = groups // 2
+    edges = target_ref.shape[1]
+    target = target_ref[...]
+    owner = jnp.right_shift(target, own.bit_length() - 1)
+    local = jnp.bitwise_and(target, own - 1)
+    bucket = owner * groups + jnp.right_shift(local, 4)
+    bucket = jnp.where(mask_ref[...] != 0, bucket, -1)
+    buckets = holders * groups
+
+    block = 256
+    rows = lax.broadcasted_iota(jnp.int32, (block, block), 0)
+    cols = lax.broadcasted_iota(jnp.int32, (block, block), 1)
+    upto = jnp.where(rows <= cols, 1.0, 0.0).astype(BF16)
+    numbers = lax.broadcasted_iota(jnp.int32, (buckets, block), 0)
+    carry = jnp.zeros((buckets, 1), F32)
+    slots = []
+    for b in range(edges // block):
+        here = bucket[:, b * block : (b + 1) * block]
+        hot = numbers == here
+        within = nn(hot.astype(F32).astype(BF16), upto) + carry
+        rank = jnp.sum(jnp.where(hot, within - 1.0, 0.0), axis=0, keepdims=True).astype(jnp.int32)
+        carry = within[:, block - 1 : block]
+        slots.append(jnp.where((here >= 0) & (rank < CAP), here * CAP + rank, -1))
+    worst = jnp.max(carry, axis=0, keepdims=True)
+    flag = jnp.where(worst > CAP, 1.0, 0.0)
+    slot = jnp.concatenate(slots, axis=1)
+    slot_ref[...] = slot
+
+    data_ref[16:32, :] = jnp.zeros((16, edges), F32)
+    data_ref[0:16, :] = feats_ref[...].astype(F32)
+    source = source_ref[...]
+    data_ref[16:17, :] = jnp.right_shift(source, 6).astype(F32)
+    data_ref[17:18, :] = jnp.bitwise_and(source, 63).astype(F32)
+    data_ref[18:19, :] = (local + 1).astype(F32)
+    data = data_ref[...].astype(BF16)
+
+    tags = []
+    for t in range(own // H):
+        label = label_ref[:, t * H : (t + 1) * H]
+        tags += [jnp.right_shift(label, 6).astype(F32), jnp.bitwise_and(label, 63).astype(F32)]
+    tags.append(jnp.broadcast_to(flag, (1, H)))
+    tags.append(jnp.zeros((16 - 3 * blocks - len(tags), H), F32))
+    high, low = slot_hots(slot, holders * blocks)
+    together = min(4, holders)
+    for s0 in range(0, holders, together):
+        part = high[s0 * blocks : (s0 + together) * blocks, :]
+        spread = (part[:, None, :] * data[None, :, :]).reshape(together * blocks * 32, edges)
+        moved = nt(spread, low)
+        for n in range(together):
+            out = out_ref.at[s0 + n]
+            out[0:own, :] = states_ref[...]
+            ids = []
+            for q in range(blocks):
+                at = (n * blocks + q) * 32
+                out[own + 16 * q : own + 16 * (q + 1), :] = moved[at : at + 16, :].astype(BF16)
+                ids.append(moved[at + 16 : at + 19, :])
+            out[own + 16 * blocks : own + 16 * blocks + 16, :] = jnp.concatenate(ids + tags, axis=0).astype(BF16)
+
+
+def swap_rows(outer, inner, flip=None):
+    n = outer * inner
+    rows = lax.broadcasted_iota(jnp.int32, (n, n), 0)
+    cols = lax.broadcasted_iota(jnp.int32, (n, n), 1)
+    number = rows % inner
+    if flip is not None:
+        number = jnp.bitwise_xor(number, flip)
+    return jnp.where(number * outer + rows // inner == cols, 1.0, 0.0).astype(BF16)
+
+
+def split_kernel(w_ref, out_ref):
+    order = swap_rows(16, 16)
+    for ib in range(0, H, 32):
+        sides = []
+        for half in range(2):
+            rows = [w_ref[:, (ib + 16 * half + i) * H : (ib + 16 * half + i + 1) * H] for i in range(16)]
+            sides.append(jnp.concatenate(rows, axis=0))
+        moved = nn(order, jnp.concatenate(sides, axis=1)).astype(BF16)
+        for half in range(2):
+            at = ib + 16 * half
+            out_ref[:, at : at + 16, :] = moved[:, half * H : (half + 1) * H].reshape(16, 16, H)
+
+
+def front_kernel(shape, chunks, *refs):
+    holders, own, groups = shape
+    blocks = groups // 2
+    refs = list(refs)
+    take = lambda n: [refs.pop(0) for _ in range(n)]
+    piece_ref, given, states_ref, own_label_ref, t_in, b2_ref, w1_ref, b1_ref, wi_ref, wh_ref, bi_ref, bh_ref, cot_ref = take(13)
+    new_ref, direct_ref, d_ref, lat_out, near_out, meta_out, flag_ref = take(7)
+    keeps_out = take(len(chunks))
+    sends_out = take(len(chunks))
+    table_ref, p_ref, sum_ref, small_ref, dt_ref, rows_ref, bias_ref, extra_ref, t_ref, lat_ref, near_ref, meta_ref = take(12)
+    keeps = take(len(chunks))
+    sends = take(len(chunks))
+    (sems,) = refs
+    waiting = []
+
+    def copy(source, target):
+        moving = pltpu.make_async_copy(source, target, sems.at[len(waiting)])
+        moving.start()
+        waiting.append(moving)
+        return moving
+
+    t_copy = copy(t_in, t_ref)
+
+    nodes = holders * own
+    lanes = holders * CAP
+    ident = eye(H)
+    tags_at = own + 16 * blocks
+
+    flag = jnp.zeros((1, 1), F32)
+    for s in range(holders):
+        tags = given[s, tags_at : tags_at + 16, :].astype(F32)
+        flag = jnp.maximum(flag, tags[3 * blocks + 2 * (own // H) : 3 * blocks + 2 * (own // H) + 1, 0:1])
+        for t in range(own // H):
+            at = s * own + t * H
+            table_ref[0:H, at : at + H] = nt(ident, given[s, t * H : (t + 1) * H, :]).astype(BF16)
+            both = tags[3 * blocks + 2 * t : 3 * blocks + 2 * t + 2, :]
+            table_ref[H : H + 16, at : at + H] = jnp.concatenate([both, jnp.zeros((14, H), F32)], axis=0).astype(BF16)
+    flag_ref[...] = jnp.broadcast_to(flag, flag_ref.shape)
+    for t in range(own // H):
+        label = own_label_ref[:, t * H : (t + 1) * H]
+        label = jnp.concatenate([jnp.right_shift(label, 6), jnp.bitwise_and(label, 63)], axis=0).astype(F32)
+        cols = nt(ident, jnp.concatenate([label, jnp.zeros((14, H), F32)], axis=0).astype(BF16))
+        small_ref[t * H : (t + 1) * H, 0:1] = cols[:, 0:1] * 64.0 + cols[:, 1:2]
+
+    low_lanes = lax.broadcasted_iota(jnp.int32, (24, H), 1) < CAP
+    for q in range(blocks):
+        for s in range(0, holders, 2):
+            parts = []
+            for n in range(2):
+                feats = given[s + n, own + 16 * q : own + 16 * (q + 1), :].astype(F32)
+                ids = given[s + n, tags_at : tags_at + 16, :].astype(F32)[3 * q : 3 * q + 3, :]
+                parts.append(jnp.concatenate([feats, ids, jnp.zeros((5, H), F32)], axis=0))
+            first, second = parts
+            at = slice(s // 2 * H, (s // 2 + 1) * H)
+            meta_ref[2 * q, 0:24, at] = jnp.where(low_lanes, first, pltpu.roll(second, CAP, 1))
+            meta_ref[2 * q + 1, 0:24, at] = jnp.where(low_lanes, pltpu.roll(first, CAP, 1), second)
+
+    w1 = nt(ident, w1_ref[...]).astype(BF16)
+    b1 = nt(ident, jnp.broadcast_to(b1_ref[...].astype(F32), (16, H)).astype(BF16))[:, 0:1]
+
+    def group_step(g, unused):
+        data = meta_ref[g, 0:24, :]
+        source = (data[16:17, :] * 64.0 + data[17:18, :]).astype(jnp.int32)
+        meta_ref[g, 19:20, :] = source.astype(F32)
+        picked = jnp.zeros((H + 16, lanes), F32)
+        for c in range(0, nodes, 256):
+            picked = picked + nn(table_ref[:, c : c + 256], one_hot_rows(source - c, 256))
+        near = picked[0:H, :].astype(BF16)
+        label = picked[H : H + 1, :] * 64.0 + picked[H + 1 : H + 2, :]
+        inside = data[18:19, :] - 1.0 - (g * GROUP).astype(F32)
+        numbers = lax.broadcasted_iota(jnp.int32, (GROUP, lanes), 0).astype(F32)
+        own_label = small_ref[pl.ds(pl.multiple_of(g * GROUP, GROUP), GROUP), 0:1]
+        member = jnp.where((numbers == inside) & (own_label == label), 1.0, 0.0)
+        meta_ref[g, 32 : 32 + GROUP, :] = member
+        member = member.astype(BF16)
+        before = nn(w1, data[0:16, :].astype(BF16)) + b1
+        latent = (before / (1.0 + jnp.exp(-before))).astype(BF16)
+        lat_ref[g] = latent
+        near_ref[g] = near
+        spread = (latent[:, None, :] * member[None, :, :]).reshape(H * GROUP, lanes)
+        at = pl.ds(pl.multiple_of(g * GROUP, GROUP), GROUP)
+        p_ref[:, at, :] = nt(spread, near).reshape(H, GROUP, H).astype(BF16)
+        sum_ref[at, :] = nt(member, near)
+        return unused
+
+    lax.fori_loop(0, groups, group_step, 0, unroll=UNROLL)
+    copy(lat_ref, lat_out)
+    copy(near_ref, near_out)
+    copy(meta_ref, meta_out)
+
+    def agg_step(n, total):
+        left = jnp.concatenate([p_ref[n * AGG + m] for m in range(AGG)], axis=1)
+        right = jnp.concatenate([t_ref[n * AGG + m] for m in range(AGG)], axis=1)
+        return total + nt(left, right)
+
+    total = nt(sum_ref[...].astype(BF16), b2_ref[...])
+    t_copy.wait()
+    total = lax.fori_loop(0, H // AGG, agg_step, total)
+
+    mixed = total.astype(BF16)
+    prior = states_ref[...]
+    prior_f = prior.astype(F32)
+    cot = cot_ref[...].astype(F32)
+    wi, wh = wi_ref[...], wh_ref[...]
+    gi = nn(mixed, wi) + bi_ref[...]
+    gh = nn(prior, wh) + bh_ref[...]
+    r = jax.nn.sigmoid(gi[:, 0:H] + gh[:, 0:H])
+    u = jax.nn.sigmoid(gi[:, H : 2 * H] + gh[:, H : 2 * H])
+    n = jnp.tanh(gi[:, 2 * H :] + r * gh[:, 2 * H :])
+    new_ref[...] = ((1.0 - u) * n + u * prior_f).astype(BF16)
+    d_pre = (1.0 - u) * cot * (1.0 - n * n)
+    d_r = d_pre * gh[:, 2 * H :] * r * (1.0 - r)
+    d_u = (prior_f - n) * cot * u * (1.0 - u)
+    d_gi = jnp.concatenate([d_r, d_u, d_pre], axis=1)
+    d_gh = jnp.concatenate([d_r, d_u, d_pre * r], axis=1)
+
+    def halves(x):
+        high = x.astype(BF16)
+        return high, (x - high.astype(F32)).astype(BF16)
+
+    def twice(x):
+        return jnp.concatenate([x, x], axis=1)
+
+    gi_high, gi_low = halves(d_gi)
+    gh_high, gh_low = halves(d_gh)
+    d_agg = nt(jnp.concatenate([gi_high, gi_low], axis=1), twice(wi)).astype(BF16)
+    d_ref[...] = d_agg
+    dt_ref[...] = nt(ident, d_agg).astype(BF16)
+    direct_ref[...] = u * cot + nt(jnp.concatenate([gh_high, gh_low], axis=1), twice(wh))
+
+    piece_me = piece_ref[0]
+    for rel in list(range(PIECES // 2, PIECES)) + list(range(PIECES // 2)):
+        k0 = jnp.bitwise_xor(piece_me, rel) * UNITS
+        for m in range(0, UNITS, 2):
+            out = nn(dt_ref[...], jnp.concatenate([p_ref[k0 + m], p_ref[k0 + m + 1]], axis=1)).astype(BF16)
+            for c, chunk in enumerate(chunks):
+                dest = sends[c] if rel >= PIECES // 2 else keeps[c]
+                for h in range(2):
+                    rows = slice((m + h) * chunk.rows, (m + h + 1) * chunk.rows)
+                    dest[chunk.place(rel), rows, :] = out[chunk.first : chunk.first + chunk.rows, h * H : (h + 1) * H]
+        if rel == PIECES - 1:
+            for c in range(len(chunks) - 1):
+                copy(sends[c], sends_out[c])
+        if rel == PIECES // 2 - 1:
+            for c in range(len(chunks) - 1):
+                copy(keeps[c], keeps_out[c])
+
+    mixed_t = nt(ident, mixed).astype(BF16)
+    prior_t = nt(ident, prior).astype(BF16)
+    from_input = nn(twice(mixed_t), jnp.concatenate([gi_high, gi_low], axis=0))
+    from_state = nn(twice(prior_t), jnp.concatenate([gh_high, gh_low], axis=0))
+    for t in range(3):
+        rows_ref[t] = from_input[:, t * H : (t + 1) * H]
+        rows_ref[3 + t] = from_state[:, t * H : (t + 1) * H]
+    rows_ref[6] = nn(dt_ref[...], sum_ref[...].astype(BF16))
+    bias_ref[...] = jnp.zeros_like(bias_ref)
+    for n, part in enumerate((d_gi, d_gh)):
+        part = jnp.sum(part, axis=0, keepdims=True)
+        for t in range(3):
+            bias_ref[3 * n + t : 3 * n + t + 1, :] = part[:, t * H : (t + 1) * H]
+    extra_ref[...] = jnp.zeros_like(extra_ref)
+    last = chunks[-1]
+    for rel in range(PIECES):
+        p = jnp.bitwise_xor(piece_me, rel)
+        for t in range(7):
+            extra_ref[UNITS * t : UNITS * (t + 1), :] = rows_ref[t, pl.ds(p * UNITS, UNITS), :]
+        extra_ref[28:29, :] = bias_ref[pl.ds(p, 1), :]
+        dest = sends[-1] if rel >= PIECES // 2 else keeps[-1]
+        dest[last.place(rel), UNITS * last.rows : last.height, :] = extra_ref[...].astype(BF16)
+    copy(sends[-1], sends_out[-1])
+    copy(keeps[-1], keeps_out[-1])
+    for moving in waiting[1:]:
+        moving.wait()
+
+
+def spread_kernel(shape, d_ref, t_ref, b2_ref, wide_ref, bias_ref, dp_ref):
+    holders, own, groups = shape
+    d = d_ref[...]
+    bias_ref[...] = nn(d, b2_ref[...])
+    order = swap_rows(16, 16)
+    for n in range(0, 16, 2):
+        out = nn(d, jnp.concatenate([t_ref[n], t_ref[n + 1]], axis=1)).astype(BF16)
+        dp_ref[n] = out[:, :H]
+        dp_ref[n + 1] = out[:, H:]
+    for g in range(0, groups, 2):
+        sides = [dp_ref[:, (g + n) * GROUP : (g + n + 1) * GROUP, :].reshape(256, H) for n in range(2)]
+        moved = nn(order, jnp.concatenate(sides, axis=1)).astype(BF16)
+        for n in range(2):
+            for v in range(GROUP):
+                wide_ref[g + n, :, v * H : (v + 1) * H] = moved[v * 16 : (v + 1) * 16, n * H : (n + 1) * H]
+
+
+def back_kernel(shape, count, *refs):
+    holders, own, groups = shape
+    wide_ref, bias_ref, w1_ref, b1_ref, lat_ref, near_ref, meta_ref, part_in_ref, first_in_ref = refs[:9]
+    part_ref, first_ref, edge_ref = refs[9:]
+    nodes = holders * own
+    lanes = holders * CAP
+    ident = eye(H)
+    part_ref[...] = part_in_ref[...]
+    w1n = w1_ref[...]
+    w1 = nt(ident, w1n).astype(BF16)
+    b1 = nt(ident, jnp.broadcast_to(b1_ref[...].astype(F32), (16, H)).astype(BF16))[:, 0:1]
+    one_row = jnp.where(lax.broadcasted_iota(jnp.int32, (16, lanes), 0) == 0, 1.0, 0.0).astype(BF16)
+
+    def group_step(g, first_total):
+        data = meta_ref[g, 0:16, :].astype(BF16)
+        source = meta_ref[g, 19:20, :].astype(jnp.int32)
+        member = meta_ref[g, 32 : 32 + GROUP, :].astype(BF16)
+        latent = lat_ref[g]
+        near = near_ref[g]
+        wide = wide_ref[g]
+        spread = (near[None, :, :] * member[:, None, :]).reshape(GROUP * H, lanes)
+        d_latent = nn(wide, spread)
+        tall = jnp.concatenate([wide[:, v * H : (v + 1) * H] for v in range(GROUP)], axis=0)
+        wide_t = nt(ident, tall).astype(BF16)
+        spread = (latent[None, :, :] * member[:, None, :]).reshape(GROUP * H, lanes)
+        d_near = nn(wide_t, spread)
+        bias_rows = bias_ref[pl.ds(pl.multiple_of(g * GROUP, GROUP), GROUP), :].astype(BF16)
+        bias_t = nt(ident, bias_rows).astype(BF16)
+        d_near = (d_near + nn(bias_t, member)).astype(BF16)
+        for c in range(0, nodes, 256):
+            part_ref[c : c + 256, :] += nt(one_hot_rows(source - c, 256), d_near)
+        before = nn(w1, data) + b1
+        gate = 1.0 / (1.0 + jnp.exp(-before))
+        d_before = (d_latent * gate * (1.0 + before * (1.0 - gate))).astype(BF16)
+        edge_ref[g] = nn(w1n, d_before)
+        return first_total + nt(jnp.concatenate([data, one_row], axis=0), d_before)
+
+    first_ref[...] = lax.fori_loop(0, count, group_step, first_in_ref[...])
+
+
+def return_kernel(shape, me_ref, part_ref, first_ref, *refs):
+    holders, own, groups = shape
+    blocks = groups // 2
+    edges, (keep_d, keep_e, send_ref, slab_ref) = refs[:-4], refs[-4:]
+    low_lanes = lax.broadcasted_iota(jnp.int32, (16, H), 1) < CAP
+    pick = lambda g, at: edges[g * len(edges) // groups][g % (groups // len(edges)), :, at]
+    for q in range(blocks):
+        for s in range(0, holders, 2):
+            at = slice(s // 2 * H, (s // 2 + 1) * H)
+            even, odd = pick(2 * q, at), pick(2 * q + 1, at)
+            slab_ref[s, 16 * q : 16 * (q + 1), :] = jnp.where(low_lanes, even, pltpu.roll(odd, CAP, 1)).astype(BF16)
+            slab_ref[s + 1, 16 * q : 16 * (q + 1), :] = jnp.where(low_lanes, pltpu.roll(even, CAP, 1), odd).astype(BF16)
+    half = holders // 2
+    for rel in range(holders):
+        h = jnp.bitwise_xor(me_ref[0], rel)
+        rows = part_ref[pl.ds(pl.multiple_of(h * own, own), own), :].astype(BF16)
+        n = rel // 2
+        if rel % 2 == 0:
+            keep_d[n] = rows
+            keep_e[n] = slab_ref[h]
+        else:
+            send_ref[n * own : (n + 1) * own, :] = rows
+            at = half * own + n * 16 * blocks
+            send_ref[at : at + 16 * blocks, :] = slab_ref[h]
+    at = half * (own + 16 * blocks)
+    send_ref[at : at + 32, :] = first_ref[...].astype(BF16)
+
+
+def gather_kernel(shape, me_ref, slot_ref, direct_ref, part_ref, slabs_ref, state_ref, edge_ref, data_ref):
+    holders, own, groups = shape
+    blocks = groups // 2
+    state_ref[...] = direct_ref[...] + part_ref[...].astype(F32)
+    for rel in range(holders):
+        h = jnp.bitwise_xor(me_ref[0], rel)
+        data_ref[pl.ds(pl.multiple_of(h * 16 * blocks, 16), 16 * blocks), :] = slabs_ref[rel]
+    edges = slot_ref.shape[1]
+    data = data_ref[...]
+    count = holders * blocks
+    block = 512
+    for b in range(edges // block):
+        high, low = slot_hots(slot_ref[:, b * block : (b + 1) * block], count)
+        high = high.astype(F32)
+        found = nn(data, low)
+        total = jnp.zeros((16, block), F32)
+        for n in range(count):
+            total = total + found[16 * n : 16 * (n + 1), :] * high[n : n + 1, :]
+        edge_ref[:, b * block : (b + 1) * block] = total
+
+
+class Chunk:
+    def __init__(self, first, rows, extra, order):
+        self.first, self.rows, self.extra, self.order = first, rows, extra, order
+        self.height = UNITS * rows + extra
+
+    def place(self, rel):
+        at = 0
+        for bit in self.order:
+            at = at * 2 + (rel >> bit & 1)
+        return at
+
+    def shape(self):
+        return (2,) * len(self.order) + (self.height, H)
+
+
+def plan(batch, edge):
+    core, x = [edge], [edge << n for n in range(1, batch.bit_length() - 1)]
+    z = [2 << n for n in reversed(range(3 - len(x)))]
+    bits = z + [1] + x + core
+    chunks = [Chunk(0, 64, 0, (3, 2, 1, 0)), Chunk(64, 64, EXTRA, (2, 3, 1, 0))]
+    device = lax.axis_index(("batch", "edge")).astype(jnp.int32)
+    piece = sum(jnp.where(device & mask != 0, 1 << n, 0) for n, mask in enumerate(bits))
+    return bits, chunks, piece.astype(jnp.int32).reshape(1)
+
+
+def swap(x, mask, devices):
+    return lax.ppermute(x, ("batch", "edge"), [(i, i ^ mask) for i in range(devices)])
+
+
+def add(terms):
+    total = terms[0].astype(F32)
+    for term in terms[1:]:
+        total = total + term.astype(F32)
+    return total.astype(BF16)
+
+
+def rounded(x):
+    return lax.reduce_precision(x.astype(F32), 8, 7).astype(BF16)
+
+
+def assemble_kernel(chunks, piece_ref, *refs):
+    count = len(chunks)
+    pairs = refs[: 2 * count]
+    w_out, wi_ref, wh_ref, b2_ref, bi_ref, bh_ref, rows_ref, extra_ref, bias_ref, order_ref, sems = refs[2 * count :]
+    me = piece_ref[0]
+    flip = jnp.bitwise_and(me, 1)
+    order_ref[...] = swap_rows(32, 2 * UNITS, flip * UNITS)
+
+    def moving(step):
+        pair = jnp.bitwise_xor(jnp.right_shift(me, 1), step)
+        rows = pl.ds(pl.multiple_of(pair * 2 * UNITS, 2 * UNITS), 2 * UNITS)
+        return pltpu.make_async_copy(rows_ref.at[step % 4], w_out.at[rows, :], sems.at[step % 4])
+
+    for step in range(PIECES // 2):
+        if step >= 4:
+            moving(step - 4).wait()
+        rel = 2 * step
+        which = rel // (PIECES // 2)
+        blocks = [pairs[2 * c + which] for c in range(count)]
+        places = [[chunk.place(rel + n) for n in range(2)] for chunk in chunks]
+        for ib in range(0, H, 64):
+            sides = []
+            for half in range(2):
+                at = ib + 32 * half
+                c = max(n for n in range(count) if chunks[n].first <= at)
+                first, rows = chunks[c].first, chunks[c].rows
+                sides.append(
+                    jnp.concatenate(
+                        [
+                            blocks[c][places[c][n], m * rows + at - first : m * rows + at - first + 32, :]
+                            for n in range(2)
+                            for m in range(UNITS)
+                        ],
+                        axis=0,
+                    )
+                )
+            moved = nn(order_ref[...], jnp.concatenate(sides, axis=1))
+            for half in range(2):
+                for i in range(32):
+                    at = (ib + 32 * half + i) * H
+                    rows_ref[step % 4, :, at : at + H] = moved[8 * i : 8 * (i + 1), half * H : (half + 1) * H]
+        moving(step).start()
+        for n in range(2):
+            start = UNITS * chunks[-1].rows
+            extra = blocks[-1][places[-1][n], start : start + EXTRA, :].astype(F32)
+            p = jnp.bitwise_xor(me, rel + n)
+            for t in range(7):
+                extra_ref[t, pl.ds(p * UNITS, UNITS), :] = extra[UNITS * t : UNITS * (t + 1), :]
+            bias_ref[pl.ds(p, 1), :] = extra[28:29, :]
+    for t in range(3):
+        wi_ref[:, t * H : (t + 1) * H] = extra_ref[t]
+        wh_ref[:, t * H : (t + 1) * H] = extra_ref[3 + t]
+        bi_ref[t * H : (t + 1) * H] = bias_ref[t : t + 1, :].reshape(H)
+        bh_ref[t * H : (t + 1) * H] = bias_ref[3 + t : 4 + t, :].reshape(H)
+    b2_ref[...] = extra_ref[6]
+    for step in range(PIECES // 2 - 4, PIECES // 2):
+        moving(step).wait()
+
+
+def vmem():
+    return pl.BlockSpec(memory_space=pltpu.VMEM)
+
+
+def anywhere():
+    return pl.BlockSpec(memory_space=pl.ANY)
+
+
+def smem():
+    return pl.BlockSpec(memory_space=pltpu.SMEM)
+
+
+def cost(us):
+    return pl.CostEstimate(flops=int(us * 1e9), bytes_accessed=int(us * 3e6), transcendentals=0)
+
+
+def params():
+    return pltpu.CompilerParams(vmem_limit_bytes=VMEM_LIMIT)
+
+
+def fast_path(batch, edge, args):
+    (states, edge_feats, molecule, source, target, edge_mask, w_edge_in, b_edge_in, w_edge_out, b_edge_out,
+     w_input, w_hidden, b_input, b_hidden, cotangent) = args
+    devices = batch * edge
+    states_here = states[0]
+    own = states_here.shape[0]
+    edges = source.shape[1]
+    holders, groups = edge, own // GROUP
+    shape = (holders, own, groups)
+    blocks = groups // 2
+    bits, chunks, piece_arr = plan(batch, edge)
+    rest = [m for m in (1 << n for n in range(devices.bit_length() - 1)) if m not in bits]
+    me_arr = lax.axis_index("edge").astype(jnp.int32).reshape(1)
+    lanes = holders * CAP
+
+    slots_out, slot = pl.pallas_call(
+        functools.partial(sort_kernel, shape),
+        name="edges_to_slots",
+        out_shape=[
+            jax.ShapeDtypeStruct((holders, own + 16 * blocks + 16, H), BF16),
+            jax.ShapeDtypeStruct((1, edges), jnp.int32),
+        ],
+        in_specs=[vmem()] * 6,
+        out_specs=[vmem()] * 2,
+        scratch_shapes=[pltpu.VMEM((32, edges), F32)],
+        compiler_params=params(),
+    )(target, source, edge_mask, molecule, jnp.swapaxes(edge_feats, 1, 2)[0], states_here)
+    given = lax.all_to_all(slots_out, "edge", 0, 0)
+
+    t_units = pl.pallas_call(
+        split_kernel,
+        name="split_weight",
+        grid=(H // 16,),
+        in_specs=[pl.BlockSpec((16, H * H), lambda i: (i, 0))],
+        out_specs=pl.BlockSpec((16, H, H), lambda i: (i, 0, 0)),
+        out_shape=jax.ShapeDtypeStruct((H, H, H), BF16),
+        compiler_params=params(),
+    )(w_edge_out)
+    b2 = b_edge_out.reshape(H, H)
+    b1 = b_edge_in.reshape(1, H)
+    half = [jax.ShapeDtypeStruct((PIECES // 2, c.height, H), BF16) for c in chunks]
+    front = pl.pallas_call(
+        functools.partial(front_kernel, shape, chunks),
+        name="messages_update_weight_gradient",
+        out_shape=[
+            jax.ShapeDtypeStruct((own, H), BF16),
+            jax.ShapeDtypeStruct((own, H), F32),
+            jax.ShapeDtypeStruct((own, H), BF16),
+            jax.ShapeDtypeStruct((groups, H, lanes), BF16),
+            jax.ShapeDtypeStruct((groups, H, lanes), BF16),
+            jax.ShapeDtypeStruct((groups, 32 + GROUP, lanes), F32),
+            jax.ShapeDtypeStruct((8, H), F32),
+        ]
+        + half
+        + half,
+        in_specs=[smem()] + [vmem()] * 3 + [anywhere()] + [vmem()] * 8,
+        out_specs=[vmem()] * 3 + [anywhere()] * 3 + [vmem()] + [anywhere()] * (2 * len(chunks)),
+        scratch_shapes=[
+            pltpu.VMEM((H + 16, holders * own), BF16),
+            pltpu.VMEM((H, own, H), BF16),
+            pltpu.VMEM((own, H), F32),
+            pltpu.VMEM((own, H), F32),
+            pltpu.VMEM((H, own), BF16),
+            pltpu.VMEM((7, H, H), F32),
+            pltpu.VMEM((PIECES, H), F32),
+            pltpu.VMEM((EXTRA, H), F32),
+            pltpu.VMEM((H, H, H), BF16),
+            pltpu.VMEM((groups, H, lanes), BF16),
+            pltpu.VMEM((groups, H, lanes), BF16),
+            pltpu.VMEM((groups, 32 + GROUP, lanes), F32),
+        ]
+        + [pltpu.VMEM(h.shape, BF16) for h in half] * 2
+        + [pltpu.SemaphoreType.DMA((4 + 2 * len(chunks),))],
+        compiler_params=params(),
+    )(
+        piece_arr, given, states_here, molecule, t_units, b2, w_edge_in, b1, w_input, w_hidden,
+        b_input.astype(F32).reshape(1, -1), b_hidden.astype(F32).reshape(1, -1), cotangent[0],
+    )
+    new_states, direct, d_agg, latent, near, meta, flag = front[:7]
+    keeps = front[7 : 7 + len(chunks)]
+    sends = front[7 + len(chunks) :]
+
+    got = [swap(sends[c].reshape(chunk.shape()), bits[-1], devices) for c, chunk in enumerate(chunks)]
+    terms = [[keeps[c].reshape(chunk.shape()), got[c]] for c, chunk in enumerate(chunks)]
+
+    def scatter_step(step, work):
+        sent = [add([t[1] for t in terms[c]]) for c in range(len(chunks))]
+        given, run = work
+        sent, given = lax.optimization_barrier((sent, given))
+        got = [swap(sent[c], bits[chunk.order[step]], devices) for c, chunk in enumerate(chunks)]
+        result = run(given)
+        got, result = lax.optimization_barrier((got, result))
+        for c in range(len(chunks)):
+            terms[c] = [t[0] for t in terms[c]] + [got[c]]
+        return result
+
+    matrix_gradients = pl.pallas_call(
+        functools.partial(spread_kernel, shape),
+        name="matrix_gradients",
+        out_shape=[jax.ShapeDtypeStruct((groups, H, GROUP * H), BF16), jax.ShapeDtypeStruct((own, H), F32)],
+        grid=(H // 16,),
+        in_specs=[
+            pl.BlockSpec((own, H), lambda i: (0, 0)),
+            pl.BlockSpec((16, H, H), lambda i: (i, 0, 0)),
+            pl.BlockSpec((H, H), lambda i: (0, 0)),
+        ],
+        out_specs=[
+            pl.BlockSpec((groups, 16, GROUP * H), lambda i: (0, i, 0)),
+            pl.BlockSpec((own, H), lambda i: (0, 0)),
+        ],
+        scratch_shapes=[pltpu.VMEM((16, own, H), BF16)],
+        compiler_params=params(),
+        cost_estimate=cost(6),
+    )
+
+    part = jnp.zeros((holders * own, H), F32)
+    first = jnp.concatenate([jnp.zeros((24, H), F32), flag], axis=0)
+    count = groups // BACK
+    edge_parts = []
+    pending = []
+
+    def back_step(n, wide, bias, part, first):
+        at = slice(n * count, (n + 1) * count)
+        part, first, edge_part = pl.pallas_call(
+            functools.partial(back_kernel, shape, count),
+            name="edge_gradients",
+            out_shape=[
+                jax.ShapeDtypeStruct((holders * own, H), F32),
+                jax.ShapeDtypeStruct((32, H), F32),
+                jax.ShapeDtypeStruct((count, 16, lanes), F32),
+            ],
+            grid=(1,),
+            in_specs=[
+                pl.BlockSpec((count, H, GROUP * H), lambda i: (n, 0, 0)),
+                pl.BlockSpec((count * GROUP, H), lambda i: (n, 0)),
+                pl.BlockSpec((16, H), lambda i: (0, 0)),
+                pl.BlockSpec((1, H), lambda i: (0, 0)),
+                pl.BlockSpec((count, H, lanes), lambda i: (n, 0, 0)),
+                pl.BlockSpec((count, H, lanes), lambda i: (n, 0, 0)),
+                pl.BlockSpec((count, 32 + GROUP, lanes), lambda i: (n, 0, 0)),
+                pl.BlockSpec((holders * own, H), lambda i: (0, 0)),
+                pl.BlockSpec((32, H), lambda i: (0, 0)),
+            ],
+            out_specs=[
+                pl.BlockSpec((holders * own, H), lambda i: (0, 0)),
+                pl.BlockSpec((32, H), lambda i: (0, 0)),
+                pl.BlockSpec((count, 16, lanes), lambda i: (0, 0, 0)),
+            ],
+            compiler_params=params(),
+            cost_estimate=cost(24 // BACK),
+        )(wide, bias, w_edge_in, b1, latent, near, meta, part, first)
+        edge_parts.append(edge_part)
+        return part, first
+
+    steps = 4
+    state = (d_agg, part, first)
+
+    def work(step, state):
+        if step == 0:
+            d_agg, part, first = state
+            state = (*matrix_gradients(d_agg, t_units, b2), part, first)
+        wide, bias, part, first = state
+        for n in range(step * BACK // steps, (step + 1) * BACK // steps):
+            part, first = back_step(n, wide, bias, part, first)
+        return wide, bias, part, first
+
+    for step in range(steps):
+        state = scatter_step(step, (state, functools.partial(work, step)))
+    part, first = state[2:]
+
+    keep_d, keep_e, send = pl.pallas_call(
+        functools.partial(return_kernel, shape),
+        name="returned",
+        out_shape=[
+            jax.ShapeDtypeStruct((holders // 2, own, H), BF16),
+            jax.ShapeDtypeStruct((holders // 2, 16 * blocks, H), BF16),
+            jax.ShapeDtypeStruct((holders // 2 * (own + 16 * blocks) + 32, H), BF16),
+        ],
+        in_specs=[smem()] + [vmem()] * (2 + BACK),
+        out_specs=[vmem()] * 3,
+        scratch_shapes=[pltpu.VMEM((holders, 16 * blocks, H), BF16)],
+        compiler_params=params(),
+        cost_estimate=cost(2),
+    )(me_arr, part, first, *edge_parts)
+
+    slabs = keep_e[:, None]
+    mask, n, first = 1, holders // 2, rounded(first)
+    while True:
+        got = swap(send, mask, devices)
+        cut = n * own
+        keep_d = add([keep_d, got[:cut].reshape(n, own, H)])
+        got_e = got[cut:-32].reshape(n, -1, 16 * blocks, H)
+        slabs = jnp.concatenate([slabs, got_e], axis=1)
+        first = rounded(first.astype(F32) + got[-32:].astype(F32))
+        if n == 1:
+            break
+        mask, n = mask * 2, n // 2
+        send = jnp.concatenate([keep_d[1::2].reshape(-1, H), slabs[1::2].reshape(-1, H), first], axis=0)
+        keep_d, slabs = keep_d[0::2], slabs[0::2]
+    mask = edge
+    while mask < devices:
+        first = rounded(first.astype(F32) + swap(first, mask, devices).astype(F32))
+        mask *= 2
+    first = first.astype(F32)
+    state_grads, edge_grads = pl.pallas_call(
+        functools.partial(gather_kernel, shape),
+        name="slots_to_edges",
+        out_shape=[
+            jax.ShapeDtypeStruct((own, H), F32),
+            jax.ShapeDtypeStruct((edge_feats.shape[2], edges), F32),
+        ],
+        in_specs=[smem()] + [vmem()] * 4,
+        out_specs=[vmem()] * 2,
+        scratch_shapes=[pltpu.VMEM((holders * 16 * blocks, H), BF16)],
+        compiler_params=params(),
+        cost_estimate=cost(3),
+    )(me_arr, slot, direct, keep_d[0], slabs[0])
+
+    whole = [add(t) for t in terms]
+    for mask in rest:
+        whole = [rounded(w.astype(F32) + swap(w, mask, devices).astype(F32)) for w in whole]
+    return new_states, state_grads, edge_grads, first, gather_back(chunks, bits, devices, whole)
+
+
+def gather_back(chunks, bits, devices, whole):
+    for step in reversed(range(len(bits) - 1)):
+        whole = [
+            jnp.stack([w, swap(w, bits[chunk.order[step]], devices)], axis=0) for w, chunk in zip(whole, chunks)
+        ]
+    return whole
+
+
+def finish(batch, edge, results):
+    new_states, state_grads, edge_grads, first, whole = results
+    bits, chunks, piece_arr = plan(batch, edge)
+    devices = batch * edge
+    pairs = []
+    for c, chunk in enumerate(chunks):
+        other = swap(whole[c], bits[-1], devices)
+        pairs += [x.reshape(PIECES // 2, chunk.height, H) for x in (whole[c], other)]
+    grad_w2, grad_wi, grad_wh, grad_b2, grad_bi, grad_bh = pl.pallas_call(
+        functools.partial(assemble_kernel, chunks),
+        name="assemble",
+        in_specs=[smem()] + [vmem()] * (2 * len(chunks)),
+        out_specs=[anywhere()] + [vmem()] * 5,
+        scratch_shapes=[
+            pltpu.VMEM((4, 2 * UNITS, H * H), F32),
+            pltpu.VMEM((7, H, H), F32),
+            pltpu.VMEM((PIECES, H), F32),
+            pltpu.VMEM((256, 256), BF16),
+            pltpu.SemaphoreType.DMA((4,)),
+        ],
+        out_shape=[jax.ShapeDtypeStruct((H, H * H), F32)]
+        + [jax.ShapeDtypeStruct((H, 3 * H), F32)] * 2
+        + [jax.ShapeDtypeStruct((H, H), F32)]
+        + [jax.ShapeDtypeStruct((3 * H,), F32)] * 2,
+        compiler_params=params(),
+    )(piece_arr, *pairs)
+    return (
+        new_states[None],
+        state_grads[None],
+        jnp.swapaxes(edge_grads[None], 1, 2),
+        first[0:16],
+        first[16],
+        grad_w2,
+        grad_b2.reshape(-1),
+        grad_wi,
+        grad_wh,
+        grad_bi,
+        grad_bh,
+    )
+
 
 HIGH = lax.Precision.HIGHEST
 
@@ -32,23 +831,19 @@
     return jnp.dot(onehot, values, preferred_element_type=jnp.float32)
 
 
-def per_device(
-    states,
-    edge_feats,
-    molecule,
-    source,
-    target,
-    edge_mask,
-    w_edge_in,
-    b_edge_in,
-    w_edge_out,
-    b_edge_out,
-    w_input,
-    w_hidden,
-    b_input,
-    b_hidden,
-    cotangent,
-):
+def from_all(x, edge):
+    got = lax.all_to_all(jnp.broadcast_to(x[None], (edge,) + x.shape), "edge", 0, 0)
+    return got.reshape((-1,) + x.shape[1:])
+
+
+def to_owners(x, edge):
+    got = lax.all_to_all(x.reshape((edge, -1) + x.shape[1:]), "edge", 0, 0)
+    return jnp.sum(got.astype(F32), axis=0)
+
+
+def slow_path(batch, edge, args):
+    (states, edge_feats, molecule, source, target, edge_mask, w_edge_in, b_edge_in, w_edge_out, b_edge_out,
+     w_input, w_hidden, b_input, b_hidden, cotangent) = args
     states_here = states[0]
     feats = edge_feats[0]
     source_ids = source[0]
@@ -58,10 +853,10 @@
     edges = source_ids.shape[0]
     block = min(512, edges)
     count = edges // block
-    labels = lax.all_gather(molecule[0], "edge", axis=0, tiled=True)
+    labels = from_all(molecule[0], edge)
     same = (jnp.take(labels, source_ids) == jnp.take(labels, target_ids)).astype(jnp.float32)
     valid = edge_mask[0].astype(jnp.float32) * same
-    near = pick_by(source_ids, lax.all_gather(states_here, "edge", axis=0, tiled=True)).astype(
+    near = pick_by(source_ids, from_all(states_here, edge)).astype(
         jnp.bfloat16
     )
     hidden, edge_pull = jax.vjp(
@@ -83,12 +878,7 @@
 
     outgoing = lax.map(lambda item: apply(expand(item[0]), item[1]), (latent_blocks, near_blocks))
     messages = (outgoing.reshape(edges, width) * valid[:, None]).astype(jnp.bfloat16)
-    summed = lax.psum_scatter(
-        spread_by(target_ids, messages, lax.axis_size("edge") * owned),
-        "edge",
-        scatter_dimension=0,
-        tiled=True,
-    )
+    summed = to_owners(spread_by(target_ids, messages, edge * owned), edge)
     mixed = summed.astype(jnp.bfloat16).astype(jnp.float32)
     updated, update_pull = jax.vjp(
         gated_update,
@@ -104,7 +894,7 @@
         cotangent[0].astype(jnp.float32)
     )
     pulled = pick_by(
-        target_ids, lax.all_gather(d_mixed.astype(jnp.bfloat16), "edge", axis=0, tiled=True)
+        target_ids, from_all(d_mixed.astype(jnp.bfloat16), edge)
     )
     d_message = (pulled * valid[:, None]).astype(jnp.bfloat16)
     d_message_blocks = d_message.reshape(count, block, width)
@@ -142,64 +932,56 @@
     d_latent_all = per_edge[0].reshape(edges, -1)
     d_near_all = per_edge[1].reshape(edges, width)
     d_feats, grad_w1, grad_b1 = edge_pull(d_latent_all)
-    returned = lax.psum_scatter(
-        spread_by(source_ids, d_near_all, owned * lax.axis_size("edge")).astype(jnp.bfloat16),
-        "edge",
-        scatter_dimension=0,
-        tiled=True,
-    ).astype(jnp.float32)
+    returned = to_owners(spread_by(source_ids, d_near_all, owned * edge).astype(jnp.bfloat16), edge)
     state_grads = d_direct + returned
-    grad_w1, grad_b1, grad_w2, grad_b2, grad_wi, grad_wh, grad_bi, grad_bh = lax.psum(
-        (grad_w1, grad_b1, grad_w2, grad_b2, grad_wi, grad_wh, grad_bi, grad_bh), ("batch", "edge")
-    )
-    return (
-        new_states[None],
-        state_grads[None],
-        d_feats[None],
-        grad_w1,
-        grad_b1,
-        grad_w2,
-        grad_b2,
-        grad_wi,
-        grad_wh,
-        grad_bi,
-        grad_bh,
-    )
+
+    bits, chunks, piece_arr = plan(batch, edge)
+    devices = batch * edge
+    pieces = grad_w2.reshape(PIECES, UNITS, H, H)
+    small = jnp.concatenate([grad_wi, grad_wh, grad_b2.reshape(H, H)], axis=1).reshape(PIECES, UNITS, 7, H)
+    small = small.transpose(0, 2, 1, 3).reshape(PIECES, 7 * UNITS, H)
+    biases = jnp.concatenate([grad_bi, grad_bh]).reshape(6, H)
+    biases = jnp.concatenate([biases, jnp.zeros((PIECES - 6, H), F32)], axis=0)[:, None]
+    small = jnp.concatenate([small, biases, jnp.zeros((PIECES, EXTRA - 7 * UNITS - 1, H), F32)], axis=1)
+    terms = []
+    for chunk in chunks:
+        block = pieces[:, :, chunk.first : chunk.first + chunk.rows].reshape(PIECES, -1, H)
+        if chunk.extra:
+            block = jnp.concatenate([block, small], axis=1)
+        rel_of = sorted(range(PIECES // 2), key=chunk.place)
+        order = jnp.array(rel_of + [PIECES // 2 + r for r in rel_of], jnp.int32)
+        block = jnp.take(block, jnp.bitwise_xor(order, piece_arr[0]), axis=0).astype(BF16)
+        shape = chunk.shape()
+        kept, sent = block[: PIECES // 2].reshape(shape), block[PIECES // 2 :].reshape(shape)
+        total = add([kept, swap(sent, bits[-1], devices)])
+        for bit in chunk.order:
+            total = add([total[0], swap(total[1], bits[bit], devices)])
+        terms.append(total)
+    first = jnp.concatenate([grad_w1, grad_b1[None], jnp.zeros((15, H), F32)], axis=0)
+    for n in range(devices.bit_length() - 1):
+        mask = 1 << n
+        if mask not in bits:
+            terms = [rounded(w.astype(F32) + swap(w, mask, devices).astype(F32)) for w in terms]
+        first = first + swap(first, mask, devices)
+    return new_states, state_grads, d_feats.T, first, gather_back(chunks, bits, devices, terms)
+
+
+def per_device(batch, edge, *args):
+    results = fast_path(batch, edge, args)
+    overflow = results[3][24, 0] > 0.0
+    results = lax.while_loop(
+        lambda carry: carry[0], lambda carry: (jnp.bool_(False), slow_path(batch, edge, args)), (overflow, results)
+    )[1]
+    return finish(batch, edge, results)
 
 
 def solution(mesh):
+    batch, edge = mesh.shape["batch"], mesh.shape["edge"]
+    nodes, edges, all_ = P("batch", "edge", None), P("batch", "edge"), P()
     return jax.shard_map(
-        per_device,
+        functools.partial(per_device, batch, edge),
         mesh=mesh,
-        in_specs=(
-            P("batch", "edge", None),
-            P("batch", "edge", None),
-            P("batch", "edge"),
-            P("batch", "edge"),
-            P("batch", "edge"),
-            P("batch", "edge"),
-            P(),
-            P(),
-            P(),
-            P(),
-            P(),
-            P(),
-            P(),
-            P(),
-            P("batch", "edge", None),
-        ),
-        out_specs=(
-            P("batch", "edge", None),
-            P("batch", "edge", None),
-            P("batch", "edge", None),
-            P(),
-            P(),
-            P(),
-            P(),
-            P(),
-            P(),
-            P(),
-            P(),
-        ),
+        in_specs=(nodes, nodes, edges, edges, edges, edges) + (all_,) * 8 + (nodes,),
+        out_specs=(nodes, nodes, nodes) + (all_,) * 8,
         check_vma=False,
     )

time: 922 us -> 166 us (0.18)
  matrix products: 326 us -> 0 us
  waiting for transfers between devices: 266 us -> 26.3 us
  blocking collectives: 122 us -> 0 us
  local copies, waits for them, and re-layouts: 107 us -> 12 us
  Pallas kernels: 0 us -> 72.9 us
  other arithmetic: 57.1 us -> 17.7 us
  starting transfers between devices: 0.12 us -> 33.4 us
  loops' own time: 18.9 us -> 0.15 us
  between operations: 14.6 us -> 1.94 us
    dot_general x37 -> x0, matrix products: 326 us -> none  [the longest x4 88 us: backward_core(): lax.dot_general(latent, flat, (((0,), (0,)), ((), ())), preferred_element...]
    psum x1 -> x0, waiting for transfers between devices: 192 us -> none  [per_device(): lax.psum((grad_w1, grad_b1, grad_w2, grad_b2, grad_wi, grad_wh, grad_bi,...]
    all_gather x3 -> x0, blocking collectives: 83.9 us -> none  [the longest x1 30.9 us: per_device(): lax.all_gather(d_mixed.astype(jnp.bfloat16), 'edge', axis=0, tiled=True)]
    while x32 -> x0, local copies, waits for them, and re-layouts: 78.3 us -> none
    reduce_scatter x2 -> x0, waiting for transfers between devices: 74.2 us -> none  [the longest x1 59 us: per_device(): lax.psum_scatter(spread_by(target_ids, messages, lax.axis_size('edge') *...]
    pallas_call x0 -> x11, Pallas kernels: none -> 72.9 us  [the longest x4 23.7 us: back_step(): pl.pallas_call(functools.partial(back_kernel, shape, count), name='edge_g...]
    reduce_sum x6 -> x0, other arithmetic: 50.9 us -> none  [the longest x4 49.2 us: backward_core(): grad_bias = grad_bias + jnp.sum(flat.astype(jnp.float32), axis=0)]
    psum x1 -> x0, blocking collectives: 38.1 us -> none  [per_device(): lax.psum((grad_w1, grad_b1, grad_w2, grad_b2, grad_wi, grad_wh, grad_bi,...]
  transfers between devices with their start and end apart: 3 -> 26, of which waited for: 3 -> 11; matrix products, arithmetic and copies ran while one was open for 1% -> 10% of each run, Pallas kernels for 0% -> 27%
where the time goes in v1:
time: 166 us; the launch traced here: 164 us
  Pallas kernels  72.9 us (44%)
  starting transfers between devices  33.4 us (20%)
  waiting for transfers between devices  26.3 us (16%)
  other arithmetic  17.7 us (11%)
  local copies, waits for them, and re-layouts  12 us (7%)
  between operations  1.94 us (1%)
    ppermute x25, starting transfers between devices, swap(): lax.ppermute(x, ('batch', 'edge'), [(i, i ^ mask) for i in range(devices)])  26.1 us
    pallas_call x4, Pallas kernels, back_step(): pl.pallas_call(functools.partial(back_kernel, shape, count), name='edge_g...  23.7 us
    ppermute x25, waiting for transfers between devices, swap(): lax.ppermute(x, ('batch', 'edge'), [(i, i ^ mask) for i in range(devices)])  22.7 us
    pallas_call x1, Pallas kernels, fast_path(): pl.pallas_call(functools.partial(front_kernel, shape, chunks), name='mess...  17.3 us
    convert_element_type x12, other arithmetic, add(): return total.astype(BF16)  12 us
    pallas_call x1, Pallas kernels, work(): state = (*matrix_gradients(d_agg, t_units, b2), part, first)  8.8 us
    pallas_call x1, Pallas kernels, finish(): pl.pallas_call(functools.partial(assemble_kernel, chunks), name='assemble...  7.88 us
    pallas_call x1, Pallas kernels, fast_path(): pl.pallas_call(split_kernel, name='split_weight', grid=(H // 16,), in_spe...  7.6 us
  transfers between devices with their start and end apart: 26, of which 11 were waited for; matrix products, arithmetic and copies ran while one was open for 10% of the time, Pallas kernels for 27%

profile of v1, /device:TPU:0, one launch (start us, length us, event | category | flops | bytes accessed | tf_op | source)
XLA Modules:
  0.0 164.5 jit_solution(12811687471186418448)
XLA Ops:
  0.6 3.3 %edges_to_slots.1 = (bf16[8,208,128]{2,1,0:T(8,128)(2,1)}, s32[1,2048]{1,0:T(1,128)}) custom-call(s32[1,2048]{1,0:T(1,128)} %target_ref.1, s32[1,2048]{1,0:T(1,128)} %source_ref.1, s32[1,2048]{1,0:T(1,128)} %mask_ref.1, s32[1,128]{1,0:T(1,128)} %refs_3_.1, bf16[16,2048]{1,0:T(8,128)(2,1)} %bitcast.498, bf16[128,128]{1,0:T(8,128)(2,1)} %bitcast.482), custom_call_target="tpu_custom_call" | custom-call | tf_op jit(solution)/shard_map/edges_to_slots/pallas_call | solution.py:547
  4.0 7.3 %all-to-all-start.5 = ((bf16[8,208,128]{2,1,0:T(8,128)(2,1)}), bf16[8,208,128]{2,1,0:T(8,128)(2,1)S(1)}, u32[]{:S(2)}, u32[]{:S(2)}) async-start(bf16[8,208,128]{2,1,0:T(8,128)(2,1)} %get-tuple-element.302), calls=%async_computation.5 | async-start | bytes 851968 | tf_op jit(solution)/shard_map/all_to_all | solution.py:559
  11.4 7.6 %split_weight.1.refs_4_.t_ref = bf16[128,128,128]{2,1,0:T(8,128)(2,1)} custom-call(bf16[128,16384]{1,0:T(8,128)(2,1)} %w_ref.1), custom_call_target="tpu_custom_call" | custom-call | tf_op jit(solution)/shard_map/split_weight/pallas_call | solution.py:561
  20.1 3.5 %all-to-all-done.5.refs_1_ = bf16[8,208,128]{2,1,0:T(8,128)(2,1)S(1)} async-done(((bf16[8,208,128]{2,1,0:T(8,128)(2,1)}), bf16[8,208,128]{2,1,0:T(8,128)(2,1)S(1)}, u32[]{:S(2)}, u32[]{:S(2)}) %all-to-all-start.5) | async-done | bytes 426016 | tf_op jit(solution)/shard_map/all_to_all | solution.py:559
  24.5 17.3 %messages_update_weight_gradient.1 = (bf16[128,128]{1,0:T(8,128)(2,1)}, f32[128,128]{1,0:T(8,128)}, bf16[128,128]{1,0:T(8,128)(2,1)}, bf16[8,128,512]{2,1,0:T(8,...) custom-call(s32[1]{0:T(128)} %bitcast.6.refs_0_.piece_ref, ...), custom_call_target="tpu_custom_call" | custom-call | tf_op jit(solution)/shard_map/messages_update_weight_gradient/pallas_call | solution.py:573
  42.4 1.1 slice.358
  43.5 1.0 slice.364
  44.5 1.1 slice.356
  45.6 1.0 slice.361
  47.2 1.0 fusion.98
  48.2 1.0 fusion.97
  49.1 1.5 collective-permute-start.26
  50.6 8.8 %matrix_gradients.1 = (bf16[8,128,2048]{2,1,0:T(8,128)(2,1)}, f32[128,128]{1,0:T(8,128)}) custom-call(bf16[128,128]{1,0:T(8,128)(2,1)} %get-tuple-element.311.d_ref, bf16[128,128,128]{2,1,0:T(8,128)(2,1)} %split_weight.1.refs_4_.t_ref, bf16[128,128]{1,0:T(8,128)(2,1)S(1)} %bitcast.504), custom_call_target="tpu_custom_call" | custom-call | flops 6000000000 | bytes 18000000 | tf_op jit(solution)/shard_map/matrix_gradients/pallas_call | solution.py:692
  59.4 1.5 collective-permute-start.25
  61.7 5.9 %edge_gradients.4 = (f32[1024,128]{1,0:T(8,128)}, f32[32,128]{1,0:T(8,128)}, f32[2,16,512]{2,1,0:T(8,128)}) custom-call(bf16[8,128,2048]{2,1,0:T(8,128)(2,1)} %get-tuple-element.357.refs_0_, f32[128,128]{1,0:T(8,128)} %get-tuple-element.358.refs_1_, bf16[16,128]{1,0:T(8,128)(2,1)S(1)} %copy-done.40, bf16[1,128]{1,0:T(2,128)(2,1)S(1)} %bitcast.543, ...), custom_call_target="tpu_custom_call" | custom-call | flops 6000000000 | bytes 18000000 | tf_op jit(solution)/shard_map/edge_gradients/pallas_call | solution.py:655
  67.6 5.7 %collective-permute-done.25 = bf16[2,2,2,256,128]{4,3,2,1,0:T(8,128)(2,1)} collective-permute-done((bf16[2,2,2,256,128]{4,3,2,1,0:T(8,128)(2,1)}, bf16[2,2,2,256,128]{4,3,2,1,0:T(8,128)(2,1)}, u32[]{:S(2)}, u32[]{:S(2)}) %collective-permute-start.25) | collective-permute-done | bytes 524320 | tf_op jit(solution)/shard_map/ppermute | solution.py:439
  74.2 1.8 %fusion.100 = bf16[2,2,256,128]{3,2,1,0:T(8,128)(2,1)} fusion(bf16[2,2,256,128]{3,2,1,0:T(8,128)(2,1)S(1)} %bitcast.508, bf16[2,2,2,2,256,128]{5,4,3,2,1,0:T(8,128)(2,1)S(1)} %collective-permute-done.23, bf16[2,2,2,256,128]{4,3,2,1,0:T(8,128)(2,1)} %collective-permute-done.25), kind=kLoop, calls=%fused_computation.210 | loop fusion | flops 786432 | bytes 1048576 | tf_op jit(solution)/shard_map/convert_element_type | solution.py:446
  75.9 1.5 collective-permute-start.28
  78.0 5.9 %edge_gradients.5 = (f32[1024,128]{1,0:T(8,128)}, f32[32,128]{1,0:T(8,128)}, f32[2,16,512]{2,1,0:T(8,128)}) custom-call(bf16[8,128,2048]{2,1,0:T(8,128)(2,1)} %get-tuple-element.357.refs_0_, f32[128,128]{1,0:T(8,128)} %get-tuple-element.358.refs_1_, bf16[16,128]{1,0:T(8,128)(2,1)S(1)} %copy-done.40, bf16[1,128]{1,0:T(2,128)(2,1)S(1)} %bitcast.544, ...), custom_call_target="tpu_custom_call" | custom-call | flops 6000000000 | bytes 18000000 | tf_op jit(solution)/shard_map/edge_gradients/pallas_call | solution.py:655
  84.5 1.0 fusion.101
  85.5 1.7 %fusion.103 = bf16[2,256,128]{2,1,0:T(8,128)(2,1)} fusion(bf16[2,2,2,2,256,128]{5,4,3,2,1,0:T(8,128)(2,1)S(1)} %collective-permute-done.23, bf16[2,2,256,128]{3,2,1,0:T(8,128)(2,1)S(1)} %collective-permute-done.27, bf16[2,2,2,256,128]{4,3,2,1,0:T(8,128)(2,1)} %collective-permute-done.25, bf16[16,256,128]{2,1,0:T(8,128)(2,1)} %get-tuple-element.303), kind=kLoop, calls=%fused_computation.223 | loop fusion | flops 524288 | bytes 655360 | tf_op jit(solution)/shard_map/convert_element_type | solution.py:446
  87.5 1.7 %collective-permute-start.29 = (bf16[2,256,128]{2,1,0:T(8,128)(2,1)}, bf16[2,256,128]{2,1,0:T(8,128)(2,1)}, u32[]{:S(2)}, u32[]{:S(2)}) collective-permute-start(bf16[2,256,128]{2,1,0:T(8,128)(2,1)} %fusion.103), channel_id=1, source_target_pairs={{0,2},{1,3},{2,0},{3,1},{4,6},{5,7},{6,4},{7,5},{8,10},{9,11},{10,... | collective-permute-start | bytes 393224 | tf_op jit(solution)/shard_map/ppermute | solution.py:439
  89.2 5.9 %edge_gradients.6 = (f32[1024,128]{1,0:T(8,128)}, f32[32,128]{1,0:T(8,128)}, f32[2,16,512]{2,1,0:T(8,128)}) custom-call(bf16[8,128,2048]{2,1,0:T(8,128)(2,1)} %get-tuple-element.357.refs_0_, f32[128,128]{1,0:T(8,128)} %get-tuple-element.358.refs_1_, bf16[16,128]{1,0:T(8,128)(2,1)S(1)} %copy-done.40, bf16[1,128]{1,0:T(2,128)(2,1)S(1)} %bitcast.545, ...), custom_call_target="tpu_custom_call" | custom-call | flops 6000000000 | bytes 18000000 | tf_op jit(solution)/shard_map/edge_gradients/pallas_call | solution.py:655
  97.1 2.9 %collective-permute-start.31 = (bf16[256,128]{1,0:T(8,128)(2,1)S(1)}, bf16[256,128]{1,0:T(8,128)(2,1)S(1)}, u32[]{:S(2)}, u32[]{:S(2)}) collective-permute-start(bf16[256,128]{1,0:T(8,128)(2,1)S(1)} %fusion.112), channel_id=1, source_target_pairs={{0,4},{1,5},{2,6},{3,7},{4,0},{5,1},{6,2},{7,3},{8,12},{9,13},{10,... | collective-permute-start | bytes 196616 | tf_op jit(solution)/shard_map/ppermute | solution.py:439
  100.0 6.1 %edge_gradients.7 = (f32[1024,128]{1,0:T(8,128)}, f32[32,128]{1,0:T(8,128)}, f32[2,16,512]{2,1,0:T(8,128)}) custom-call(bf16[8,128,2048]{2,1,0:T(8,128)(2,1)} %get-tuple-element.357.refs_0_, f32[128,128]{1,0:T(8,128)} %get-tuple-element.358.refs_1_, bf16[16,128]{1,0:T(8,128)(2,1)S(1)} %copy-done.40, bf16[1,128]{1,0:T(2,128)(2,1)S(1)} %bitcast.546, ...), custom_call_target="tpu_custom_call" | custom-call | flops 6000000000 | bytes 18000000 | tf_op jit(solution)/shard_map/edge_gradients/pallas_call | solution.py:655
  106.1 1.0 fusion.110
  107.2 1.9 %returned.1 = (bf16[4,128,128]{2,1,0:T(8,128)(2,1)}, bf16[4,64,128]{2,1,0:T(8,128)(2,1)}, bf16[800,128]{1,0:T(8,128)(2,1)}) custom-call(s32[1]{0:T(128)} %bitcast.41.me_ref, f32[1024,128]{1,0:T(8,128)} %get-tuple-element.364.part_ref, f32[32,128]{1,0:T(8,128)} %get-tuple-element.363.first_ref, f32[2,16,512]{2,1,0:T(8,128)} %get-tuple-element.365.refs_0_, ...), custom_call_target="tpu_custom_call" | custom-call | flops 2000000000 | bytes 6000000 | tf_op jit(solution)/shard_map/returned/pallas_call | solution.py:702
  109.1 1.1 collective-permute-start.33
  111.2 2.7 %collective-permute-start.42 = (bf16[288,128]{1,0:T(8,128)(2,1)S(1)}, bf16[288,128]{1,0:T(8,128)(2,1)S(1)}, u32[]{:S(2)}, u32[]{:S(2)}) collective-permute-start(bf16[288,128]{1,0:T(8,128)(2,1)S(1)} %fusion.105), channel_id=1, source_target_pairs={{0,4},{1,5},{2,6},{3,7},{4,0},{5,1},{6,2},{7,3},{8,12},{9,13},{10,... | collective-permute-start | bytes 221192 | tf_op jit(solution)/shard_map/ppermute | solution.py:439
  117.0 2.0 %collective-permute-start.34 = (bf16[544,128]{1,0:T(8,128)(2,1)S(1)}, bf16[544,128]{1,0:T(8,128)(2,1)S(1)}, u32[]{:S(2)}, u32[]{:S(2)}) collective-permute-start(bf16[544,128]{1,0:T(8,128)(2,1)S(1)} %pad_maximum_fusion.16), channel_id=1, source_target_pairs={{0,2},{1,3},{2,0},{3,1},{4,6},{5,7},{6,4},{7,5},{8,10},{9,11},{10,... | collective-permute-start | bytes 417800 | tf_op jit(solution)/shard_map/ppermute | solution.py:439
  119.2 1.5 collective-permute-done.39
  120.7 1.3 collective-permute-start.40
  122.0 1.3 collective-permute-done.34
  123.4 2.9 %collective-permute-start.35 = (bf16[416,128]{1,0:T(8,128)(2,1)S(1)}, bf16[416,128]{1,0:T(8,128)(2,1)S(1)}, u32[]{:S(2)}, u32[]{:S(2)}) collective-permute-start(bf16[416,128]{1,0:T(8,128)(2,1)S(1)} %pad_maximum_fusion.20), channel_id=1, source_target_pairs={{0,4},{1,5},{2,6},{3,7},{4,0},{5,1},{6,2},{7,3},{8,12},{9,13},{10,... | collective-permute-start | bytes 319496 | tf_op jit(solution)/shard_map/ppermute | solution.py:439
  126.3 1.0 collective-permute-start.44
  127.4 2.8 %collective-permute-done.35 = bf16[416,128]{1,0:T(8,128)(2,1)S(1)} collective-permute-done((bf16[416,128]{1,0:T(8,128)(2,1)S(1)}, bf16[416,128]{1,0:T(8,128)(2,1)S(1)}, u32[]{:S(2)}, u32[]{:S(2)}) %collective-permute-start.35) | collective-permute-done | bytes 106528 | tf_op jit(solution)/shard_map/ppermute | solution.py:439
  131.5 1.0 collective-permute-start.37
  132.6 1.1 collective-permute-start.41
  133.8 1.3 collective-permute-start.45
  135.1 2.3 %slots_to_edges.1 = (f32[128,128]{1,0:T(8,128)}, f32[16,2048]{1,0:T(8,128)}) custom-call(s32[1]{0:T(128)} %bitcast.41.me_ref, s32[1,2048]{1,0:T(1,128)} %get-tuple-element.373.slot_ref, f32[128,128]{1,0:T(8,128)} %get-tuple-element.374.direct_ref, bf16[128,128]{1,0:T(8,128)(2,1)} %fusion.115.part_ref, bf16[8,64,128]{2,1,0:T(8,128)(2,1)} %fusion.108.slabs_ref), custom_call_target="tpu_custom_call" | custom-call | flops 3000000000 | bytes 9000000 | tf_op jit(solution)/shard_map/slots_to_edges/pallas_call | solution.py:736
  138.7 8.1 %collective-permute-done.41 = bf16[2,2,2,256,128]{4,3,2,1,0:T(8,128)(2,1)} collective-permute-done((bf16[2,2,2,256,128]{4,3,2,1,0:T(8,128)(2,1)S(1)}, bf16[2,2,2,256,128]{4,3,2,1,0:T(8,128)(2,1)}, u32[]{:S(2)}, u32[]{:S(2)}) %collective-permute-start.41) | collective-permute-done | bytes 524320 | tf_op jit(solution)/shard_map/ppermute | solution.py:439
  146.9 2.1 %pad_maximum_fusion.10 = bf16[2,2,2,2,256,128]{5,4,3,2,1,0:T(8,128)(2,1)} fusion(bf16[1,2,2,2,256,128]{5,4,3,2,1,0:T(8,128)(2,1)} %bitcast.68, bf16[1,2,2,2,256,128]{5,4,3,2,1,0:T(8,128)(2,1)S(1)} %get-tuple-element.664), kind=kLoop, calls=%fused_computation.199 | loop fusion | flops 524288 | bytes 2097152 | tf_op jit(solution)/shard_map/stack | solution.py:759
  149.1 1.1 pad_maximum_fusion.9
  151.0 1.3 slice.410
  152.3 1.2 slice_bitcast_fusion.28
  153.5 1.6 collective-permute-done.46
  155.0 1.0 copy-done.32
  156.4 7.9 %assemble.1 = (f32[128,16384]{1,0:T(8,128)}, f32[128,384]{1,0:T(8,128)}, f32[128,384]{1,0:T(8,128)}, f32[128,128]{1,0:T(8,128)}, f32[384]{0:T(512)}, /*index=5*/f32[384]{0:T(512)}) custom-call(s32[1]{0:T(128)} %bitcast.6.refs_0_.piece_ref, bf16[16,256,128]{2,1,0:T(8,128)(2,1)} %bitcast.494, bf16[16,256,128]{2,1,0:T(8,128)(2,1)} %bitcast.507, ...), custom_call_target="tpu_custom_call" | custom-call | tf_op jit(solution)/shard_map/assemble/pallas_call | solution.py:772
  (113 shorter events, 16.0 us)
Async XLA Ops:
  4.0 19.7 %all-to-all-start.5 = ((bf16[8,208,128]{2,1,0:T(8,128)(2,1)}), bf16[8,208,128]{2,1,0:T(8,128)(2,1)S(1)}, u32[]{:S(2)}, u32[]{:S(2)}) async-start(bf16[8,208,128]{2,1,0:T(8,128)(2,1)} %get-tuple-element.302), calls=%async_computation.5 | async-start | bytes 851968 | tf_op jit(solution)/shard_map/all_to_all | solution.py:559
  11.3 7.7 %copy-start.46 = (bf16[384]{0:T(512)(128)(2,1)S(1)}, bf16[384]{0:T(512)(128)(2,1)}, u32[]{:S(2)}) copy-start(bf16[384]{0:T(512)(128)(2,1)} %param.37) | copy-start | bytes 2308
  11.3 8.3 %copy-start.49 = (bf16[384]{0:T(512)(128)(2,1)S(1)}, bf16[384]{0:T(512)(128)(2,1)}, u32[]{:S(2)}) copy-start(bf16[384]{0:T(512)(128)(2,1)} %param.38) | copy-start | bytes 2308
  11.3 13.1 %copy-start.14 = (bf16[1,128,128]{2,1,0:T(8,128)(2,1)S(1)}, bf16[1,128,128]{2,1,0:T(8,128)(2,1)}, u32[]{:S(2)}) copy-start(bf16[1,128,128]{2,1,0:T(8,128)(2,1)} %param.25) | copy-start | bytes 98308
  11.3 13.1 %copy-start.17 = (bf16[128,384]{1,0:T(8,128)(2,1)S(1)}, bf16[128,384]{1,0:T(8,128)(2,1)}, u32[]{:S(2)}) copy-start(bf16[128,384]{1,0:T(8,128)(2,1)} %refs_9_.1) | copy-start | bytes 294916
  11.3 13.1 %copy-start.19 = (bf16[128,384]{1,0:T(8,128)(2,1)S(1)}, bf16[128,384]{1,0:T(8,128)(2,1)}, u32[]{:S(2)}) copy-start(bf16[128,384]{1,0:T(8,128)(2,1)} %refs_8_.1) | copy-start | bytes 294916
  11.3 13.1 %copy-start.22 = (bf16[1,128,128]{2,1,0:T(8,128)(2,1)S(1)}, bf16[1,128,128]{2,1,0:T(8,128)(2,1)}, u32[]{:S(2)}) copy-start(bf16[1,128,128]{2,1,0:T(8,128)(2,1)} %param.39) | copy-start | bytes 98308
  11.3 13.1 %copy-start.29 = (bf16[16384]{0:T(1024)(128)(2,1)S(1)}, bf16[16384]{0:T(1024)(128)(2,1)}, u32[]{:S(2)}) copy-start(bf16[16384]{0:T(1024)(128)(2,1)} %param.34) | copy-start | bytes 98308
  11.3 13.1 %copy-start.40 = (bf16[16,128]{1,0:T(8,128)(2,1)S(1)}, bf16[16,128]{1,0:T(8,128)(2,1)}, u32[]{:S(2)}) copy-start(bf16[16,128]{1,0:T(8,128)(2,1)} %refs_2_.7) | copy-start | bytes 12292
  11.4 13.1 %copy-start.53 = (s32[1,128]{1,0:T(1,128)S(1)}, s32[1,128]{1,0:T(1,128)}, u32[]{:S(2)}) copy-start(s32[1,128]{1,0:T(1,128)} %refs_3_.1) | copy-start | bytes 1540
  11.4 13.1 %copy-start.57 = (bf16[128]{0:T(256)(128)(2,1)S(1)}, bf16[128]{0:T(256)(128)(2,1)}, u32[]{:S(2)}) copy-start(bf16[128]{0:T(256)(128)(2,1)} %param.32) | copy-start | bytes 772
  41.8 4.7 %copy-start.56 = (f32[8,128]{1,0:T(8,128)S(1)}, f32[8,128]{1,0:T(8,128)}, u32[]{:S(2)}) copy-start(f32[8,128]{1,0:T(8,128)} %get-tuple-element.308) | copy-start | bytes 12292
  41.8 5.3 %collective-permute-start.23 = (bf16[2,2,2,2,256,128]{5,4,3,2,1,0:T(8,128)(2,1)}, bf16[2,2,2,2,256,128]{5,4,3,2,1,0:T(8,128)(2,1)S(1)}, u32[]{:S(2)}, u32[]{:S(2)}) collective-permute-start(bf16[2,2,2,2,256,128]{5,4,3,2,1,0:T(8,128)(2,1)} %bitcast.548), channel_id=1, source_target_pairs={{0,8},{1,9},{2,10},{3,11},{4,12},{5,13},{6,14},{7,15},{8,0},{9,1},... | collective-permute-start | bytes 3145736 | tf_op jit(solution)/shard_map/ppermute | solution.py:439
  41.9 6.2 %collective-permute-start.24 = (bf16[2,2,2,2,288,128]{5,4,3,2,1,0:T(8,128)(2,1)}, bf16[2,2,2,2,288,128]{5,4,3,2,1,0:T(8,128)(2,1)S(1)}, u32[]{:S(2)}, u32[]{:S(2)}) collective-permute-start(bf16[2,2,2,2,288,128]{5,4,3,2,1,0:T(8,128)(2,1)} %bitcast.547), channel_id=1, source_target_pairs={{0,8},{1,9},{2,10},{3,11},{4,12},{5,13},{6,14},{7,15},{8,0},{9,1},... | collective-permute-start | bytes 3538952 | tf_op jit(solution)/shard_map/ppermute | solution.py:439
  49.1 24.2 %collective-permute-start.26 = (bf16[2,2,2,288,128]{4,3,2,1,0:T(8,128)(2,1)}, bf16[2,2,2,288,128]{4,3,2,1,0:T(8,128)(2,1)S(1)}, u32[]{:S(2)}, u32[]{:S(2)}) collective-permute-start(bf16[2,2,2,288,128]{4,3,2,1,0:T(8,128)(2,1)} %fusion.97), channel_id=1, source_target_pairs={{0,1},{1,0},{2,3},{3,2},{4,5},{5,4},{6,7},{7,6},{8,9},{9,8},{10,11... | collective-permute-start | bytes 1769480 | tf_op jit(solution)/shard_map/ppermute | solution.py:439
  59.4 13.9 %collective-permute-start.25 = (bf16[2,2,2,256,128]{4,3,2,1,0:T(8,128)(2,1)}, bf16[2,2,2,256,128]{4,3,2,1,0:T(8,128)(2,1)}, u32[]{:S(2)}, u32[]{:S(2)}) collective-permute-start(bf16[2,2,2,256,128]{4,3,2,1,0:T(8,128)(2,1)} %fusion.98), channel_id=1, source_target_pairs={{0,16},{1,17},{2,18},{3,19},{4,20},{5,21},{6,22},{7,23},{8,24},{9,... | collective-permute-start | bytes 1572872 | tf_op jit(solution)/shard_map/ppermute | solution.py:439
  75.9 8.6 %collective-permute-start.28 = (bf16[2,2,288,128]{3,2,1,0:T(8,128)(2,1)}, bf16[2,2,288,128]{3,2,1,0:T(8,128)(2,1)S(1)}, u32[]{:S(2)}, u32[]{:S(2)}) collective-permute-start(bf16[2,2,288,128]{3,2,1,0:T(8,128)(2,1)} %fusion.99), channel_id=1, source_target_pairs={{0,16},{1,17},{2,18},{3,19},{4,20},{5,21},{6,22},{7,23},{8,24},{9,... | collective-permute-start | bytes 884744 | tf_op jit(solution)/shard_map/ppermute | solution.py:439
  77.4 7.0 %collective-permute-start.27 = (bf16[2,2,256,128]{3,2,1,0:T(8,128)(2,1)}, bf16[2,2,256,128]{3,2,1,0:T(8,128)(2,1)S(1)}, u32[]{:S(2)}, u32[]{:S(2)}) collective-permute-start(bf16[2,2,256,128]{3,2,1,0:T(8,128)(2,1)} %fusion.100), channel_id=1, source_target_pairs={{0,1},{1,0},{2,3},{3,2},{4,5},{5,4},{6,7},{7,6},{8,9},{9,8},{10,11... | collective-permute-start | bytes 786440 | tf_op jit(solution)/shard_map/ppermute | solution.py:439
  87.2 12.8 %copy-start.58 = (bf16[128]{0:T(256)(128)(2,1)S(1)}, bf16[128]{0:T(256)(128)(2,1)}, u32[]{:S(2)}) copy-start(bf16[128]{0:T(256)(128)(2,1)} %param.32) | copy-start | bytes 772
  87.2 7.9 %collective-permute-start.30 = (bf16[2,288,128]{2,1,0:T(8,128)(2,1)S(1)}, bf16[2,288,128]{2,1,0:T(8,128)(2,1)S(1)}, u32[]{:S(2)}, u32[]{:S(2)}) collective-permute-start(bf16[2,288,128]{2,1,0:T(8,128)(2,1)S(1)} %fusion.101), channel_id=1, source_target_pairs={{0,2},{1,3},{2,0},{3,1},{4,6},{5,7},{6,4},{7,5},{8,10},{9,11},{10,... | collective-permute-start | bytes 442376 | tf_op jit(solution)/shard_map/ppermute | solution.py:439
  87.5 7.6 %collective-permute-start.29 = (bf16[2,256,128]{2,1,0:T(8,128)(2,1)}, bf16[2,256,128]{2,1,0:T(8,128)(2,1)}, u32[]{:S(2)}, u32[]{:S(2)}) collective-permute-start(bf16[2,256,128]{2,1,0:T(8,128)(2,1)} %fusion.103), channel_id=1, source_target_pairs={{0,2},{1,3},{2,0},{3,1},{4,6},{5,7},{6,4},{7,5},{8,10},{9,11},{10,... | collective-permute-start | bytes 393224 | tf_op jit(solution)/shard_map/ppermute | solution.py:439
  97.0 9.1 %collective-permute-start.32 = (bf16[288,128]{1,0:T(8,128)(2,1)S(1)}, bf16[288,128]{1,0:T(8,128)(2,1)S(1)}, u32[]{:S(2)}, u32[]{:S(2)}) collective-permute-start(bf16[288,128]{1,0:T(8,128)(2,1)S(1)} %fusion.106), channel_id=1, source_target_pairs={{0,4},{1,5},{2,6},{3,7},{4,0},{5,1},{6,2},{7,3},{8,12},{9,13},{10,... | collective-permute-start | bytes 221192 | tf_op jit(solution)/shard_map/ppermute | solution.py:439
  97.1 9.0 %collective-permute-start.31 = (bf16[256,128]{1,0:T(8,128)(2,1)S(1)}, bf16[256,128]{1,0:T(8,128)(2,1)S(1)}, u32[]{:S(2)}, u32[]{:S(2)}) collective-permute-start(bf16[256,128]{1,0:T(8,128)(2,1)S(1)} %fusion.112), channel_id=1, source_target_pairs={{0,4},{1,5},{2,6},{3,7},{4,0},{5,1},{6,2},{7,3},{8,12},{9,13},{10,... | collective-permute-start | bytes 196616 | tf_op jit(solution)/shard_map/ppermute | solution.py:439
  107.0 7.3 %collective-permute-start.38 = (bf16[256,128]{1,0:T(8,128)(2,1)S(1)}, bf16[256,128]{1,0:T(8,128)(2,1)S(1)}, u32[]{:S(2)}, u32[]{:S(2)}) collective-permute-start(bf16[256,128]{1,0:T(8,128)(2,1)S(1)} %fusion.110), channel_id=1, source_target_pairs={{0,4},{1,5},{2,6},{3,7},{4,0},{5,1},{6,2},{7,3},{8,12},{9,13},{10,... | collective-permute-start | bytes 196616 | tf_op jit(solution)/shard_map/ppermute | solution.py:439
  109.1 7.8 %copy-start.55 = (f32[32,128]{1,0:T(8,128)S(1)}, f32[32,128]{1,0:T(8,128)}, u32[]{:S(2)}) copy-start(f32[32,128]{1,0:T(8,128)} %get-tuple-element.363.first_ref) | copy-start | bytes 49156
  109.1 6.0 %collective-permute-start.33 = (bf16[800,128]{1,0:T(8,128)(2,1)}, bf16[800,128]{1,0:T(8,128)(2,1)S(1)}, u32[]{:S(2)}, u32[]{:S(2)}) collective-permute-start(bf16[800,128]{1,0:T(8,128)(2,1)} %get-tuple-element.369), channel_id=1, source_target_pairs={{0,1},{1,0},{2,3},{3,2},{4,5},{5,4},{6,7},{7,6},{8,9},{9,8},{10,11... | collective-permute-start | bytes 614408 | tf_op jit(solution)/shard_map/ppermute | solution.py:439
  111.2 7.8 %collective-permute-start.42 = (bf16[288,128]{1,0:T(8,128)(2,1)S(1)}, bf16[288,128]{1,0:T(8,128)(2,1)S(1)}, u32[]{:S(2)}, u32[]{:S(2)}) collective-permute-start(bf16[288,128]{1,0:T(8,128)(2,1)S(1)} %fusion.105), channel_id=1, source_target_pairs={{0,4},{1,5},{2,6},{3,7},{4,0},{5,1},{6,2},{7,3},{8,12},{9,13},{10,... | collective-permute-start | bytes 221192 | tf_op jit(solution)/shard_map/ppermute | solution.py:439
  114.3 6.3 %collective-permute-start.39 = (bf16[2,256,128]{2,1,0:T(8,128)(2,1)S(1)}, bf16[2,256,128]{2,1,0:T(8,128)(2,1)S(1)}, u32[]{:S(2)}, u32[]{:S(2)}) collective-permute-start(bf16[2,256,128]{2,1,0:T(8,128)(2,1)S(1)} %get-tuple-element.675), channel_id=1, source_target_pairs={{0,2},{1,3},{2,0},{3,1},{4,6},{5,7},{6,4},{7,5},{8,10},{9,11},{10,... | collective-permute-start | bytes 393224 | tf_op jit(solution)/shard_map/ppermute | solution.py:439
  117.0 6.3 %collective-permute-start.34 = (bf16[544,128]{1,0:T(8,128)(2,1)S(1)}, bf16[544,128]{1,0:T(8,128)(2,1)S(1)}, u32[]{:S(2)}, u32[]{:S(2)}) collective-permute-start(bf16[544,128]{1,0:T(8,128)(2,1)S(1)} %pad_maximum_fusion.16), channel_id=1, source_target_pairs={{0,2},{1,3},{2,0},{3,1},{4,6},{5,7},{6,4},{7,5},{8,10},{9,11},{10,... | collective-permute-start | bytes 417800 | tf_op jit(solution)/shard_map/ppermute | solution.py:439
  119.0 7.2 %collective-permute-start.43 = (bf16[2,288,128]{2,1,0:T(8,128)(2,1)S(1)}, bf16[2,288,128]{2,1,0:T(8,128)(2,1)S(1)}, u32[]{:S(2)}, u32[]{:S(2)}) collective-permute-start(bf16[2,288,128]{2,1,0:T(8,128)(2,1)S(1)} %get-tuple-element.671), channel_id=1, source_target_pairs={{0,2},{1,3},{2,0},{3,1},{4,6},{5,7},{6,4},{7,5},{8,10},{9,11},{10,... | collective-permute-start | bytes 442376 | tf_op jit(solution)/shard_map/ppermute | solution.py:439
  120.7 11.9 %collective-permute-start.40 = (bf16[2,2,256,128]{3,2,1,0:T(8,128)(2,1)S(1)}, bf16[2,2,256,128]{3,2,1,0:T(8,128)(2,1)S(1)}, u32[]{:S(2)}, u32[]{:S(2)}) collective-permute-start(bf16[2,2,256,128]{3,2,1,0:T(8,128)(2,1)S(1)} %get-tuple-element.669), channel_id=1, source_target_pairs={{0,1},{1,0},{2,3},{3,2},{4,5},{5,4},{6,7},{7,6},{8,9},{9,8},{10,11... | collective-permute-start | bytes 786440 | tf_op jit(solution)/shard_map/ppermute | solution.py:439
  123.4 6.8 %collective-permute-start.35 = (bf16[416,128]{1,0:T(8,128)(2,1)S(1)}, bf16[416,128]{1,0:T(8,128)(2,1)S(1)}, u32[]{:S(2)}, u32[]{:S(2)}) collective-permute-start(bf16[416,128]{1,0:T(8,128)(2,1)S(1)} %pad_maximum_fusion.20), channel_id=1, source_target_pairs={{0,4},{1,5},{2,6},{3,7},{4,0},{5,1},{6,2},{7,3},{8,12},{9,13},{10,... | collective-permute-start | bytes 319496 | tf_op jit(solution)/shard_map/ppermute | solution.py:439
  126.3 7.4 %collective-permute-start.44 = (bf16[2,2,288,128]{3,2,1,0:T(8,128)(2,1)S(1)}, bf16[2,2,288,128]{3,2,1,0:T(8,128)(2,1)S(1)}, u32[]{:S(2)}, u32[]{:S(2)}) collective-permute-start(bf16[2,2,288,128]{3,2,1,0:T(8,128)(2,1)S(1)} %get-tuple-element.667), channel_id=1, source_target_pairs={{0,16},{1,17},{2,18},{3,19},{4,20},{5,21},{6,22},{7,23},{8,24},{9,... | collective-permute-start | bytes 884744 | tf_op jit(solution)/shard_map/ppermute | solution.py:439
  130.2 1.3 collective-permute-start.36
  131.5 6.0 %collective-permute-start.37 = (bf16[32,128]{1,0:T(8,128)(2,1)S(1)}, bf16[32,128]{1,0:T(8,128)(2,1)S(1)}, u32[]{:S(2)}, u32[]{:S(2)}) collective-permute-start(bf16[32,128]{1,0:T(8,128)(2,1)S(1)} %reduce-precision_convert_fusion.1), channel_id=1, source_target_pairs={{0,16},{1,17},{2,18},{3,19},{4,20},{5,21},{6,22},{7,23},{8,24},{9,... | collective-permute-start | bytes 24584 | tf_op jit(solution)/shard_map/ppermute | solution.py:439
  132.6 14.2 %collective-permute-start.41 = (bf16[2,2,2,256,128]{4,3,2,1,0:T(8,128)(2,1)S(1)}, bf16[2,2,2,256,128]{4,3,2,1,0:T(8,128)(2,1)}, u32[]{:S(2)}, u32[]{:S(2)}) collective-permute-start(bf16[2,2,2,256,128]{4,3,2,1,0:T(8,128)(2,1)S(1)} %get-tuple-element.665), channel_id=1, source_target_pairs={{0,16},{1,17},{2,18},{3,19},{4,20},{5,21},{6,22},{7,23},{8,24},{9,... | collective-permute-start | bytes 1572872 | tf_op jit(solution)/shard_map/ppermute | solution.py:439
  133.8 15.2 %collective-permute-start.45 = (bf16[2,2,2,288,128]{4,3,2,1,0:T(8,128)(2,1)S(1)}, bf16[2,2,2,288,128]{4,3,2,1,0:T(8,128)(2,1)S(1)}, u32[]{:S(2)}, u32[]{:S(2)}) collective-permute-start(bf16[2,2,2,288,128]{4,3,2,1,0:T(8,128)(2,1)S(1)} %get-tuple-element.663), channel_id=1, source_target_pairs={{0,1},{1,0},{2,3},{3,2},{4,5},{5,4},{6,7},{7,6},{8,9},{9,8},{10,11... | collective-permute-start | bytes 1769480 | tf_op jit(solution)/shard_map/ppermute | solution.py:439
  137.5 12.7 %copy-start.25 = (bf16[1,2048,16]{1,2,0:T(8,128)(2,1)S(1)}, bf16[1,2048,16]{1,2,0:T(8,128)(2,1)}, u32[]{:S(2)}) copy-start(bf16[1,2048,16]{1,2,0:T(8,128)(2,1)} %param.26) | copy-start | bytes 196612
  137.5 12.7 %copy-start.33 = (s32[1,2048]{1,0:T(1,128)S(1)}, s32[1,2048]{1,0:T(1,128)}, u32[]{:S(2)}) copy-start(s32[1,2048]{1,0:T(1,128)} %target_ref.1) | copy-start | bytes 24580
  137.5 12.7 %copy-start.35 = (s32[1,2048]{1,0:T(1,128)S(1)}, s32[1,2048]{1,0:T(1,128)}, u32[]{:S(2)}) copy-start(s32[1,2048]{1,0:T(1,128)} %source_ref.1) | copy-start | bytes 24580
  137.5 12.7 %copy-start.38 = (s32[1,2048]{1,0:T(1,128)S(1)}, s32[1,2048]{1,0:T(1,128)}, u32[]{:S(2)}) copy-start(s32[1,2048]{1,0:T(1,128)} %mask_ref.1) | copy-start | bytes 24580
  137.5 12.7 %copy-start.47 = (bf16[384]{0:T(512)(128)(2,1)S(1)}, bf16[384]{0:T(512)(128)(2,1)}, u32[]{:S(2)}) copy-start(bf16[384]{0:T(512)(128)(2,1)} %param.37) | copy-start | bytes 2308
  137.5 12.7 %copy-start.50 = (bf16[384]{0:T(512)(128)(2,1)S(1)}, bf16[384]{0:T(512)(128)(2,1)}, u32[]{:S(2)}) copy-start(bf16[384]{0:T(512)(128)(2,1)} %param.38) | copy-start | bytes 2308
  137.5 12.7 %copy-start.59 = (bf16[128]{0:T(256)(128)(2,1)S(1)}, bf16[128]{0:T(256)(128)(2,1)}, u32[]{:S(2)}) copy-start(bf16[128]{0:T(256)(128)(2,1)} %param.32) | copy-start | bytes 772
  137.6 12.6 %copy-start.52 = (f32[32,128]{1,0:T(8,128)}, f32[32,128]{1,0:T(8,128)S(1)}, u32[]{:S(2)}) copy-start(f32[32,128]{1,0:T(8,128)S(1)} %fusion.116) | copy-start | bytes 49156
  150.4 4.6 %collective-permute-start.47 = (bf16[2,2,2,2,288,128]{5,4,3,2,1,0:T(8,128)(2,1)}, bf16[2,2,2,2,288,128]{5,4,3,2,1,0:T(8,128)(2,1)S(1)}, u32[]{:S(2)}, u32[]{:S(2)}) collective-permute-start(bf16[2,2,2,2,288,128]{5,4,3,2,1,0:T(8,128)(2,1)} %get-tuple-element.1408), channel_id=1, source_target_pairs={{0,8},{1,9},{2,10},{3,11},{4,12},{5,13},{6,14},{7,15},{8,0},{9,1},... | collective-permute-start | bytes 3538952 | tf_op jit(solution)/shard_map/ppermute | solution.py:439
  150.5 4.5 %collective-permute-start.46 = (bf16[2,2,2,2,256,128]{5,4,3,2,1,0:T(8,128)(2,1)}, bf16[2,2,2,2,256,128]{5,4,3,2,1,0:T(8,128)(2,1)S(1)}, u32[]{:S(2)}, u32[]{:S(2)}) collective-permute-start(bf16[2,2,2,2,256,128]{5,4,3,2,1,0:T(8,128)(2,1)} %get-tuple-element.1407), channel_id=1, source_target_pairs={{0,8},{1,9},{2,10},{3,11},{4,12},{5,13},{6,14},{7,15},{8,0},{9,1},... | collective-permute-start | bytes 3145736 | tf_op jit(solution)/shard_map/ppermute | solution.py:439
  155.0 1.4 copy-start.31
  (2 other events, 1.8 us)

commit v2 on v1

v2 whole, which is shorter than its diff:
```python
import functools

import jax
import jax.numpy as jnp
from jax import lax
from jax.experimental import pallas as pl
from jax.experimental.pallas import tpu as pltpu
from jax.sharding import PartitionSpec as P

F32 = jnp.float32
BF16 = jnp.bfloat16
H = 128
CAP = 64
GROUP = 16
SUB = 8
SIDE = CAP // 2
PIECES = 32
UNITS = H // PIECES
EXTRA = 32
VMEM_LIMIT = 60 * 1024 * 1024
BACK = 2
UNROLL = 4
AGG = 32
WORK = {(0, 1): (0,), (1, 1): (1,)}
COST = 0.02
KSTEP = 32
MATRIX_FIRST = True


def nn(a, b):
    return lax.dot_general(a, b, (((1,), (0,)), ((), ())), preferred_element_type=F32)


def nt(a, b):
    return lax.dot_general(a, b, (((1,), (1,)), ((), ())), preferred_element_type=F32)


def eye(n):
    rows = lax.broadcasted_iota(jnp.int32, (n, n), 0)
    cols = lax.broadcasted_iota(jnp.int32, (n, n), 1)
    return jnp.where(rows == cols, 1.0, 0.0).astype(BF16)


def one_hot_rows(rel, count):
    rel = jnp.clip(rel, -1, count).astype(F32).astype(BF16)
    rows = lax.broadcasted_iota(jnp.int32, (count, rel.shape[1]), 0).astype(F32).astype(BF16)
    return jnp.where(rows == rel, jnp.ones((), BF16), jnp.zeros((), BF16))


def slot_hots(slot, count):
    return one_hot_rows(jnp.right_shift(slot, 7), count), one_hot_rows(jnp.bitwise_and(slot, H - 1), H)


def sort_kernel(shape, me_ref, target_ref, source_ref, mask_ref, label_ref, feats_ref, states_ref, out_ref, slot_ref, data_ref):
    holders, own, groups = shape
    blocks = groups // 2
    edges = target_ref.shape[1]
    target = target_ref[...]
    owner = jnp.right_shift(target, own.bit_length() - 1)
    local = jnp.bitwise_and(target, own - 1)
    bucket = owner * (2 * groups) + jnp.right_shift(local, 3)
    bucket = jnp.where(mask_ref[...] != 0, bucket, -1)
    buckets = holders * groups * 2
    turn = jnp.bitwise_and(me_ref[0], 3)

    block = 256
    rows = lax.broadcasted_iota(jnp.int32, (block, block), 0)
    cols = lax.broadcasted_iota(jnp.int32, (block, block), 1)
    upto = jnp.where(rows <= cols, 1.0, 0.0).astype(BF16)
    numbers = lax.broadcasted_iota(jnp.int32, (buckets, block), 0)
    carry = jnp.zeros((buckets, 1), F32)
    slots = []
    for b in range(edges // block):
        here = bucket[:, b * block : (b + 1) * block]
        hot = numbers == here
        within = nn(hot.astype(F32).astype(BF16), upto) + carry
        rank = jnp.sum(jnp.where(hot, within - 1.0, 0.0), axis=0, keepdims=True).astype(jnp.int32)
        carry = within[:, block - 1 : block]
        at = jnp.where(jnp.bitwise_and(here, 1) == 0, rank, CAP - 1 - rank)
        side = jnp.bitwise_and(jnp.bitwise_and(here, 2) + jnp.right_shift(at, 5) + turn, 3)
        place = jnp.right_shift(here, 2) * H + side * SIDE + jnp.bitwise_and(at, SIDE - 1)
        slots.append(jnp.where((here >= 0) & (rank < CAP), place, -1))
    both = carry + jnp.concatenate([carry[1:, :], carry[:1, :]], axis=0)
    first_of_two = jnp.bitwise_and(lax.broadcasted_iota(jnp.int32, (buckets, 1), 0), 1) == 0
    worst = jnp.max(jnp.where(first_of_two, both, 0.0), axis=0, keepdims=True)
    flag = jnp.where(worst > CAP, 1.0, 0.0)
    slot = jnp.concatenate(slots, axis=1)
    slot_ref[...] = slot

    data_ref[16:32, :] = jnp.zeros((16, edges), F32)
    data_ref[0:16, :] = feats_ref[...].astype(F32)
    source = source_ref[...]
    data_ref[16:17, :] = jnp.right_shift(source, 6).astype(F32)
    data_ref[17:18, :] = jnp.bitwise_and(source, 63).astype(F32)
    data_ref[18:19, :] = (local + 1).astype(F32)
    data = data_ref[...].astype(BF16)

    tags = []
    for t in range(own // H):
        label = label_ref[:, t * H : (t + 1) * H]
        tags += [jnp.right_shift(label, 6).astype(F32), jnp.bitwise_and(label, 63).astype(F32)]
    tags.append(jnp.broadcast_to(flag, (1, H)))
    tags.append(jnp.zeros((16 - 3 * blocks - len(tags), H), F32))
    high, low = slot_hots(slot, holders * blocks)
    together = min(4, holders)
    for s0 in range(0, holders, together):
        part = high[s0 * blocks : (s0 + together) * blocks, :]
        spread = (part[:, None, :] * data[None, :, :]).reshape(together * blocks * 32, edges)
        moved = nt(spread, low)
        for n in range(together):
            out = out_ref.at[s0 + n]
            out[0:own, :] = states_ref[...]
            ids = []
            for q in range(blocks):
                at = (n * blocks + q) * 32
                out[own + 16 * q : own + 16 * (q + 1), :] = moved[at : at + 16, :].astype(BF16)
                ids.append(moved[at + 16 : at + 19, :])
            out[own + 16 * blocks : own + 16 * blocks + 16, :] = jnp.concatenate(ids + tags, axis=0).astype(BF16)


def swap_rows(outer, inner, flip=None):
    n = outer * inner
    rows = lax.broadcasted_iota(jnp.int32, (n, n), 0)
    cols = lax.broadcasted_iota(jnp.int32, (n, n), 1)
    number = jnp.bitwise_and(rows, inner - 1)
    if flip is not None:
        number = jnp.bitwise_xor(number, flip)
    source = number * outer + jnp.right_shift(rows, inner.bit_length() - 1)
    return jnp.where(source == cols, 1.0, 0.0).astype(BF16)


def split_kernel(w_ref, out_ref, order_ref):
    @pl.when(pl.program_id(0) == 0)
    def _():
        order_ref[...] = swap_rows(16, 16)

    order = order_ref[...]
    for ib in range(0, H, 32):
        sides = []
        for half in range(2):
            rows = [w_ref[:, (ib + 16 * half + i) * H : (ib + 16 * half + i + 1) * H] for i in range(16)]
            sides.append(jnp.concatenate(rows, axis=0))
        moved = nn(order, jnp.concatenate(sides, axis=1)).astype(BF16)
        for half in range(2):
            at = ib + 16 * half
            out_ref[:, at : at + 16, :] = moved[:, half * H : (half + 1) * H].reshape(16, 16, H)


def front_kernel(shape, chunks, *refs):
    holders, own, groups = shape
    blocks = groups // 2
    refs = list(refs)
    take = lambda n: [refs.pop(0) for _ in range(n)]
    piece_ref, given, states_ref, own_label_ref, t_in, b2_ref, w1_ref, b1_ref, wi_ref, wh_ref, bi_ref, bh_ref, cot_ref = take(13)
    new_ref, direct_ref, d_ref, crossed_ref, lat_out, near_out, meta_out = take(7)
    outs = take(3 * len(chunks) + 1)
    table_ref, p_ref, sum_ref, small_ref, dt_ref, rows_ref, bias_ref, extra_ref, t_ref, lat_ref, near_ref, meta_ref = take(12)
    built = take(3 * len(chunks) + 1)
    (sems,) = refs
    waiting = []

    def copy(source, target):
        moving = pltpu.make_async_copy(source, target, sems.at[len(waiting)])
        moving.start()
        waiting.append(moving)
        return moving

    t_copy = copy(t_in, t_ref)

    nodes = holders * own
    lanes = holders * SIDE
    ident = eye(H)
    tags_at = own + 16 * blocks

    flag = jnp.zeros((1, 1), F32)
    for s in range(holders):
        tags = given[s, tags_at : tags_at + 16, :].astype(F32)
        flag = jnp.maximum(flag, tags[3 * blocks + 2 * (own // H) : 3 * blocks + 2 * (own // H) + 1, 0:1])
        for t in range(own // H):
            at = s * own + t * H
            table_ref[0:H, at : at + H] = nt(ident, given[s, t * H : (t + 1) * H, :]).astype(BF16)
            both = tags[3 * blocks + 2 * t : 3 * blocks + 2 * t + 2, :]
            table_ref[H : H + 16, at : at + H] = jnp.concatenate([both, jnp.zeros((14, H), F32)], axis=0).astype(BF16)
    for t in range(own // H):
        label = own_label_ref[:, t * H : (t + 1) * H]
        label = jnp.concatenate([jnp.right_shift(label, 6), jnp.bitwise_and(label, 63)], axis=0).astype(F32)
        cols = nt(ident, jnp.concatenate([label, jnp.zeros((14, H), F32)], axis=0).astype(BF16))
        small_ref[t * H : (t + 1) * H, 0:1] = cols[:, 0:1] * 64.0 + cols[:, 1:2]

    side = lax.broadcasted_iota(jnp.int32, (24, H), 1) // SIDE
    crossing = jnp.zeros((1, H), F32)
    for q in range(blocks):
        for s in range(0, holders, 4):
            parts = []
            for n in range(4):
                feats = given[s + n, own + 16 * q : own + 16 * (q + 1), :].astype(F32)
                ids = given[s + n, tags_at : tags_at + 16, :].astype(F32)[3 * q : 3 * q + 3, :]
                parts.append(jnp.concatenate([feats, ids, jnp.zeros((5, H), F32)], axis=0))
            at = slice(s // 4 * H, (s // 4 + 1) * H)
            for u in range(4):
                page = parts[(3 - u) % 4]
                for c in range(3):
                    page = jnp.where(side == c, parts[(c - u) % 4], page)
                meta_ref[4 * q + u, 0:24, at] = page
                low = float((4 * q + u) * SUB)
                node = page[18:19, :] - 1.0
                outside = (node >= 0.0) & ((node < low) | (node >= low + SUB))
                crossing = jnp.maximum(crossing, jnp.where(outside, 1.0, 0.0))
    crossed = jnp.max(crossing) > 0.0
    crossed_ref[0] = crossed.astype(jnp.int32)

    w1 = nt(ident, w1_ref[...]).astype(BF16)
    b1 = nt(ident, jnp.broadcast_to(b1_ref[...].astype(F32), (16, H)).astype(BF16))[:, 0:1]

    def both_pages(ref, g, rows):
        return jnp.concatenate([ref[2 * g + n, rows, :] for n in range(2)], axis=1)

    def group_step(usual, g, unused):
        data = both_pages(meta_ref, g, slice(0, 24))
        source = (data[16:17, :] * 64.0 + data[17:18, :]).astype(jnp.int32)
        picked = jnp.zeros((H + 16, 2 * lanes), F32)
        for c in range(0, nodes, 256):
            picked = picked + nn(table_ref[:, c : c + 256], one_hot_rows(source - c, 256))
        near = picked[0:H, :].astype(BF16)
        label = picked[H : H + 1, :] * 64.0 + picked[H + 1 : H + 2, :]
        inside = data[18:19, :] - 1.0 - (g * GROUP).astype(F32)
        numbers = lax.broadcasted_iota(jnp.int32, (GROUP, 2 * lanes), 0).astype(F32)
        own_label = small_ref[pl.ds(pl.multiple_of(g * GROUP, GROUP), GROUP), 0:1]
        member = jnp.where((numbers == inside) & (own_label == label), 1.0, 0.0)
        before = nn(w1, data[0:16, :].astype(BF16)) + b1
        latent = before / (1.0 + jnp.exp(-before))
        made = []
        for n in range(2):
            page = slice(n * lanes, (n + 1) * lanes)
            meta_ref[2 * g + n, 24:25, :] = source[:, page].astype(F32)
            meta_ref[2 * g + n, 32 : 32 + GROUP, :] = member[:, page]
            lat_ref[2 * g + n] = latent[:, page].astype(BF16)
            near_ref[2 * g + n] = near[:, page]
            mine = member[n * SUB : (n + 1) * SUB, :]
            if usual:
                units, states, mine = latent[:, page], near[:, page], mine[:, page]
            else:
                units, states = latent, near
            spread = (units[:, None, :] * mine[None, :, :]).reshape(H * SUB, -1).astype(BF16)
            made.append(nt(spread, states).reshape(H, SUB, H))
        at = pl.ds(pl.multiple_of(g * GROUP, GROUP), GROUP)
        p_ref[:, at, :] = jnp.concatenate(made, axis=1).astype(BF16)
        sum_ref[at, :] = nt(member.astype(BF16), near)
        return unused

    @pl.when(jnp.logical_not(crossed))
    def _():
        lax.fori_loop(0, groups, functools.partial(group_step, True), 0, unroll=UNROLL)

    @pl.when(crossed)
    def _():
        lax.fori_loop(0, groups, functools.partial(group_step, False), 0)

    copy(lat_ref, lat_out)
    copy(near_ref, near_out)
    copy(meta_ref, meta_out)

    def agg_step(n, total):
        left = jnp.concatenate([p_ref[n * AGG + m] for m in range(AGG)], axis=1)
        right = jnp.concatenate([t_ref[n * AGG + m] for m in range(AGG)], axis=1)
        return total + nt(left, right)

    total = nt(sum_ref[...].astype(BF16), b2_ref[...])
    t_copy.wait()
    total = lax.fori_loop(0, H // AGG, agg_step, total)

    mixed = total.astype(BF16)
    prior = states_ref[...]
    prior_f = prior.astype(F32)
    cot = cot_ref[...].astype(F32)
    wi, wh = wi_ref[...], wh_ref[...]
    gi = nn(mixed, wi) + bi_ref[...]
    gh = nn(prior, wh) + bh_ref[...]
    r = jax.nn.sigmoid(gi[:, 0:H] + gh[:, 0:H])
    u = jax.nn.sigmoid(gi[:, H : 2 * H] + gh[:, H : 2 * H])
    n = jnp.tanh(gi[:, 2 * H :] + r * gh[:, 2 * H :])
    new_ref[...] = ((1.0 - u) * n + u * prior_f).astype(BF16)
    d_pre = (1.0 - u) * cot * (1.0 - n * n)
    d_r = d_pre * gh[:, 2 * H :] * r * (1.0 - r)
    d_u = (prior_f - n) * cot * u * (1.0 - u)
    d_gi = jnp.concatenate([d_r, d_u, d_pre], axis=1)
    d_gh = jnp.concatenate([d_r, d_u, d_pre * r], axis=1)

    def halves(x):
        high = x.astype(BF16)
        return high, (x - high.astype(F32)).astype(BF16)

    def twice(x):
        return jnp.concatenate([x, x], axis=1)

    gi_high, gi_low = halves(d_gi)
    gh_high, gh_low = halves(d_gh)
    d_agg = nt(jnp.concatenate([gi_high, gi_low], axis=1), twice(wi)).astype(BF16)
    d_ref[...] = d_agg
    dt_ref[...] = nt(ident, d_agg).astype(BF16)
    direct_ref[...] = u * cot + nt(jnp.concatenate([gh_high, gh_low], axis=1), twice(wh))

    piece_me = piece_ref[0]
    joint = built[-1]

    def dest(c, rel):
        place = chunks[c].place(rel)
        if rel >= PIECES // 2:
            return joint, place, chunks[c].offset
        for n, count in enumerate((PIECES // 8, PIECES // 8, PIECES // 4)):
            if place < count:
                return built[3 * c + n], place, 0
            place -= count

    for rel in list(range(PIECES // 2, PIECES)) + list(range(PIECES // 2)):
        k0 = jnp.bitwise_xor(piece_me, rel) * UNITS
        for m in range(0, UNITS, 2):
            out = nn(dt_ref[...], jnp.concatenate([p_ref[k0 + m], p_ref[k0 + m + 1]], axis=1)).astype(BF16)
            for c, chunk in enumerate(chunks):
                ref, place, offset = dest(c, rel)
                for h in range(2):
                    start = offset + (m + h) * chunk.rows
                    ref[place, start : start + chunk.rows, :] = out[
                        chunk.first : chunk.first + chunk.rows, h * H : (h + 1) * H
                    ]
        if rel == PIECES // 2 - 1:
            for n in range(3):
                copy(built[n], outs[n])

    mixed_t = nt(ident, mixed).astype(BF16)
    prior_t = nt(ident, prior).astype(BF16)
    from_input = nn(twice(mixed_t), jnp.concatenate([gi_high, gi_low], axis=0))
    from_state = nn(twice(prior_t), jnp.concatenate([gh_high, gh_low], axis=0))
    for t in range(3):
        rows_ref[t] = from_input[:, t * H : (t + 1) * H]
        rows_ref[3 + t] = from_state[:, t * H : (t + 1) * H]
    rows_ref[6] = nn(dt_ref[...], sum_ref[...].astype(BF16))
    bias_ref[...] = jnp.zeros_like(bias_ref)
    for n, part in enumerate((d_gi, d_gh)):
        part = jnp.sum(part, axis=0, keepdims=True)
        for t in range(3):
            bias_ref[3 * n + t : 3 * n + t + 1, :] = part[:, t * H : (t + 1) * H]
    extra_ref[...] = jnp.zeros_like(extra_ref)
    extra_ref[29:30, :] = jnp.broadcast_to(flag, (1, H))
    last = chunks[-1]
    for rel in list(range(PIECES // 2, PIECES)) + list(range(PIECES // 2)):
        p = jnp.bitwise_xor(piece_me, rel)
        for t in range(7):
            extra_ref[UNITS * t : UNITS * (t + 1), :] = rows_ref[t, pl.ds(p * UNITS, UNITS), :]
        extra_ref[28:29, :] = bias_ref[pl.ds(p, 1), :]
        ref, place, offset = dest(len(chunks) - 1, rel)
        ref[place, offset + UNITS * last.rows : offset + last.height, :] = extra_ref[...].astype(BF16)
        if rel == PIECES - 1:
            copy(joint, outs[-1])
    for n in range(3, len(built) - 1):
        copy(built[n], outs[n])
    for moving in waiting[1:]:
        moving.wait()


def spread_kernel(shape, d_ref, t_ref, b2_ref, wide_ref, bias_ref, dp_ref, order_ref):
    holders, own, groups = shape
    d = d_ref[...]

    @pl.when(pl.program_id(0) == 0)
    def _():
        bias_ref[...] = nn(d, b2_ref[...])
        order_ref[...] = swap_rows(16, 16)

    order = order_ref[...]
    for n in range(0, t_ref.shape[0], 2):
        out = nn(d, jnp.concatenate([t_ref[n], t_ref[n + 1]], axis=1)).astype(BF16)
        dp_ref[n] = out[:, :H]
        dp_ref[n + 1] = out[:, H:]
    for k in range(0, t_ref.shape[0], 16):
        for g in range(0, groups, 2):
            sides = [dp_ref[k : k + 16, (g + n) * GROUP : (g + n + 1) * GROUP, :].reshape(256, H) for n in range(2)]
            moved = nn(order, jnp.concatenate(sides, axis=1)).astype(BF16)
            for n in range(2):
                for v in range(GROUP):
                    wide_ref[g + n, k : k + 16, v * H : (v + 1) * H] = moved[v * 16 : (v + 1) * 16, n * H : (n + 1) * H]


def back_kernel(shape, count, begins, *refs):
    holders, own, groups = shape
    crossed_ref, wide_ref, bias_ref, w1_ref, b1_ref, lat_ref, near_ref, meta_ref = refs[:8]
    part_ref, first_ref, edge_ref = refs[-3:]
    nodes = holders * own
    lanes = holders * SIDE
    ident = eye(H)
    if begins:
        part_ref[...] = jnp.zeros_like(part_ref)
        first_ref[...] = jnp.zeros_like(first_ref)
    else:
        part_ref[...] = refs[8][...]
        first_ref[...] = refs[9][...]
    w1n = w1_ref[...]
    w1 = nt(ident, w1n).astype(BF16)
    b1 = nt(ident, jnp.broadcast_to(b1_ref[...].astype(F32), (16, H)).astype(BF16))[:, 0:1]
    one_row = jnp.where(lax.broadcasted_iota(jnp.int32, (16, 2 * lanes), 0) == 0, 1.0, 0.0).astype(BF16)

    def both_pages(ref, g, rows):
        return jnp.concatenate([ref[2 * g + n, rows, :] for n in range(2)], axis=1)

    def group_step(usual, g, first_total):
        wide = wide_ref[g]
        wide_t = jnp.concatenate([wide[:, v * H : (v + 1) * H].T for v in range(GROUP)], axis=1)
        bias_rows = bias_ref[pl.ds(pl.multiple_of(g * GROUP, GROUP), GROUP), :].astype(BF16)
        bias_t = nt(ident, bias_rows).astype(BF16)
        data = both_pages(meta_ref, g, slice(0, 16)).astype(BF16)
        source = both_pages(meta_ref, g, slice(24, 25)).astype(jnp.int32)
        member = both_pages(meta_ref, g, slice(32, 32 + GROUP)).astype(BF16)
        d_latent, d_near = [], []
        for n in range(2):
            low, number = (n * SUB, SUB) if usual else (0, GROUP)
            mine = meta_ref[2 * g + n, 32 + low : 32 + low + number, :].astype(BF16)
            part = slice(low * H, (low + number) * H)
            spread = (near_ref[2 * g + n][None, :, :] * mine[:, None, :]).reshape(number * H, lanes)
            d_latent.append(nn(wide[:, part], spread))
            spread = (lat_ref[2 * g + n][None, :, :] * mine[:, None, :]).reshape(number * H, lanes)
            d_near.append(nn(wide_t[:, part], spread))
        d_latent = jnp.concatenate(d_latent, axis=1)
        d_near = (jnp.concatenate(d_near, axis=1) + nn(bias_t, member)).astype(BF16)
        for c in range(0, nodes, 256):
            part_ref[c : c + 256, :] += nt(one_hot_rows(source - c, 256), d_near)
        before = nn(w1, data) + b1
        gate = 1.0 / (1.0 + jnp.exp(-before))
        d_before = (d_latent * gate * (1.0 + before * (1.0 - gate))).astype(BF16)
        edges = nn(w1n, d_before)
        for n in range(2):
            edge_ref[2 * g + n] = edges[:, n * lanes : (n + 1) * lanes]
        return first_total + nt(jnp.concatenate([data, one_row], axis=0), d_before)

    @pl.when(crossed_ref[0] == 0)
    def _():
        first_ref[...] = lax.fori_loop(
            0, count, functools.partial(group_step, True), first_ref[...], unroll=min(2, count)
        )

    @pl.when(crossed_ref[0] != 0)
    def _():
        first_ref[...] = lax.fori_loop(0, count, functools.partial(group_step, False), first_ref[...])


def return_kernel(shape, masks, me_ref, part_ref, *refs):
    holders, own, groups = shape
    blocks = groups // 2
    edges, (keep_d, keep_e, send_ref, slab_ref) = refs[:-4], refs[-4:]
    side = lax.broadcasted_iota(jnp.int32, (16, H), 1) // SIDE
    each = 2 * groups // len(edges)
    for q in range(blocks):
        for s in range(holders):
            at = slice(s // 4 * H, (s // 4 + 1) * H)
            parts = [edges[(4 * q + u) // each][(4 * q + u) % each, :, at] for u in range(4)]
            page = parts[(3 - s) % 4]
            for c in range(3):
                page = jnp.where(side == c, parts[(c - s) % 4], page)
            slab_ref[s, 16 * q : 16 * (q + 1), :] = page.astype(BF16)
    half = holders // 2
    for n in range(holders):
        rel = sum(mask for i, mask in enumerate(reversed(masks)) if n >> i & 1)
        h = jnp.bitwise_xor(me_ref[0], rel)
        rows = part_ref[pl.ds(pl.multiple_of(h * own, own), own), :].astype(BF16)
        if n < half:
            keep_d[n] = rows
            keep_e[n] = slab_ref[h]
        else:
            send_ref[(n - half) * own : (n - half + 1) * own, :] = rows
            at = half * own + (n - half) * 16 * blocks
            send_ref[at : at + 16 * blocks, :] = slab_ref[h]


def gather_kernel(shape, sources, me_ref, slot_ref, direct_ref, part_ref, slabs_ref, state_ref, edge_ref, data_ref):
    holders, own, groups = shape
    blocks = groups // 2
    state_ref[...] = direct_ref[...] + part_ref[...].astype(F32)
    for n, rel in enumerate(sources):
        h = jnp.bitwise_xor(me_ref[0], rel)
        data_ref[pl.ds(pl.multiple_of(h * 16 * blocks, 16), 16 * blocks), :] = slabs_ref[n]
    edges = slot_ref.shape[1]
    data = data_ref[...]
    count = holders * blocks
    block = 512
    for b in range(edges // block):
        high, low = slot_hots(slot_ref[:, b * block : (b + 1) * block], count)
        high = high.astype(F32)
        found = nn(data, low)
        total = jnp.zeros((16, block), F32)
        for n in range(count):
            total = total + found[16 * n : 16 * (n + 1), :] * high[n : n + 1, :]
        edge_ref[:, b * block : (b + 1) * block] = total


class Chunk:
    def __init__(self, first, rows, extra, order, offset):
        self.first, self.rows, self.extra, self.order, self.offset = first, rows, extra, order, offset
        self.height = UNITS * rows + extra

    def place(self, rel):
        at = 0
        for bit in self.order:
            at = at * 2 + (rel >> bit & 1)
        return at

    def shape(self):
        return (2,) * len(self.order) + (self.height, H)


def plan(batch, edge):
    core, x = [edge], [edge << n for n in range(1, batch.bit_length() - 1)]
    z = [2 << n for n in reversed(range(3 - len(x)))]
    bits = z + [1] + x + core
    chunks = [Chunk(0, 64, 0, (3, 2, 1, 0), 0), Chunk(64, 64, EXTRA, (2, 3, 1, 0), 64 * UNITS)]
    device = lax.axis_index(("batch", "edge")).astype(jnp.int32)
    piece = sum(jnp.where(device & mask != 0, 1 << n, 0) for n, mask in enumerate(bits))
    return bits, chunks, piece.astype(jnp.int32).reshape(1)


def swap(x, mask, devices):
    return lax.ppermute(x, ("batch", "edge"), [(i, i ^ mask) for i in range(devices)])


def add(terms):
    total = terms[0].astype(F32)
    for term in terms[1:]:
        total = total + term.astype(F32)
    return total.astype(BF16)


def rounded(x):
    return lax.reduce_precision(x.astype(F32), 8, 7).astype(BF16)


def unpack(chunks, half, me, order_ref, given, block_refs, w_out, rows_ref, sems, beside=lambda: None):
    steps = PIECES // 8
    width = 4 * UNITS

    def coming(step):
        copies = []
        for c, chunk in enumerate(chunks):
            at = pl.ds(chunk.place(4 * step), 4)
            copies.append(pltpu.make_async_copy(given[c].at[at], block_refs[c].at[at], sems.at[2 + len(chunks) * step + c]))
        return copies

    def leaving(step):
        start = jnp.bitwise_xor(jnp.right_shift(me, 2), step + half * steps) * width
        rows = pl.ds(pl.multiple_of(start, width), width)
        return pltpu.make_async_copy(rows_ref.at[step % 2], w_out.at[rows, :], sems.at[step % 2])

    for step in range(steps):
        for copy in coming(step):
            copy.start()
    order_ref[...] = swap_rows(32, 2 * UNITS, jnp.bitwise_and(me, 1) * UNITS)
    beside()
    for step in range(steps):
        for copy in coming(step):
            copy.wait()
        if step >= 2:
            leaving(step - 2).wait()
        for pair in range(2):
            rel = 4 * step + 2 * pair
            places = [[chunk.place(rel + n) for n in range(2)] for chunk in chunks]
            upper = jnp.bitwise_xor(jnp.bitwise_and(jnp.right_shift(me, 1), 1), pair)
            at_rows = pl.ds(pl.multiple_of(upper * 2 * UNITS, 2 * UNITS), 2 * UNITS)
            for ib in range(0, H, 64):
                sides = []
                for side in range(2):
                    at = ib + 32 * side
                    c = max(n for n in range(len(chunks)) if chunks[n].first <= at)
                    first, rows = chunks[c].first, chunks[c].rows
                    parts = [
                        block_refs[c][places[c][n], m * rows + at - first : m * rows + at - first + 32, :]
                        for n in range(2)
                        for m in range(UNITS)
                    ]
                    sides.append(jnp.concatenate(parts, axis=0))
                moved = nn(order_ref[...], jnp.concatenate(sides, axis=1))
                for side in range(2):
                    for i in range(32):
                        at = (ib + 32 * side + i) * H
                        rows_ref[step % 2, at_rows, at : at + H] = moved[8 * i : 8 * (i + 1), side * H : (side + 1) * H]
        leaving(step).start()

    def end():
        for step in range(steps - 2, steps):
            leaving(step).wait()

    return end


def small_pieces(chunks, half, me, block_refs, extra_ref, bias_ref):
    last = chunks[-1]
    start = UNITS * last.rows
    for n in range(PIECES // 2):
        extra = block_refs[-1][last.place(n), start : start + EXTRA, :].astype(F32)
        p = jnp.bitwise_xor(me, n + half * PIECES // 2)
        for t in range(7):
            extra_ref[t, pl.ds(p * UNITS, UNITS), :] = extra[UNITS * t : UNITS * (t + 1), :]
        bias_ref[pl.ds(p, 1), :] = extra[28:29, :]


def own_half_kernel(chunks, piece_ref, *refs):
    count = len(chunks)
    given, (w_out, extra_ref, bias_ref) = refs[:count], refs[count : count + 3]
    block_refs, (rows_ref, order_ref, sems) = refs[count + 3 : 2 * count + 3], refs[2 * count + 3 :]
    me = piece_ref[0]
    extra_ref[...] = jnp.zeros_like(extra_ref)
    bias_ref[...] = jnp.zeros_like(bias_ref)
    end = unpack(chunks, 0, me, order_ref, given, block_refs, w_out, rows_ref, sems)
    small_pieces(chunks, 0, me, block_refs, extra_ref, bias_ref)
    end()


def other_half_kernel(chunks, piece_ref, *refs):
    count = len(chunks)
    given, (first_ref, extra_in, bias_in, w_in) = refs[:count], refs[count : count + 4]
    w_out, w1_ref, b1_ref, wi_ref, wh_ref, b2_ref, bi_ref, bh_ref = refs[count + 4 : count + 12]
    block_refs = refs[count + 12 : 2 * count + 12]
    rows_ref, order_ref, extra_ref, bias_ref, sems = refs[2 * count + 12 :]
    me = piece_ref[0]

    def beside():
        w1_ref[...] = first_ref[0:16, :].astype(F32)
        b1_ref[...] = first_ref[16:17, :].astype(F32).reshape(H)
        extra_ref[...] = extra_in[...]
        bias_ref[...] = bias_in[...]

    end = unpack(chunks, 1, me, order_ref, given, block_refs, w_out, rows_ref, sems, beside)
    small_pieces(chunks, 1, me, block_refs, extra_ref, bias_ref)
    for t in range(3):
        wi_ref[:, t * H : (t + 1) * H] = extra_ref[t]
        wh_ref[:, t * H : (t + 1) * H] = extra_ref[3 + t]
        bi_ref[t * H : (t + 1) * H] = bias_ref[t : t + 1, :].reshape(H)
        bh_ref[t * H : (t + 1) * H] = bias_ref[3 + t : 4 + t, :].reshape(H)
    b2_ref[...] = extra_ref[6]
    end()


def vmem():
    return pl.BlockSpec(memory_space=pltpu.VMEM)


def anywhere():
    return pl.BlockSpec(memory_space=pl.ANY)


def smem():
    return pl.BlockSpec(memory_space=pltpu.SMEM)


def cost(us):
    return pl.CostEstimate(flops=int(us * COST * 1e9), bytes_accessed=int(us * COST * 3e6), transcendentals=0)


def params():
    return pltpu.CompilerParams(vmem_limit_bytes=VMEM_LIMIT)


def fast_path(batch, edge, args):
    (states, edge_feats, molecule, source, target, edge_mask, w_edge_in, b_edge_in, w_edge_out, b_edge_out,
     w_input, w_hidden, b_input, b_hidden, cotangent) = args
    devices = batch * edge
    states_here = states[0]
    own = states_here.shape[0]
    edges = source.shape[1]
    holders, groups = edge, own // GROUP
    shape = (holders, own, groups)
    blocks = groups // 2
    bits, chunks, piece_arr = plan(batch, edge)
    rest = [m for m in (1 << n for n in range(devices.bit_length() - 1)) if m not in bits]
    me_arr = lax.axis_index("edge").astype(jnp.int32).reshape(1)
    lanes = holders * SIDE
    pages = 2 * groups

    slots_out, slot = pl.pallas_call(
        functools.partial(sort_kernel, shape),
        name="edges_to_slots",
        out_shape=[
            jax.ShapeDtypeStruct((holders, own + 16 * blocks + 16, H), BF16),
            jax.ShapeDtypeStruct((1, edges), jnp.int32),
        ],
        in_specs=[smem()] + [vmem()] * 6,
        out_specs=[vmem()] * 2,
        scratch_shapes=[pltpu.VMEM((32, edges), F32)],
        compiler_params=params(),
    )(me_arr, target, source, edge_mask, molecule, jnp.swapaxes(edge_feats, 1, 2)[0], states_here)
    given = lax.all_to_all(slots_out, "edge", 0, 0)

    t_units = pl.pallas_call(
        split_kernel,
        name="split_weight",
        grid=(H // 16,),
        in_specs=[pl.BlockSpec((16, H * H), lambda i: (i, 0))],
        out_specs=pl.BlockSpec((16, H, H), lambda i: (i, 0, 0)),
        out_shape=jax.ShapeDtypeStruct((H, H, H), BF16),
        scratch_shapes=[pltpu.VMEM((256, 256), BF16)],
        compiler_params=params(),
        cost_estimate=cost(6),
    )(w_edge_out)
    b2 = b_edge_out.reshape(H, H)
    b1 = b_edge_in.reshape(1, H)
    built = [jax.ShapeDtypeStruct((PIECES // n, c.height, H), BF16) for c in chunks for n in (8, 8, 4)]
    built.append(jax.ShapeDtypeStruct((PIECES // 2, sum(c.height for c in chunks), H), BF16))
    front = pl.pallas_call(
        functools.partial(front_kernel, shape, chunks),
        name="messages_update_weight_gradient",
        out_shape=[
            jax.ShapeDtypeStruct((own, H), BF16),
            jax.ShapeDtypeStruct((own, H), F32),
            jax.ShapeDtypeStruct((own, H), BF16),
            jax.ShapeDtypeStruct((1,), jnp.int32),
            jax.ShapeDtypeStruct((pages, H, lanes), BF16),
            jax.ShapeDtypeStruct((pages, H, lanes), BF16),
            jax.ShapeDtypeStruct((pages, 32 + GROUP, lanes), F32),
        ]
        + built,
        in_specs=[smem()] + [vmem()] * 3 + [anywhere()] + [vmem()] * 8,
        out_specs=[vmem()] * 3 + [smem()] + [anywhere()] * (3 + len(built)),
        scratch_shapes=[
            pltpu.VMEM((H + 16, holders * own), BF16),
            pltpu.VMEM((H, own, H), BF16),
            pltpu.VMEM((own, H), F32),
            pltpu.VMEM((own, H), F32),
            pltpu.VMEM((H, own), BF16),
            pltpu.VMEM((7, H, H), F32),
            pltpu.VMEM((PIECES, H), F32),
            pltpu.VMEM((EXTRA, H), F32),
            pltpu.VMEM((H, H, H), BF16),
            pltpu.VMEM((pages, H, lanes), BF16),
            pltpu.VMEM((pages, H, lanes), BF16),
            pltpu.VMEM((pages, 32 + GROUP, lanes), F32),
        ]
        + [pltpu.VMEM(h.shape, BF16) for h in built]
        + [pltpu.SemaphoreType.DMA((4 + len(built),))],
        compiler_params=params(),
    )(
        piece_arr, given, states_here, molecule, t_units, b2, w_edge_in, b1, w_input, w_hidden,
        b_input.astype(F32).reshape(1, -1), b_hidden.astype(F32).reshape(1, -1), cotangent[0],
    )
    new_states, direct, d_agg, crossed, latent, near, meta = front[:7]
    built = front[7:]

    matrix_gradients = pl.pallas_call(
        functools.partial(spread_kernel, shape),
        name="matrix_gradients",
        out_shape=[jax.ShapeDtypeStruct((groups, H, GROUP * H), BF16), jax.ShapeDtypeStruct((own, H), F32)],
        grid=(H // KSTEP,),
        in_specs=[
            pl.BlockSpec((own, H), lambda i: (0, 0)),
            pl.BlockSpec((KSTEP, H, H), lambda i: (i, 0, 0)),
            pl.BlockSpec((H, H), lambda i: (0, 0)),
        ],
        out_specs=[
            pl.BlockSpec((groups, KSTEP, GROUP * H), lambda i: (0, i, 0)),
            pl.BlockSpec((own, H), lambda i: (0, 0)),
        ],
        scratch_shapes=[pltpu.VMEM((KSTEP, own, H), BF16), pltpu.VMEM((256, 256), BF16)],
        compiler_params=params(),
        cost_estimate=cost(6),
    )

    count = groups // BACK
    edge_parts = []
    pending = []

    def back_step(n, wide, bias, sums):
        whole_spec = lambda shp: pl.BlockSpec(shp, lambda i: (0, 0))
        *sums, edge_part = pl.pallas_call(
            functools.partial(back_kernel, shape, count, not sums),
            name="edge_gradients",
            out_shape=[
                jax.ShapeDtypeStruct((holders * own, H), F32),
                jax.ShapeDtypeStruct((32, H), F32),
                jax.ShapeDtypeStruct((2 * count, 16, lanes), F32),
            ],
            grid=(1,),
            in_specs=[
                smem(),
                pl.BlockSpec((count, H, GROUP * H), lambda i: (n, 0, 0)),
                pl.BlockSpec((count * GROUP, H), lambda i: (n, 0)),
                whole_spec((16, H)),
                whole_spec((1, H)),
                pl.BlockSpec((2 * count, H, lanes), lambda i: (n, 0, 0)),
                pl.BlockSpec((2 * count, H, lanes), lambda i: (n, 0, 0)),
                pl.BlockSpec((2 * count, 32 + GROUP, lanes), lambda i: (n, 0, 0)),
            ]
            + [whole_spec((holders * own, H)), whole_spec((32, H))][: len(sums)],
            out_specs=[
                whole_spec((holders * own, H)),
                whole_spec((32, H)),
                pl.BlockSpec((2 * count, 16, lanes), lambda i: (0, 0, 0)),
            ],
            compiler_params=params(),
            cost_estimate=cost(24 // BACK),
        )(crossed, wide, bias, w_edge_in, b1, latent, near, meta, *sums)
        edge_parts.append(edge_part)
        return tuple(sums)

    if MATRIX_FIRST:
        sent, d_agg = lax.optimization_barrier((built[-1], d_agg))
        other = swap(sent, bits[-1], devices)
        other, (wide, bias) = lax.optimization_barrier((other, matrix_gradients(d_agg, t_units, b2)))
    else:
        other = swap(built[-1], bits[-1], devices)
        wide, bias = matrix_gradients(d_agg, t_units, b2)
    other = other.reshape((2,) * 4 + (-1, H))
    kept = [
        {(0, 0): built[3 * c], (0, 1): built[3 * c + 1], (1,): built[3 * c + 2]} for c in range(len(chunks))
    ]
    got = [[] for _ in chunks]

    def mine(c, path):
        for head, x in kept[c].items():
            if path[: len(head)] == head:
                return x.reshape((2,) * (4 - len(head)) + x.shape[1:])[path[len(head) :]]

    def partial_sum(c, path):
        rows = slice(chunks[c].offset, chunks[c].offset + chunks[c].height)
        parts = [mine(c, path), other[path][..., rows, :]]
        for n, x in enumerate(got[c]):
            parts.append(x[path[n + 1 :]])
        return add(parts)

    def scatter_step(c, step, work=None, given=()):
        begun = partial_sum(c, (0,) * step + (1,))
        mask = bits[chunks[c].order[step]]
        if work is None:
            got[c].append(swap(begun, mask, devices))
            return None
        begun, given = lax.optimization_barrier((begun, given))
        new, result = lax.optimization_barrier((swap(begun, mask, devices), work(*given)))
        got[c].append(new)
        return result

    def work_on(numbers, wide, bias):
        def run(*sums):
            for n in numbers:
                sums = back_step(n, wide, bias, sums)
            return sums

        return run

    def gather_step(x, mask):
        return jnp.stack([x, swap(x, mask, devices)], axis=0)

    back_masks = [m for m in (1 << n for n in range(edge.bit_length() - 1))]

    def send_back(part, *edge_parts):
        return pl.pallas_call(
            functools.partial(return_kernel, shape, back_masks),
            name="returned",
            out_shape=[
                jax.ShapeDtypeStruct((holders // 2, own, H), BF16),
                jax.ShapeDtypeStruct((holders // 2, 16 * blocks, H), BF16),
                jax.ShapeDtypeStruct((holders // 2 * (own + 16 * blocks), H), BF16),
            ],
            in_specs=[smem()] + [vmem()] * (1 + BACK),
            out_specs=[vmem()] * 3,
            scratch_shapes=[pltpu.VMEM((holders, 16 * blocks, H), BF16)],
            compiler_params=params(),
            cost_estimate=cost(2),
        )(me_arr, part, *edge_parts)

    sums = ()
    for step in range(4):
        for c in range(len(chunks)):
            if (step, c) in WORK:
                sums = scatter_step(c, step, work_on(WORK[step, c], wide, bias), sums)
            else:
                scatter_step(c, step)
    parts = [partial_sum(c, (0,) * 4) for c in range(len(chunks))]
    for mask in rest:
        parts = [rounded(x.astype(F32) + swap(x, mask, devices).astype(F32)) for x in parts]
    overflow = parts[-1][UNITS * chunks[-1].rows + 29, 0] > 0.0
    for step in (3, 2, 1, 0):
        for c, chunk in enumerate(chunks):
            parts[c] = gather_step(parts[c], bits[chunk.order[step]])
    part, first = sums
    keep_d, keep_e, send = send_back(part, *edge_parts)

    first = rounded(first)
    slabs, sources = keep_e[:, None], [0]
    for mask in back_masks:
        n = keep_d.shape[0]
        cut = n * own
        arrived = swap(jnp.concatenate([send, first], axis=0), mask, devices)
        keep_d = add([keep_d, arrived[:cut].reshape(n, own, H)])
        slabs = jnp.concatenate([slabs, arrived[cut:-32].reshape(n, -1, 16 * blocks, H)], axis=1)
        first = rounded(first.astype(F32) + arrived[-32:].astype(F32))
        sources = sources + [s ^ mask for s in sources]
        if n > 1:
            send = jnp.concatenate([keep_d[n // 2 :].reshape(-1, H), slabs[n // 2 :].reshape(-1, H)], axis=0)
            keep_d, slabs = keep_d[: n // 2], slabs[: n // 2]
    mask = edge
    while mask < devices:
        first = rounded(first.astype(F32) + swap(first, mask, devices).astype(F32))
        mask *= 2
    state_grads, edge_grads = pl.pallas_call(
        functools.partial(gather_kernel, shape, sources),
        name="slots_to_edges",
        out_shape=[
            jax.ShapeDtypeStruct((own, H), F32),
            jax.ShapeDtypeStruct((edge_feats.shape[2], edges), F32),
        ],
        in_specs=[smem()] + [vmem()] * 4,
        out_specs=[vmem()] * 2,
        scratch_shapes=[pltpu.VMEM((holders * 16 * blocks, H), BF16)],
        compiler_params=params(),
        cost_estimate=cost(3),
    )(me_arr, slot, direct, keep_d[0], slabs[0])
    return overflow, (new_states, state_grads, edge_grads, first, parts)


def gather_back(chunks, bits, devices, whole):
    for step in reversed(range(len(bits) - 1)):
        whole = [
            jnp.stack([w, swap(w, bits[chunk.order[step]], devices)], axis=0) for w, chunk in zip(whole, chunks)
        ]
    return whole


def finish(batch, edge, results):
    new_states, state_grads, edge_grads, first, whole = results
    bits, chunks, piece_arr = plan(batch, edge)
    devices = batch * edge
    whole = [x.reshape(PIECES // 2, chunk.height, H) for x, chunk in zip(whole, chunks)]
    others = [swap(x, bits[-1], devices) for x in whole]
    small = [jax.ShapeDtypeStruct((7, H, H), F32), jax.ShapeDtypeStruct((PIECES, H), F32)]
    scratch = [pltpu.VMEM((PIECES // 2, chunk.height, H), BF16) for chunk in chunks] + [
        pltpu.VMEM((2, 4 * UNITS, H * H), F32),
        pltpu.VMEM((256, 256), BF16),
    ]
    semaphores = [pltpu.SemaphoreType.DMA((2 + len(chunks) * PIECES // 8,))]
    grad_w2, extras, biases = pl.pallas_call(
        functools.partial(own_half_kernel, chunks),
        name="assemble_own_half",
        in_specs=[smem()] + [anywhere()] * len(chunks),
        out_specs=[anywhere(), vmem(), vmem()],
        scratch_shapes=scratch + semaphores,
        out_shape=[jax.ShapeDtypeStruct((H, H * H), F32)] + small,
        compiler_params=params(),
        cost_estimate=cost(4),
    )(piece_arr, *whole)
    grad_w2, grad_w1, grad_b1, grad_wi, grad_wh, grad_b2, grad_bi, grad_bh = pl.pallas_call(
        functools.partial(other_half_kernel, chunks),
        name="assemble_other_half",
        in_specs=[smem()] + [anywhere()] * len(chunks) + [vmem()] * 3 + [anywhere()],
        out_specs=[anywhere()] + [vmem()] * 7,
        scratch_shapes=scratch + [pltpu.VMEM(x.shape, F32) for x in small] + semaphores,
        out_shape=[
            jax.ShapeDtypeStruct((H, H * H), F32),
            jax.ShapeDtypeStruct((16, H), F32),
            jax.ShapeDtypeStruct((H,), F32),
        ]
        + [jax.ShapeDtypeStruct((H, 3 * H), F32)] * 2
        + [jax.ShapeDtypeStruct((H, H), F32)]
        + [jax.ShapeDtypeStruct((3 * H,), F32)] * 2,
        input_output_aliases={len(chunks) + 4: 0},
        compiler_params=params(),
    )(piece_arr, *others, first, extras, biases, grad_w2)
    return (
        new_states[None],
        state_grads[None],
        jnp.swapaxes(edge_grads[None], 1, 2),
        grad_w1,
        grad_b1,
        grad_w2,
        grad_b2.reshape(-1),
        grad_wi,
        grad_wh,
        grad_bi,
        grad_bh,
    )


HIGH = lax.Precision.HIGHEST


def gated_update(mixed, prior, w_input, w_hidden, b_input, b_hidden):
    width = prior.shape[1]
    from_input = jnp.dot(mixed, w_input, precision=HIGH) + b_input
    from_state = jnp.dot(prior, w_hidden, precision=HIGH) + b_hidden
    reset = jax.nn.sigmoid(from_input[:, :width] + from_state[:, :width])
    update = jax.nn.sigmoid(from_input[:, width : 2 * width] + from_state[:, width : 2 * width])
    candidate = jnp.tanh(from_input[:, 2 * width :] + reset * from_state[:, 2 * width :])
    return (1.0 - update) * candidate + update * prior


def edge_hidden(feats, w_edge_in, b_edge_in):
    return jax.nn.silu(jnp.dot(feats, w_edge_in, precision=HIGH) + b_edge_in)


def pick_by(index_rows, piece):
    columns = lax.broadcasted_iota(jnp.int32, (1, piece.shape[0]), 1)
    onehot = (index_rows[:, None] == columns).astype(jnp.bfloat16)
    return jnp.dot(onehot, piece, preferred_element_type=jnp.float32)


def spread_by(index_rows, values, count):
    rows = lax.broadcasted_iota(jnp.int32, (count, 1), 0)
    onehot = (rows == index_rows[None, :]).astype(jnp.bfloat16)
    return jnp.dot(onehot, values, preferred_element_type=jnp.float32)


def from_all(x, edge):
    got = lax.all_to_all(jnp.broadcast_to(x[None], (edge,) + x.shape), "edge", 0, 0)
    return got.reshape((-1,) + x.shape[1:])


def to_owners(x, edge):
    got = lax.all_to_all(x.reshape((edge, -1) + x.shape[1:]), "edge", 0, 0)
    return jnp.sum(got.astype(F32), axis=0)


def slow_path(batch, edge, args):
    (states, edge_feats, molecule, source, target, edge_mask, w_edge_in, b_edge_in, w_edge_out, b_edge_out,
     w_input, w_hidden, b_input, b_hidden, cotangent) = args
    states_here = states[0]
    feats = edge_feats[0]
    source_ids = source[0]
    target_ids = target[0]
    width = states_here.shape[1]
    owned = states_here.shape[0]
    edges = source_ids.shape[0]
    block = min(512, edges)
    count = edges // block
    labels = from_all(molecule[0], edge)
    same = (jnp.take(labels, source_ids) == jnp.take(labels, target_ids)).astype(jnp.float32)
    valid = edge_mask[0].astype(jnp.float32) * same
    near = pick_by(source_ids, from_all(states_here, edge)).astype(
        jnp.bfloat16
    )
    hidden, edge_pull = jax.vjp(
        edge_hidden,
        feats.astype(jnp.float32),
        w_edge_in.astype(jnp.float32),
        b_edge_in.astype(jnp.float32),
    )
    latent_blocks = hidden.astype(jnp.bfloat16).reshape(count, block, -1)
    near_blocks = near.reshape(count, block, width)
    bias_out = b_edge_out.astype(jnp.float32)

    def expand(latent):
        flat = jnp.dot(latent, w_edge_out, preferred_element_type=jnp.float32) + bias_out
        return flat.astype(jnp.bfloat16).reshape(latent.shape[0], width, width)

    def apply(mats, vectors):
        return jnp.einsum("bij,bj->bi", mats, vectors, preferred_element_type=jnp.float32)

    outgoing = lax.map(lambda item: apply(expand(item[0]), item[1]), (latent_blocks, near_blocks))
    messages = (outgoing.reshape(edges, width) * valid[:, None]).astype(jnp.bfloat16)
    summed = to_owners(spread_by(target_ids, messages, edge * owned), edge)
    mixed = summed.astype(jnp.bfloat16).astype(jnp.float32)
    updated, update_pull = jax.vjp(
        gated_update,
        mixed,
        states_here.astype(jnp.float32),
        w_input.astype(jnp.float32),
        w_hidden.astype(jnp.float32),
        b_input.astype(jnp.float32),
        b_hidden.astype(jnp.float32),
    )
    new_states = updated.astype(jnp.bfloat16)
    d_mixed, d_direct, grad_wi, grad_wh, grad_bi, grad_bh = update_pull(
        cotangent[0].astype(jnp.float32)
    )
    pulled = pick_by(
        target_ids, from_all(d_mixed.astype(jnp.bfloat16), edge)
    )
    d_message = (pulled * valid[:, None]).astype(jnp.bfloat16)
    d_message_blocks = d_message.reshape(count, block, width)

    def backward_core(carry, mats, latent, vectors, d_out):
        grad_weight, grad_bias = carry
        outer = (
            d_out.astype(jnp.float32)[:, :, None] * vectors.astype(jnp.float32)[:, None, :]
        ).astype(jnp.bfloat16)
        flat = outer.reshape(latent.shape[0], width * width)
        d_latent = lax.dot_general(
            flat, w_edge_out, (((1,), (1,)), ((), ())), preferred_element_type=jnp.float32
        )
        grad_weight = grad_weight + lax.dot_general(
            latent, flat, (((0,), (0,)), ((), ())), preferred_element_type=jnp.float32
        )
        grad_bias = grad_bias + jnp.sum(flat.astype(jnp.float32), axis=0)
        d_vectors = jnp.einsum(
            "bij,bi->bj", mats, d_out, preferred_element_type=jnp.float32
        ).astype(jnp.bfloat16)
        return ((grad_weight, grad_bias), (d_latent, d_vectors))

    start_carry = (
        jnp.zeros((w_edge_out.shape[0], width * width), jnp.float32),
        jnp.zeros((width * width,), jnp.float32),
    )

    def backward_block(carry, item):
        return backward_core(carry, expand(item[0]), item[0], item[1], item[2])

    sums_out, per_edge = lax.scan(
        backward_block, start_carry, (latent_blocks, near_blocks, d_message_blocks)
    )
    grad_w2, grad_b2 = sums_out
    d_latent_all = per_edge[0].reshape(edges, -1)
    d_near_all = per_edge[1].reshape(edges, width)
    d_feats, grad_w1, grad_b1 = edge_pull(d_latent_all)
    returned = to_owners(spread_by(source_ids, d_near_all, owned * edge).astype(jnp.bfloat16), edge)
    state_grads = d_direct + returned

    bits, chunks, piece_arr = plan(batch, edge)
    devices = batch * edge
    pieces = grad_w2.reshape(PIECES, UNITS, H, H)
    small = jnp.concatenate([grad_wi, grad_wh, grad_b2.reshape(H, H)], axis=1).reshape(PIECES, UNITS, 7, H)
    small = small.transpose(0, 2, 1, 3).reshape(PIECES, 7 * UNITS, H)
    biases = jnp.concatenate([grad_bi, grad_bh]).reshape(6, H)
    biases = jnp.concatenate([biases, jnp.zeros((PIECES - 6, H), F32)], axis=0)[:, None]
    small = jnp.concatenate([small, biases, jnp.zeros((PIECES, EXTRA - 7 * UNITS - 1, H), F32)], axis=1)
    terms = []
    for chunk in chunks:
        block = pieces[:, :, chunk.first : chunk.first + chunk.rows].reshape(PIECES, -1, H)
        if chunk.extra:
            block = jnp.concatenate([block, small], axis=1)
        rel_of = sorted(range(PIECES // 2), key=chunk.place)
        order = jnp.array(rel_of + [PIECES // 2 + r for r in rel_of], jnp.int32)
        block = jnp.take(block, jnp.bitwise_xor(order, piece_arr[0]), axis=0).astype(BF16)
        shape = chunk.shape()
        kept, sent = block[: PIECES // 2].reshape(shape), block[PIECES // 2 :].reshape(shape)
        total = add([kept, swap(sent, bits[-1], devices)])
        for bit in chunk.order:
            total = add([total[0], swap(total[1], bits[bit], devices)])
        terms.append(total)
    first = jnp.concatenate([grad_w1, grad_b1[None], jnp.zeros((15, H), F32)], axis=0)
    for n in range(devices.bit_length() - 1):
        mask = 1 << n
        if mask not in bits:
            terms = [rounded(w.astype(F32) + swap(w, mask, devices).astype(F32)) for w in terms]
        first = first + swap(first, mask, devices)
    return new_states, state_grads, d_feats.T, first.astype(BF16), gather_back(chunks, bits, devices, terms)


def per_device(batch, edge, *args):
    overflow, results = fast_path(batch, edge, args)
    results = lax.while_loop(
        lambda carry: carry[0], lambda carry: (jnp.bool_(False), slow_path(batch, edge, args)), (overflow, results)
    )[1]
    return finish(batch, edge, results)


def solution(mesh):
    batch, edge = mesh.shape["batch"], mesh.shape["edge"]
    nodes, edges, all_ = P("batch", "edge", None), P("batch", "edge"), P()
    return jax.shard_map(
        functools.partial(per_device, batch, edge),
        mesh=mesh,
        in_specs=(nodes, nodes, edges, edges, edges, edges) + (all_,) * 8 + (nodes,),
        out_specs=(nodes, nodes, nodes) + (all_,) * 8,
        check_vma=False,
    )
```

time: 166 us -> 146 us (0.88)
  Pallas kernels: 72.9 us -> 62.7 us
  local copies, waits for them, and re-layouts: 12 us -> 5.34 us
  starting transfers between devices: 33.4 us -> 31 us
    pallas_call x8 -> x7, Pallas kernels: 44.6 us -> 37.7 us  [the longest x2 16.4 us: back_step(): pl.pallas_call(functools.partial(back_kernel, shape, count, not sums), na...]
    slice x12 -> x8, local copies, waits for them, and re-layouts: 5.99 us -> 0.64 us  [the longest x1 0.51 us: fast_path(): overflow = parts[-1][UNITS * chunks[-1].rows + 29, 0] > 0.0]
    pallas_call x1, Pallas kernels: 17.3 us -> 14.1 us  [fast_path(): pl.pallas_call(functools.partial(front_kernel, shape, chunks), name='mess...]
    ppermute x25 -> x24, starting transfers between devices: 26.1 us -> 23.8 us  [swap(): lax.ppermute(x, ('batch', 'edge'), [(i, i ^ mask) for i in range(devices)])]
    convert_element_type x4 -> x6, other arithmetic: 0.03 us -> 2.1 us  [rounded(): return lax.reduce_precision(x.astype(F32), 8, 7).astype(BF16)]
    ppermute x25 -> x24, waiting for transfers between devices: 22.7 us -> 23.7 us  [swap(): lax.ppermute(x, ('batch', 'edge'), [(i, i ^ mask) for i in range(devices)])]
  transfers between devices with their start and end apart: 26 -> 25, of which waited for: 11 -> 10; matrix products, arithmetic and copies ran while one was open for 10% -> 13% of each run, Pallas kernels for 27% -> 27%
where the time goes in v2:
time: 146 us; the launch traced here: 145 us
  Pallas kernels  62.7 us (43%)
  starting transfers between devices  31 us (21%)
  waiting for transfers between devices  25.9 us (18%)
  other arithmetic  17.9 us (12%)
  local copies, waits for them, and re-layouts  5.34 us (4%)
  between operations  1.84 us (1%)
    ppermute x24, starting transfers between devices, swap(): lax.ppermute(x, ('batch', 'edge'), [(i, i ^ mask) for i in range(devices)])  23.8 us
    ppermute x24, waiting for transfers between devices, swap(): lax.ppermute(x, ('batch', 'edge'), [(i, i ^ mask) for i in range(devices)])  23.7 us
    pallas_call x2, Pallas kernels, back_step(): pl.pallas_call(functools.partial(back_kernel, shape, count, not sums), na...  16.4 us
    pallas_call x1, Pallas kernels, fast_path(): pl.pallas_call(functools.partial(front_kernel, shape, chunks), name='mess...  14.1 us
    convert_element_type x12, other arithmetic, add(): return total.astype(BF16)  11.1 us
    pallas_call x1, Pallas kernels, fast_path(): pl.pallas_call(split_kernel, name='split_weight', grid=(H // 16,), in_spe...  7.62 us
    all_to_all x1, starting transfers between devices, fast_path(): given = lax.all_to_all(slots_out, 'edge', 0, 0)  7.28 us
    pallas_call x1, Pallas kernels, fast_path(): matrix_gradients(d_agg, t_units, b2)  6.32 us
  transfers between devices with their start and end apart: 25, of which 10 were waited for; matrix products, arithmetic and copies ran while one was open for 13% of the time, Pallas kernels for 27%

profile of v2, /device:TPU:0, one launch (start us, length us, event | category | flops | bytes accessed | tf_op | source)
XLA Modules:
  0.0 144.8 jit_solution(544574165080345457)
XLA Ops:
  0.6 3.4 %edges_to_slots.1 = (bf16[8,208,128]{2,1,0:T(8,128)(2,1)}, s32[1,2048]{1,0:T(1,128)}) custom-call(s32[1]{0:T(128)} %bitcast.7.me_ref, s32[1,2048]{1,0:T(1,128)} %target_ref.1, s32[1,2048]{1,0:T(1,128)} %source_ref.1, s32[1,2048]{1,0:T(1,128)} %mask_ref.1, s32[1,128]{1,0:T(1,128)} %refs_3_.3, bf16[16,2048]{1,0:T(8,128)(2,1)} %bitcast.9.feats_ref, ...), custom_call_target="tpu_custom_call" | custom-call | tf_op jit(solution)/shard_map/edges_to_slots/pallas_call | solution.py:675
  4.0 7.3 %all-to-all-start.5 = ((bf16[8,208,128]{2,1,0:T(8,128)(2,1)}), bf16[8,208,128]{2,1,0:T(8,128)(2,1)S(1)}, u32[]{:S(2)}, u32[]{:S(2)}) async-start(bf16[8,208,128]{2,1,0:T(8,128)(2,1)} %get-tuple-element.273), calls=%async_computation.5 | async-start | bytes 851968 | tf_op jit(solution)/shard_map/all_to_all | solution.py:687
  11.3 1.2 reshape.468.refs_10_
  12.5 1.2 reshape.470.refs_11_
  13.8 7.6 %split_weight.1.refs_4_.t_ref = bf16[128,128,128]{2,1,0:T(8,128)(2,1)} custom-call(bf16[128,16384]{1,0:T(8,128)(2,1)} %w_ref.1), custom_call_target="tpu_custom_call" | custom-call | flops 120000000 | bytes 360000 | tf_op jit(solution)/shard_map/split_weight/pallas_call | solution.py:689
  21.4 2.3 %all-to-all-done.5.refs_1_ = bf16[8,208,128]{2,1,0:T(8,128)(2,1)S(1)} async-done(((bf16[8,208,128]{2,1,0:T(8,128)(2,1)}), bf16[8,208,128]{2,1,0:T(8,128)(2,1)S(1)}, u32[]{:S(2)}, u32[]{:S(2)}) %all-to-all-start.5) | async-done | bytes 426016 | tf_op jit(solution)/shard_map/all_to_all | solution.py:687
  23.7 0.8 copy-done.21
  24.5 14.1 %messages_update_weight_gradient.1 = (bf16[128,128]{1,0:T(8,128)(2,1)}, f32[128,128]{1,0:T(8,128)}, bf16[128,128]{1,0:T(8,128)(2,1)}, s32[1]{0:T(128)}, bf16[16,...) custom-call(s32[1]{0:T(128)} %bitcast.6.refs_0_.piece_ref, ...), custom_call_target="tpu_custom_call" | custom-call | tf_op jit(solution)/shard_map/messages_update_weight_gradient/pallas_call | solution.py:704
  38.6 6.3 %matrix_gradients.1 = (bf16[8,128,2048]{2,1,0:T(8,128)(2,1)}, f32[128,128]{1,0:T(8,128)}) custom-call(bf16[128,128]{1,0:T(8,128)(2,1)} %get-tuple-element.278.d_ref, bf16[128,128,128]{2,1,0:T(8,128)(2,1)} %split_weight.1.refs_4_.t_ref, bf16[128,128]{1,0:T(8,128)(2,1)} %bitcast.11.refs_5_.b2_ref), custom_call_target="tpu_custom_call" | custom-call | flops 120000000 | bytes 360000 | tf_op jit(solution)/shard_map/matrix_gradients/pallas_call | solution.py:802
  45.0 0.9 fusion.98
  46.0 1.5 %collective-permute-start.33 = (bf16[2,2,2,256,128]{4,3,2,1,0:T(8,128)(2,1)}, bf16[2,2,2,256,128]{4,3,2,1,0:T(8,128)(2,1)S(1)}, u32[]{:S(2)}, u32[]{:S(2)}) collective-permute-start(bf16[2,2,2,256,128]{4,3,2,1,0:T(8,128)(2,1)} %fusion.98), channel_id=1, source_target_pairs={{0,16},{1,17},{2,18},{3,19},{4,20},{5,21},{6,22},{7,23},{8,24},{9,... | collective-permute-start | bytes 1572872 | tf_op jit(solution)/shard_map/ppermute | solution.py:520
  47.7 1.5 %collective-permute-start.24 = (bf16[2,2,2,288,128]{4,3,2,1,0:T(8,128)(2,1)S(1)}, bf16[2,2,2,288,128]{4,3,2,1,0:T(8,128)(2,1)S(1)}, u32[]{:S(2)}, u32[]{:S(2)}) collective-permute-start(bf16[2,2,2,288,128]{4,3,2,1,0:T(8,128)(2,1)S(1)} %fusion.97), channel_id=1, source_target_pairs={{0,1},{1,0},{2,3},{3,2},{4,5},{5,4},{6,7},{7,6},{8,9},{9,8},{10,11... | collective-permute-start | bytes 1769480 | tf_op jit(solution)/shard_map/ppermute | solution.py:520
  49.2 8.1 %edge_gradients.2 = (f32[1024,128]{1,0:T(8,128)}, f32[32,128]{1,0:T(8,128)}, f32[8,16,256]{2,1,0:T(8,128)}) custom-call(s32[1]{0:T(128)} %get-tuple-element.283.refs_0_, bf16[8,128,2048]{2,1,0:T(8,128)(2,1)} %get-tuple-element.284.refs_1_, f32[128,128]{1,0:T(8,128)} %get-tuple-element.285.refs_2_, bf16[16,128]{1,0:T(8,128)(2,1)S(1)} %copy-done.31, ...), custom_call_target="tpu_custom_call" | custom-call | flops 240000000 | bytes 720000 | tf_op jit(solution)/shard_map/edge_gradients/pallas_call | solution.py:768
  57.4 3.1 %collective-permute-done.33 = bf16[2,2,2,256,128]{4,3,2,1,0:T(8,128)(2,1)S(1)} collective-permute-done((bf16[2,2,2,256,128]{4,3,2,1,0:T(8,128)(2,1)}, bf16[2,2,2,256,128]{4,3,2,1,0:T(8,128)(2,1)S(1)}, u32[]{:S(2)}, u32[]{:S(2)}) %collective-permute-start.33) | collective-permute-done | bytes 524320 | tf_op jit(solution)/shard_map/ppermute | solution.py:520
  60.5 1.9 %fusion.100 = bf16[2,2,256,128]{3,2,1,0:T(8,128)(2,1)} fusion(bf16[2,2,256,128]{3,2,1,0:T(8,128)(2,1)} %bitcast.535, bf16[2,2,2,256,128]{4,3,2,1,0:T(8,128)(2,1)S(1)} %collective-permute-done.33, bf16[2,2,544,128]{3,2,1,0:T(8,128)(2,1)S(1)} %slice_bitcast_fusion.16), kind=kLoop, calls=%fused_computation.210 | loop fusion | flops 786432 | bytes 1048576 | tf_op jit(solution)/shard_map/convert_element_type | solution.py:527
  62.4 1.5 %collective-permute-start.34 = (bf16[2,2,256,128]{3,2,1,0:T(8,128)(2,1)}, bf16[2,2,256,128]{3,2,1,0:T(8,128)(2,1)}, u32[]{:S(2)}, u32[]{:S(2)}) collective-permute-start(bf16[2,2,256,128]{3,2,1,0:T(8,128)(2,1)} %fusion.100), channel_id=1, source_target_pairs={{0,1},{1,0},{2,3},{3,2},{4,5},{5,4},{6,7},{7,6},{8,9},{9,8},{10,11... | collective-permute-start | bytes 786440 | tf_op jit(solution)/shard_map/ppermute | solution.py:520
  63.9 0.8 fusion.99
  64.7 1.5 %collective-permute-start.25 = (bf16[2,2,288,128]{3,2,1,0:T(8,128)(2,1)}, bf16[2,2,288,128]{3,2,1,0:T(8,128)(2,1)}, u32[]{:S(2)}, u32[]{:S(2)}) collective-permute-start(bf16[2,2,288,128]{3,2,1,0:T(8,128)(2,1)} %fusion.99), channel_id=1, source_target_pairs={{0,16},{1,17},{2,18},{3,19},{4,20},{5,21},{6,22},{7,23},{8,24},{9,... | collective-permute-start | bytes 884744 | tf_op jit(solution)/shard_map/ppermute | solution.py:520
  66.2 8.2 %edge_gradients.3 = (f32[1024,128]{1,0:T(8,128)}, f32[32,128]{1,0:T(8,128)}, f32[8,16,256]{2,1,0:T(8,128)}) custom-call(s32[1]{0:T(128)} %get-tuple-element.283.refs_0_, bf16[8,128,2048]{2,1,0:T(8,128)(2,1)} %get-tuple-element.284.refs_1_, f32[128,128]{1,0:T(8,128)} %get-tuple-element.285.refs_2_, bf16[16,128]{1,0:T(8,128)(2,1)S(1)} %copy-done.31, ...), custom_call_target="tpu_custom_call" | custom-call | flops 240000000 | bytes 720000 | tf_op jit(solution)/shard_map/edge_gradients/pallas_call | solution.py:768
  74.4 1.7 %fusion.102 = bf16[2,256,128]{2,1,0:T(8,128)(2,1)} fusion(bf16[2,2,256,128]{3,2,1,0:T(8,128)(2,1)} %collective-permute-done.34, bf16[2,2,2,256,128]{4,3,2,1,0:T(8,128)(2,1)S(1)} %copy-done.28, bf16[2,544,128]{2,1,0:T(8,128)(2,1)S(1)} %slice_bitcast_fusion.17, bf16[4,256,128]{2,1,0:T(8,128)(2,1)} %get-tuple-element.313), kind=kLoop, calls=%fused_computation.220 | loop fusion | flops 524288 | bytes 655360 | tf_op jit(solution)/shard_map/convert_element_type | solution.py:527
  76.2 1.7 %fusion.101 = bf16[2,288,128]{2,1,0:T(8,128)(2,1)} fusion(bf16[2,544,128]{2,1,0:T(8,128)(2,1)S(1)} %slice_bitcast_fusion.17, bf16[2,2,288,128]{3,2,1,0:T(8,128)(2,1)} %collective-permute-done.25, bf16[2,2,2,288,128]{4,3,2,1,0:T(8,128)(2,1)S(1)} %collective-permute-done.24, bf16[4,288,128]{2,1,0:T(8,128)(2,1)S(1)} %copy-done.29), kind=kLoop, calls=%fused_computation.214 | loop fusion | flops 589824 | bytes 737280 | tf_op jit(solution)/shard_map/convert_element_type | solution.py:527
  77.8 2.0 %collective-permute-start.26 = (bf16[2,288,128]{2,1,0:T(8,128)(2,1)}, bf16[2,288,128]{2,1,0:T(8,128)(2,1)S(1)}, u32[]{:S(2)}, u32[]{:S(2)}) collective-permute-start(bf16[2,288,128]{2,1,0:T(8,128)(2,1)} %fusion.101), channel_id=1, source_target_pairs={{0,2},{1,3},{2,0},{3,1},{4,6},{5,7},{6,4},{7,5},{8,10},{9,11},{10,... | collective-permute-start | bytes 442376 | tf_op jit(solution)/shard_map/ppermute | solution.py:520
  79.8 1.9 %returned.1 = (bf16[4,128,128]{2,1,0:T(8,128)(2,1)}, bf16[4,64,128]{2,1,0:T(8,128)(2,1)}, bf16[768,128]{1,0:T(8,128)(2,1)}) custom-call(s32[1]{0:T(128)} %bitcast.7.me_ref, f32[1024,128]{1,0:T(8,128)} %get-tuple-element.304.part_ref, f32[8,16,256]{2,1,0:T(8,128)} %get-tuple-element.305.refs_0_, f32[8,16,256]{2,1,0:T(8,128)} %get-tuple-element.306.refs_1_), custom_call_target="tpu_custom_call" | custom-call | flops 40000000 | bytes 120000 | tf_op jit(solution)/shard_map/returned/pallas_call | solution.py:849
  81.8 0.8 reduce-precision_convert_fusion.5
  82.8 0.9 fusion.108
  84.2 0.9 pad_maximum_fusion.15
  85.8 3.2 %collective-permute-done.36 = bf16[256,128]{1,0:T(8,128)(2,1)S(1)} collective-permute-done((bf16[256,128]{1,0:T(8,128)(2,1)S(1)}, bf16[256,128]{1,0:T(8,128)(2,1)S(1)}, u32[]{:S(2)}, u32[]{:S(2)}) %collective-permute-start.36) | collective-permute-done | bytes 65568 | tf_op jit(solution)/shard_map/ppermute | solution.py:520
  89.0 1.0 fusion.110
  90.5 0.9 fusion.104
  91.4 2.5 %collective-permute-start.27 = (bf16[288,128]{1,0:T(8,128)(2,1)S(1)}, bf16[288,128]{1,0:T(8,128)(2,1)S(1)}, u32[]{:S(2)}, u32[]{:S(2)}) collective-permute-start(bf16[288,128]{1,0:T(8,128)(2,1)S(1)} %fusion.104), channel_id=1, source_target_pairs={{0,4},{1,5},{2,6},{3,7},{4,0},{5,1},{6,2},{7,3},{8,12},{9,13},{10,... | collective-permute-start | bytes 221192 | tf_op jit(solution)/shard_map/ppermute | solution.py:520
  93.9 2.0 %collective-permute-done.37 = bf16[256,128]{1,0:T(8,128)(2,1)S(1)} collective-permute-done((bf16[256,128]{1,0:T(8,128)(2,1)S(1)}, bf16[256,128]{1,0:T(8,128)(2,1)S(1)}, u32[]{:S(2)}, u32[]{:S(2)}) %collective-permute-start.37) | collective-permute-done | bytes 65568 | tf_op jit(solution)/shard_map/ppermute | solution.py:520
  96.9 1.0 fusion.106
  97.8 2.6 %collective-permute-start.41 = (bf16[288,128]{1,0:T(8,128)(2,1)S(1)}, bf16[288,128]{1,0:T(8,128)(2,1)S(1)}, u32[]{:S(2)}, u32[]{:S(2)}) collective-permute-start(bf16[288,128]{1,0:T(8,128)(2,1)S(1)} %fusion.106), channel_id=1, source_target_pairs={{0,4},{1,5},{2,6},{3,7},{4,0},{5,1},{6,2},{7,3},{8,12},{9,13},{10,... | collective-permute-start | bytes 221192 | tf_op jit(solution)/shard_map/ppermute | solution.py:520
  101.7 1.6 %collective-permute-done.41 = bf16[288,128]{1,0:T(8,128)(2,1)S(1)} collective-permute-done((bf16[288,128]{1,0:T(8,128)(2,1)S(1)}, bf16[288,128]{1,0:T(8,128)(2,1)S(1)}, u32[]{:S(2)}, u32[]{:S(2)}) %collective-permute-start.41) | collective-permute-done | bytes 73760 | tf_op jit(solution)/shard_map/ppermute | solution.py:520
  103.3 2.5 %collective-permute-start.42 = (bf16[2,288,128]{2,1,0:T(8,128)(2,1)S(1)}, bf16[2,288,128]{2,1,0:T(8,128)(2,1)S(1)}, u32[]{:S(2)}, u32[]{:S(2)}) collective-permute-start(bf16[2,288,128]{2,1,0:T(8,128)(2,1)S(1)} %get-tuple-element.613), channel_id=1, source_target_pairs={{0,2},{1,3},{2,0},{3,1},{4,6},{5,7},{6,4},{7,5},{8,10},{9,11},{10,... | collective-permute-start | bytes 442376 | tf_op jit(solution)/shard_map/ppermute | solution.py:520
  105.8 1.2 collective-permute-start.39
  107.1 1.7 %collective-permute-start.30 = (bf16[416,128]{1,0:T(8,128)(2,1)S(1)}, bf16[416,128]{1,0:T(8,128)(2,1)S(1)}, u32[]{:S(2)}, u32[]{:S(2)}) collective-permute-start(bf16[416,128]{1,0:T(8,128)(2,1)S(1)} %pad_maximum_fusion.20), channel_id=1, source_target_pairs={{0,4},{1,5},{2,6},{3,7},{4,0},{5,1},{6,2},{7,3},{8,12},{9,13},{10,... | collective-permute-start | bytes 319496 | tf_op jit(solution)/shard_map/ppermute | solution.py:520
  109.7 4.2 %collective-permute-done.30 = bf16[416,128]{1,0:T(8,128)(2,1)S(1)} collective-permute-done((bf16[416,128]{1,0:T(8,128)(2,1)S(1)}, bf16[416,128]{1,0:T(8,128)(2,1)S(1)}, u32[]{:S(2)}, u32[]{:S(2)}) %collective-permute-start.30) | collective-permute-done | bytes 106528 | tf_op jit(solution)/shard_map/ppermute | solution.py:520
  115.0 0.9 collective-permute-done.43
  115.9 1.1 collective-permute-start.44
  117.0 0.9 collective-permute-start.32
  118.5 2.4 %slots_to_edges.1 = (f32[128,128]{1,0:T(8,128)}, f32[16,2048]{1,0:T(8,128)}) custom-call(s32[1]{0:T(128)} %bitcast.7.me_ref, s32[1,2048]{1,0:T(1,128)} %get-tuple-element.302.slot_ref, f32[128,128]{1,0:T(8,128)} %get-tuple-element.303.direct_ref, bf16[128,128]{1,0:T(8,128)(2,1)} %fusion.114.part_ref, bf16[8,64,128]{2,1,0:T(8,128)(2,1)} %maximum_bitcast_fusion.slabs_ref), custom_call_target="tpu_custom_call" | custom-call | flops 60000000 | bytes 180000 | tf_op jit(solution)/shard_map/slots_to_edges/pallas_call | solution.py:898
  120.9 8.3 %collective-permute-done.32 = bf16[32,128]{1,0:T(8,128)(2,1)S(1)} collective-permute-done((bf16[32,128]{1,0:T(8,128)(2,1)S(1)}, bf16[32,128]{1,0:T(8,128)(2,1)S(1)}, u32[]{:S(2)}, u32[]{:S(2)}) %collective-permute-start.32) | collective-permute-done | bytes 8224 | tf_op jit(solution)/shard_map/ppermute | solution.py:520
  129.8 1.1 pad_maximum_fusion.10
  130.9 1.1 pad_maximum_fusion.9
  132.5 4.8 %assemble_own_half.1 = (f32[128,16384]{1,0:T(8,128)}, f32[7,128,128]{2,1,0:T(8,128)}, f32[32,128]{1,0:T(8,128)}) custom-call(s32[1]{0:T(128)} %bitcast.6.refs_0_.piece_ref, bf16[16,256,128]{2,1,0:T(8,128)(2,1)} %bitcast.498, bf16[16,288,128]{2,1,0:T(8,128)(2,1)} %bitcast.494), custom_call_target="tpu_custom_call" | custom-call | flops 80000000 | bytes 240000 | tf_op jit(solution)/shard_map/assemble_own_half/pallas_call | solution.py:934
  137.4 1.0 copy-done.24
  138.8 5.9 %assemble_other_half.1 = (f32[128,16384]{1,0:T(8,128)}, f32[16,128]{1,0:T(8,128)}, f32[128]{0:T(128)}, f32[128,384]{1,0:T(8,128)}, f32[128,384]{1,0:T(8,128)}, /...) custom-call(s32[1]{0:T(128)} %bitcast.6.refs_0_.piece_ref, ...), custom_call_target="tpu_custom_call", output_to_operand_aliasing={{0}: (6, {})} | custom-call | tf_op jit(solution)/shard_map/assemble_other_half/pallas_call | solution.py:944
  (95 shorter events, 8.2 us)
Async XLA Ops:
  4.0 19.7 %all-to-all-start.5 = ((bf16[8,208,128]{2,1,0:T(8,128)(2,1)}), bf16[8,208,128]{2,1,0:T(8,128)(2,1)S(1)}, u32[]{:S(2)}, u32[]{:S(2)}) async-start(bf16[8,208,128]{2,1,0:T(8,128)(2,1)} %get-tuple-element.273), calls=%async_computation.5 | async-start | bytes 851968 | tf_op jit(solution)/shard_map/all_to_all | solution.py:687
  13.8 10.7 %copy-start.16 = (bf16[128,384]{1,0:T(8,128)(2,1)S(1)}, bf16[128,384]{1,0:T(8,128)(2,1)}, u32[]{:S(2)}) copy-start(bf16[128,384]{1,0:T(8,128)(2,1)} %refs_9_.1) | copy-start | bytes 294916
  13.8 10.7 %copy-start.19 = (bf16[1,128,128]{2,1,0:T(8,128)(2,1)S(1)}, bf16[1,128,128]{2,1,0:T(8,128)(2,1)}, u32[]{:S(2)}) copy-start(bf16[1,128,128]{2,1,0:T(8,128)(2,1)} %param.39) | copy-start | bytes 98308
  13.8 10.7 %copy-start.31 = (bf16[16,128]{1,0:T(8,128)(2,1)S(1)}, bf16[16,128]{1,0:T(8,128)(2,1)}, u32[]{:S(2)}) copy-start(bf16[16,128]{1,0:T(8,128)(2,1)} %refs_3_.5) | copy-start | bytes 12292
  13.8 10.7 %copy-start.43 = (s32[1,128]{1,0:T(1,128)S(1)}, s32[1,128]{1,0:T(1,128)}, u32[]{:S(2)}) copy-start(s32[1,128]{1,0:T(1,128)} %refs_3_.3) | copy-start | bytes 1540
  13.8 10.7 %copy-start.45 = (bf16[128]{0:T(256)(128)(2,1)S(1)}, bf16[128]{0:T(256)(128)(2,1)}, u32[]{:S(2)}) copy-start(bf16[128]{0:T(256)(128)(2,1)} %param.32) | copy-start | bytes 772
  23.7 0.8 copy-start.21
  38.5 6.5 %copy-start.26 = (bf16[8,256,128]{2,1,0:T(8,128)(2,1)S(1)}, bf16[8,256,128]{2,1,0:T(8,128)(2,1)}, u32[]{:S(2)}) copy-start(bf16[8,256,128]{2,1,0:T(8,128)(2,1)} %get-tuple-element.314) | copy-start | bytes 1572868
  38.5 6.4 %collective-permute-start.23 = (bf16[16,544,128]{2,1,0:T(8,128)(2,1)}, bf16[16,544,128]{2,1,0:T(8,128)(2,1)S(1)}, u32[]{:S(2)}, u32[]{:S(2)}) collective-permute-start(bf16[16,544,128]{2,1,0:T(8,128)(2,1)} %get-tuple-element.277), channel_id=1, source_target_pairs={{0,8},{1,9},{2,10},{3,11},{4,12},{5,13},{6,14},{7,15},{8,0},{9,1},... | collective-permute-start | bytes 6684680 | tf_op jit(solution)/shard_map/ppermute | solution.py:520
  44.9 2.6 %copy-start.25 = (bf16[8,288,128]{2,1,0:T(8,128)(2,1)S(1)}, bf16[8,288,128]{2,1,0:T(8,128)(2,1)}, u32[]{:S(2)}) copy-start(bf16[8,288,128]{2,1,0:T(8,128)(2,1)} %get-tuple-element.282) | copy-start | bytes 1769476
  46.0 14.5 %collective-permute-start.33 = (bf16[2,2,2,256,128]{4,3,2,1,0:T(8,128)(2,1)}, bf16[2,2,2,256,128]{4,3,2,1,0:T(8,128)(2,1)S(1)}, u32[]{:S(2)}, u32[]{:S(2)}) collective-permute-start(bf16[2,2,2,256,128]{4,3,2,1,0:T(8,128)(2,1)} %fusion.98), channel_id=1, source_target_pairs={{0,16},{1,17},{2,18},{3,19},{4,20},{5,21},{6,22},{7,23},{8,24},{9,... | collective-permute-start | bytes 1572872 | tf_op jit(solution)/shard_map/ppermute | solution.py:520
  47.7 16.2 %collective-permute-start.24 = (bf16[2,2,2,288,128]{4,3,2,1,0:T(8,128)(2,1)S(1)}, bf16[2,2,2,288,128]{4,3,2,1,0:T(8,128)(2,1)S(1)}, u32[]{:S(2)}, u32[]{:S(2)}) collective-permute-start(bf16[2,2,2,288,128]{4,3,2,1,0:T(8,128)(2,1)S(1)} %fusion.97), channel_id=1, source_target_pairs={{0,1},{1,0},{2,3},{3,2},{4,5},{5,4},{6,7},{7,6},{8,9},{9,8},{10,11... | collective-permute-start | bytes 1769480 | tf_op jit(solution)/shard_map/ppermute | solution.py:520
  57.3 6.5 %copy-start.30 = (bf16[4,288,128]{2,1,0:T(8,128)(2,1)S(1)}, bf16[4,288,128]{2,1,0:T(8,128)(2,1)}, u32[]{:S(2)}) copy-start(bf16[4,288,128]{2,1,0:T(8,128)(2,1)} %get-tuple-element.292) | copy-start | bytes 884740
  60.5 4.2 %copy-start.27 = (bf16[2,2,2,256,128]{4,3,2,1,0:T(8,128)(2,1)}, bf16[2,2,2,256,128]{4,3,2,1,0:T(8,128)(2,1)S(1)}, u32[]{:S(2)}) copy-start(bf16[2,2,2,256,128]{4,3,2,1,0:T(8,128)(2,1)S(1)} %collective-permute-done.33) | copy-start | bytes 1572868
  62.4 12.0 %collective-permute-start.34 = (bf16[2,2,256,128]{3,2,1,0:T(8,128)(2,1)}, bf16[2,2,256,128]{3,2,1,0:T(8,128)(2,1)}, u32[]{:S(2)}, u32[]{:S(2)}) collective-permute-start(bf16[2,2,256,128]{3,2,1,0:T(8,128)(2,1)} %fusion.100), channel_id=1, source_target_pairs={{0,1},{1,0},{2,3},{3,2},{4,5},{5,4},{6,7},{7,6},{8,9},{9,8},{10,11... | collective-permute-start | bytes 786440 | tf_op jit(solution)/shard_map/ppermute | solution.py:520
  64.7 11.5 %collective-permute-start.25 = (bf16[2,2,288,128]{3,2,1,0:T(8,128)(2,1)}, bf16[2,2,288,128]{3,2,1,0:T(8,128)(2,1)}, u32[]{:S(2)}, u32[]{:S(2)}) collective-permute-start(bf16[2,2,288,128]{3,2,1,0:T(8,128)(2,1)} %fusion.99), channel_id=1, source_target_pairs={{0,16},{1,17},{2,18},{3,19},{4,20},{5,21},{6,22},{7,23},{8,24},{9,... | collective-permute-start | bytes 884744 | tf_op jit(solution)/shard_map/ppermute | solution.py:520
  66.2 8.2 %copy-start.28 = (bf16[2,2,2,256,128]{4,3,2,1,0:T(8,128)(2,1)S(1)}, bf16[2,2,2,256,128]{4,3,2,1,0:T(8,128)(2,1)}, u32[]{:S(2)}) copy-start(bf16[2,2,2,256,128]{4,3,2,1,0:T(8,128)(2,1)} %copy-done.27) | copy-start | bytes 1572868
  66.2 9.9 %copy-start.29 = (bf16[4,288,128]{2,1,0:T(8,128)(2,1)S(1)}, bf16[4,288,128]{2,1,0:T(8,128)(2,1)}, u32[]{:S(2)}) copy-start(bf16[4,288,128]{2,1,0:T(8,128)(2,1)} %get-tuple-element.274) | copy-start | bytes 884740
  76.1 6.7 %collective-permute-start.35 = (bf16[2,256,128]{2,1,0:T(8,128)(2,1)}, bf16[2,256,128]{2,1,0:T(8,128)(2,1)}, u32[]{:S(2)}, u32[]{:S(2)}) collective-permute-start(bf16[2,256,128]{2,1,0:T(8,128)(2,1)} %fusion.102), channel_id=1, source_target_pairs={{0,2},{1,3},{2,0},{3,1},{4,6},{5,7},{6,4},{7,5},{8,10},{9,11},{10,... | collective-permute-start | bytes 393224 | tf_op jit(solution)/shard_map/ppermute | solution.py:520
  77.8 12.7 %collective-permute-start.26 = (bf16[2,288,128]{2,1,0:T(8,128)(2,1)}, bf16[2,288,128]{2,1,0:T(8,128)(2,1)S(1)}, u32[]{:S(2)}, u32[]{:S(2)}) collective-permute-start(bf16[2,288,128]{2,1,0:T(8,128)(2,1)} %fusion.101), channel_id=1, source_target_pairs={{0,2},{1,3},{2,0},{3,1},{4,6},{5,7},{6,4},{7,5},{8,10},{9,11},{10,... | collective-permute-start | bytes 442376 | tf_op jit(solution)/shard_map/ppermute | solution.py:520
  81.8 14.3 %copy-start.34 = (bf16[4,128,128]{2,1,0:T(8,128)(2,1)S(1)}, bf16[4,128,128]{2,1,0:T(8,128)(2,1)}, u32[]{:S(2)}) copy-start(bf16[4,128,128]{2,1,0:T(8,128)(2,1)} %get-tuple-element.307) | copy-start | bytes 393220
  81.8 15.1 %copy-start.33 = (bf16[4,64,128]{2,1,0:T(8,128)(2,1)S(1)}, bf16[4,64,128]{2,1,0:T(8,128)(2,1)}, u32[]{:S(2)}) copy-start(bf16[4,64,128]{2,1,0:T(8,128)(2,1)} %get-tuple-element.310) | copy-start | bytes 196612
  83.7 5.2 %collective-permute-start.36 = (bf16[256,128]{1,0:T(8,128)(2,1)S(1)}, bf16[256,128]{1,0:T(8,128)(2,1)S(1)}, u32[]{:S(2)}, u32[]{:S(2)}) collective-permute-start(bf16[256,128]{1,0:T(8,128)(2,1)S(1)} %fusion.108), channel_id=1, source_target_pairs={{0,4},{1,5},{2,6},{3,7},{4,0},{5,1},{6,2},{7,3},{8,12},{9,13},{10,... | collective-permute-start | bytes 196616 | tf_op jit(solution)/shard_map/ppermute | solution.py:520
  85.2 10.8 %collective-permute-start.28 = (bf16[800,128]{1,0:T(8,128)(2,1)S(1)}, bf16[800,128]{1,0:T(8,128)(2,1)S(1)}, u32[]{:S(2)}, u32[]{:S(2)}) collective-permute-start(bf16[800,128]{1,0:T(8,128)(2,1)S(1)} %pad_maximum_fusion.15), channel_id=1, source_target_pairs={{0,1},{1,0},{2,3},{3,2},{4,5},{5,4},{6,7},{7,6},{8,9},{9,8},{10,11... | collective-permute-start | bytes 614408 | tf_op jit(solution)/shard_map/ppermute | solution.py:520
  89.9 6.0 %collective-permute-start.37 = (bf16[256,128]{1,0:T(8,128)(2,1)S(1)}, bf16[256,128]{1,0:T(8,128)(2,1)S(1)}, u32[]{:S(2)}, u32[]{:S(2)}) collective-permute-start(bf16[256,128]{1,0:T(8,128)(2,1)S(1)} %fusion.110), channel_id=1, source_target_pairs={{0,4},{1,5},{2,6},{3,7},{4,0},{5,1},{6,2},{7,3},{8,12},{9,13},{10,... | collective-permute-start | bytes 196616 | tf_op jit(solution)/shard_map/ppermute | solution.py:520
  91.4 5.4 %collective-permute-start.27 = (bf16[288,128]{1,0:T(8,128)(2,1)S(1)}, bf16[288,128]{1,0:T(8,128)(2,1)S(1)}, u32[]{:S(2)}, u32[]{:S(2)}) collective-permute-start(bf16[288,128]{1,0:T(8,128)(2,1)S(1)} %fusion.104), channel_id=1, source_target_pairs={{0,4},{1,5},{2,6},{3,7},{4,0},{5,1},{6,2},{7,3},{8,12},{9,13},{10,... | collective-permute-start | bytes 221192 | tf_op jit(solution)/shard_map/ppermute | solution.py:520
  95.9 9.8 %collective-permute-start.38 = (bf16[2,256,128]{2,1,0:T(8,128)(2,1)S(1)}, bf16[2,256,128]{2,1,0:T(8,128)(2,1)S(1)}, u32[]{:S(2)}, u32[]{:S(2)}) collective-permute-start(bf16[2,256,128]{2,1,0:T(8,128)(2,1)S(1)} %get-tuple-element.617), channel_id=1, source_target_pairs={{0,2},{1,3},{2,0},{3,1},{4,6},{5,7},{6,4},{7,5},{8,10},{9,11},{10,... | collective-permute-start | bytes 393224 | tf_op jit(solution)/shard_map/ppermute | solution.py:520
  97.8 5.4 %collective-permute-start.41 = (bf16[288,128]{1,0:T(8,128)(2,1)S(1)}, bf16[288,128]{1,0:T(8,128)(2,1)S(1)}, u32[]{:S(2)}, u32[]{:S(2)}) collective-permute-start(bf16[288,128]{1,0:T(8,128)(2,1)S(1)} %fusion.106), channel_id=1, source_target_pairs={{0,4},{1,5},{2,6},{3,7},{4,0},{5,1},{6,2},{7,3},{8,12},{9,13},{10,... | collective-permute-start | bytes 221192 | tf_op jit(solution)/shard_map/ppermute | solution.py:520
  100.4 6.5 %collective-permute-start.29 = (bf16[544,128]{1,0:T(8,128)(2,1)S(1)}, bf16[544,128]{1,0:T(8,128)(2,1)S(1)}, u32[]{:S(2)}, u32[]{:S(2)}) collective-permute-start(bf16[544,128]{1,0:T(8,128)(2,1)S(1)} %pad_maximum_fusion.17), channel_id=1, source_target_pairs={{0,2},{1,3},{2,0},{3,1},{4,6},{5,7},{6,4},{7,5},{8,10},{9,11},{10,... | collective-permute-start | bytes 417800 | tf_op jit(solution)/shard_map/ppermute | solution.py:520
  103.3 5.8 %collective-permute-start.42 = (bf16[2,288,128]{2,1,0:T(8,128)(2,1)S(1)}, bf16[2,288,128]{2,1,0:T(8,128)(2,1)S(1)}, u32[]{:S(2)}, u32[]{:S(2)}) collective-permute-start(bf16[2,288,128]{2,1,0:T(8,128)(2,1)S(1)} %get-tuple-element.613), channel_id=1, source_target_pairs={{0,2},{1,3},{2,0},{3,1},{4,6},{5,7},{6,4},{7,5},{8,10},{9,11},{10,... | collective-permute-start | bytes 442376 | tf_op jit(solution)/shard_map/ppermute | solution.py:520
  105.8 8.8 %collective-permute-start.39 = (bf16[2,2,256,128]{3,2,1,0:T(8,128)(2,1)S(1)}, bf16[2,2,256,128]{3,2,1,0:T(8,128)(2,1)S(1)}, u32[]{:S(2)}, u32[]{:S(2)}) collective-permute-start(bf16[2,2,256,128]{3,2,1,0:T(8,128)(2,1)S(1)} %get-tuple-element.611), channel_id=1, source_target_pairs={{0,1},{1,0},{2,3},{3,2},{4,5},{5,4},{6,7},{7,6},{8,9},{9,8},{10,11... | collective-permute-start | bytes 786440 | tf_op jit(solution)/shard_map/ppermute | solution.py:520
  107.1 6.8 %collective-permute-start.30 = (bf16[416,128]{1,0:T(8,128)(2,1)S(1)}, bf16[416,128]{1,0:T(8,128)(2,1)S(1)}, u32[]{:S(2)}, u32[]{:S(2)}) collective-permute-start(bf16[416,128]{1,0:T(8,128)(2,1)S(1)} %pad_maximum_fusion.20), channel_id=1, source_target_pairs={{0,4},{1,5},{2,6},{3,7},{4,0},{5,1},{6,2},{7,3},{8,12},{9,13},{10,... | collective-permute-start | bytes 319496 | tf_op jit(solution)/shard_map/ppermute | solution.py:520
  109.1 6.8 %collective-permute-start.43 = (bf16[2,2,288,128]{3,2,1,0:T(8,128)(2,1)S(1)}, bf16[2,2,288,128]{3,2,1,0:T(8,128)(2,1)S(1)}, u32[]{:S(2)}, u32[]{:S(2)}) collective-permute-start(bf16[2,2,288,128]{3,2,1,0:T(8,128)(2,1)S(1)} %get-tuple-element.609), channel_id=1, source_target_pairs={{0,16},{1,17},{2,18},{3,19},{4,20},{5,21},{6,22},{7,23},{8,24},{9,... | collective-permute-start | bytes 884744 | tf_op jit(solution)/shard_map/ppermute | solution.py:520
  113.9 3.1 %collective-permute-start.31 = (bf16[32,128]{1,0:T(8,128)(2,1)S(1)}, bf16[32,128]{1,0:T(8,128)(2,1)S(1)}, u32[]{:S(2)}, u32[]{:S(2)}) collective-permute-start(bf16[32,128]{1,0:T(8,128)(2,1)S(1)} %reduce-precision_convert_fusion.2), channel_id=1, source_target_pairs={{0,8},{1,9},{2,10},{3,11},{4,12},{5,13},{6,14},{7,15},{8,0},{9,1},... | collective-permute-start | bytes 24584 | tf_op jit(solution)/shard_map/ppermute | solution.py:520
  114.6 15.2 %collective-permute-start.40 = (bf16[2,2,2,256,128]{4,3,2,1,0:T(8,128)(2,1)S(1)}, bf16[2,2,2,256,128]{4,3,2,1,0:T(8,128)(2,1)S(1)}, u32[]{:S(2)}, u32[]{:S(2)}) collective-permute-start(bf16[2,2,2,256,128]{4,3,2,1,0:T(8,128)(2,1)S(1)} %get-tuple-element.607), channel_id=1, source_target_pairs={{0,16},{1,17},{2,18},{3,19},{4,20},{5,21},{6,22},{7,23},{8,24},{9,... | collective-permute-start | bytes 1572872 | tf_op jit(solution)/shard_map/ppermute | solution.py:520
  115.9 14.9 %collective-permute-start.44 = (bf16[2,2,2,288,128]{4,3,2,1,0:T(8,128)(2,1)S(1)}, bf16[2,2,2,288,128]{4,3,2,1,0:T(8,128)(2,1)S(1)}, u32[]{:S(2)}, u32[]{:S(2)}) collective-permute-start(bf16[2,2,2,288,128]{4,3,2,1,0:T(8,128)(2,1)S(1)} %get-tuple-element.605), channel_id=1, source_target_pairs={{0,1},{1,0},{2,3},{3,2},{4,5},{5,4},{6,7},{7,6},{8,9},{9,8},{10,11... | collective-permute-start | bytes 1769480 | tf_op jit(solution)/shard_map/ppermute | solution.py:520
  117.0 12.2 %collective-permute-start.32 = (bf16[32,128]{1,0:T(8,128)(2,1)S(1)}, bf16[32,128]{1,0:T(8,128)(2,1)S(1)}, u32[]{:S(2)}, u32[]{:S(2)}) collective-permute-start(bf16[32,128]{1,0:T(8,128)(2,1)S(1)} %reduce-precision_convert_fusion.1), channel_id=1, source_target_pairs={{0,16},{1,17},{2,18},{3,19},{4,20},{5,21},{6,22},{7,23},{8,24},{9,... | collective-permute-start | bytes 24584 | tf_op jit(solution)/shard_map/ppermute | solution.py:520
  118.5 13.5 %copy-start.39 = (bf16[384]{0:T(512)(128)(2,1)S(1)}, bf16[384]{0:T(512)(128)(2,1)}, u32[]{:S(2)}) copy-start(bf16[384]{0:T(512)(128)(2,1)} %param.37) | copy-start | bytes 2308
  118.5 13.5 %copy-start.41 = (bf16[384]{0:T(512)(128)(2,1)S(1)}, bf16[384]{0:T(512)(128)(2,1)}, u32[]{:S(2)}) copy-start(bf16[384]{0:T(512)(128)(2,1)} %param.38) | copy-start | bytes 2308
  132.0 5.4 %collective-permute-start.46 = (bf16[16,288,128]{2,1,0:T(8,128)(2,1)}, bf16[16,288,128]{2,1,0:T(8,128)(2,1)S(1)}, u32[]{:S(2)}, u32[]{:S(2)}) collective-permute-start(bf16[16,288,128]{2,1,0:T(8,128)(2,1)} %bitcast.493), channel_id=1, source_target_pairs={{0,8},{1,9},{2,10},{3,11},{4,12},{5,13},{6,14},{7,15},{8,0},{9,1},... | collective-permute-start | bytes 3538952 | tf_op jit(solution)/shard_map/ppermute | solution.py:520
  132.0 5.3 %collective-permute-start.45 = (bf16[16,256,128]{2,1,0:T(8,128)(2,1)}, bf16[16,256,128]{2,1,0:T(8,128)(2,1)S(1)}, u32[]{:S(2)}, u32[]{:S(2)}) collective-permute-start(bf16[16,256,128]{2,1,0:T(8,128)(2,1)} %bitcast.497), channel_id=1, source_target_pairs={{0,8},{1,9},{2,10},{3,11},{4,12},{5,13},{6,14},{7,15},{8,0},{9,1},... | collective-permute-start | bytes 3145736 | tf_op jit(solution)/shard_map/ppermute | solution.py:520
  137.4 1.0 copy-start.24
  137.4 1.3 copy-start.23

commit v3 on v2

--- a/solution.py
+++ b/solution.py
@@ -17,11 +17,17 @@
 PIECES = 32
 UNITS = H // PIECES
 EXTRA = 32
+CHUNKS = (
+    (0, 64, 0, ((3,), (2,), (1,), (0,))),
+    (64, 64, EXTRA, ((2,), (3,), (1,), (0,))),
+)
 VMEM_LIMIT = 60 * 1024 * 1024
-BACK = 2
 UNROLL = 4
+BACK_UNROLL = 2
 AGG = 32
-WORK = {(0, 1): (0,), (1, 1): (1,)}
+TIED = (0, 1)
+GIVE = 2
+LAST_GIVE = 0
 COST = 0.02
 KSTEP = 32
 MATRIX_FIRST = True
@@ -153,9 +159,9 @@
     take = lambda n: [refs.pop(0) for _ in range(n)]
     piece_ref, given, states_ref, own_label_ref, t_in, b2_ref, w1_ref, b1_ref, wi_ref, wh_ref, bi_ref, bh_ref, cot_ref = take(13)
     new_ref, direct_ref, d_ref, crossed_ref, lat_out, near_out, meta_out = take(7)
-    outs = take(3 * len(chunks) + 1)
+    outs = take(sum(len(chunk.heads) for chunk in chunks) + 1)
     table_ref, p_ref, sum_ref, small_ref, dt_ref, rows_ref, bias_ref, extra_ref, t_ref, lat_ref, near_ref, meta_ref = take(12)
-    built = take(3 * len(chunks) + 1)
+    built = take(len(outs))
     (sems,) = refs
     waiting = []
 
@@ -307,25 +313,12 @@
         place = chunks[c].place(rel)
         if rel >= PIECES // 2:
             return joint, place, chunks[c].offset
-        for n, count in enumerate((PIECES // 8, PIECES // 8, PIECES // 4)):
+        before = sum(len(chunk.heads) for chunk in chunks[:c])
+        for n, head in enumerate(chunks[c].heads):
+            count = PIECES // 2 >> len(head)
             if place < count:
-                return built[3 * c + n], place, 0
+                return built[before + n], place, 0
             place -= count
-
-    for rel in list(range(PIECES // 2, PIECES)) + list(range(PIECES // 2)):
-        k0 = jnp.bitwise_xor(piece_me, rel) * UNITS
-        for m in range(0, UNITS, 2):
-            out = nn(dt_ref[...], jnp.concatenate([p_ref[k0 + m], p_ref[k0 + m + 1]], axis=1)).astype(BF16)
-            for c, chunk in enumerate(chunks):
-                ref, place, offset = dest(c, rel)
-                for h in range(2):
-                    start = offset + (m + h) * chunk.rows
-                    ref[place, start : start + chunk.rows, :] = out[
-                        chunk.first : chunk.first + chunk.rows, h * H : (h + 1) * H
-                    ]
-        if rel == PIECES // 2 - 1:
-            for n in range(3):
-                copy(built[n], outs[n])
 
     mixed_t = nt(ident, mixed).astype(BF16)
     prior_t = nt(ident, prior).astype(BF16)
@@ -350,9 +343,21 @@
         extra_ref[28:29, :] = bias_ref[pl.ds(p, 1), :]
         ref, place, offset = dest(len(chunks) - 1, rel)
         ref[place, offset + UNITS * last.rows : offset + last.height, :] = extra_ref[...].astype(BF16)
+
+    for rel in list(range(PIECES // 2, PIECES)) + list(range(PIECES // 2)):
+        k0 = jnp.bitwise_xor(piece_me, rel) * UNITS
+        for m in range(0, UNITS, 2):
+            out = nn(dt_ref[...], jnp.concatenate([p_ref[k0 + m], p_ref[k0 + m + 1]], axis=1)).astype(BF16)
+            for c, chunk in enumerate(chunks):
+                ref, place, offset = dest(c, rel)
+                for h in range(2):
+                    start = offset + (m + h) * chunk.rows
+                    ref[place, start : start + chunk.rows, :] = out[
+                        chunk.first : chunk.first + chunk.rows, h * H : (h + 1) * H
+                    ]
         if rel == PIECES - 1:
             copy(joint, outs[-1])
-    for n in range(3, len(built) - 1):
+    for n in range(len(built) - 1):
         copy(built[n], outs[n])
     for moving in waiting[1:]:
         moving.wait()
@@ -381,19 +386,29 @@
                     wide_ref[g + n, k : k + 16, v * H : (v + 1) * H] = moved[v * 16 : (v + 1) * 16, n * H : (n + 1) * H]
 
 
-def back_kernel(shape, count, begins, *refs):
+def back_kernel(shape, masks, me_ref, *refs):
     holders, own, groups = shape
-    crossed_ref, wide_ref, bias_ref, w1_ref, b1_ref, lat_ref, near_ref, meta_ref = refs[:8]
-    part_ref, first_ref, edge_ref = refs[-3:]
+    blocks = groups // 2
+    crossed_ref, wide_in, bias_ref, w1_ref, b1_ref, lat_in, near_in, meta_in = refs[:8]
+    keep_d, keep_e, send_ref, first_ref = refs[8:12]
+    part_ref, edge_ref, sum_ref, slab_ref, wide_ref, lat_ref, near_ref, meta_ref, sems = refs[12:]
+
+    def coming(g):
+        pages = pl.ds(2 * g, 2)
+        return [
+            pltpu.make_async_copy(wide_in.at[g], wide_ref.at[g], sems.at[0, g]),
+            pltpu.make_async_copy(lat_in.at[pages], lat_ref.at[pages], sems.at[1, g]),
+            pltpu.make_async_copy(near_in.at[pages], near_ref.at[pages], sems.at[2, g]),
+            pltpu.make_async_copy(meta_in.at[pages], meta_ref.at[pages], sems.at[3, g]),
+        ]
+
+    for g in range(groups):
+        for copy in coming(g):
+            copy.start()
     nodes = holders * own
     lanes = holders * SIDE
     ident = eye(H)
-    if begins:
-        part_ref[...] = jnp.zeros_like(part_ref)
-        first_ref[...] = jnp.zeros_like(first_ref)
-    else:
-        part_ref[...] = refs[8][...]
-        first_ref[...] = refs[9][...]
+    part_ref[...] = jnp.zeros_like(part_ref)
     w1n = w1_ref[...]
     w1 = nt(ident, w1n).astype(BF16)
     b1 = nt(ident, jnp.broadcast_to(b1_ref[...].astype(F32), (16, H)).astype(BF16))[:, 0:1]
@@ -403,6 +418,8 @@
         return jnp.concatenate([ref[2 * g + n, rows, :] for n in range(2)], axis=1)
 
     def group_step(usual, g, first_total):
+        for copy in coming(g):
+            copy.wait()
         wide = wide_ref[g]
         wide_t = jnp.concatenate([wide[:, v * H : (v + 1) * H].T for v in range(GROUP)], axis=1)
         bias_rows = bias_ref[pl.ds(pl.multiple_of(g * GROUP, GROUP), GROUP), :].astype(BF16)
@@ -431,32 +448,28 @@
             edge_ref[2 * g + n] = edges[:, n * lanes : (n + 1) * lanes]
         return first_total + nt(jnp.concatenate([data, one_row], axis=0), d_before)
 
+    none = jnp.zeros((32, H), F32)
+
     @pl.when(crossed_ref[0] == 0)
     def _():
-        first_ref[...] = lax.fori_loop(
-            0, count, functools.partial(group_step, True), first_ref[...], unroll=min(2, count)
-        )
+        sum_ref[...] = lax.fori_loop(0, groups, functools.partial(group_step, True), none, unroll=BACK_UNROLL)
 
     @pl.when(crossed_ref[0] != 0)
     def _():
-        first_ref[...] = lax.fori_loop(0, count, functools.partial(group_step, False), first_ref[...])
-
-
-def return_kernel(shape, masks, me_ref, part_ref, *refs):
-    holders, own, groups = shape
-    blocks = groups // 2
-    edges, (keep_d, keep_e, send_ref, slab_ref) = refs[:-4], refs[-4:]
+        sum_ref[...] = lax.fori_loop(0, groups, functools.partial(group_step, False), none)
+
+    first = sum_ref[...].astype(BF16)
+    first_ref[...] = first
+    half = holders // 2
     side = lax.broadcasted_iota(jnp.int32, (16, H), 1) // SIDE
-    each = 2 * groups // len(edges)
     for q in range(blocks):
         for s in range(holders):
             at = slice(s // 4 * H, (s // 4 + 1) * H)
-            parts = [edges[(4 * q + u) // each][(4 * q + u) % each, :, at] for u in range(4)]
+            parts = [edge_ref[4 * q + u, :, at] for u in range(4)]
             page = parts[(3 - s) % 4]
             for c in range(3):
                 page = jnp.where(side == c, parts[(c - s) % 4], page)
             slab_ref[s, 16 * q : 16 * (q + 1), :] = page.astype(BF16)
-    half = holders // 2
     for n in range(holders):
         rel = sum(mask for i, mask in enumerate(reversed(masks)) if n >> i & 1)
         h = jnp.bitwise_xor(me_ref[0], rel)
@@ -492,9 +505,12 @@
 
 
 class Chunk:
-    def __init__(self, first, rows, extra, order, offset):
-        self.first, self.rows, self.extra, self.order, self.offset = first, rows, extra, order, offset
+    def __init__(self, first, rows, extra, steps, offset):
+        self.first, self.rows, self.extra, self.steps, self.offset = first, rows, extra, steps, offset
         self.height = UNITS * rows + extra
+        self.order = sum(steps, ())
+        ways = [(n,) for n in range(2)] if len(steps[0]) == 1 else [(n, m) for n in range(2) for m in range(2)]
+        self.heads = [(0, 0), (0, 1), (1,)] if len(steps[0]) == 1 else ways
 
     def place(self, rel):
         at = 0
@@ -505,12 +521,23 @@
     def shape(self):
         return (2,) * len(self.order) + (self.height, H)
 
+    def partners(self, step, bits):
+        group = self.steps[step]
+        found = []
+        for n in range(1, 2 ** len(group)):
+            path = tuple(n >> (len(group) - 1 - i) & 1 for i in range(len(group)))
+            found.append((path, sum(bits[bit] for bit, on in zip(group, path) if on)))
+        return found
+
 
 def plan(batch, edge):
     core, x = [edge], [edge << n for n in range(1, batch.bit_length() - 1)]
     z = [2 << n for n in reversed(range(3 - len(x)))]
     bits = z + [1] + x + core
-    chunks = [Chunk(0, 64, 0, (3, 2, 1, 0), 0), Chunk(64, 64, EXTRA, (2, 3, 1, 0), 64 * UNITS)]
+    chunks, offset = [], 0
+    for first, rows, extra, steps in CHUNKS:
+        chunks.append(Chunk(first, rows, extra, steps, offset))
+        offset += chunks[-1].height
     device = lax.axis_index(("batch", "edge")).astype(jnp.int32)
     piece = sum(jnp.where(device & mask != 0, 1 << n, 0) for n, mask in enumerate(bits))
     return bits, chunks, piece.astype(jnp.int32).reshape(1)
@@ -531,46 +558,42 @@
     return lax.reduce_precision(x.astype(F32), 8, 7).astype(BF16)
 
 
-def unpack(chunks, half, me, order_ref, given, block_refs, w_out, rows_ref, sems, beside=lambda: None):
-    steps = PIECES // 8
+def jobs_of(chunks, arrived, cores):
+    found = []
+    for core in cores:
+        for c, chunk in enumerate(chunks):
+            last, beside = chunk.order[:2]
+            for n in range(2):
+                found.append((c, core, core * PIECES // 2 + (arrived << last) + (n << beside), 4 * n))
+    return found
+
+
+def unpack(chunks, jobs, me, order_ref, sources, block_refs, w_out, rows_ref, sems, beside=lambda: None):
     width = 4 * UNITS
-
-    def coming(step):
-        copies = []
-        for c, chunk in enumerate(chunks):
-            at = pl.ds(chunk.place(4 * step), 4)
-            copies.append(pltpu.make_async_copy(given[c].at[at], block_refs[c].at[at], sems.at[2 + len(chunks) * step + c]))
-        return copies
-
-    def leaving(step):
-        start = jnp.bitwise_xor(jnp.right_shift(me, 2), step + half * steps) * width
-        rows = pl.ds(pl.multiple_of(start, width), width)
-        return pltpu.make_async_copy(rows_ref.at[step % 2], w_out.at[rows, :], sems.at[step % 2])
-
-    for step in range(steps):
-        for copy in coming(step):
-            copy.start()
+    coming, leaving = [], []
+    for n, (c, core, rel, place) in enumerate(jobs):
+        coming.append(pltpu.make_async_copy(sources[n].at[pl.ds(place, 4)], block_refs[n], sems.at[n]))
+        rows = pl.ds(pl.multiple_of(jnp.bitwise_xor(jnp.right_shift(me, 2), rel // 4) * width, width), width)
+        lanes = pl.ds(chunks[c].first * H, chunks[c].rows * H)
+        leaving.append(pltpu.make_async_copy(rows_ref.at[n % 3], w_out.at[rows, lanes], sems.at[len(jobs) + n]))
+    for copy in coming:
+        copy.start()
     order_ref[...] = swap_rows(32, 2 * UNITS, jnp.bitwise_and(me, 1) * UNITS)
     beside()
-    for step in range(steps):
-        for copy in coming(step):
-            copy.wait()
-        if step >= 2:
-            leaving(step - 2).wait()
+    for n, (c, core, rel, place) in enumerate(jobs):
+        coming[n].wait()
+        if n >= 3:
+            leaving[n - 3].wait()
+        rows = chunks[c].rows
         for pair in range(2):
-            rel = 4 * step + 2 * pair
-            places = [[chunk.place(rel + n) for n in range(2)] for chunk in chunks]
             upper = jnp.bitwise_xor(jnp.bitwise_and(jnp.right_shift(me, 1), 1), pair)
             at_rows = pl.ds(pl.multiple_of(upper * 2 * UNITS, 2 * UNITS), 2 * UNITS)
-            for ib in range(0, H, 64):
+            for ib in range(0, rows, 64):
                 sides = []
-                for side in range(2):
-                    at = ib + 32 * side
-                    c = max(n for n in range(len(chunks)) if chunks[n].first <= at)
-                    first, rows = chunks[c].first, chunks[c].rows
+                for at in (ib, ib + 32):
                     parts = [
-                        block_refs[c][places[c][n], m * rows + at - first : m * rows + at - first + 32, :]
-                        for n in range(2)
+                        block_refs[n][2 * pair + i, m * rows + at : m * rows + at + 32, :]
+                        for i in range(2)
                         for m in range(UNITS)
                     ]
                     sides.append(jnp.concatenate(parts, axis=0))
@@ -578,55 +601,80 @@
                 for side in range(2):
                     for i in range(32):
                         at = (ib + 32 * side + i) * H
-                        rows_ref[step % 2, at_rows, at : at + H] = moved[8 * i : 8 * (i + 1), side * H : (side + 1) * H]
-        leaving(step).start()
+                        rows_ref[n % 3, at_rows, at : at + H] = moved[8 * i : 8 * (i + 1), side * H : (side + 1) * H]
+        leaving[n].start()
 
     def end():
-        for step in range(steps - 2, steps):
-            leaving(step).wait()
+        for copy in leaving[-3:]:
+            copy.wait()
 
     return end
 
 
-def small_pieces(chunks, half, me, block_refs, extra_ref, bias_ref):
-    last = chunks[-1]
-    start = UNITS * last.rows
-    for n in range(PIECES // 2):
-        extra = block_refs[-1][last.place(n), start : start + EXTRA, :].astype(F32)
-        p = jnp.bitwise_xor(me, n + half * PIECES // 2)
-        for t in range(7):
-            extra_ref[t, pl.ds(p * UNITS, UNITS), :] = extra[UNITS * t : UNITS * (t + 1), :]
-        bias_ref[pl.ds(p, 1), :] = extra[28:29, :]
-
-
-def own_half_kernel(chunks, piece_ref, *refs):
+def small_piece(me, rel, extra, extra_ref, bias_ref):
+    p = jnp.bitwise_xor(me, rel)
+    extra = extra.astype(F32)
+    for t in range(7):
+        extra_ref[t, pl.ds(p * UNITS, UNITS), :] = extra[UNITS * t : UNITS * (t + 1), :]
+    bias_ref[pl.ds(p, 1), :] = extra[28:29, :]
+
+
+def small_pieces(chunks, jobs, me, block_refs, extra_ref, bias_ref):
+    start = UNITS * chunks[-1].rows
+    for n, (c, core, rel, place) in enumerate(jobs):
+        if c == len(chunks) - 1:
+            for i in range(4):
+                small_piece(me, rel + i, block_refs[n][i, start : start + EXTRA, :], extra_ref, bias_ref)
+
+
+def early_kernel(chunks, piece_ref, *refs):
     count = len(chunks)
-    given, (w_out, extra_ref, bias_ref) = refs[:count], refs[count : count + 3]
-    block_refs, (rows_ref, order_ref, sems) = refs[count + 3 : 2 * count + 3], refs[2 * count + 3 :]
+    jobs = jobs_of(chunks, 0, (0, 1))
+    sources = [refs[core * count + c] for c, core, rel, place in jobs]
+    w_out, extra_ref, bias_ref = refs[2 * count : 2 * count + 3]
+    block_refs, (rows_ref, order_ref, sems) = refs[2 * count + 3 : -3], refs[-3:]
     me = piece_ref[0]
     extra_ref[...] = jnp.zeros_like(extra_ref)
     bias_ref[...] = jnp.zeros_like(bias_ref)
-    end = unpack(chunks, 0, me, order_ref, given, block_refs, w_out, rows_ref, sems)
-    small_pieces(chunks, 0, me, block_refs, extra_ref, bias_ref)
+    end = unpack(chunks, jobs, me, order_ref, sources, block_refs, w_out, rows_ref, sems)
+    small_pieces(chunks, jobs, me, block_refs, extra_ref, bias_ref)
     end()
 
 
-def other_half_kernel(chunks, piece_ref, *refs):
+def late_kernel(chunks, piece_ref, *refs):
     count = len(chunks)
-    given, (first_ref, extra_in, bias_in, w_in) = refs[:count], refs[count : count + 4]
-    w_out, w1_ref, b1_ref, wi_ref, wh_ref, b2_ref, bi_ref, bh_ref = refs[count + 4 : count + 12]
-    block_refs = refs[count + 12 : 2 * count + 12]
-    rows_ref, order_ref, extra_ref, bias_ref, sems = refs[2 * count + 12 :]
+    jobs = jobs_of(chunks, 1, (0,))
+    sources = [refs[c] for c, core, rel, place in jobs]
+    w_in, w_out = refs[count : count + 2]
+    block_refs, (rows_ref, order_ref, sems) = refs[count + 2 : -3], refs[-3:]
+    unpack(chunks, jobs, piece_ref[0], order_ref, sources, block_refs, w_out, rows_ref, sems)()
+
+
+def last_kernel(chunks, piece_ref, *refs):
+    count = len(chunks)
+    jobs = jobs_of(chunks, 1, (1,))
+    sources = [refs[c] for c, core, rel, place in jobs]
+    own_last, first_ref, extra_in, bias_in, w_in = refs[count : count + 5]
+    w_out, w1_ref, b1_ref, wi_ref, wh_ref, b2_ref, bi_ref, bh_ref = refs[count + 5 : count + 13]
+    block_refs, (rows_ref, order_ref, small_ref, extra_ref, bias_ref, sems) = refs[count + 13 : -6], refs[-6:]
     me = piece_ref[0]
+    start = UNITS * chunks[-1].rows
+    small = pltpu.make_async_copy(own_last.at[:, start : start + EXTRA, :], small_ref, sems.at[2 * len(jobs)])
 
     def beside():
+        small.start()
         w1_ref[...] = first_ref[0:16, :].astype(F32)
         b1_ref[...] = first_ref[16:17, :].astype(F32).reshape(H)
         extra_ref[...] = extra_in[...]
         bias_ref[...] = bias_in[...]
-
-    end = unpack(chunks, 1, me, order_ref, given, block_refs, w_out, rows_ref, sems, beside)
-    small_pieces(chunks, 1, me, block_refs, extra_ref, bias_ref)
+        small.wait()
+        for c, core, rel, place in jobs_of(chunks, 1, (0,)):
+            if c == count - 1:
+                for i in range(4):
+                    small_piece(me, rel + i, small_ref[place + i], extra_ref, bias_ref)
+
+    end = unpack(chunks, jobs, me, order_ref, sources, block_refs, w_out, rows_ref, sems, beside)
+    small_pieces(chunks, jobs, me, block_refs, extra_ref, bias_ref)
     for t in range(3):
         wi_ref[:, t * H : (t + 1) * H] = extra_ref[t]
         wh_ref[:, t * H : (t + 1) * H] = extra_ref[3 + t]
@@ -634,6 +682,34 @@
         bh_ref[t * H : (t + 1) * H] = bias_ref[3 + t : 4 + t, :].reshape(H)
     b2_ref[...] = extra_ref[6]
     end()
+
+
+def unpack_scratch(chunks, jobs, more=()):
+    return (
+        [pltpu.VMEM((4, chunks[c].height, H), BF16) for c, core, rel, place in jobs]
+        + [pltpu.VMEM((3, 4 * UNITS, max(chunk.rows for chunk in chunks) * H), F32), pltpu.VMEM((256, 256), BF16)]
+        + list(more)
+        + [pltpu.SemaphoreType.DMA((2 * len(jobs) + 1,))]
+    )
+
+
+W_SHAPE = jax.ShapeDtypeStruct((H, H * H), F32)
+SMALL = [jax.ShapeDtypeStruct((7, H, H), F32), jax.ShapeDtypeStruct((PIECES, H), F32)]
+
+
+def early_half(chunks, bits, devices, piece_arr, parts):
+    parts = [x.reshape(PIECES // 4, chunk.height, H) for x, chunk in zip(parts, chunks)]
+    others = [swap(x, bits[-1], devices) for x in parts]
+    return pl.pallas_call(
+        functools.partial(early_kernel, chunks),
+        name="assemble_early",
+        in_specs=[smem()] + [anywhere()] * (2 * len(chunks)),
+        out_specs=[anywhere(), vmem(), vmem()],
+        scratch_shapes=unpack_scratch(chunks, jobs_of(chunks, 0, (0, 1))),
+        out_shape=[W_SHAPE] + SMALL,
+        compiler_params=params(),
+        cost_estimate=cost(6),
+    )(piece_arr, *parts, *others)
 
 
 def vmem():
@@ -699,7 +775,7 @@
     )(w_edge_out)
     b2 = b_edge_out.reshape(H, H)
     b1 = b_edge_in.reshape(1, H)
-    built = [jax.ShapeDtypeStruct((PIECES // n, c.height, H), BF16) for c in chunks for n in (8, 8, 4)]
+    built = [jax.ShapeDtypeStruct((PIECES // 2 >> len(h), c.height, H), BF16) for c in chunks for h in c.heads]
     built.append(jax.ShapeDtypeStruct((PIECES // 2, sum(c.height for c in chunks), H), BF16))
     front = pl.pallas_call(
         functools.partial(front_kernel, shape, chunks),
@@ -759,42 +835,34 @@
         cost_estimate=cost(6),
     )
 
-    count = groups // BACK
-    edge_parts = []
-    pending = []
-
-    def back_step(n, wide, bias, sums):
-        whole_spec = lambda shp: pl.BlockSpec(shp, lambda i: (0, 0))
-        *sums, edge_part = pl.pallas_call(
-            functools.partial(back_kernel, shape, count, not sums),
+    back_masks = [1 << n for n in range(edge.bit_length() - 1)]
+
+    def edge_work(wide, bias):
+        return pl.pallas_call(
+            functools.partial(back_kernel, shape, back_masks),
             name="edge_gradients",
             out_shape=[
-                jax.ShapeDtypeStruct((holders * own, H), F32),
-                jax.ShapeDtypeStruct((32, H), F32),
-                jax.ShapeDtypeStruct((2 * count, 16, lanes), F32),
+                jax.ShapeDtypeStruct((holders // 2, own, H), BF16),
+                jax.ShapeDtypeStruct((holders // 2, 16 * blocks, H), BF16),
+                jax.ShapeDtypeStruct((holders // 2 * (own + 16 * blocks), H), BF16),
+                jax.ShapeDtypeStruct((32, H), BF16),
             ],
-            grid=(1,),
-            in_specs=[
-                smem(),
-                pl.BlockSpec((count, H, GROUP * H), lambda i: (n, 0, 0)),
-                pl.BlockSpec((count * GROUP, H), lambda i: (n, 0)),
-                whole_spec((16, H)),
-                whole_spec((1, H)),
-                pl.BlockSpec((2 * count, H, lanes), lambda i: (n, 0, 0)),
-                pl.BlockSpec((2 * count, H, lanes), lambda i: (n, 0, 0)),
-                pl.BlockSpec((2 * count, 32 + GROUP, lanes), lambda i: (n, 0, 0)),
-            ]
-            + [whole_spec((holders * own, H)), whole_spec((32, H))][: len(sums)],
-            out_specs=[
-                whole_spec((holders * own, H)),
-                whole_spec((32, H)),
-                pl.BlockSpec((2 * count, 16, lanes), lambda i: (0, 0, 0)),
+            in_specs=[smem()] * 2 + [anywhere()] + [vmem()] * 3 + [anywhere()] * 3,
+            out_specs=[vmem()] * 4,
+            scratch_shapes=[
+                pltpu.VMEM((holders * own, H), F32),
+                pltpu.VMEM((pages, 16, lanes), F32),
+                pltpu.VMEM((32, H), F32),
+                pltpu.VMEM((holders, 16 * blocks, H), BF16),
+                pltpu.VMEM((groups, H, GROUP * H), BF16),
+                pltpu.VMEM((pages, H, lanes), BF16),
+                pltpu.VMEM((pages, H, lanes), BF16),
+                pltpu.VMEM((pages, 32 + GROUP, lanes), F32),
+                pltpu.SemaphoreType.DMA((4, groups)),
             ],
             compiler_params=params(),
-            cost_estimate=cost(24 // BACK),
-        )(crossed, wide, bias, w_edge_in, b1, latent, near, meta, *sums)
-        edge_parts.append(edge_part)
-        return tuple(sums)
+            cost_estimate=cost(14),
+        )(me_arr, crossed, wide, bias, w_edge_in, b1, latent, near, meta)
 
     if MATRIX_FIRST:
         sent, d_agg = lax.optimization_barrier((built[-1], d_agg))
@@ -804,9 +872,8 @@
         other = swap(built[-1], bits[-1], devices)
         wide, bias = matrix_gradients(d_agg, t_units, b2)
     other = other.reshape((2,) * 4 + (-1, H))
-    kept = [
-        {(0, 0): built[3 * c], (0, 1): built[3 * c + 1], (1,): built[3 * c + 2]} for c in range(len(chunks))
-    ]
+    arrays = iter(built)
+    kept = [{head: next(arrays) for head in chunk.heads} for chunk in chunks]
     got = [[] for _ in chunks]
 
     def mine(c, path):
@@ -817,70 +884,45 @@
     def partial_sum(c, path):
         rows = slice(chunks[c].offset, chunks[c].offset + chunks[c].height)
         parts = [mine(c, path), other[path][..., rows, :]]
-        for n, x in enumerate(got[c]):
-            parts.append(x[path[n + 1 :]])
+        for n, arrays in enumerate(got[c]):
+            done = sum(len(group) for group in chunks[c].steps[: n + 1])
+            parts += [x[path[done:]] for x in arrays]
         return add(parts)
 
-    def scatter_step(c, step, work=None, given=()):
-        begun = partial_sum(c, (0,) * step + (1,))
-        mask = bits[chunks[c].order[step]]
-        if work is None:
-            got[c].append(swap(begun, mask, devices))
-            return None
-        begun, given = lax.optimization_barrier((begun, given))
-        new, result = lax.optimization_barrier((swap(begun, mask, devices), work(*given)))
-        got[c].append(new)
+    def scatter_step(step, work=None, given=()):
+        begun = []
+        for c, chunk in enumerate(chunks):
+            done = (0,) * sum(len(group) for group in chunk.steps[:step])
+            if step < len(chunk.steps):
+                begun.append([partial_sum(c, done + path) for path, mask in chunk.partners(step, bits)])
+            else:
+                begun.append([])
+        if work is not None:
+            begun, given = lax.optimization_barrier((begun, given))
+        new = [
+            [swap(x, mask, devices) for x, (path, mask) in zip(begun[c], chunk.partners(step, bits))] if begun[c] else []
+            for c, chunk in enumerate(chunks)
+        ]
+        result = None
+        if work is not None:
+            result = work(*given)
+            for c in TIED:
+                new[c], result = lax.optimization_barrier((new[c], result))
+        for c in range(len(chunks)):
+            if new[c]:
+                got[c].append(new[c])
         return result
 
-    def work_on(numbers, wide, bias):
-        def run(*sums):
-            for n in numbers:
-                sums = back_step(n, wide, bias, sums)
-            return sums
-
-        return run
-
-    def gather_step(x, mask):
-        return jnp.stack([x, swap(x, mask, devices)], axis=0)
-
-    back_masks = [m for m in (1 << n for n in range(edge.bit_length() - 1))]
-
-    def send_back(part, *edge_parts):
-        return pl.pallas_call(
-            functools.partial(return_kernel, shape, back_masks),
-            name="returned",
-            out_shape=[
-                jax.ShapeDtypeStruct((holders // 2, own, H), BF16),
-                jax.ShapeDtypeStruct((holders // 2, 16 * blocks, H), BF16),
-                jax.ShapeDtypeStruct((holders // 2 * (own + 16 * blocks), H), BF16),
-            ],
-            in_specs=[smem()] + [vmem()] * (1 + BACK),
-            out_specs=[vmem()] * 3,
-            scratch_shapes=[pltpu.VMEM((holders, 16 * blocks, H), BF16)],
-            compiler_params=params(),
-            cost_estimate=cost(2),
-        )(me_arr, part, *edge_parts)
-
-    sums = ()
-    for step in range(4):
-        for c in range(len(chunks)):
-            if (step, c) in WORK:
-                sums = scatter_step(c, step, work_on(WORK[step, c], wide, bias), sums)
-            else:
-                scatter_step(c, step)
-    parts = [partial_sum(c, (0,) * 4) for c in range(len(chunks))]
-    for mask in rest:
-        parts = [rounded(x.astype(F32) + swap(x, mask, devices).astype(F32)) for x in parts]
-    overflow = parts[-1][UNITS * chunks[-1].rows + 29, 0] > 0.0
-    for step in (3, 2, 1, 0):
-        for c, chunk in enumerate(chunks):
-            parts[c] = gather_step(parts[c], bits[chunk.order[step]])
-    part, first = sums
-    keep_d, keep_e, send = send_back(part, *edge_parts)
-
-    first = rounded(first)
+    keep_d, keep_e, send, first = scatter_step(0, edge_work, (wide, bias))
+    for n in range(edge.bit_length() - 1, devices.bit_length() - 1):
+        first = rounded(first.astype(F32) + swap(first, 1 << n, devices).astype(F32))
+    scatter_step(1)
     slabs, sources = keep_e[:, None], [0]
-    for mask in back_masks:
+
+    def give_back(mask, after):
+        nonlocal keep_d, slabs, sources, send, first
+        if after is not None:
+            send, after = lax.optimization_barrier((send, after))
         n = keep_d.shape[0]
         cut = n * own
         arrived = swap(jnp.concatenate([send, first], axis=0), mask, devices)
@@ -891,10 +933,23 @@
         if n > 1:
             send = jnp.concatenate([keep_d[n // 2 :].reshape(-1, H), slabs[n // 2 :].reshape(-1, H)], axis=0)
             keep_d, slabs = keep_d[: n // 2], slabs[: n // 2]
-    mask = edge
-    while mask < devices:
-        first = rounded(first.astype(F32) + swap(first, mask, devices).astype(F32))
-        mask *= 2
+
+    give_back(1, got[1][1])
+    scatter_step(2)
+    scatter_step(3)
+    parts = [partial_sum(c, (0,) * 4) for c in range(len(chunks))]
+    for mask in rest:
+        parts = [rounded(x.astype(F32) + swap(x, mask, devices).astype(F32)) for x in parts]
+    overflow = parts[-1][UNITS * chunks[-1].rows + 29, 0] > 0.0
+    for step in (3, 2, 1):
+        if step == GIVE:
+            for mask in back_masks[1:-1]:
+                give_back(mask, parts[0] if mask == 2 else None)
+        for c, chunk in enumerate(chunks):
+            parts[c] = gather_step(chunk, step, bits, devices, parts[c])
+    give_back(back_masks[-1], parts[LAST_GIVE])
+    came = [swap(x, bits[chunk.order[0]], devices) for x, chunk in zip(parts, chunks)]
+    early = early_half(chunks, bits, devices, piece_arr, parts)
     state_grads, edge_grads = pl.pallas_call(
         functools.partial(gather_kernel, shape, sources),
         name="slots_to_edges",
@@ -908,56 +963,47 @@
         compiler_params=params(),
         cost_estimate=cost(3),
     )(me_arr, slot, direct, keep_d[0], slabs[0])
-    return overflow, (new_states, state_grads, edge_grads, first, parts)
-
-
-def gather_back(chunks, bits, devices, whole):
-    for step in reversed(range(len(bits) - 1)):
-        whole = [
-            jnp.stack([w, swap(w, bits[chunk.order[step]], devices)], axis=0) for w, chunk in zip(whole, chunks)
-        ]
-    return whole
+    return overflow, (new_states, state_grads, edge_grads, first, came, early)
+
+
+def gather_step(chunk, step, bits, devices, x):
+    partners = chunk.partners(step, bits)
+    all_ = jnp.stack([x] + [swap(x, mask, devices) for path, mask in partners], axis=0)
+    return all_.reshape((2,) * len(chunk.steps[step]) + x.shape)
 
 
 def finish(batch, edge, results):
-    new_states, state_grads, edge_grads, first, whole = results
+    new_states, state_grads, edge_grads, first, came, early = results
     bits, chunks, piece_arr = plan(batch, edge)
     devices = batch * edge
-    whole = [x.reshape(PIECES // 2, chunk.height, H) for x, chunk in zip(whole, chunks)]
-    others = [swap(x, bits[-1], devices) for x in whole]
-    small = [jax.ShapeDtypeStruct((7, H, H), F32), jax.ShapeDtypeStruct((PIECES, H), F32)]
-    scratch = [pltpu.VMEM((PIECES // 2, chunk.height, H), BF16) for chunk in chunks] + [
-        pltpu.VMEM((2, 4 * UNITS, H * H), F32),
-        pltpu.VMEM((256, 256), BF16),
-    ]
-    semaphores = [pltpu.SemaphoreType.DMA((2 + len(chunks) * PIECES // 8,))]
-    grad_w2, extras, biases = pl.pallas_call(
-        functools.partial(own_half_kernel, chunks),
-        name="assemble_own_half",
-        in_specs=[smem()] + [anywhere()] * len(chunks),
-        out_specs=[anywhere(), vmem(), vmem()],
-        scratch_shapes=scratch + semaphores,
-        out_shape=[jax.ShapeDtypeStruct((H, H * H), F32)] + small,
+    came = [x.reshape(PIECES // 4, chunk.height, H) for x, chunk in zip(came, chunks)]
+    others = [swap(x, bits[-1], devices) for x in came]
+    grad_w2, extras, biases = early
+    grad_w2 = pl.pallas_call(
+        functools.partial(late_kernel, chunks),
+        name="assemble_late",
+        in_specs=[smem()] + [anywhere()] * (len(chunks) + 1),
+        out_specs=anywhere(),
+        scratch_shapes=unpack_scratch(chunks, jobs_of(chunks, 1, (0,))),
+        out_shape=W_SHAPE,
+        input_output_aliases={len(chunks) + 1: 0},
         compiler_params=params(),
         cost_estimate=cost(4),
-    )(piece_arr, *whole)
+    )(piece_arr, *came, grad_w2)
+    more = [pltpu.VMEM((PIECES // 4, EXTRA, H), BF16)] + [pltpu.VMEM(x.shape, F32) for x in SMALL]
     grad_w2, grad_w1, grad_b1, grad_wi, grad_wh, grad_b2, grad_bi, grad_bh = pl.pallas_call(
-        functools.partial(other_half_kernel, chunks),
-        name="assemble_other_half",
-        in_specs=[smem()] + [anywhere()] * len(chunks) + [vmem()] * 3 + [anywhere()],
+        functools.partial(last_kernel, chunks),
+        name="assemble_last",
+        in_specs=[smem()] + [anywhere()] * (len(chunks) + 1) + [vmem()] * 3 + [anywhere()],
         out_specs=[anywhere()] + [vmem()] * 7,
-        scratch_shapes=scratch + [pltpu.VMEM(x.shape, F32) for x in small] + semaphores,
-        out_shape=[
-            jax.ShapeDtypeStruct((H, H * H), F32),
-            jax.ShapeDtypeStruct((16, H), F32),
-            jax.ShapeDtypeStruct((H,), F32),
-        ]
+        scratch_shapes=unpack_scratch(chunks, jobs_of(chunks, 1, (1,)), more),
+        out_shape=[W_SHAPE, jax.ShapeDtypeStruct((16, H), F32), jax.ShapeDtypeStruct((H,), F32)]
         + [jax.ShapeDtypeStruct((H, 3 * H), F32)] * 2
         + [jax.ShapeDtypeStruct((H, H), F32)]
         + [jax.ShapeDtypeStruct((3 * H,), F32)] * 2,
-        input_output_aliases={len(chunks) + 4: 0},
+        input_output_aliases={len(chunks) + 5: 0},
         compiler_params=params(),
-    )(piece_arr, *others, first, extras, biases, grad_w2)
+    )(piece_arr, *others, came[-1], first, extras, biases, grad_w2)
     return (
         new_states[None],
         state_grads[None],
@@ -1125,8 +1171,9 @@
         shape = chunk.shape()
         kept, sent = block[: PIECES // 2].reshape(shape), block[PIECES // 2 :].reshape(shape)
         total = add([kept, swap(sent, bits[-1], devices)])
-        for bit in chunk.order:
-            total = add([total[0], swap(total[1], bits[bit], devices)])
+        for step in range(len(chunk.steps)):
+            zero = (0,) * len(chunk.steps[step])
+            total = add([total[zero]] + [swap(total[path], mask, devices) for path, mask in chunk.partners(step, bits)])
         terms.append(total)
     first = jnp.concatenate([grad_w1, grad_b1[None], jnp.zeros((15, H), F32)], axis=0)
     for n in range(devices.bit_length() - 1):
@@ -1134,7 +1181,11 @@
         if mask not in bits:
             terms = [rounded(w.astype(F32) + swap(w, mask, devices).astype(F32)) for w in terms]
         first = first + swap(first, mask, devices)
-    return new_states, state_grads, d_feats.T, first.astype(BF16), gather_back(chunks, bits, devices, terms)
+    for step in (3, 2, 1):
+        terms = [gather_step(chunk, step, bits, devices, x) for x, chunk in zip(terms, chunks)]
+    came = [swap(x, bits[chunk.order[0]], devices) for x, chunk in zip(terms, chunks)]
+    early = early_half(chunks, bits, devices, piece_arr, terms)
+    return new_states, state_grads, d_feats.T, first.astype(BF16), came, early
 
 
 def per_device(batch, edge, *args):

time: 146 us -> 136 us (0.932)
  other arithmetic: 17.9 us -> 7.56 us
  Pallas kernels: 62.7 us -> 59.3 us
  waiting for transfers between devices: 25.9 us -> 28.9 us
  local copies, waits for them, and re-layouts: 5.34 us -> 7.43 us
    convert_element_type x12, other arithmetic: 11.1 us -> 4.64 us  [add(): return total.astype(BF16)]
    pallas_call x5 -> x4, Pallas kernels: 29 us -> 25.8 us  [the longest x1 13.1 us: edge_work(): pl.pallas_call(functools.partial(back_kernel, shape, back_masks), name='e...]
    ppermute x24 -> x26, waiting for transfers between devices: 23.7 us -> 26.5 us  [swap(): lax.ppermute(x, ('batch', 'edge'), [(i, i ^ mask) for i in range(devices)])]
    another operation x8 -> x6, other arithmetic: 2.48 us -> 0.22 us  [gather_step(): jnp.stack([x] + [swap(x, mask, devices) for path, mask in partners], axis=0)]
    unnamed x36, local copies, waits for them, and re-layouts: 2.16 us -> 4.25 us
    ppermute x24 -> x26, starting transfers between devices: 23.8 us -> 22.6 us  [swap(): lax.ppermute(x, ('batch', 'edge'), [(i, i ^ mask) for i in range(devices)])]
  transfers between devices with their start and end apart: 25 -> 27, of which waited for: 10 -> 14; matrix products, arithmetic and copies ran while one was open for 13% -> 7% of each run, Pallas kernels for 27% -> 28%
where the time goes in v3:
time: 136 us; the launch traced here: 135 us
  Pallas kernels  59.3 us (44%)
  starting transfers between devices  29.9 us (22%)
  waiting for transfers between devices  28.9 us (21%)
  other arithmetic  7.56 us (6%)
  local copies, waits for them, and re-layouts  7.43 us (5%)
  between operations  1.96 us (1%)
    ppermute x26, waiting for transfers between devices, swap(): lax.ppermute(x, ('batch', 'edge'), [(i, i ^ mask) for i in range(devices)])  26.5 us
    ppermute x26, starting transfers between devices, swap(): lax.ppermute(x, ('batch', 'edge'), [(i, i ^ mask) for i in range(devices)])  22.6 us
    pallas_call x1, Pallas kernels, fast_path(): pl.pallas_call(functools.partial(front_kernel, shape, chunks), name='mess...  13.9 us
    pallas_call x1, Pallas kernels, edge_work(): pl.pallas_call(functools.partial(back_kernel, shape, back_masks), name='e...  13.1 us
    pallas_call x1, Pallas kernels, fast_path(): pl.pallas_call(split_kernel, name='split_weight', grid=(H // 16,), in_spe...  7.53 us
    all_to_all x1, starting transfers between devices, fast_path(): given = lax.all_to_all(slots_out, 'edge', 0, 0)  7.28 us
    pallas_call x1, Pallas kernels, fast_path(): matrix_gradients(d_agg, t_units, b2)  6.35 us
    pallas_call x1, Pallas kernels, early_half(): pl.pallas_call(functools.partial(early_kernel, chunks), name='assemble_ea...  5.28 us
  transfers between devices with their start and end apart: 27, of which 14 were waited for; matrix products, arithmetic and copies ran while one was open for 7% of the time, Pallas kernels for 28%

profile of v3, /device:TPU:0, one launch (start us, length us, event | category | flops | bytes accessed | tf_op | source)
XLA Modules:
  0.0 135.1 jit_solution(5319758328079409073)
XLA Ops:
  0.6 3.4 %edges_to_slots.1 = (bf16[8,208,128]{2,1,0:T(8,128)(2,1)}, s32[1,2048]{1,0:T(1,128)}) custom-call(s32[1]{0:T(128)} %bitcast.7.me_ref, s32[1,2048]{1,0:T(1,128)} %target_ref.1, s32[1,2048]{1,0:T(1,128)} %source_ref.1, s32[1,2048]{1,0:T(1,128)} %mask_ref.1, s32[1,128]{1,0:T(1,128)} %refs_3_.2, bf16[16,2048]{1,0:T(8,128)(2,1)} %bitcast.9.feats_ref, ...), custom_call_target="tpu_custom_call" | custom-call | tf_op jit(solution)/shard_map/edges_to_slots/pallas_call | solution.py:751
  4.0 7.3 %all-to-all-start.5 = ((bf16[8,208,128]{2,1,0:T(8,128)(2,1)}), bf16[8,208,128]{2,1,0:T(8,128)(2,1)S(1)}, u32[]{:S(2)}, u32[]{:S(2)}) async-start(bf16[8,208,128]{2,1,0:T(8,128)(2,1)} %get-tuple-element.294), calls=%async_computation.5 | async-start | bytes 851968 | tf_op jit(solution)/shard_map/all_to_all | solution.py:763
  11.3 1.2 reshape.491.refs_10_
  12.6 1.2 reshape.493.refs_11_
  13.8 7.5 %split_weight.1.refs_4_.t_ref = bf16[128,128,128]{2,1,0:T(8,128)(2,1)} custom-call(bf16[128,16384]{1,0:T(8,128)(2,1)} %w_ref.1), custom_call_target="tpu_custom_call" | custom-call | flops 120000000 | bytes 360000 | tf_op jit(solution)/shard_map/split_weight/pallas_call | solution.py:765
  21.3 2.4 %all-to-all-done.5.refs_1_ = bf16[8,208,128]{2,1,0:T(8,128)(2,1)S(1)} async-done(((bf16[8,208,128]{2,1,0:T(8,128)(2,1)}), bf16[8,208,128]{2,1,0:T(8,128)(2,1)S(1)}, u32[]{:S(2)}, u32[]{:S(2)}) %all-to-all-start.5) | async-done | bytes 426016 | tf_op jit(solution)/shard_map/all_to_all | solution.py:763
  23.7 0.8 copy-done.23
  24.5 13.9 %messages_update_weight_gradient.1 = (bf16[128,128]{1,0:T(8,128)(2,1)}, f32[128,128]{1,0:T(8,128)}, bf16[128,128]{1,0:T(8,128)(2,1)}, s32[1]{0:T(128)}, bf16[16,...) custom-call(s32[1]{0:T(128)} %bitcast.6.refs_0_.piece_ref, ...), custom_call_target="tpu_custom_call" | custom-call | tf_op jit(solution)/shard_map/messages_update_weight_gradient/pallas_call | solution.py:780
  38.5 6.3 %matrix_gradients.1 = (bf16[8,128,2048]{2,1,0:T(8,128)(2,1)}, f32[128,128]{1,0:T(8,128)}) custom-call(bf16[128,128]{1,0:T(8,128)(2,1)} %get-tuple-element.299.d_ref, bf16[128,128,128]{2,1,0:T(8,128)(2,1)} %split_weight.1.refs_4_.t_ref, bf16[128,128]{1,0:T(8,128)(2,1)} %bitcast.11.refs_5_.b2_ref), custom_call_target="tpu_custom_call" | custom-call | flops 120000000 | bytes 360000 | tf_op jit(solution)/shard_map/matrix_gradients/pallas_call | solution.py:870
  45.2 0.9 fusion.96
  46.1 1.5 %collective-permute-start.26 = (bf16[2,2,2,288,128]{4,3,2,1,0:T(8,128)(2,1)S(1)}, bf16[2,2,2,288,128]{4,3,2,1,0:T(8,128)(2,1)S(1)}, u32[]{:S(2)}, u32[]{:S(2)}) collective-permute-start(bf16[2,2,2,288,128]{4,3,2,1,0:T(8,128)(2,1)S(1)} %fusion.95), channel_id=1, source_target_pairs={{0,1},{1,0},{2,3},{3,2},{4,5},{5,4},{6,7},{7,6},{8,9},{9,8},{10,11... | collective-permute-start | bytes 1769480 | tf_op jit(solution)/shard_map/ppermute | solution.py:547
  47.6 1.5 %collective-permute-start.27 = (bf16[2,2,2,256,128]{4,3,2,1,0:T(8,128)(2,1)}, bf16[2,2,2,256,128]{4,3,2,1,0:T(8,128)(2,1)S(1)}, u32[]{:S(2)}, u32[]{:S(2)}) collective-permute-start(bf16[2,2,2,256,128]{4,3,2,1,0:T(8,128)(2,1)} %fusion.96), channel_id=1, source_target_pairs={{0,16},{1,17},{2,18},{3,19},{4,20},{5,21},{6,22},{7,23},{8,24},{9,... | collective-permute-start | bytes 1572872 | tf_op jit(solution)/shard_map/ppermute | solution.py:547
  49.1 13.1 %edge_gradients.1 = (bf16[4,128,128]{2,1,0:T(8,128)(2,1)}, bf16[4,64,128]{2,1,0:T(8,128)(2,1)}, bf16[768,128]{1,0:T(8,128)(2,1)}, bf16[32,128]{1,0:T(8,128)(2,1)}) custom-call(s32[1]{0:T(128)} %bitcast.7.me_ref, s32[1]{0:T(128)} %get-tuple-element.309.refs_0_, bf16[8,128,2048]{2,1,0:T(8,128)(2,1)} %get-tuple-element.310.refs_1_, ...), custom_call_target="tpu_custom_call" | custom-call | flops 280000000 | bytes 840000 | tf_op jit(solution)/shard_map/edge_gradients/pallas_call | solution.py:841
  62.4 1.1 fusion.98
  63.6 0.8 collective-permute-start.34
  64.4 0.7 reduce-precision_convert_fusion.4
  65.1 1.5 %collective-permute-start.32 = (bf16[32,128]{1,0:T(8,128)(2,1)S(1)}, bf16[32,128]{1,0:T(8,128)(2,1)S(1)}, u32[]{:S(2)}, u32[]{:S(2)}) collective-permute-start(bf16[32,128]{1,0:T(8,128)(2,1)S(1)} %reduce-precision_convert_fusion.4), channel_id=1, source_target_pairs={{0,16},{1,17},{2,18},{3,19},{4,20},{5,21},{6,22},{7,23},{8,24},{9,... | collective-permute-start | bytes 24584 | tf_op jit(solution)/shard_map/ppermute | solution.py:547
  66.6 1.1 fusion.97
  68.7 3.6 %collective-permute-done.34 = bf16[2,2,256,128]{3,2,1,0:T(8,128)(2,1)S(1)} collective-permute-done((bf16[2,2,256,128]{3,2,1,0:T(8,128)(2,1)S(1)}, bf16[2,2,256,128]{3,2,1,0:T(8,128)(2,1)S(1)}, u32[]{:S(2)}, u32[]{:S(2)}) %collective-permute-start.34) | collective-permute-done | bytes 262176 | tf_op jit(solution)/shard_map/ppermute | solution.py:547
  72.3 1.0 fusion.100
  73.6 3.0 %collective-permute-done.28 = bf16[2,2,288,128]{3,2,1,0:T(8,128)(2,1)S(1)} collective-permute-done((bf16[2,2,288,128]{3,2,1,0:T(8,128)(2,1)S(1)}, bf16[2,2,288,128]{3,2,1,0:T(8,128)(2,1)S(1)}, u32[]{:S(2)}, u32[]{:S(2)}) %collective-permute-start.28) | collective-permute-done | bytes 294944 | tf_op jit(solution)/shard_map/ppermute | solution.py:547
  76.7 1.6 %collective-permute-done.35 = bf16[2,256,128]{2,1,0:T(8,128)(2,1)S(1)} collective-permute-done((bf16[2,256,128]{2,1,0:T(8,128)(2,1)S(1)}, bf16[2,256,128]{2,1,0:T(8,128)(2,1)S(1)}, u32[]{:S(2)}, u32[]{:S(2)}) %collective-permute-start.35) | collective-permute-done | bytes 131104 | tf_op jit(solution)/shard_map/ppermute | solution.py:547
  78.4 0.6 collective-permute-start.36
  79.1 1.2 collective-permute-start.33
  80.3 3.9 %collective-permute-done.36 = bf16[256,128]{1,0:T(8,128)(2,1)S(1)} collective-permute-done((bf16[256,128]{1,0:T(8,128)(2,1)S(1)}, bf16[256,128]{1,0:T(8,128)(2,1)S(1)}, u32[]{:S(2)}, u32[]{:S(2)}) %collective-permute-start.36) | collective-permute-done | bytes 65568 | tf_op jit(solution)/shard_map/ppermute | solution.py:547
  84.5 2.8 %collective-permute-start.30 = (bf16[288,128]{1,0:T(8,128)(2,1)S(1)}, bf16[288,128]{1,0:T(8,128)(2,1)S(1)}, u32[]{:S(2)}, u32[]{:S(2)}) collective-permute-start(bf16[288,128]{1,0:T(8,128)(2,1)S(1)} %fusion.102), channel_id=1, source_target_pairs={{0,4},{1,5},{2,6},{3,7},{4,0},{5,1},{6,2},{7,3},{8,12},{9,13},{10,... | collective-permute-start | bytes 221192 | tf_op jit(solution)/shard_map/ppermute | solution.py:547
  87.4 2.4 %collective-permute-done.37 = bf16[256,128]{1,0:T(8,128)(2,1)S(1)} collective-permute-done((bf16[256,128]{1,0:T(8,128)(2,1)S(1)}, bf16[256,128]{1,0:T(8,128)(2,1)S(1)}, u32[]{:S(2)}, u32[]{:S(2)}) %collective-permute-start.37) | collective-permute-done | bytes 65568 | tf_op jit(solution)/shard_map/ppermute | solution.py:547
  90.7 2.2 %collective-permute-start.43 = (bf16[288,128]{1,0:T(8,128)(2,1)S(1)}, bf16[288,128]{1,0:T(8,128)(2,1)S(1)}, u32[]{:S(2)}, u32[]{:S(2)}) collective-permute-start(bf16[288,128]{1,0:T(8,128)(2,1)S(1)} %fusion.104), channel_id=1, source_target_pairs={{0,4},{1,5},{2,6},{3,7},{4,0},{5,1},{6,2},{7,3},{8,12},{9,13},{10,... | collective-permute-start | bytes 221192 | tf_op jit(solution)/shard_map/ppermute | solution.py:547
  93.2 3.0 %collective-permute-done.43 = bf16[288,128]{1,0:T(8,128)(2,1)S(1)} collective-permute-done((bf16[288,128]{1,0:T(8,128)(2,1)S(1)}, bf16[288,128]{1,0:T(8,128)(2,1)S(1)}, u32[]{:S(2)}, u32[]{:S(2)}) %collective-permute-start.43) | collective-permute-done | bytes 73760 | tf_op jit(solution)/shard_map/ppermute | solution.py:547
  96.2 2.3 %collective-permute-start.44 = (bf16[2,288,128]{2,1,0:T(8,128)(2,1)S(1)}, bf16[2,288,128]{2,1,0:T(8,128)(2,1)S(1)}, u32[]{:S(2)}, u32[]{:S(2)}) collective-permute-start(bf16[2,288,128]{2,1,0:T(8,128)(2,1)S(1)} %get-tuple-element.653), channel_id=1, source_target_pairs={{0,2},{1,3},{2,0},{3,1},{4,6},{5,7},{6,4},{7,5},{8,10},{9,11},{10,... | collective-permute-start | bytes 442376 | tf_op jit(solution)/shard_map/ppermute | solution.py:547
  98.5 1.1 collective-permute-start.40
  99.8 1.7 %collective-permute-done.44 = bf16[2,288,128]{2,1,0:T(8,128)(2,1)S(1)} collective-permute-done((bf16[2,288,128]{2,1,0:T(8,128)(2,1)S(1)}, bf16[2,288,128]{2,1,0:T(8,128)(2,1)S(1)}, u32[]{:S(2)}, u32[]{:S(2)}) %collective-permute-start.44) | collective-permute-done | bytes 147488 | tf_op jit(solution)/shard_map/ppermute | solution.py:547
  101.6 1.4 %collective-permute-start.45 = (bf16[2,2,288,128]{3,2,1,0:T(8,128)(2,1)S(1)}, bf16[2,2,288,128]{3,2,1,0:T(8,128)(2,1)S(1)}, u32[]{:S(2)}, u32[]{:S(2)}) collective-permute-start(bf16[2,2,288,128]{3,2,1,0:T(8,128)(2,1)S(1)} %get-tuple-element.649), channel_id=1, source_target_pairs={{0,16},{1,17},{2,18},{3,19},{4,20},{5,21},{6,22},{7,23},{8,24},{9,... | collective-permute-start | bytes 884744 | tf_op jit(solution)/shard_map/ppermute | solution.py:547
  103.1 1.9 %collective-permute-done.40 = bf16[2,2,256,128]{3,2,1,0:T(8,128)(2,1)S(1)} collective-permute-done((bf16[2,2,256,128]{3,2,1,0:T(8,128)(2,1)S(1)}, bf16[2,2,256,128]{3,2,1,0:T(8,128)(2,1)S(1)}, u32[]{:S(2)}, u32[]{:S(2)}) %collective-permute-start.40) | collective-permute-done | bytes 262176 | tf_op jit(solution)/shard_map/ppermute | solution.py:547
  105.0 0.7 collective-permute-start.41
  105.7 3.0 %collective-permute-done.45 = bf16[2,2,288,128]{3,2,1,0:T(8,128)(2,1)S(1)} collective-permute-done((bf16[2,2,288,128]{3,2,1,0:T(8,128)(2,1)S(1)}, bf16[2,2,288,128]{3,2,1,0:T(8,128)(2,1)S(1)}, u32[]{:S(2)}, u32[]{:S(2)}) %collective-permute-start.45) | collective-permute-done | bytes 294944 | tf_op jit(solution)/shard_map/ppermute | solution.py:547
  108.9 1.1 collective-permute-start.46
  111.1 1.7 %collective-permute-start.42 = (bf16[2,2,2,256,128]{4,3,2,1,0:T(8,128)(2,1)S(1)}, bf16[2,2,2,256,128]{4,3,2,1,0:T(8,128)(2,1)S(1)}, u32[]{:S(2)}, u32[]{:S(2)}) collective-permute-start(bf16[2,2,2,256,128]{4,3,2,1,0:T(8,128)(2,1)S(1)} %pad_maximum_fusion.8), channel_id=1, source_target_pairs={{0,16},{1,17},{2,18},{3,19},{4,20},{5,21},{6,22},{7,23},{8,24},{9,... | collective-permute-start | bytes 1572872 | tf_op jit(solution)/shard_map/ppermute | solution.py:547
  112.9 0.7 maximum_bitcast_fusion.slabs_ref
  114.2 2.3 %slots_to_edges.1 = (f32[128,128]{1,0:T(8,128)}, f32[16,2048]{1,0:T(8,128)}) custom-call(s32[1]{0:T(128)} %bitcast.7.me_ref, s32[1,2048]{1,0:T(1,128)} %get-tuple-element.326.slot_ref, f32[128,128]{1,0:T(8,128)} %get-tuple-element.327.direct_ref, bf16[128,128]{1,0:T(8,128)(2,1)} %fusion.112.part_ref, bf16[8,64,128]{2,1,0:T(8,128)(2,1)} %maximum_bitcast_fusion.slabs_ref), custom_call_target="tpu_custom_call" | custom-call | flops 60000000 | bytes 180000 | tf_op jit(solution)/shard_map/slots_to_edges/pallas_call | solution.py:953
  117.1 0.8 copy-done.28
  117.9 0.8 copy-done.26
  118.7 5.3 %assemble_early.2 = (f32[128,16384]{1,0:T(8,128)}, f32[7,128,128]{2,1,0:T(8,128)}, f32[32,128]{1,0:T(8,128)}) custom-call(s32[1]{0:T(128)} %bitcast.6.refs_0_.piece_ref, bf16[8,256,128]{2,1,0:T(8,128)(2,1)} %bitcast.499, bf16[8,288,128]{2,1,0:T(8,128)(2,1)} %bitcast.491, bf16[8,256,128]{2,1,0:T(8,128)(2,1)} %copy-done.28, bf16[8,288,128]{2,1,0:T(8,128)(2,1)} %copy-done.26), custom_call_target="tpu_custom_call" | custom-call | flops 120000000 | bytes 360000 | tf_op jit(solution)/shard_map/assemble_early/pallas_call | solution.py:703
  124.0 1.2 collective-permute-done.42
  125.2 0.8 copy-done.31
  126.5 3.2 %assemble_late.1.refs_6_ = f32[128,16384]{1,0:T(8,128)} custom-call(s32[1]{0:T(128)} %bitcast.6.refs_0_.piece_ref, bf16[8,256,128]{2,1,0:T(8,128)(2,1)} %bitcast.510, bf16[8,288,128]{2,1,0:T(8,128)(2,1)} %bitcast.83.refs_1_.refs_2_, f32[128,16384]{1,0:T(8,128)} %get-tuple-element.351.refs_2_), custom_call_target="tpu_custom_call", output_to_operand_aliasing={{}: (3, {})} | custom-call | flops 80000000 | bytes 240000 | tf_op jit(solution)/shard_map/assemble_late/pallas_call | solution.py:982
  129.7 0.8 copy-done.30
  130.7 4.2 %assemble_last.1 = (f32[128,16384]{1,0:T(8,128)}, f32[16,128]{1,0:T(8,128)}, f32[128]{0:T(128)}, f32[128,384]{1,0:T(8,128)}, f32[128,384]{1,0:T(8,128)}, /*index...) custom-call(s32[1]{0:T(128)} %bitcast.6.refs_0_.piece_ref, ...), custom_call_target="tpu_custom_call", output_to_operand_aliasing={{0}: (7, {})} | custom-call | tf_op jit(solution)/shard_map/assemble_last/pallas_call | solution.py:994
  (97 shorter events, 6.5 us)
Async XLA Ops:
  4.0 19.7 %all-to-all-start.5 = ((bf16[8,208,128]{2,1,0:T(8,128)(2,1)}), bf16[8,208,128]{2,1,0:T(8,128)(2,1)S(1)}, u32[]{:S(2)}, u32[]{:S(2)}) async-start(bf16[8,208,128]{2,1,0:T(8,128)(2,1)} %get-tuple-element.294), calls=%async_computation.5 | async-start | bytes 851968 | tf_op jit(solution)/shard_map/all_to_all | solution.py:763
  23.7 0.8 copy-start.23
  38.4 6.5 %copy-start.27 = (bf16[8,288,128]{2,1,0:T(8,128)(2,1)S(1)}, bf16[8,288,128]{2,1,0:T(8,128)(2,1)}, u32[]{:S(2)}) copy-start(bf16[8,288,128]{2,1,0:T(8,128)(2,1)} %get-tuple-element.304) | copy-start | bytes 1769476
  38.5 6.7 %copy-start.29 = (bf16[8,256,128]{2,1,0:T(8,128)(2,1)S(1)}, bf16[8,256,128]{2,1,0:T(8,128)(2,1)}, u32[]{:S(2)}) copy-start(bf16[8,256,128]{2,1,0:T(8,128)(2,1)} %get-tuple-element.303) | copy-start | bytes 1572868
  38.5 6.4 %collective-permute-start.25 = (bf16[16,544,128]{2,1,0:T(8,128)(2,1)}, bf16[16,544,128]{2,1,0:T(8,128)(2,1)S(1)}, u32[]{:S(2)}, u32[]{:S(2)}) collective-permute-start(bf16[16,544,128]{2,1,0:T(8,128)(2,1)} %get-tuple-element.298), channel_id=1, source_target_pairs={{0,8},{1,9},{2,10},{3,11},{4,12},{5,13},{6,14},{7,15},{8,0},{9,1},... | collective-permute-start | bytes 6684680 | tf_op jit(solution)/shard_map/ppermute | solution.py:547
  46.1 16.3 %collective-permute-start.26 = (bf16[2,2,2,288,128]{4,3,2,1,0:T(8,128)(2,1)S(1)}, bf16[2,2,2,288,128]{4,3,2,1,0:T(8,128)(2,1)S(1)}, u32[]{:S(2)}, u32[]{:S(2)}) collective-permute-start(bf16[2,2,2,288,128]{4,3,2,1,0:T(8,128)(2,1)S(1)} %fusion.95), channel_id=1, source_target_pairs={{0,1},{1,0},{2,3},{3,2},{4,5},{5,4},{6,7},{7,6},{8,9},{9,8},{10,11... | collective-permute-start | bytes 1769480 | tf_op jit(solution)/shard_map/ppermute | solution.py:547
  47.6 14.8 %collective-permute-start.27 = (bf16[2,2,2,256,128]{4,3,2,1,0:T(8,128)(2,1)}, bf16[2,2,2,256,128]{4,3,2,1,0:T(8,128)(2,1)S(1)}, u32[]{:S(2)}, u32[]{:S(2)}) collective-permute-start(bf16[2,2,2,256,128]{4,3,2,1,0:T(8,128)(2,1)} %fusion.96), channel_id=1, source_target_pairs={{0,16},{1,17},{2,18},{3,19},{4,20},{5,21},{6,22},{7,23},{8,24},{9,... | collective-permute-start | bytes 1572872 | tf_op jit(solution)/shard_map/ppermute | solution.py:547
  62.2 14.4 %copy-start.34 = (bf16[4,288,128]{2,1,0:T(8,128)(2,1)S(1)}, bf16[4,288,128]{2,1,0:T(8,128)(2,1)}, u32[]{:S(2)}) copy-start(bf16[4,288,128]{2,1,0:T(8,128)(2,1)} %get-tuple-element.295) | copy-start | bytes 884740
  62.2 16.1 %copy-start.36 = (bf16[4,256,128]{2,1,0:T(8,128)(2,1)S(1)}, bf16[4,256,128]{2,1,0:T(8,128)(2,1)}, u32[]{:S(2)}) copy-start(bf16[4,256,128]{2,1,0:T(8,128)(2,1)} %get-tuple-element.333) | copy-start | bytes 786436
  62.2 16.8 %copy-start.37 = (bf16[768,128]{1,0:T(8,128)(2,1)S(1)}, bf16[768,128]{1,0:T(8,128)(2,1)}, u32[]{:S(2)}) copy-start(bf16[768,128]{1,0:T(8,128)(2,1)} %get-tuple-element.330) | copy-start | bytes 589828
  62.2 27.7 %copy-start.38 = (bf16[4,128,128]{2,1,0:T(8,128)(2,1)S(1)}, bf16[4,128,128]{2,1,0:T(8,128)(2,1)}, u32[]{:S(2)}) copy-start(bf16[4,128,128]{2,1,0:T(8,128)(2,1)} %get-tuple-element.328) | copy-start | bytes 393220
  62.3 27.8 %copy-start.35 = (bf16[4,64,128]{2,1,0:T(8,128)(2,1)S(1)}, bf16[4,64,128]{2,1,0:T(8,128)(2,1)}, u32[]{:S(2)}) copy-start(bf16[4,64,128]{2,1,0:T(8,128)(2,1)} %get-tuple-element.332) | copy-start | bytes 196612
  62.4 2.0 %collective-permute-start.31 = (bf16[32,128]{1,0:T(8,128)(2,1)}, bf16[32,128]{1,0:T(8,128)(2,1)S(1)}, u32[]{:S(2)}, u32[]{:S(2)}) collective-permute-start(bf16[32,128]{1,0:T(8,128)(2,1)} %get-tuple-element.331), channel_id=1, source_target_pairs={{0,8},{1,9},{2,10},{3,11},{4,12},{5,13},{6,14},{7,15},{8,0},{9,1},... | collective-permute-start | bytes 24584 | tf_op jit(solution)/shard_map/ppermute | solution.py:547
  63.6 8.7 %collective-permute-start.34 = (bf16[2,2,256,128]{3,2,1,0:T(8,128)(2,1)S(1)}, bf16[2,2,256,128]{3,2,1,0:T(8,128)(2,1)S(1)}, u32[]{:S(2)}, u32[]{:S(2)}) collective-permute-start(bf16[2,2,256,128]{3,2,1,0:T(8,128)(2,1)S(1)} %fusion.98), channel_id=1, source_target_pairs={{0,1},{1,0},{2,3},{3,2},{4,5},{5,4},{6,7},{7,6},{8,9},{9,8},{10,11... | collective-permute-start | bytes 786440 | tf_op jit(solution)/shard_map/ppermute | solution.py:547
  65.1 3.7 %collective-permute-start.32 = (bf16[32,128]{1,0:T(8,128)(2,1)S(1)}, bf16[32,128]{1,0:T(8,128)(2,1)S(1)}, u32[]{:S(2)}, u32[]{:S(2)}) collective-permute-start(bf16[32,128]{1,0:T(8,128)(2,1)S(1)} %reduce-precision_convert_fusion.4), channel_id=1, source_target_pairs={{0,16},{1,17},{2,18},{3,19},{4,20},{5,21},{6,22},{7,23},{8,24},{9,... | collective-permute-start | bytes 24584 | tf_op jit(solution)/shard_map/ppermute | solution.py:547
  67.6 8.9 %collective-permute-start.28 = (bf16[2,2,288,128]{3,2,1,0:T(8,128)(2,1)S(1)}, bf16[2,2,288,128]{3,2,1,0:T(8,128)(2,1)S(1)}, u32[]{:S(2)}, u32[]{:S(2)}) collective-permute-start(bf16[2,2,288,128]{3,2,1,0:T(8,128)(2,1)S(1)} %fusion.97), channel_id=1, source_target_pairs={{0,16},{1,17},{2,18},{3,19},{4,20},{5,21},{6,22},{7,23},{8,24},{9,... | collective-permute-start | bytes 884744 | tf_op jit(solution)/shard_map/ppermute | solution.py:547
  73.3 5.1 %collective-permute-start.35 = (bf16[2,256,128]{2,1,0:T(8,128)(2,1)S(1)}, bf16[2,256,128]{2,1,0:T(8,128)(2,1)S(1)}, u32[]{:S(2)}, u32[]{:S(2)}) collective-permute-start(bf16[2,256,128]{2,1,0:T(8,128)(2,1)S(1)} %fusion.100), channel_id=1, source_target_pairs={{0,2},{1,3},{2,0},{3,1},{4,6},{5,7},{6,4},{7,5},{8,10},{9,11},{10,... | collective-permute-start | bytes 393224 | tf_op jit(solution)/shard_map/ppermute | solution.py:547
  76.7 7.8 %collective-permute-start.29 = (bf16[2,288,128]{2,1,0:T(8,128)(2,1)S(1)}, bf16[2,288,128]{2,1,0:T(8,128)(2,1)S(1)}, u32[]{:S(2)}, u32[]{:S(2)}) collective-permute-start(bf16[2,288,128]{2,1,0:T(8,128)(2,1)S(1)} %fusion.99), channel_id=1, source_target_pairs={{0,2},{1,3},{2,0},{3,1},{4,6},{5,7},{6,4},{7,5},{8,10},{9,11},{10,... | collective-permute-start | bytes 442376 | tf_op jit(solution)/shard_map/ppermute | solution.py:547
  78.4 5.7 %collective-permute-start.36 = (bf16[256,128]{1,0:T(8,128)(2,1)S(1)}, bf16[256,128]{1,0:T(8,128)(2,1)S(1)}, u32[]{:S(2)}, u32[]{:S(2)}) collective-permute-start(bf16[256,128]{1,0:T(8,128)(2,1)S(1)} %fusion.107), channel_id=1, source_target_pairs={{0,4},{1,5},{2,6},{3,7},{4,0},{5,1},{6,2},{7,3},{8,12},{9,13},{10,... | collective-permute-start | bytes 196616 | tf_op jit(solution)/shard_map/ppermute | solution.py:547
  79.1 10.8 %collective-permute-start.33 = (bf16[800,128]{1,0:T(8,128)(2,1)S(1)}, bf16[800,128]{1,0:T(8,128)(2,1)S(1)}, u32[]{:S(2)}, u32[]{:S(2)}) collective-permute-start(bf16[800,128]{1,0:T(8,128)(2,1)S(1)} %pad_maximum_fusion.11), channel_id=1, source_target_pairs={{0,1},{1,0},{2,3},{3,2},{4,5},{5,4},{6,7},{7,6},{8,9},{9,8},{10,11... | collective-permute-start | bytes 614408 | tf_op jit(solution)/shard_map/ppermute | solution.py:547
  84.2 5.6 %collective-permute-start.37 = (bf16[256,128]{1,0:T(8,128)(2,1)S(1)}, bf16[256,128]{1,0:T(8,128)(2,1)S(1)}, u32[]{:S(2)}, u32[]{:S(2)}) collective-permute-start(bf16[256,128]{1,0:T(8,128)(2,1)S(1)} %fusion.109), channel_id=1, source_target_pairs={{0,4},{1,5},{2,6},{3,7},{4,0},{5,1},{6,2},{7,3},{8,12},{9,13},{10,... | collective-permute-start | bytes 196616 | tf_op jit(solution)/shard_map/ppermute | solution.py:547
  84.5 6.1 %collective-permute-start.30 = (bf16[288,128]{1,0:T(8,128)(2,1)S(1)}, bf16[288,128]{1,0:T(8,128)(2,1)S(1)}, u32[]{:S(2)}, u32[]{:S(2)}) collective-permute-start(bf16[288,128]{1,0:T(8,128)(2,1)S(1)} %fusion.102), channel_id=1, source_target_pairs={{0,4},{1,5},{2,6},{3,7},{4,0},{5,1},{6,2},{7,3},{8,12},{9,13},{10,... | collective-permute-start | bytes 221192 | tf_op jit(solution)/shard_map/ppermute | solution.py:547
  89.8 8.6 %collective-permute-start.39 = (bf16[2,256,128]{2,1,0:T(8,128)(2,1)S(1)}, bf16[2,256,128]{2,1,0:T(8,128)(2,1)S(1)}, u32[]{:S(2)}, u32[]{:S(2)}) collective-permute-start(bf16[2,256,128]{2,1,0:T(8,128)(2,1)S(1)} %get-tuple-element.659), channel_id=1, source_target_pairs={{0,2},{1,3},{2,0},{3,1},{4,6},{5,7},{6,4},{7,5},{8,10},{9,11},{10,... | collective-permute-start | bytes 393224 | tf_op jit(solution)/shard_map/ppermute | solution.py:547
  90.7 5.4 %collective-permute-start.43 = (bf16[288,128]{1,0:T(8,128)(2,1)S(1)}, bf16[288,128]{1,0:T(8,128)(2,1)S(1)}, u32[]{:S(2)}, u32[]{:S(2)}) collective-permute-start(bf16[288,128]{1,0:T(8,128)(2,1)S(1)} %fusion.104), channel_id=1, source_target_pairs={{0,4},{1,5},{2,6},{3,7},{4,0},{5,1},{6,2},{7,3},{8,12},{9,13},{10,... | collective-permute-start | bytes 221192 | tf_op jit(solution)/shard_map/ppermute | solution.py:547
  92.9 6.8 %collective-permute-start.38 = (bf16[544,128]{1,0:T(8,128)(2,1)S(1)}, bf16[544,128]{1,0:T(8,128)(2,1)S(1)}, u32[]{:S(2)}, u32[]{:S(2)}) collective-permute-start(bf16[544,128]{1,0:T(8,128)(2,1)S(1)} %pad_maximum_fusion.13), channel_id=1, source_target_pairs={{0,2},{1,3},{2,0},{3,1},{4,6},{5,7},{6,4},{7,5},{8,10},{9,11},{10,... | collective-permute-start | bytes 417800 | tf_op jit(solution)/shard_map/ppermute | solution.py:547
  96.2 5.4 %collective-permute-start.44 = (bf16[2,288,128]{2,1,0:T(8,128)(2,1)S(1)}, bf16[2,288,128]{2,1,0:T(8,128)(2,1)S(1)}, u32[]{:S(2)}, u32[]{:S(2)}) collective-permute-start(bf16[2,288,128]{2,1,0:T(8,128)(2,1)S(1)} %get-tuple-element.653), channel_id=1, source_target_pairs={{0,2},{1,3},{2,0},{3,1},{4,6},{5,7},{6,4},{7,5},{8,10},{9,11},{10,... | collective-permute-start | bytes 442376 | tf_op jit(solution)/shard_map/ppermute | solution.py:547
  98.5 6.4 %collective-permute-start.40 = (bf16[2,2,256,128]{3,2,1,0:T(8,128)(2,1)S(1)}, bf16[2,2,256,128]{3,2,1,0:T(8,128)(2,1)S(1)}, u32[]{:S(2)}, u32[]{:S(2)}) collective-permute-start(bf16[2,2,256,128]{3,2,1,0:T(8,128)(2,1)S(1)} %get-tuple-element.651), channel_id=1, source_target_pairs={{0,1},{1,0},{2,3},{3,2},{4,5},{5,4},{6,7},{7,6},{8,9},{9,8},{10,11... | collective-permute-start | bytes 786440 | tf_op jit(solution)/shard_map/ppermute | solution.py:547
  101.6 7.1 %collective-permute-start.45 = (bf16[2,2,288,128]{3,2,1,0:T(8,128)(2,1)S(1)}, bf16[2,2,288,128]{3,2,1,0:T(8,128)(2,1)S(1)}, u32[]{:S(2)}, u32[]{:S(2)}) collective-permute-start(bf16[2,2,288,128]{3,2,1,0:T(8,128)(2,1)S(1)} %get-tuple-element.649), channel_id=1, source_target_pairs={{0,16},{1,17},{2,18},{3,19},{4,20},{5,21},{6,22},{7,23},{8,24},{9,... | collective-permute-start | bytes 884744 | tf_op jit(solution)/shard_map/ppermute | solution.py:547
  105.0 12.1 %copy-start.22 = (bf16[2,2,2,256,128]{4,3,2,1,0:T(8,128)(2,1)}, bf16[2,2,2,256,128]{4,3,2,1,0:T(8,128)(2,1)S(1)}, u32[]{:S(2)}) copy-start(bf16[2,2,2,256,128]{4,3,2,1,0:T(8,128)(2,1)S(1)} %pad_maximum_fusion.8) | copy-start | bytes 1572868
  105.0 7.9 %collective-permute-start.41 = (bf16[416,128]{1,0:T(8,128)(2,1)S(1)}, bf16[416,128]{1,0:T(8,128)(2,1)S(1)}, u32[]{:S(2)}, u32[]{:S(2)}) collective-permute-start(bf16[416,128]{1,0:T(8,128)(2,1)S(1)} %pad_maximum_fusion.17), channel_id=1, source_target_pairs={{0,4},{1,5},{2,6},{3,7},{4,0},{5,1},{6,2},{7,3},{8,12},{9,13},{10,... | collective-permute-start | bytes 319496 | tf_op jit(solution)/shard_map/ppermute | solution.py:547
  108.8 8.3 %copy-start.21 = (bf16[2,2,2,288,128]{4,3,2,1,0:T(8,128)(2,1)}, bf16[2,2,2,288,128]{4,3,2,1,0:T(8,128)(2,1)S(1)}, u32[]{:S(2)}) copy-start(bf16[2,2,2,288,128]{4,3,2,1,0:T(8,128)(2,1)S(1)} %pad_maximum_fusion.7) | copy-start | bytes 1769476
  108.8 8.3 %collective-permute-start.48 = (bf16[8,288,128]{2,1,0:T(8,128)(2,1)S(1)}, bf16[8,288,128]{2,1,0:T(8,128)(2,1)S(1)}, u32[]{:S(2)}, u32[]{:S(2)}) collective-permute-start(bf16[8,288,128]{2,1,0:T(8,128)(2,1)S(1)} %bitcast.490), channel_id=1, source_target_pairs={{0,8},{1,9},{2,10},{3,11},{4,12},{5,13},{6,14},{7,15},{8,0},{9,1},... | collective-permute-start | bytes 1769480 | tf_op jit(solution)/shard_map/ppermute | solution.py:547
  108.9 16.3 %collective-permute-start.46 = (bf16[2,2,2,288,128]{4,3,2,1,0:T(8,128)(2,1)S(1)}, bf16[2,2,2,288,128]{4,3,2,1,0:T(8,128)(2,1)}, u32[]{:S(2)}, u32[]{:S(2)}) collective-permute-start(bf16[2,2,2,288,128]{4,3,2,1,0:T(8,128)(2,1)S(1)} %pad_maximum_fusion.7), channel_id=1, source_target_pairs={{0,1},{1,0},{2,3},{3,2},{4,5},{5,4},{6,7},{7,6},{8,9},{9,8},{10,11... | collective-permute-start | bytes 1769480 | tf_op jit(solution)/shard_map/ppermute | solution.py:547
  111.1 14.1 %collective-permute-start.42 = (bf16[2,2,2,256,128]{4,3,2,1,0:T(8,128)(2,1)S(1)}, bf16[2,2,2,256,128]{4,3,2,1,0:T(8,128)(2,1)S(1)}, u32[]{:S(2)}, u32[]{:S(2)}) collective-permute-start(bf16[2,2,2,256,128]{4,3,2,1,0:T(8,128)(2,1)S(1)} %pad_maximum_fusion.8), channel_id=1, source_target_pairs={{0,16},{1,17},{2,18},{3,19},{4,20},{5,21},{6,22},{7,23},{8,24},{9,... | collective-permute-start | bytes 1572872 | tf_op jit(solution)/shard_map/ppermute | solution.py:547
  112.8 4.3 %collective-permute-start.47 = (bf16[8,256,128]{2,1,0:T(8,128)(2,1)S(1)}, bf16[8,256,128]{2,1,0:T(8,128)(2,1)S(1)}, u32[]{:S(2)}, u32[]{:S(2)}) collective-permute-start(bf16[8,256,128]{2,1,0:T(8,128)(2,1)S(1)} %bitcast.498), channel_id=1, source_target_pairs={{0,8},{1,9},{2,10},{3,11},{4,12},{5,13},{6,14},{7,15},{8,0},{9,1},... | collective-permute-start | bytes 1572872 | tf_op jit(solution)/shard_map/ppermute | solution.py:547
  117.1 0.8 copy-start.28
  117.9 0.8 copy-start.26
  125.2 0.8 copy-start.31
  126.0 3.7 %collective-permute-start.50 = (bf16[8,288,128]{2,1,0:T(8,128)(2,1)}, bf16[8,288,128]{2,1,0:T(8,128)(2,1)S(1)}, u32[]{:S(2)}, u32[]{:S(2)}) collective-permute-start(bf16[8,288,128]{2,1,0:T(8,128)(2,1)} %bitcast.83.refs_1_.refs_2_), channel_id=1, source_target_pairs={{0,8},{1,9},{2,10},{3,11},{4,12},{5,13},{6,14},{7,15},{8,0},{9,1},... | collective-permute-start | bytes 1769480 | tf_op jit(solution)/shard_map/ppermute | solution.py:547
  126.0 3.7 %collective-permute-start.49 = (bf16[8,256,128]{2,1,0:T(8,128)(2,1)}, bf16[8,256,128]{2,1,0:T(8,128)(2,1)S(1)}, u32[]{:S(2)}, u32[]{:S(2)}) collective-permute-start(bf16[8,256,128]{2,1,0:T(8,128)(2,1)} %bitcast.509), channel_id=1, source_target_pairs={{0,8},{1,9},{2,10},{3,11},{4,12},{5,13},{6,14},{7,15},{8,0},{9,1},... | collective-permute-start | bytes 1572872 | tf_op jit(solution)/shard_map/ppermute | solution.py:547
  126.5 4.2 %copy-start.33 = (f32[7,128,128]{2,1,0:T(8,128)S(1)}, f32[7,128,128]{2,1,0:T(8,128)}, u32[]{:S(2)}) copy-start(f32[7,128,128]{2,1,0:T(8,128)} %get-tuple-element.349.refs_4_) | copy-start | bytes 1376260
  126.5 4.2 %copy-start.43 = (bf16[32,128]{1,0:T(8,128)(2,1)S(1)}, bf16[32,128]{1,0:T(8,128)(2,1)}, u32[]{:S(2)}) copy-start(bf16[32,128]{1,0:T(8,128)(2,1)} %get-tuple-element.348.refs_3_) | copy-start | bytes 24580
  126.5 4.2 %copy-start.44 = (f32[32,128]{1,0:T(8,128)S(1)}, f32[32,128]{1,0:T(8,128)}, u32[]{:S(2)}) copy-start(f32[32,128]{1,0:T(8,128)} %get-tuple-element.350.refs_5_) | copy-start | bytes 49156
  129.7 0.8 copy-start.30
  129.7 1.0 copy-start.25

commit v4 on v3

--- a/solution.py
+++ b/solution.py
@@ -23,13 +23,13 @@
 )
 VMEM_LIMIT = 60 * 1024 * 1024
 UNROLL = 4
-BACK_UNROLL = 2
+BACK_UNROLL = 4
 AGG = 32
 TIED = (0, 1)
 GIVE = 2
 LAST_GIVE = 0
 COST = 0.02
-KSTEP = 32
+KSTEP = 64
 MATRIX_FIRST = True
 
 
@@ -74,12 +74,13 @@
     cols = lax.broadcasted_iota(jnp.int32, (block, block), 1)
     upto = jnp.where(rows <= cols, 1.0, 0.0).astype(BF16)
     numbers = lax.broadcasted_iota(jnp.int32, (buckets, block), 0)
+    hots = [numbers == bucket[:, b * block : (b + 1) * block] for b in range(edges // block)]
+    counts = nn(jnp.concatenate([hot.astype(F32).astype(BF16) for hot in hots], axis=0), upto)
     carry = jnp.zeros((buckets, 1), F32)
     slots = []
-    for b in range(edges // block):
+    for b, hot in enumerate(hots):
         here = bucket[:, b * block : (b + 1) * block]
-        hot = numbers == here
-        within = nn(hot.astype(F32).astype(BF16), upto) + carry
+        within = counts[b * buckets : (b + 1) * buckets, :] + carry
         rank = jnp.sum(jnp.where(hot, within - 1.0, 0.0), axis=0, keepdims=True).astype(jnp.int32)
         carry = within[:, block - 1 : block]
         at = jnp.where(jnp.bitwise_and(here, 1) == 0, rank, CAP - 1 - rank)
@@ -325,9 +326,9 @@
     from_input = nn(twice(mixed_t), jnp.concatenate([gi_high, gi_low], axis=0))
     from_state = nn(twice(prior_t), jnp.concatenate([gh_high, gh_low], axis=0))
     for t in range(3):
-        rows_ref[t] = from_input[:, t * H : (t + 1) * H]
-        rows_ref[3 + t] = from_state[:, t * H : (t + 1) * H]
-    rows_ref[6] = nn(dt_ref[...], sum_ref[...].astype(BF16))
+        rows_ref[t, 0:H, :] = from_input[:, t * H : (t + 1) * H]
+        rows_ref[3 + t, 0:H, :] = from_state[:, t * H : (t + 1) * H]
+    rows_ref[6, 0:H, :] = nn(dt_ref[...], sum_ref[...].astype(BF16))
     bias_ref[...] = jnp.zeros_like(bias_ref)
     for n, part in enumerate((d_gi, d_gh)):
         part = jnp.sum(part, axis=0, keepdims=True)
@@ -664,23 +665,23 @@
     def beside():
         small.start()
         w1_ref[...] = first_ref[0:16, :].astype(F32)
-        b1_ref[...] = first_ref[16:17, :].astype(F32).reshape(H)
+        b1_ref[...] = first_ref[16:32, :].astype(F32)[0:1, :].reshape(H)
         extra_ref[...] = extra_in[...]
         bias_ref[...] = bias_in[...]
-        small.wait()
-        for c, core, rel, place in jobs_of(chunks, 1, (0,)):
-            if c == count - 1:
-                for i in range(4):
-                    small_piece(me, rel + i, small_ref[place + i], extra_ref, bias_ref)
 
     end = unpack(chunks, jobs, me, order_ref, sources, block_refs, w_out, rows_ref, sems, beside)
     small_pieces(chunks, jobs, me, block_refs, extra_ref, bias_ref)
+    small.wait()
+    for c, core, rel, place in jobs_of(chunks, 1, (0,)):
+        if c == count - 1:
+            for i in range(4):
+                small_piece(me, rel + i, small_ref[place + i], extra_ref, bias_ref)
     for t in range(3):
-        wi_ref[:, t * H : (t + 1) * H] = extra_ref[t]
-        wh_ref[:, t * H : (t + 1) * H] = extra_ref[3 + t]
+        wi_ref[:, t * H : (t + 1) * H] = extra_ref[t, 0:H, :]
+        wh_ref[:, t * H : (t + 1) * H] = extra_ref[3 + t, 0:H, :]
         bi_ref[t * H : (t + 1) * H] = bias_ref[t : t + 1, :].reshape(H)
         bh_ref[t * H : (t + 1) * H] = bias_ref[3 + t : 4 + t, :].reshape(H)
-    b2_ref[...] = extra_ref[6]
+    b2_ref[...] = extra_ref[6, 0:H, :]
     end()
 
 
@@ -694,7 +695,7 @@
 
 
 W_SHAPE = jax.ShapeDtypeStruct((H, H * H), F32)
-SMALL = [jax.ShapeDtypeStruct((7, H, H), F32), jax.ShapeDtypeStruct((PIECES, H), F32)]
+SMALL = [jax.ShapeDtypeStruct((7, H + 8, H), F32), jax.ShapeDtypeStruct((PIECES + 8, H), F32)]
 
 
 def early_half(chunks, bits, devices, piece_arr, parts):
@@ -798,8 +799,8 @@
             pltpu.VMEM((own, H), F32),
             pltpu.VMEM((own, H), F32),
             pltpu.VMEM((H, own), BF16),
-            pltpu.VMEM((7, H, H), F32),
-            pltpu.VMEM((PIECES, H), F32),
+            pltpu.VMEM((7, H + 8, H), F32),
+            pltpu.VMEM((PIECES + 8, H), F32),
             pltpu.VMEM((EXTRA, H), F32),
             pltpu.VMEM((H, H, H), BF16),
             pltpu.VMEM((pages, H, lanes), BF16),
@@ -942,6 +943,8 @@
         parts = [rounded(x.astype(F32) + swap(x, mask, devices).astype(F32)) for x in parts]
     overflow = parts[-1][UNITS * chunks[-1].rows + 29, 0] > 0.0
     for step in (3, 2, 1):
+        if step == 2:
+            parts[1], overflow = lax.optimization_barrier((parts[1], overflow))
         if step == GIVE:
             for mask in back_masks[1:-1]:
                 give_back(mask, parts[0] if mask == 2 else None)

time: 136 us -> 134 us (0.985)
  waiting for transfers between devices: 28.9 us -> 25.7 us
  starting transfers between devices: 29.9 us -> 32.6 us
    ppermute x26, waiting for transfers between devices: 26.5 us -> 23.4 us  [swap(): lax.ppermute(x, ('batch', 'edge'), [(i, i ^ mask) for i in range(devices)])]
    ppermute x26, starting transfers between devices: 22.6 us -> 25.3 us  [swap(): lax.ppermute(x, ('batch', 'edge'), [(i, i ^ mask) for i in range(devices)])]
where the time goes in v4:
time: 134 us; the launch traced here: 133 us
  Pallas kernels  58.1 us (43%)
  starting transfers between devices  32.6 us (24%)
  waiting for transfers between devices  25.7 us (19%)
  other arithmetic  7.57 us (6%)
  local copies, waits for them, and re-layouts  7.34 us (5%)
  between operations  1.97 us (1%)
    ppermute x26, starting transfers between devices, swap(): lax.ppermute(x, ('batch', 'edge'), [(i, i ^ mask) for i in range(devices)])  25.3 us
    ppermute x26, waiting for transfers between devices, swap(): lax.ppermute(x, ('batch', 'edge'), [(i, i ^ mask) for i in range(devices)])  23.4 us
    pallas_call x1, Pallas kernels, fast_path(): pl.pallas_call(functools.partial(front_kernel, shape, chunks), name='mess...  13.9 us
    pallas_call x1, Pallas kernels, edge_work(): pl.pallas_call(functools.partial(back_kernel, shape, back_masks), name='e...  12.9 us
    pallas_call x1, Pallas kernels, fast_path(): pl.pallas_call(split_kernel, name='split_weight', grid=(H // 16,), in_spe...  7.54 us
    all_to_all x1, starting transfers between devices, fast_path(): given = lax.all_to_all(slots_out, 'edge', 0, 0)  7.27 us
    pallas_call x1, Pallas kernels, fast_path(): matrix_gradients(d_agg, t_units, b2)  5.7 us
    pallas_call x1, Pallas kernels, early_half(): pl.pallas_call(functools.partial(early_kernel, chunks), name='assemble_ea...  5.28 us
  transfers between devices with their start and end apart: 27, of which 14 were waited for; matrix products, arithmetic and copies ran while one was open for 7% of the time, Pallas kernels for 28%

profile of v4, /device:TPU:0, one launch (start us, length us, event | category | flops | bytes accessed | tf_op | source)
XLA Modules:
  0.0 133.3 jit_solution(13903243962951580830)
XLA Ops:
  0.6 3.4 %edges_to_slots.1 = (bf16[8,208,128]{2,1,0:T(8,128)(2,1)}, s32[1,2048]{1,0:T(1,128)}) custom-call(s32[1]{0:T(128)} %bitcast.7.me_ref, s32[1,2048]{1,0:T(1,128)} %target_ref.1, s32[1,2048]{1,0:T(1,128)} %source_ref.1, s32[1,2048]{1,0:T(1,128)} %mask_ref.1, s32[1,128]{1,0:T(1,128)} %refs_3_.2, bf16[16,2048]{1,0:T(8,128)(2,1)} %bitcast.9.feats_ref, ...), custom_call_target="tpu_custom_call" | custom-call | tf_op jit(solution)/shard_map/edges_to_slots/pallas_call | solution.py:752
  4.0 7.3 %all-to-all-start.5 = ((bf16[8,208,128]{2,1,0:T(8,128)(2,1)}), bf16[8,208,128]{2,1,0:T(8,128)(2,1)S(1)}, u32[]{:S(2)}, u32[]{:S(2)}) async-start(bf16[8,208,128]{2,1,0:T(8,128)(2,1)} %get-tuple-element.296), calls=%async_computation.5 | async-start | bytes 851968 | tf_op jit(solution)/shard_map/all_to_all | solution.py:764
  11.3 1.2 reshape.491.refs_10_
  12.6 1.2 reshape.493.refs_11_
  13.8 7.5 %split_weight.1.refs_4_.t_ref = bf16[128,128,128]{2,1,0:T(8,128)(2,1)} custom-call(bf16[128,16384]{1,0:T(8,128)(2,1)} %w_ref.1), custom_call_target="tpu_custom_call" | custom-call | flops 120000000 | bytes 360000 | tf_op jit(solution)/shard_map/split_weight/pallas_call | solution.py:766
  21.3 2.4 %all-to-all-done.5.refs_1_ = bf16[8,208,128]{2,1,0:T(8,128)(2,1)S(1)} async-done(((bf16[8,208,128]{2,1,0:T(8,128)(2,1)}), bf16[8,208,128]{2,1,0:T(8,128)(2,1)S(1)}, u32[]{:S(2)}, u32[]{:S(2)}) %all-to-all-start.5) | async-done | bytes 426016 | tf_op jit(solution)/shard_map/all_to_all | solution.py:764
  23.7 0.8 copy-done.23
  24.5 13.9 %messages_update_weight_gradient.1 = (bf16[128,128]{1,0:T(8,128)(2,1)}, f32[128,128]{1,0:T(8,128)}, bf16[128,128]{1,0:T(8,128)(2,1)}, s32[1]{0:T(128)}, bf16[16,...) custom-call(s32[1]{0:T(128)} %bitcast.6.refs_0_.piece_ref, ...), custom_call_target="tpu_custom_call" | custom-call | tf_op jit(solution)/shard_map/messages_update_weight_gradient/pallas_call | solution.py:781
  38.5 5.7 %matrix_gradients.1 = (bf16[8,128,2048]{2,1,0:T(8,128)(2,1)}, f32[128,128]{1,0:T(8,128)}) custom-call(bf16[128,128]{1,0:T(8,128)(2,1)} %get-tuple-element.301.d_ref, bf16[128,128,128]{2,1,0:T(8,128)(2,1)} %split_weight.1.refs_4_.t_ref, bf16[128,128]{1,0:T(8,128)(2,1)} %bitcast.11.refs_5_.b2_ref), custom_call_target="tpu_custom_call" | custom-call | flops 120000000 | bytes 360000 | tf_op jit(solution)/shard_map/matrix_gradients/pallas_call | solution.py:871
  44.5 0.9 fusion.96
  45.4 1.5 %collective-permute-start.26 = (bf16[2,2,2,288,128]{4,3,2,1,0:T(8,128)(2,1)S(1)}, bf16[2,2,2,288,128]{4,3,2,1,0:T(8,128)(2,1)S(1)}, u32[]{:S(2)}, u32[]{:S(2)}) collective-permute-start(bf16[2,2,2,288,128]{4,3,2,1,0:T(8,128)(2,1)S(1)} %fusion.95), channel_id=1, source_target_pairs={{0,1},{1,0},{2,3},{3,2},{4,5},{5,4},{6,7},{7,6},{8,9},{9,8},{10,11... | collective-permute-start | bytes 1769480 | tf_op jit(solution)/shard_map/ppermute | solution.py:548
  46.9 1.5 %collective-permute-start.27 = (bf16[2,2,2,256,128]{4,3,2,1,0:T(8,128)(2,1)}, bf16[2,2,2,256,128]{4,3,2,1,0:T(8,128)(2,1)S(1)}, u32[]{:S(2)}, u32[]{:S(2)}) collective-permute-start(bf16[2,2,2,256,128]{4,3,2,1,0:T(8,128)(2,1)} %fusion.96), channel_id=1, source_target_pairs={{0,16},{1,17},{2,18},{3,19},{4,20},{5,21},{6,22},{7,23},{8,24},{9,... | collective-permute-start | bytes 1572872 | tf_op jit(solution)/shard_map/ppermute | solution.py:548
  48.4 12.9 %edge_gradients.1 = (bf16[4,128,128]{2,1,0:T(8,128)(2,1)}, bf16[4,64,128]{2,1,0:T(8,128)(2,1)}, bf16[768,128]{1,0:T(8,128)(2,1)}, bf16[32,128]{1,0:T(8,128)(2,1)}) custom-call(s32[1]{0:T(128)} %bitcast.7.me_ref, s32[1]{0:T(128)} %get-tuple-element.311.refs_0_, bf16[8,128,2048]{2,1,0:T(8,128)(2,1)} %get-tuple-element.312.refs_1_, ...), custom_call_target="tpu_custom_call" | custom-call | flops 280000000 | bytes 840000 | tf_op jit(solution)/shard_map/edge_gradients/pallas_call | solution.py:842
  61.5 1.1 fusion.98
  62.6 1.1 collective-permute-start.35
  63.7 0.7 reduce-precision_convert_fusion.4
  64.4 1.5 %collective-permute-start.33 = (bf16[32,128]{1,0:T(8,128)(2,1)S(1)}, bf16[32,128]{1,0:T(8,128)(2,1)S(1)}, u32[]{:S(2)}, u32[]{:S(2)}) collective-permute-start(bf16[32,128]{1,0:T(8,128)(2,1)S(1)} %reduce-precision_convert_fusion.4), channel_id=1, source_target_pairs={{0,16},{1,17},{2,18},{3,19},{4,20},{5,21},{6,22},{7,23},{8,24},{9,... | collective-permute-start | bytes 24584 | tf_op jit(solution)/shard_map/ppermute | solution.py:548
  65.9 1.1 fusion.97
  68.1 3.3 %collective-permute-done.35 = bf16[2,2,256,128]{3,2,1,0:T(8,128)(2,1)S(1)} collective-permute-done((bf16[2,2,256,128]{3,2,1,0:T(8,128)(2,1)S(1)}, bf16[2,2,256,128]{3,2,1,0:T(8,128)(2,1)S(1)}, u32[]{:S(2)}, u32[]{:S(2)}) %collective-permute-start.35) | collective-permute-done | bytes 262176 | tf_op jit(solution)/shard_map/ppermute | solution.py:548
  71.3 1.0 fusion.100
  72.9 3.0 %collective-permute-done.28 = bf16[2,2,288,128]{3,2,1,0:T(8,128)(2,1)S(1)} collective-permute-done((bf16[2,2,288,128]{3,2,1,0:T(8,128)(2,1)S(1)}, bf16[2,2,288,128]{3,2,1,0:T(8,128)(2,1)S(1)}, u32[]{:S(2)}, u32[]{:S(2)}) %collective-permute-start.28) | collective-permute-done | bytes 294944 | tf_op jit(solution)/shard_map/ppermute | solution.py:548
  76.1 1.3 %collective-permute-done.36 = bf16[2,256,128]{2,1,0:T(8,128)(2,1)S(1)} collective-permute-done((bf16[2,256,128]{2,1,0:T(8,128)(2,1)S(1)}, bf16[2,256,128]{2,1,0:T(8,128)(2,1)S(1)}, u32[]{:S(2)}, u32[]{:S(2)}) %collective-permute-start.36) | collective-permute-done | bytes 131104 | tf_op jit(solution)/shard_map/ppermute | solution.py:548
  77.5 0.7 collective-permute-start.37
  78.2 1.3 %collective-permute-start.34 = (bf16[800,128]{1,0:T(8,128)(2,1)S(1)}, bf16[800,128]{1,0:T(8,128)(2,1)S(1)}, u32[]{:S(2)}, u32[]{:S(2)}) collective-permute-start(bf16[800,128]{1,0:T(8,128)(2,1)S(1)} %pad_maximum_fusion.11), channel_id=1, source_target_pairs={{0,1},{1,0},{2,3},{3,2},{4,5},{5,4},{6,7},{7,6},{8,9},{9,8},{10,11... | collective-permute-start | bytes 614408 | tf_op jit(solution)/shard_map/ppermute | solution.py:548
  79.6 3.8 %collective-permute-done.37 = bf16[256,128]{1,0:T(8,128)(2,1)S(1)} collective-permute-done((bf16[256,128]{1,0:T(8,128)(2,1)S(1)}, bf16[256,128]{1,0:T(8,128)(2,1)S(1)}, u32[]{:S(2)}, u32[]{:S(2)}) %collective-permute-start.37) | collective-permute-done | bytes 65568 | tf_op jit(solution)/shard_map/ppermute | solution.py:548
  83.8 2.8 %collective-permute-start.30 = (bf16[288,128]{1,0:T(8,128)(2,1)S(1)}, bf16[288,128]{1,0:T(8,128)(2,1)S(1)}, u32[]{:S(2)}, u32[]{:S(2)}) collective-permute-start(bf16[288,128]{1,0:T(8,128)(2,1)S(1)} %fusion.102), channel_id=1, source_target_pairs={{0,4},{1,5},{2,6},{3,7},{4,0},{5,1},{6,2},{7,3},{8,12},{9,13},{10,... | collective-permute-start | bytes 221192 | tf_op jit(solution)/shard_map/ppermute | solution.py:548
  86.6 2.4 %collective-permute-done.38 = bf16[256,128]{1,0:T(8,128)(2,1)S(1)} collective-permute-done((bf16[256,128]{1,0:T(8,128)(2,1)S(1)}, bf16[256,128]{1,0:T(8,128)(2,1)S(1)}, u32[]{:S(2)}, u32[]{:S(2)}) %collective-permute-start.38) | collective-permute-done | bytes 65568 | tf_op jit(solution)/shard_map/ppermute | solution.py:548
  89.9 2.4 %collective-permute-start.31 = (bf16[288,128]{1,0:T(8,128)(2,1)S(1)}, bf16[288,128]{1,0:T(8,128)(2,1)S(1)}, u32[]{:S(2)}, u32[]{:S(2)}) collective-permute-start(bf16[288,128]{1,0:T(8,128)(2,1)S(1)} %fusion.104), channel_id=1, source_target_pairs={{0,4},{1,5},{2,6},{3,7},{4,0},{5,1},{6,2},{7,3},{8,12},{9,13},{10,... | collective-permute-start | bytes 221192 | tf_op jit(solution)/shard_map/ppermute | solution.py:548
  93.6 1.7 %collective-permute-done.31 = bf16[288,128]{1,0:T(8,128)(2,1)S(1)} collective-permute-done((bf16[288,128]{1,0:T(8,128)(2,1)S(1)}, bf16[288,128]{1,0:T(8,128)(2,1)S(1)}, u32[]{:S(2)}, u32[]{:S(2)}) %collective-permute-start.31) | collective-permute-done | bytes 73760 | tf_op jit(solution)/shard_map/ppermute | solution.py:548
  95.3 2.2 %collective-permute-start.44 = (bf16[2,288,128]{2,1,0:T(8,128)(2,1)S(1)}, bf16[2,288,128]{2,1,0:T(8,128)(2,1)S(1)}, u32[]{:S(2)}, u32[]{:S(2)}) collective-permute-start(bf16[2,288,128]{2,1,0:T(8,128)(2,1)S(1)} %pad_maximum_fusion.12), channel_id=1, source_target_pairs={{0,2},{1,3},{2,0},{3,1},{4,6},{5,7},{6,4},{7,5},{8,10},{9,11},{10,... | collective-permute-start | bytes 442376 | tf_op jit(solution)/shard_map/ppermute | solution.py:548
  97.6 1.3 collective-permute-start.41
  99.0 1.7 %collective-permute-done.44 = bf16[2,288,128]{2,1,0:T(8,128)(2,1)S(1)} collective-permute-done((bf16[2,288,128]{2,1,0:T(8,128)(2,1)S(1)}, bf16[2,288,128]{2,1,0:T(8,128)(2,1)S(1)}, u32[]{:S(2)}, u32[]{:S(2)}) %collective-permute-start.44) | collective-permute-done | bytes 147488 | tf_op jit(solution)/shard_map/ppermute | solution.py:548
  100.7 2.0 %collective-permute-start.45 = (bf16[2,2,288,128]{3,2,1,0:T(8,128)(2,1)S(1)}, bf16[2,2,288,128]{3,2,1,0:T(8,128)(2,1)S(1)}, u32[]{:S(2)}, u32[]{:S(2)}) collective-permute-start(bf16[2,2,288,128]{3,2,1,0:T(8,128)(2,1)S(1)} %get-tuple-element.653), channel_id=1, source_target_pairs={{0,16},{1,17},{2,18},{3,19},{4,20},{5,21},{6,22},{7,23},{8,24},{9,... | collective-permute-start | bytes 884744 | tf_op jit(solution)/shard_map/ppermute | solution.py:548
  102.7 1.3 collective-permute-done.41
  104.1 1.1 collective-permute-start.42
  105.2 2.6 %collective-permute-done.45 = bf16[2,2,288,128]{3,2,1,0:T(8,128)(2,1)S(1)} collective-permute-done((bf16[2,2,288,128]{3,2,1,0:T(8,128)(2,1)S(1)}, bf16[2,2,288,128]{3,2,1,0:T(8,128)(2,1)S(1)}, u32[]{:S(2)}, u32[]{:S(2)}) %collective-permute-start.45) | collective-permute-done | bytes 294944 | tf_op jit(solution)/shard_map/ppermute | solution.py:548
  107.9 1.5 %collective-permute-start.46 = (bf16[2,2,2,288,128]{4,3,2,1,0:T(8,128)(2,1)S(1)}, bf16[2,2,2,288,128]{4,3,2,1,0:T(8,128)(2,1)}, u32[]{:S(2)}, u32[]{:S(2)}) collective-permute-start(bf16[2,2,2,288,128]{4,3,2,1,0:T(8,128)(2,1)S(1)} %pad_maximum_fusion.7), channel_id=1, source_target_pairs={{0,1},{1,0},{2,3},{3,2},{4,5},{5,4},{6,7},{7,6},{8,9},{9,8},{10,11... | collective-permute-start | bytes 1769480 | tf_op jit(solution)/shard_map/ppermute | solution.py:548
  109.4 2.0 %collective-permute-start.43 = (bf16[2,2,2,256,128]{4,3,2,1,0:T(8,128)(2,1)S(1)}, bf16[2,2,2,256,128]{4,3,2,1,0:T(8,128)(2,1)S(1)}, u32[]{:S(2)}, u32[]{:S(2)}) collective-permute-start(bf16[2,2,2,256,128]{4,3,2,1,0:T(8,128)(2,1)S(1)} %pad_maximum_fusion.8), channel_id=1, source_target_pairs={{0,16},{1,17},{2,18},{3,19},{4,20},{5,21},{6,22},{7,23},{8,24},{9,... | collective-permute-start | bytes 1572872 | tf_op jit(solution)/shard_map/ppermute | solution.py:548
  111.4 0.7 maximum_bitcast_fusion.slabs_ref
  112.7 2.3 %slots_to_edges.1 = (f32[128,128]{1,0:T(8,128)}, f32[16,2048]{1,0:T(8,128)}) custom-call(s32[1]{0:T(128)} %bitcast.7.me_ref, s32[1,2048]{1,0:T(1,128)} %get-tuple-element.329.slot_ref, f32[128,128]{1,0:T(8,128)} %get-tuple-element.330.direct_ref, bf16[128,128]{1,0:T(8,128)(2,1)} %fusion.112.part_ref, bf16[8,64,128]{2,1,0:T(8,128)(2,1)} %maximum_bitcast_fusion.slabs_ref), custom_call_target="tpu_custom_call" | custom-call | flops 60000000 | bytes 180000 | tf_op jit(solution)/shard_map/slots_to_edges/pallas_call | solution.py:956
  115.7 0.8 copy-done.28
  116.4 0.8 copy-done.26
  117.3 5.3 %assemble_early.2 = (f32[128,16384]{1,0:T(8,128)}, f32[7,136,128]{2,1,0:T(8,128)}, f32[40,128]{1,0:T(8,128)}) custom-call(s32[1]{0:T(128)} %bitcast.6.refs_0_.piece_ref, bf16[8,256,128]{2,1,0:T(8,128)(2,1)} %bitcast.498, bf16[8,288,128]{2,1,0:T(8,128)(2,1)} %bitcast.490, bf16[8,256,128]{2,1,0:T(8,128)(2,1)} %copy-done.28, bf16[8,288,128]{2,1,0:T(8,128)(2,1)} %copy-done.26), custom_call_target="tpu_custom_call" | custom-call | flops 120000000 | bytes 360000 | tf_op jit(solution)/shard_map/assemble_early/pallas_call | solution.py:704
  122.5 1.1 collective-permute-done.43
  123.7 0.7 copy-done.31
  125.0 3.2 %assemble_late.1.refs_6_ = f32[128,16384]{1,0:T(8,128)} custom-call(s32[1]{0:T(128)} %bitcast.6.refs_0_.piece_ref, bf16[8,256,128]{2,1,0:T(8,128)(2,1)} %bitcast.510, bf16[8,288,128]{2,1,0:T(8,128)(2,1)} %bitcast.83.refs_1_.refs_2_, f32[128,16384]{1,0:T(8,128)} %get-tuple-element.355.refs_2_), custom_call_target="tpu_custom_call", output_to_operand_aliasing={{}: (3, {})} | custom-call | flops 80000000 | bytes 240000 | tf_op jit(solution)/shard_map/assemble_late/pallas_call | solution.py:985
  128.2 0.8 copy-done.30
  129.2 3.9 %assemble_last.1 = (f32[128,16384]{1,0:T(8,128)}, f32[16,128]{1,0:T(8,128)}, f32[128]{0:T(128)}, f32[128,384]{1,0:T(8,128)}, f32[128,384]{1,0:T(8,128)}, /*index...) custom-call(s32[1]{0:T(128)} %bitcast.6.refs_0_.piece_ref, ...), custom_call_target="tpu_custom_call", output_to_operand_aliasing={{0}: (7, {})} | custom-call | tf_op jit(solution)/shard_map/assemble_last/pallas_call | solution.py:997
  (97 shorter events, 6.6 us)
Async XLA Ops:
  4.0 19.7 %all-to-all-start.5 = ((bf16[8,208,128]{2,1,0:T(8,128)(2,1)}), bf16[8,208,128]{2,1,0:T(8,128)(2,1)S(1)}, u32[]{:S(2)}, u32[]{:S(2)}) async-start(bf16[8,208,128]{2,1,0:T(8,128)(2,1)} %get-tuple-element.296), calls=%async_computation.5 | async-start | bytes 851968 | tf_op jit(solution)/shard_map/all_to_all | solution.py:764
  23.7 0.8 copy-start.23
  38.4 5.9 %copy-start.27 = (bf16[8,288,128]{2,1,0:T(8,128)(2,1)S(1)}, bf16[8,288,128]{2,1,0:T(8,128)(2,1)}, u32[]{:S(2)}) copy-start(bf16[8,288,128]{2,1,0:T(8,128)(2,1)} %get-tuple-element.306) | copy-start | bytes 1769476
  38.4 6.1 %copy-start.29 = (bf16[8,256,128]{2,1,0:T(8,128)(2,1)S(1)}, bf16[8,256,128]{2,1,0:T(8,128)(2,1)}, u32[]{:S(2)}) copy-start(bf16[8,256,128]{2,1,0:T(8,128)(2,1)} %get-tuple-element.305) | copy-start | bytes 1572868
  38.4 5.8 %collective-permute-start.25 = (bf16[16,544,128]{2,1,0:T(8,128)(2,1)}, bf16[16,544,128]{2,1,0:T(8,128)(2,1)S(1)}, u32[]{:S(2)}, u32[]{:S(2)}) collective-permute-start(bf16[16,544,128]{2,1,0:T(8,128)(2,1)} %get-tuple-element.300), channel_id=1, source_target_pairs={{0,8},{1,9},{2,10},{3,11},{4,12},{5,13},{6,14},{7,15},{8,0},{9,1},... | collective-permute-start | bytes 6684680 | tf_op jit(solution)/shard_map/ppermute | solution.py:548
  45.4 16.0 %collective-permute-start.26 = (bf16[2,2,2,288,128]{4,3,2,1,0:T(8,128)(2,1)S(1)}, bf16[2,2,2,288,128]{4,3,2,1,0:T(8,128)(2,1)S(1)}, u32[]{:S(2)}, u32[]{:S(2)}) collective-permute-start(bf16[2,2,2,288,128]{4,3,2,1,0:T(8,128)(2,1)S(1)} %fusion.95), channel_id=1, source_target_pairs={{0,1},{1,0},{2,3},{3,2},{4,5},{5,4},{6,7},{7,6},{8,9},{9,8},{10,11... | collective-permute-start | bytes 1769480 | tf_op jit(solution)/shard_map/ppermute | solution.py:548
  46.9 14.5 %collective-permute-start.27 = (bf16[2,2,2,256,128]{4,3,2,1,0:T(8,128)(2,1)}, bf16[2,2,2,256,128]{4,3,2,1,0:T(8,128)(2,1)S(1)}, u32[]{:S(2)}, u32[]{:S(2)}) collective-permute-start(bf16[2,2,2,256,128]{4,3,2,1,0:T(8,128)(2,1)} %fusion.96), channel_id=1, source_target_pairs={{0,16},{1,17},{2,18},{3,19},{4,20},{5,21},{6,22},{7,23},{8,24},{9,... | collective-permute-start | bytes 1572872 | tf_op jit(solution)/shard_map/ppermute | solution.py:548
  61.3 14.6 %copy-start.34 = (bf16[4,288,128]{2,1,0:T(8,128)(2,1)S(1)}, bf16[4,288,128]{2,1,0:T(8,128)(2,1)}, u32[]{:S(2)}) copy-start(bf16[4,288,128]{2,1,0:T(8,128)(2,1)} %get-tuple-element.297) | copy-start | bytes 884740
  61.3 16.1 %copy-start.36 = (bf16[4,256,128]{2,1,0:T(8,128)(2,1)S(1)}, bf16[4,256,128]{2,1,0:T(8,128)(2,1)}, u32[]{:S(2)}) copy-start(bf16[4,256,128]{2,1,0:T(8,128)(2,1)} %get-tuple-element.336) | copy-start | bytes 786436
  61.3 16.9 %copy-start.37 = (bf16[768,128]{1,0:T(8,128)(2,1)S(1)}, bf16[768,128]{1,0:T(8,128)(2,1)}, u32[]{:S(2)}) copy-start(bf16[768,128]{1,0:T(8,128)(2,1)} %get-tuple-element.333) | copy-start | bytes 589828
  61.3 27.8 %copy-start.38 = (bf16[4,128,128]{2,1,0:T(8,128)(2,1)S(1)}, bf16[4,128,128]{2,1,0:T(8,128)(2,1)}, u32[]{:S(2)}) copy-start(bf16[4,128,128]{2,1,0:T(8,128)(2,1)} %get-tuple-element.331) | copy-start | bytes 393220
  61.3 27.9 %copy-start.35 = (bf16[4,64,128]{2,1,0:T(8,128)(2,1)S(1)}, bf16[4,64,128]{2,1,0:T(8,128)(2,1)}, u32[]{:S(2)}) copy-start(bf16[4,64,128]{2,1,0:T(8,128)(2,1)} %get-tuple-element.335) | copy-start | bytes 196612
  61.4 2.3 %collective-permute-start.32 = (bf16[32,128]{1,0:T(8,128)(2,1)}, bf16[32,128]{1,0:T(8,128)(2,1)S(1)}, u32[]{:S(2)}, u32[]{:S(2)}) collective-permute-start(bf16[32,128]{1,0:T(8,128)(2,1)} %get-tuple-element.334), channel_id=1, source_target_pairs={{0,8},{1,9},{2,10},{3,11},{4,12},{5,13},{6,14},{7,15},{8,0},{9,1},... | collective-permute-start | bytes 24584 | tf_op jit(solution)/shard_map/ppermute | solution.py:548
  62.6 8.7 %collective-permute-start.35 = (bf16[2,2,256,128]{3,2,1,0:T(8,128)(2,1)S(1)}, bf16[2,2,256,128]{3,2,1,0:T(8,128)(2,1)S(1)}, u32[]{:S(2)}, u32[]{:S(2)}) collective-permute-start(bf16[2,2,256,128]{3,2,1,0:T(8,128)(2,1)S(1)} %fusion.98), channel_id=1, source_target_pairs={{0,1},{1,0},{2,3},{3,2},{4,5},{5,4},{6,7},{7,6},{8,9},{9,8},{10,11... | collective-permute-start | bytes 786440 | tf_op jit(solution)/shard_map/ppermute | solution.py:548
  64.4 3.7 %collective-permute-start.33 = (bf16[32,128]{1,0:T(8,128)(2,1)S(1)}, bf16[32,128]{1,0:T(8,128)(2,1)S(1)}, u32[]{:S(2)}, u32[]{:S(2)}) collective-permute-start(bf16[32,128]{1,0:T(8,128)(2,1)S(1)} %reduce-precision_convert_fusion.4), channel_id=1, source_target_pairs={{0,16},{1,17},{2,18},{3,19},{4,20},{5,21},{6,22},{7,23},{8,24},{9,... | collective-permute-start | bytes 24584 | tf_op jit(solution)/shard_map/ppermute | solution.py:548
  67.0 8.9 %collective-permute-start.28 = (bf16[2,2,288,128]{3,2,1,0:T(8,128)(2,1)S(1)}, bf16[2,2,288,128]{3,2,1,0:T(8,128)(2,1)S(1)}, u32[]{:S(2)}, u32[]{:S(2)}) collective-permute-start(bf16[2,2,288,128]{3,2,1,0:T(8,128)(2,1)S(1)} %fusion.97), channel_id=1, source_target_pairs={{0,16},{1,17},{2,18},{3,19},{4,20},{5,21},{6,22},{7,23},{8,24},{9,... | collective-permute-start | bytes 884744 | tf_op jit(solution)/shard_map/ppermute | solution.py:548
  72.3 5.1 %collective-permute-start.36 = (bf16[2,256,128]{2,1,0:T(8,128)(2,1)S(1)}, bf16[2,256,128]{2,1,0:T(8,128)(2,1)S(1)}, u32[]{:S(2)}, u32[]{:S(2)}) collective-permute-start(bf16[2,256,128]{2,1,0:T(8,128)(2,1)S(1)} %fusion.100), channel_id=1, source_target_pairs={{0,2},{1,3},{2,0},{3,1},{4,6},{5,7},{6,4},{7,5},{8,10},{9,11},{10,... | collective-permute-start | bytes 393224 | tf_op jit(solution)/shard_map/ppermute | solution.py:548
  76.0 7.7 %collective-permute-start.29 = (bf16[2,288,128]{2,1,0:T(8,128)(2,1)S(1)}, bf16[2,288,128]{2,1,0:T(8,128)(2,1)S(1)}, u32[]{:S(2)}, u32[]{:S(2)}) collective-permute-start(bf16[2,288,128]{2,1,0:T(8,128)(2,1)S(1)} %fusion.99), channel_id=1, source_target_pairs={{0,2},{1,3},{2,0},{3,1},{4,6},{5,7},{6,4},{7,5},{8,10},{9,11},{10,... | collective-permute-start | bytes 442376 | tf_op jit(solution)/shard_map/ppermute | solution.py:548
  77.5 5.9 %collective-permute-start.37 = (bf16[256,128]{1,0:T(8,128)(2,1)S(1)}, bf16[256,128]{1,0:T(8,128)(2,1)S(1)}, u32[]{:S(2)}, u32[]{:S(2)}) collective-permute-start(bf16[256,128]{1,0:T(8,128)(2,1)S(1)} %fusion.107), channel_id=1, source_target_pairs={{0,4},{1,5},{2,6},{3,7},{4,0},{5,1},{6,2},{7,3},{8,12},{9,13},{10,... | collective-permute-start | bytes 196616 | tf_op jit(solution)/shard_map/ppermute | solution.py:548
  78.2 10.9 %collective-permute-start.34 = (bf16[800,128]{1,0:T(8,128)(2,1)S(1)}, bf16[800,128]{1,0:T(8,128)(2,1)S(1)}, u32[]{:S(2)}, u32[]{:S(2)}) collective-permute-start(bf16[800,128]{1,0:T(8,128)(2,1)S(1)} %pad_maximum_fusion.11), channel_id=1, source_target_pairs={{0,1},{1,0},{2,3},{3,2},{4,5},{5,4},{6,7},{7,6},{8,9},{9,8},{10,11... | collective-permute-start | bytes 614408 | tf_op jit(solution)/shard_map/ppermute | solution.py:548
  83.5 5.5 %collective-permute-start.38 = (bf16[256,128]{1,0:T(8,128)(2,1)S(1)}, bf16[256,128]{1,0:T(8,128)(2,1)S(1)}, u32[]{:S(2)}, u32[]{:S(2)}) collective-permute-start(bf16[256,128]{1,0:T(8,128)(2,1)S(1)} %fusion.109), channel_id=1, source_target_pairs={{0,4},{1,5},{2,6},{3,7},{4,0},{5,1},{6,2},{7,3},{8,12},{9,13},{10,... | collective-permute-start | bytes 196616 | tf_op jit(solution)/shard_map/ppermute | solution.py:548
  83.8 6.0 %collective-permute-start.30 = (bf16[288,128]{1,0:T(8,128)(2,1)S(1)}, bf16[288,128]{1,0:T(8,128)(2,1)S(1)}, u32[]{:S(2)}, u32[]{:S(2)}) collective-permute-start(bf16[288,128]{1,0:T(8,128)(2,1)S(1)} %fusion.102), channel_id=1, source_target_pairs={{0,4},{1,5},{2,6},{3,7},{4,0},{5,1},{6,2},{7,3},{8,12},{9,13},{10,... | collective-permute-start | bytes 221192 | tf_op jit(solution)/shard_map/ppermute | solution.py:548
  89.0 8.5 %collective-permute-start.40 = (bf16[2,256,128]{2,1,0:T(8,128)(2,1)S(1)}, bf16[2,256,128]{2,1,0:T(8,128)(2,1)S(1)}, u32[]{:S(2)}, u32[]{:S(2)}) collective-permute-start(bf16[2,256,128]{2,1,0:T(8,128)(2,1)S(1)} %get-tuple-element.661), channel_id=1, source_target_pairs={{0,2},{1,3},{2,0},{3,1},{4,6},{5,7},{6,4},{7,5},{8,10},{9,11},{10,... | collective-permute-start | bytes 393224 | tf_op jit(solution)/shard_map/ppermute | solution.py:548
  89.9 5.4 %collective-permute-start.31 = (bf16[288,128]{1,0:T(8,128)(2,1)S(1)}, bf16[288,128]{1,0:T(8,128)(2,1)S(1)}, u32[]{:S(2)}, u32[]{:S(2)}) collective-permute-start(bf16[288,128]{1,0:T(8,128)(2,1)S(1)} %fusion.104), channel_id=1, source_target_pairs={{0,4},{1,5},{2,6},{3,7},{4,0},{5,1},{6,2},{7,3},{8,12},{9,13},{10,... | collective-permute-start | bytes 221192 | tf_op jit(solution)/shard_map/ppermute | solution.py:548
  92.3 6.5 %collective-permute-start.39 = (bf16[544,128]{1,0:T(8,128)(2,1)S(1)}, bf16[544,128]{1,0:T(8,128)(2,1)S(1)}, u32[]{:S(2)}, u32[]{:S(2)}) collective-permute-start(bf16[544,128]{1,0:T(8,128)(2,1)S(1)} %pad_maximum_fusion.13), channel_id=1, source_target_pairs={{0,2},{1,3},{2,0},{3,1},{4,6},{5,7},{6,4},{7,5},{8,10},{9,11},{10,... | collective-permute-start | bytes 417800 | tf_op jit(solution)/shard_map/ppermute | solution.py:548
  95.3 5.3 %collective-permute-start.44 = (bf16[2,288,128]{2,1,0:T(8,128)(2,1)S(1)}, bf16[2,288,128]{2,1,0:T(8,128)(2,1)S(1)}, u32[]{:S(2)}, u32[]{:S(2)}) collective-permute-start(bf16[2,288,128]{2,1,0:T(8,128)(2,1)S(1)} %pad_maximum_fusion.12), channel_id=1, source_target_pairs={{0,2},{1,3},{2,0},{3,1},{4,6},{5,7},{6,4},{7,5},{8,10},{9,11},{10,... | collective-permute-start | bytes 442376 | tf_op jit(solution)/shard_map/ppermute | solution.py:548
  97.6 6.4 %collective-permute-start.41 = (bf16[2,2,256,128]{3,2,1,0:T(8,128)(2,1)S(1)}, bf16[2,2,256,128]{3,2,1,0:T(8,128)(2,1)S(1)}, u32[]{:S(2)}, u32[]{:S(2)}) collective-permute-start(bf16[2,2,256,128]{3,2,1,0:T(8,128)(2,1)S(1)} %get-tuple-element.655), channel_id=1, source_target_pairs={{0,1},{1,0},{2,3},{3,2},{4,5},{5,4},{6,7},{7,6},{8,9},{9,8},{10,11... | collective-permute-start | bytes 786440 | tf_op jit(solution)/shard_map/ppermute | solution.py:548
  100.7 7.0 %collective-permute-start.45 = (bf16[2,2,288,128]{3,2,1,0:T(8,128)(2,1)S(1)}, bf16[2,2,288,128]{3,2,1,0:T(8,128)(2,1)S(1)}, u32[]{:S(2)}, u32[]{:S(2)}) collective-permute-start(bf16[2,2,288,128]{3,2,1,0:T(8,128)(2,1)S(1)} %get-tuple-element.653), channel_id=1, source_target_pairs={{0,16},{1,17},{2,18},{3,19},{4,20},{5,21},{6,22},{7,23},{8,24},{9,... | collective-permute-start | bytes 884744 | tf_op jit(solution)/shard_map/ppermute | solution.py:548
  104.1 11.6 %copy-start.22 = (bf16[2,2,2,256,128]{4,3,2,1,0:T(8,128)(2,1)}, bf16[2,2,2,256,128]{4,3,2,1,0:T(8,128)(2,1)S(1)}, u32[]{:S(2)}) copy-start(bf16[2,2,2,256,128]{4,3,2,1,0:T(8,128)(2,1)S(1)} %pad_maximum_fusion.8) | copy-start | bytes 1572868
  104.1 7.3 %collective-permute-start.42 = (bf16[416,128]{1,0:T(8,128)(2,1)S(1)}, bf16[416,128]{1,0:T(8,128)(2,1)S(1)}, u32[]{:S(2)}, u32[]{:S(2)}) collective-permute-start(bf16[416,128]{1,0:T(8,128)(2,1)S(1)} %pad_maximum_fusion.17), channel_id=1, source_target_pairs={{0,4},{1,5},{2,6},{3,7},{4,0},{5,1},{6,2},{7,3},{8,12},{9,13},{10,... | collective-permute-start | bytes 319496 | tf_op jit(solution)/shard_map/ppermute | solution.py:548
  107.8 7.9 %copy-start.21 = (bf16[2,2,2,288,128]{4,3,2,1,0:T(8,128)(2,1)}, bf16[2,2,2,288,128]{4,3,2,1,0:T(8,128)(2,1)S(1)}, u32[]{:S(2)}) copy-start(bf16[2,2,2,288,128]{4,3,2,1,0:T(8,128)(2,1)S(1)} %pad_maximum_fusion.7) | copy-start | bytes 1769476
  107.8 7.9 %collective-permute-start.48 = (bf16[8,288,128]{2,1,0:T(8,128)(2,1)S(1)}, bf16[8,288,128]{2,1,0:T(8,128)(2,1)S(1)}, u32[]{:S(2)}, u32[]{:S(2)}) collective-permute-start(bf16[8,288,128]{2,1,0:T(8,128)(2,1)S(1)} %bitcast.489), channel_id=1, source_target_pairs={{0,8},{1,9},{2,10},{3,11},{4,12},{5,13},{6,14},{7,15},{8,0},{9,1},... | collective-permute-start | bytes 1769480 | tf_op jit(solution)/shard_map/ppermute | solution.py:548
  107.9 15.8 %collective-permute-start.46 = (bf16[2,2,2,288,128]{4,3,2,1,0:T(8,128)(2,1)S(1)}, bf16[2,2,2,288,128]{4,3,2,1,0:T(8,128)(2,1)}, u32[]{:S(2)}, u32[]{:S(2)}) collective-permute-start(bf16[2,2,2,288,128]{4,3,2,1,0:T(8,128)(2,1)S(1)} %pad_maximum_fusion.7), channel_id=1, source_target_pairs={{0,1},{1,0},{2,3},{3,2},{4,5},{5,4},{6,7},{7,6},{8,9},{9,8},{10,11... | collective-permute-start | bytes 1769480 | tf_op jit(solution)/shard_map/ppermute | solution.py:548
  109.4 14.3 %collective-permute-start.43 = (bf16[2,2,2,256,128]{4,3,2,1,0:T(8,128)(2,1)S(1)}, bf16[2,2,2,256,128]{4,3,2,1,0:T(8,128)(2,1)S(1)}, u32[]{:S(2)}, u32[]{:S(2)}) collective-permute-start(bf16[2,2,2,256,128]{4,3,2,1,0:T(8,128)(2,1)S(1)} %pad_maximum_fusion.8), channel_id=1, source_target_pairs={{0,16},{1,17},{2,18},{3,19},{4,20},{5,21},{6,22},{7,23},{8,24},{9,... | collective-permute-start | bytes 1572872 | tf_op jit(solution)/shard_map/ppermute | solution.py:548
  111.4 4.3 %collective-permute-start.47 = (bf16[8,256,128]{2,1,0:T(8,128)(2,1)S(1)}, bf16[8,256,128]{2,1,0:T(8,128)(2,1)S(1)}, u32[]{:S(2)}, u32[]{:S(2)}) collective-permute-start(bf16[8,256,128]{2,1,0:T(8,128)(2,1)S(1)} %bitcast.497), channel_id=1, source_target_pairs={{0,8},{1,9},{2,10},{3,11},{4,12},{5,13},{6,14},{7,15},{8,0},{9,1},... | collective-permute-start | bytes 1572872 | tf_op jit(solution)/shard_map/ppermute | solution.py:548
  115.6 0.8 copy-start.28
  116.4 0.8 copy-start.26
  123.6 0.8 copy-start.31
  124.5 3.7 %collective-permute-start.50 = (bf16[8,288,128]{2,1,0:T(8,128)(2,1)}, bf16[8,288,128]{2,1,0:T(8,128)(2,1)S(1)}, u32[]{:S(2)}, u32[]{:S(2)}) collective-permute-start(bf16[8,288,128]{2,1,0:T(8,128)(2,1)} %bitcast.83.refs_1_.refs_2_), channel_id=1, source_target_pairs={{0,8},{1,9},{2,10},{3,11},{4,12},{5,13},{6,14},{7,15},{8,0},{9,1},... | collective-permute-start | bytes 1769480 | tf_op jit(solution)/shard_map/ppermute | solution.py:548
  124.5 3.7 %collective-permute-start.49 = (bf16[8,256,128]{2,1,0:T(8,128)(2,1)}, bf16[8,256,128]{2,1,0:T(8,128)(2,1)S(1)}, u32[]{:S(2)}, u32[]{:S(2)}) collective-permute-start(bf16[8,256,128]{2,1,0:T(8,128)(2,1)} %bitcast.509), channel_id=1, source_target_pairs={{0,8},{1,9},{2,10},{3,11},{4,12},{5,13},{6,14},{7,15},{8,0},{9,1},... | collective-permute-start | bytes 1572872 | tf_op jit(solution)/shard_map/ppermute | solution.py:548
  125.0 4.2 %copy-start.33 = (f32[7,136,128]{2,1,0:T(8,128)S(1)}, f32[7,136,128]{2,1,0:T(8,128)}, u32[]{:S(2)}) copy-start(f32[7,136,128]{2,1,0:T(8,128)} %get-tuple-element.353.refs_4_) | copy-start | bytes 1462276
  125.0 4.2 %copy-start.43 = (bf16[32,128]{1,0:T(8,128)(2,1)S(1)}, bf16[32,128]{1,0:T(8,128)(2,1)}, u32[]{:S(2)}) copy-start(bf16[32,128]{1,0:T(8,128)(2,1)} %get-tuple-element.352.refs_3_) | copy-start | bytes 24580
  125.0 4.2 %copy-start.44 = (f32[40,128]{1,0:T(8,128)S(1)}, f32[40,128]{1,0:T(8,128)}, u32[]{:S(2)}) copy-start(f32[40,128]{1,0:T(8,128)} %get-tuple-element.354.refs_5_) | copy-start | bytes 61444
  128.1 0.8 copy-start.30
  128.2 1.0 copy-start.25

commit v5 on v4

--- a/solution.py
+++ b/solution.py
@@ -24,7 +24,7 @@
 VMEM_LIMIT = 60 * 1024 * 1024
 UNROLL = 4
 BACK_UNROLL = 4
-AGG = 32
+AGG = 64
 TIED = (0, 1)
 GIVE = 2
 LAST_GIVE = 0

time: 134 us -> 134 us (level)
  no operation moved by 1% of the time
where the time goes in v5:
time: 134 us; the launch traced here: 133 us
  Pallas kernels  57.8 us (43%)
  starting transfers between devices  33.5 us (25%)
  waiting for transfers between devices  24.7 us (18%)
  other arithmetic  7.57 us (6%)
  local copies, waits for them, and re-layouts  7.02 us (5%)
  between operations  1.97 us (1%)
    ppermute x26, starting transfers between devices, swap(): lax.ppermute(x, ('batch', 'edge'), [(i, i ^ mask) for i in range(devices)])  26.2 us
    ppermute x26, waiting for transfers between devices, swap(): lax.ppermute(x, ('batch', 'edge'), [(i, i ^ mask) for i in range(devices)])  22.4 us
    pallas_call x1, Pallas kernels, fast_path(): pl.pallas_call(functools.partial(front_kernel, shape, chunks), name='mess...  13.6 us
    pallas_call x1, Pallas kernels, edge_work(): pl.pallas_call(functools.partial(back_kernel, shape, back_masks), name='e...  12.9 us
    pallas_call x1, Pallas kernels, fast_path(): pl.pallas_call(split_kernel, name='split_weight', grid=(H // 16,), in_spe...  7.54 us
    all_to_all x1, starting transfers between devices, fast_path(): given = lax.all_to_all(slots_out, 'edge', 0, 0)  7.27 us
    pallas_call x1, Pallas kernels, fast_path(): matrix_gradients(d_agg, t_units, b2)  5.7 us
    pallas_call x1, Pallas kernels, early_half(): pl.pallas_call(functools.partial(early_kernel, chunks), name='assemble_ea...  5.29 us
  transfers between devices with their start and end apart: 27, of which 14 were waited for; matrix products, arithmetic and copies ran while one was open for 7% of the time, Pallas kernels for 28%

profile of v5, /device:TPU:0, one launch (start us, length us, event | category | flops | bytes accessed | tf_op | source)
XLA Modules:
  0.0 132.6 jit_solution(14549641770190328774)
XLA Ops:
  0.6 3.4 %edges_to_slots.1 = (bf16[8,208,128]{2,1,0:T(8,128)(2,1)}, s32[1,2048]{1,0:T(1,128)}) custom-call(s32[1]{0:T(128)} %bitcast.7.me_ref, s32[1,2048]{1,0:T(1,128)} %target_ref.1, s32[1,2048]{1,0:T(1,128)} %source_ref.1, s32[1,2048]{1,0:T(1,128)} %mask_ref.1, s32[1,128]{1,0:T(1,128)} %refs_3_.2, bf16[16,2048]{1,0:T(8,128)(2,1)} %bitcast.9.feats_ref, ...), custom_call_target="tpu_custom_call" | custom-call | tf_op jit(solution)/shard_map/edges_to_slots/pallas_call | solution.py:752
  4.0 7.3 %all-to-all-start.5 = ((bf16[8,208,128]{2,1,0:T(8,128)(2,1)}), bf16[8,208,128]{2,1,0:T(8,128)(2,1)S(1)}, u32[]{:S(2)}, u32[]{:S(2)}) async-start(bf16[8,208,128]{2,1,0:T(8,128)(2,1)} %get-tuple-element.296), calls=%async_computation.5 | async-start | bytes 851968 | tf_op jit(solution)/shard_map/all_to_all | solution.py:764
  11.3 1.2 reshape.491.refs_10_
  12.6 1.2 reshape.493.refs_11_
  13.8 7.5 %split_weight.1.refs_4_.t_ref = bf16[128,128,128]{2,1,0:T(8,128)(2,1)} custom-call(bf16[128,16384]{1,0:T(8,128)(2,1)} %w_ref.1), custom_call_target="tpu_custom_call" | custom-call | flops 120000000 | bytes 360000 | tf_op jit(solution)/shard_map/split_weight/pallas_call | solution.py:766
  21.3 2.4 %all-to-all-done.5.refs_1_ = bf16[8,208,128]{2,1,0:T(8,128)(2,1)S(1)} async-done(((bf16[8,208,128]{2,1,0:T(8,128)(2,1)}), bf16[8,208,128]{2,1,0:T(8,128)(2,1)S(1)}, u32[]{:S(2)}, u32[]{:S(2)}) %all-to-all-start.5) | async-done | bytes 426016 | tf_op jit(solution)/shard_map/all_to_all | solution.py:764
  23.7 0.8 copy-done.23
  24.5 13.6 %messages_update_weight_gradient.1 = (bf16[128,128]{1,0:T(8,128)(2,1)}, f32[128,128]{1,0:T(8,128)}, bf16[128,128]{1,0:T(8,128)(2,1)}, s32[1]{0:T(128)}, bf16[16,...) custom-call(s32[1]{0:T(128)} %bitcast.6.refs_0_.piece_ref, ...), custom_call_target="tpu_custom_call" | custom-call | tf_op jit(solution)/shard_map/messages_update_weight_gradient/pallas_call | solution.py:781
  38.2 5.7 %matrix_gradients.1 = (bf16[8,128,2048]{2,1,0:T(8,128)(2,1)}, f32[128,128]{1,0:T(8,128)}) custom-call(bf16[128,128]{1,0:T(8,128)(2,1)} %get-tuple-element.301.d_ref, bf16[128,128,128]{2,1,0:T(8,128)(2,1)} %split_weight.1.refs_4_.t_ref, bf16[128,128]{1,0:T(8,128)(2,1)} %bitcast.11.refs_5_.b2_ref), custom_call_target="tpu_custom_call" | custom-call | flops 120000000 | bytes 360000 | tf_op jit(solution)/shard_map/matrix_gradients/pallas_call | solution.py:871
  44.2 0.9 fusion.96
  45.1 1.5 %collective-permute-start.26 = (bf16[2,2,2,288,128]{4,3,2,1,0:T(8,128)(2,1)S(1)}, bf16[2,2,2,288,128]{4,3,2,1,0:T(8,128)(2,1)S(1)}, u32[]{:S(2)}, u32[]{:S(2)}) collective-permute-start(bf16[2,2,2,288,128]{4,3,2,1,0:T(8,128)(2,1)S(1)} %fusion.95), channel_id=1, source_target_pairs={{0,1},{1,0},{2,3},{3,2},{4,5},{5,4},{6,7},{7,6},{8,9},{9,8},{10,11... | collective-permute-start | bytes 1769480 | tf_op jit(solution)/shard_map/ppermute | solution.py:548
  46.6 1.5 %collective-permute-start.27 = (bf16[2,2,2,256,128]{4,3,2,1,0:T(8,128)(2,1)}, bf16[2,2,2,256,128]{4,3,2,1,0:T(8,128)(2,1)S(1)}, u32[]{:S(2)}, u32[]{:S(2)}) collective-permute-start(bf16[2,2,2,256,128]{4,3,2,1,0:T(8,128)(2,1)} %fusion.96), channel_id=1, source_target_pairs={{0,16},{1,17},{2,18},{3,19},{4,20},{5,21},{6,22},{7,23},{8,24},{9,... | collective-permute-start | bytes 1572872 | tf_op jit(solution)/shard_map/ppermute | solution.py:548
  48.1 12.9 %edge_gradients.1 = (bf16[4,128,128]{2,1,0:T(8,128)(2,1)}, bf16[4,64,128]{2,1,0:T(8,128)(2,1)}, bf16[768,128]{1,0:T(8,128)(2,1)}, bf16[32,128]{1,0:T(8,128)(2,1)}) custom-call(s32[1]{0:T(128)} %bitcast.7.me_ref, s32[1]{0:T(128)} %get-tuple-element.311.refs_0_, bf16[8,128,2048]{2,1,0:T(8,128)(2,1)} %get-tuple-element.312.refs_1_, ...), custom_call_target="tpu_custom_call" | custom-call | flops 280000000 | bytes 840000 | tf_op jit(solution)/shard_map/edge_gradients/pallas_call | solution.py:842
  61.2 1.1 fusion.98
  62.3 1.1 collective-permute-start.35
  63.4 0.7 reduce-precision_convert_fusion.4
  64.1 1.5 %collective-permute-start.33 = (bf16[32,128]{1,0:T(8,128)(2,1)S(1)}, bf16[32,128]{1,0:T(8,128)(2,1)S(1)}, u32[]{:S(2)}, u32[]{:S(2)}) collective-permute-start(bf16[32,128]{1,0:T(8,128)(2,1)S(1)} %reduce-precision_convert_fusion.4), channel_id=1, source_target_pairs={{0,16},{1,17},{2,18},{3,19},{4,20},{5,21},{6,22},{7,23},{8,24},{9,... | collective-permute-start | bytes 24584 | tf_op jit(solution)/shard_map/ppermute | solution.py:548
  65.6 1.1 fusion.97
  67.7 3.3 %collective-permute-done.35 = bf16[2,2,256,128]{3,2,1,0:T(8,128)(2,1)S(1)} collective-permute-done((bf16[2,2,256,128]{3,2,1,0:T(8,128)(2,1)S(1)}, bf16[2,2,256,128]{3,2,1,0:T(8,128)(2,1)S(1)}, u32[]{:S(2)}, u32[]{:S(2)}) %collective-permute-start.35) | collective-permute-done | bytes 262176 | tf_op jit(solution)/shard_map/ppermute | solution.py:548
  71.0 1.0 fusion.100
  72.5 3.0 %collective-permute-done.28 = bf16[2,2,288,128]{3,2,1,0:T(8,128)(2,1)S(1)} collective-permute-done((bf16[2,2,288,128]{3,2,1,0:T(8,128)(2,1)S(1)}, bf16[2,2,288,128]{3,2,1,0:T(8,128)(2,1)S(1)}, u32[]{:S(2)}, u32[]{:S(2)}) %collective-permute-start.28) | collective-permute-done | bytes 294944 | tf_op jit(solution)/shard_map/ppermute | solution.py:548
  75.7 1.4 %collective-permute-done.36 = bf16[2,256,128]{2,1,0:T(8,128)(2,1)S(1)} collective-permute-done((bf16[2,256,128]{2,1,0:T(8,128)(2,1)S(1)}, bf16[2,256,128]{2,1,0:T(8,128)(2,1)S(1)}, u32[]{:S(2)}, u32[]{:S(2)}) %collective-permute-start.36) | collective-permute-done | bytes 131104 | tf_op jit(solution)/shard_map/ppermute | solution.py:548
  77.2 0.7 collective-permute-start.37
  77.9 1.3 %collective-permute-start.34 = (bf16[800,128]{1,0:T(8,128)(2,1)S(1)}, bf16[800,128]{1,0:T(8,128)(2,1)S(1)}, u32[]{:S(2)}, u32[]{:S(2)}) collective-permute-start(bf16[800,128]{1,0:T(8,128)(2,1)S(1)} %pad_maximum_fusion.11), channel_id=1, source_target_pairs={{0,1},{1,0},{2,3},{3,2},{4,5},{5,4},{6,7},{7,6},{8,9},{9,8},{10,11... | collective-permute-start | bytes 614408 | tf_op jit(solution)/shard_map/ppermute | solution.py:548
  79.2 3.9 %collective-permute-done.37 = bf16[256,128]{1,0:T(8,128)(2,1)S(1)} collective-permute-done((bf16[256,128]{1,0:T(8,128)(2,1)S(1)}, bf16[256,128]{1,0:T(8,128)(2,1)S(1)}, u32[]{:S(2)}, u32[]{:S(2)}) %collective-permute-start.37) | collective-permute-done | bytes 65568 | tf_op jit(solution)/shard_map/ppermute | solution.py:548
  83.5 2.8 %collective-permute-start.30 = (bf16[288,128]{1,0:T(8,128)(2,1)S(1)}, bf16[288,128]{1,0:T(8,128)(2,1)S(1)}, u32[]{:S(2)}, u32[]{:S(2)}) collective-permute-start(bf16[288,128]{1,0:T(8,128)(2,1)S(1)} %fusion.102), channel_id=1, source_target_pairs={{0,4},{1,5},{2,6},{3,7},{4,0},{5,1},{6,2},{7,3},{8,12},{9,13},{10,... | collective-permute-start | bytes 221192 | tf_op jit(solution)/shard_map/ppermute | solution.py:548
  86.3 2.3 %collective-permute-done.38 = bf16[256,128]{1,0:T(8,128)(2,1)S(1)} collective-permute-done((bf16[256,128]{1,0:T(8,128)(2,1)S(1)}, bf16[256,128]{1,0:T(8,128)(2,1)S(1)}, u32[]{:S(2)}, u32[]{:S(2)}) %collective-permute-start.38) | collective-permute-done | bytes 65568 | tf_op jit(solution)/shard_map/ppermute | solution.py:548
  89.5 3.0 %collective-permute-start.31 = (bf16[288,128]{1,0:T(8,128)(2,1)S(1)}, bf16[288,128]{1,0:T(8,128)(2,1)S(1)}, u32[]{:S(2)}, u32[]{:S(2)}) collective-permute-start(bf16[288,128]{1,0:T(8,128)(2,1)S(1)} %fusion.104), channel_id=1, source_target_pairs={{0,4},{1,5},{2,6},{3,7},{4,0},{5,1},{6,2},{7,3},{8,12},{9,13},{10,... | collective-permute-start | bytes 221192 | tf_op jit(solution)/shard_map/ppermute | solution.py:548
  93.8 1.4 %collective-permute-done.31 = bf16[288,128]{1,0:T(8,128)(2,1)S(1)} collective-permute-done((bf16[288,128]{1,0:T(8,128)(2,1)S(1)}, bf16[288,128]{1,0:T(8,128)(2,1)S(1)}, u32[]{:S(2)}, u32[]{:S(2)}) %collective-permute-start.31) | collective-permute-done | bytes 73760 | tf_op jit(solution)/shard_map/ppermute | solution.py:548
  95.2 1.5 %collective-permute-start.44 = (bf16[2,288,128]{2,1,0:T(8,128)(2,1)S(1)}, bf16[2,288,128]{2,1,0:T(8,128)(2,1)S(1)}, u32[]{:S(2)}, u32[]{:S(2)}) collective-permute-start(bf16[2,288,128]{2,1,0:T(8,128)(2,1)S(1)} %pad_maximum_fusion.12), channel_id=1, source_target_pairs={{0,2},{1,3},{2,0},{3,1},{4,6},{5,7},{6,4},{7,5},{8,10},{9,11},{10,... | collective-permute-start | bytes 442376 | tf_op jit(solution)/shard_map/ppermute | solution.py:548
  96.7 1.8 %collective-permute-start.41 = (bf16[2,2,256,128]{3,2,1,0:T(8,128)(2,1)S(1)}, bf16[2,2,256,128]{3,2,1,0:T(8,128)(2,1)S(1)}, u32[]{:S(2)}, u32[]{:S(2)}) collective-permute-start(bf16[2,2,256,128]{3,2,1,0:T(8,128)(2,1)S(1)} %get-tuple-element.655), channel_id=1, source_target_pairs={{0,1},{1,0},{2,3},{3,2},{4,5},{5,4},{6,7},{7,6},{8,9},{9,8},{10,11... | collective-permute-start | bytes 786440 | tf_op jit(solution)/shard_map/ppermute | solution.py:548
  98.6 1.8 %collective-permute-done.44 = bf16[2,288,128]{2,1,0:T(8,128)(2,1)S(1)} collective-permute-done((bf16[2,288,128]{2,1,0:T(8,128)(2,1)S(1)}, bf16[2,288,128]{2,1,0:T(8,128)(2,1)S(1)}, u32[]{:S(2)}, u32[]{:S(2)}) %collective-permute-start.44) | collective-permute-done | bytes 147488 | tf_op jit(solution)/shard_map/ppermute | solution.py:548
  100.4 1.9 %collective-permute-start.45 = (bf16[2,2,288,128]{3,2,1,0:T(8,128)(2,1)S(1)}, bf16[2,2,288,128]{3,2,1,0:T(8,128)(2,1)S(1)}, u32[]{:S(2)}, u32[]{:S(2)}) collective-permute-start(bf16[2,2,288,128]{3,2,1,0:T(8,128)(2,1)S(1)} %get-tuple-element.653), channel_id=1, source_target_pairs={{0,16},{1,17},{2,18},{3,19},{4,20},{5,21},{6,22},{7,23},{8,24},{9,... | collective-permute-start | bytes 884744 | tf_op jit(solution)/shard_map/ppermute | solution.py:548
  102.4 0.7 collective-permute-done.41
  103.2 2.1 %collective-permute-start.42 = (bf16[416,128]{1,0:T(8,128)(2,1)S(1)}, bf16[416,128]{1,0:T(8,128)(2,1)S(1)}, u32[]{:S(2)}, u32[]{:S(2)}) collective-permute-start(bf16[416,128]{1,0:T(8,128)(2,1)S(1)} %pad_maximum_fusion.17), channel_id=1, source_target_pairs={{0,4},{1,5},{2,6},{3,7},{4,0},{5,1},{6,2},{7,3},{8,12},{9,13},{10,... | collective-permute-start | bytes 319496 | tf_op jit(solution)/shard_map/ppermute | solution.py:548
  105.3 2.1 %collective-permute-done.45 = bf16[2,2,288,128]{3,2,1,0:T(8,128)(2,1)S(1)} collective-permute-done((bf16[2,2,288,128]{3,2,1,0:T(8,128)(2,1)S(1)}, bf16[2,2,288,128]{3,2,1,0:T(8,128)(2,1)S(1)}, u32[]{:S(2)}, u32[]{:S(2)}) %collective-permute-start.45) | collective-permute-done | bytes 294944 | tf_op jit(solution)/shard_map/ppermute | solution.py:548
  107.5 1.2 collective-permute-start.46
  108.7 2.0 %collective-permute-start.43 = (bf16[2,2,2,256,128]{4,3,2,1,0:T(8,128)(2,1)S(1)}, bf16[2,2,2,256,128]{4,3,2,1,0:T(8,128)(2,1)S(1)}, u32[]{:S(2)}, u32[]{:S(2)}) collective-permute-start(bf16[2,2,2,256,128]{4,3,2,1,0:T(8,128)(2,1)S(1)} %pad_maximum_fusion.8), channel_id=1, source_target_pairs={{0,16},{1,17},{2,18},{3,19},{4,20},{5,21},{6,22},{7,23},{8,24},{9,... | collective-permute-start | bytes 1572872 | tf_op jit(solution)/shard_map/ppermute | solution.py:548
  110.7 0.7 maximum_bitcast_fusion.slabs_ref
  111.4 0.6 fusion.112.part_ref
  112.0 2.3 %slots_to_edges.1 = (f32[128,128]{1,0:T(8,128)}, f32[16,2048]{1,0:T(8,128)}) custom-call(s32[1]{0:T(128)} %bitcast.7.me_ref, s32[1,2048]{1,0:T(1,128)} %get-tuple-element.329.slot_ref, f32[128,128]{1,0:T(8,128)} %get-tuple-element.330.direct_ref, bf16[128,128]{1,0:T(8,128)(2,1)} %fusion.112.part_ref, bf16[8,64,128]{2,1,0:T(8,128)(2,1)} %maximum_bitcast_fusion.slabs_ref), custom_call_target="tpu_custom_call" | custom-call | flops 60000000 | bytes 180000 | tf_op jit(solution)/shard_map/slots_to_edges/pallas_call | solution.py:956
  115.0 0.8 copy-done.28
  115.8 0.8 copy-done.26
  116.6 5.3 %assemble_early.2 = (f32[128,16384]{1,0:T(8,128)}, f32[7,136,128]{2,1,0:T(8,128)}, f32[40,128]{1,0:T(8,128)}) custom-call(s32[1]{0:T(128)} %bitcast.6.refs_0_.piece_ref, bf16[8,256,128]{2,1,0:T(8,128)(2,1)} %bitcast.498, bf16[8,288,128]{2,1,0:T(8,128)(2,1)} %bitcast.490, bf16[8,256,128]{2,1,0:T(8,128)(2,1)} %copy-done.28, bf16[8,288,128]{2,1,0:T(8,128)(2,1)} %copy-done.26), custom_call_target="tpu_custom_call" | custom-call | flops 120000000 | bytes 360000 | tf_op jit(solution)/shard_map/assemble_early/pallas_call | solution.py:704
  121.9 1.1 collective-permute-done.43
  124.3 3.2 %assemble_late.1.refs_6_ = f32[128,16384]{1,0:T(8,128)} custom-call(s32[1]{0:T(128)} %bitcast.6.refs_0_.piece_ref, bf16[8,256,128]{2,1,0:T(8,128)(2,1)} %bitcast.510, bf16[8,288,128]{2,1,0:T(8,128)(2,1)} %bitcast.83.refs_1_.refs_2_, f32[128,16384]{1,0:T(8,128)} %get-tuple-element.355.refs_2_), custom_call_target="tpu_custom_call", output_to_operand_aliasing={{}: (3, {})} | custom-call | flops 80000000 | bytes 240000 | tf_op jit(solution)/shard_map/assemble_late/pallas_call | solution.py:985
  127.5 0.8 copy-done.30
  128.5 3.9 %assemble_last.1 = (f32[128,16384]{1,0:T(8,128)}, f32[16,128]{1,0:T(8,128)}, f32[128]{0:T(128)}, f32[128,384]{1,0:T(8,128)}, f32[128,384]{1,0:T(8,128)}, /*index...) custom-call(s32[1]{0:T(128)} %bitcast.6.refs_0_.piece_ref, ...), custom_call_target="tpu_custom_call", output_to_operand_aliasing={{0}: (7, {})} | custom-call | tf_op jit(solution)/shard_map/assemble_last/pallas_call | solution.py:997
  (97 shorter events, 6.7 us)
Async XLA Ops:
  4.0 19.7 %all-to-all-start.5 = ((bf16[8,208,128]{2,1,0:T(8,128)(2,1)}), bf16[8,208,128]{2,1,0:T(8,128)(2,1)S(1)}, u32[]{:S(2)}, u32[]{:S(2)}) async-start(bf16[8,208,128]{2,1,0:T(8,128)(2,1)} %get-tuple-element.296), calls=%async_computation.5 | async-start | bytes 851968 | tf_op jit(solution)/shard_map/all_to_all | solution.py:764
  23.7 0.8 copy-start.23
  38.1 5.9 %copy-start.27 = (bf16[8,288,128]{2,1,0:T(8,128)(2,1)S(1)}, bf16[8,288,128]{2,1,0:T(8,128)(2,1)}, u32[]{:S(2)}) copy-start(bf16[8,288,128]{2,1,0:T(8,128)(2,1)} %get-tuple-element.306) | copy-start | bytes 1769476
  38.1 6.1 %copy-start.29 = (bf16[8,256,128]{2,1,0:T(8,128)(2,1)S(1)}, bf16[8,256,128]{2,1,0:T(8,128)(2,1)}, u32[]{:S(2)}) copy-start(bf16[8,256,128]{2,1,0:T(8,128)(2,1)} %get-tuple-element.305) | copy-start | bytes 1572868
  38.1 5.8 %collective-permute-start.25 = (bf16[16,544,128]{2,1,0:T(8,128)(2,1)}, bf16[16,544,128]{2,1,0:T(8,128)(2,1)S(1)}, u32[]{:S(2)}, u32[]{:S(2)}) collective-permute-start(bf16[16,544,128]{2,1,0:T(8,128)(2,1)} %get-tuple-element.300), channel_id=1, source_target_pairs={{0,8},{1,9},{2,10},{3,11},{4,12},{5,13},{6,14},{7,15},{8,0},{9,1},... | collective-permute-start | bytes 6684680 | tf_op jit(solution)/shard_map/ppermute | solution.py:548
  45.1 16.0 %collective-permute-start.26 = (bf16[2,2,2,288,128]{4,3,2,1,0:T(8,128)(2,1)S(1)}, bf16[2,2,2,288,128]{4,3,2,1,0:T(8,128)(2,1)S(1)}, u32[]{:S(2)}, u32[]{:S(2)}) collective-permute-start(bf16[2,2,2,288,128]{4,3,2,1,0:T(8,128)(2,1)S(1)} %fusion.95), channel_id=1, source_target_pairs={{0,1},{1,0},{2,3},{3,2},{4,5},{5,4},{6,7},{7,6},{8,9},{9,8},{10,11... | collective-permute-start | bytes 1769480 | tf_op jit(solution)/shard_map/ppermute | solution.py:548
  46.6 14.5 %collective-permute-start.27 = (bf16[2,2,2,256,128]{4,3,2,1,0:T(8,128)(2,1)}, bf16[2,2,2,256,128]{4,3,2,1,0:T(8,128)(2,1)S(1)}, u32[]{:S(2)}, u32[]{:S(2)}) collective-permute-start(bf16[2,2,2,256,128]{4,3,2,1,0:T(8,128)(2,1)} %fusion.96), channel_id=1, source_target_pairs={{0,16},{1,17},{2,18},{3,19},{4,20},{5,21},{6,22},{7,23},{8,24},{9,... | collective-permute-start | bytes 1572872 | tf_op jit(solution)/shard_map/ppermute | solution.py:548
  60.9 14.6 %copy-start.34 = (bf16[4,288,128]{2,1,0:T(8,128)(2,1)S(1)}, bf16[4,288,128]{2,1,0:T(8,128)(2,1)}, u32[]{:S(2)}) copy-start(bf16[4,288,128]{2,1,0:T(8,128)(2,1)} %get-tuple-element.297) | copy-start | bytes 884740
  61.0 16.1 %copy-start.36 = (bf16[4,256,128]{2,1,0:T(8,128)(2,1)S(1)}, bf16[4,256,128]{2,1,0:T(8,128)(2,1)}, u32[]{:S(2)}) copy-start(bf16[4,256,128]{2,1,0:T(8,128)(2,1)} %get-tuple-element.336) | copy-start | bytes 786436
  61.0 16.9 %copy-start.37 = (bf16[768,128]{1,0:T(8,128)(2,1)S(1)}, bf16[768,128]{1,0:T(8,128)(2,1)}, u32[]{:S(2)}) copy-start(bf16[768,128]{1,0:T(8,128)(2,1)} %get-tuple-element.333) | copy-start | bytes 589828
  61.0 27.7 %copy-start.38 = (bf16[4,128,128]{2,1,0:T(8,128)(2,1)S(1)}, bf16[4,128,128]{2,1,0:T(8,128)(2,1)}, u32[]{:S(2)}) copy-start(bf16[4,128,128]{2,1,0:T(8,128)(2,1)} %get-tuple-element.331) | copy-start | bytes 393220
  61.0 27.8 %copy-start.35 = (bf16[4,64,128]{2,1,0:T(8,128)(2,1)S(1)}, bf16[4,64,128]{2,1,0:T(8,128)(2,1)}, u32[]{:S(2)}) copy-start(bf16[4,64,128]{2,1,0:T(8,128)(2,1)} %get-tuple-element.335) | copy-start | bytes 196612
  61.1 2.3 %collective-permute-start.32 = (bf16[32,128]{1,0:T(8,128)(2,1)}, bf16[32,128]{1,0:T(8,128)(2,1)S(1)}, u32[]{:S(2)}, u32[]{:S(2)}) collective-permute-start(bf16[32,128]{1,0:T(8,128)(2,1)} %get-tuple-element.334), channel_id=1, source_target_pairs={{0,8},{1,9},{2,10},{3,11},{4,12},{5,13},{6,14},{7,15},{8,0},{9,1},... | collective-permute-start | bytes 24584 | tf_op jit(solution)/shard_map/ppermute | solution.py:548
  62.3 8.7 %collective-permute-start.35 = (bf16[2,2,256,128]{3,2,1,0:T(8,128)(2,1)S(1)}, bf16[2,2,256,128]{3,2,1,0:T(8,128)(2,1)S(1)}, u32[]{:S(2)}, u32[]{:S(2)}) collective-permute-start(bf16[2,2,256,128]{3,2,1,0:T(8,128)(2,1)S(1)} %fusion.98), channel_id=1, source_target_pairs={{0,1},{1,0},{2,3},{3,2},{4,5},{5,4},{6,7},{7,6},{8,9},{9,8},{10,11... | collective-permute-start | bytes 786440 | tf_op jit(solution)/shard_map/ppermute | solution.py:548
  64.1 3.7 %collective-permute-start.33 = (bf16[32,128]{1,0:T(8,128)(2,1)S(1)}, bf16[32,128]{1,0:T(8,128)(2,1)S(1)}, u32[]{:S(2)}, u32[]{:S(2)}) collective-permute-start(bf16[32,128]{1,0:T(8,128)(2,1)S(1)} %reduce-precision_convert_fusion.4), channel_id=1, source_target_pairs={{0,16},{1,17},{2,18},{3,19},{4,20},{5,21},{6,22},{7,23},{8,24},{9,... | collective-permute-start | bytes 24584 | tf_op jit(solution)/shard_map/ppermute | solution.py:548
  66.6 8.9 %collective-permute-start.28 = (bf16[2,2,288,128]{3,2,1,0:T(8,128)(2,1)S(1)}, bf16[2,2,288,128]{3,2,1,0:T(8,128)(2,1)S(1)}, u32[]{:S(2)}, u32[]{:S(2)}) collective-permute-start(bf16[2,2,288,128]{3,2,1,0:T(8,128)(2,1)S(1)} %fusion.97), channel_id=1, source_target_pairs={{0,16},{1,17},{2,18},{3,19},{4,20},{5,21},{6,22},{7,23},{8,24},{9,... | collective-permute-start | bytes 884744 | tf_op jit(solution)/shard_map/ppermute | solution.py:548
  72.0 5.1 %collective-permute-start.36 = (bf16[2,256,128]{2,1,0:T(8,128)(2,1)S(1)}, bf16[2,256,128]{2,1,0:T(8,128)(2,1)S(1)}, u32[]{:S(2)}, u32[]{:S(2)}) collective-permute-start(bf16[2,256,128]{2,1,0:T(8,128)(2,1)S(1)} %fusion.100), channel_id=1, source_target_pairs={{0,2},{1,3},{2,0},{3,1},{4,6},{5,7},{6,4},{7,5},{8,10},{9,11},{10,... | collective-permute-start | bytes 393224 | tf_op jit(solution)/shard_map/ppermute | solution.py:548
  75.7 7.7 %collective-permute-start.29 = (bf16[2,288,128]{2,1,0:T(8,128)(2,1)S(1)}, bf16[2,288,128]{2,1,0:T(8,128)(2,1)S(1)}, u32[]{:S(2)}, u32[]{:S(2)}) collective-permute-start(bf16[2,288,128]{2,1,0:T(8,128)(2,1)S(1)} %fusion.99), channel_id=1, source_target_pairs={{0,2},{1,3},{2,0},{3,1},{4,6},{5,7},{6,4},{7,5},{8,10},{9,11},{10,... | collective-permute-start | bytes 442376 | tf_op jit(solution)/shard_map/ppermute | solution.py:548
  77.2 5.9 %collective-permute-start.37 = (bf16[256,128]{1,0:T(8,128)(2,1)S(1)}, bf16[256,128]{1,0:T(8,128)(2,1)S(1)}, u32[]{:S(2)}, u32[]{:S(2)}) collective-permute-start(bf16[256,128]{1,0:T(8,128)(2,1)S(1)} %fusion.107), channel_id=1, source_target_pairs={{0,4},{1,5},{2,6},{3,7},{4,0},{5,1},{6,2},{7,3},{8,12},{9,13},{10,... | collective-permute-start | bytes 196616 | tf_op jit(solution)/shard_map/ppermute | solution.py:548
  77.9 10.8 %collective-permute-start.34 = (bf16[800,128]{1,0:T(8,128)(2,1)S(1)}, bf16[800,128]{1,0:T(8,128)(2,1)S(1)}, u32[]{:S(2)}, u32[]{:S(2)}) collective-permute-start(bf16[800,128]{1,0:T(8,128)(2,1)S(1)} %pad_maximum_fusion.11), channel_id=1, source_target_pairs={{0,1},{1,0},{2,3},{3,2},{4,5},{5,4},{6,7},{7,6},{8,9},{9,8},{10,11... | collective-permute-start | bytes 614408 | tf_op jit(solution)/shard_map/ppermute | solution.py:548
  83.2 5.4 %collective-permute-start.38 = (bf16[256,128]{1,0:T(8,128)(2,1)S(1)}, bf16[256,128]{1,0:T(8,128)(2,1)S(1)}, u32[]{:S(2)}, u32[]{:S(2)}) collective-permute-start(bf16[256,128]{1,0:T(8,128)(2,1)S(1)} %fusion.109), channel_id=1, source_target_pairs={{0,4},{1,5},{2,6},{3,7},{4,0},{5,1},{6,2},{7,3},{8,12},{9,13},{10,... | collective-permute-start | bytes 196616 | tf_op jit(solution)/shard_map/ppermute | solution.py:548
  83.5 6.0 %collective-permute-start.30 = (bf16[288,128]{1,0:T(8,128)(2,1)S(1)}, bf16[288,128]{1,0:T(8,128)(2,1)S(1)}, u32[]{:S(2)}, u32[]{:S(2)}) collective-permute-start(bf16[288,128]{1,0:T(8,128)(2,1)S(1)} %fusion.102), channel_id=1, source_target_pairs={{0,4},{1,5},{2,6},{3,7},{4,0},{5,1},{6,2},{7,3},{8,12},{9,13},{10,... | collective-permute-start | bytes 221192 | tf_op jit(solution)/shard_map/ppermute | solution.py:548
  88.6 8.0 %collective-permute-start.40 = (bf16[2,256,128]{2,1,0:T(8,128)(2,1)S(1)}, bf16[2,256,128]{2,1,0:T(8,128)(2,1)S(1)}, u32[]{:S(2)}, u32[]{:S(2)}) collective-permute-start(bf16[2,256,128]{2,1,0:T(8,128)(2,1)S(1)} %get-tuple-element.661), channel_id=1, source_target_pairs={{0,2},{1,3},{2,0},{3,1},{4,6},{5,7},{6,4},{7,5},{8,10},{9,11},{10,... | collective-permute-start | bytes 393224 | tf_op jit(solution)/shard_map/ppermute | solution.py:548
  89.5 5.6 %collective-permute-start.31 = (bf16[288,128]{1,0:T(8,128)(2,1)S(1)}, bf16[288,128]{1,0:T(8,128)(2,1)S(1)}, u32[]{:S(2)}, u32[]{:S(2)}) collective-permute-start(bf16[288,128]{1,0:T(8,128)(2,1)S(1)} %fusion.104), channel_id=1, source_target_pairs={{0,4},{1,5},{2,6},{3,7},{4,0},{5,1},{6,2},{7,3},{8,12},{9,13},{10,... | collective-permute-start | bytes 221192 | tf_op jit(solution)/shard_map/ppermute | solution.py:548
  92.5 6.0 %collective-permute-start.39 = (bf16[544,128]{1,0:T(8,128)(2,1)S(1)}, bf16[544,128]{1,0:T(8,128)(2,1)S(1)}, u32[]{:S(2)}, u32[]{:S(2)}) collective-permute-start(bf16[544,128]{1,0:T(8,128)(2,1)S(1)} %pad_maximum_fusion.13), channel_id=1, source_target_pairs={{0,2},{1,3},{2,0},{3,1},{4,6},{5,7},{6,4},{7,5},{8,10},{9,11},{10,... | collective-permute-start | bytes 417800 | tf_op jit(solution)/shard_map/ppermute | solution.py:548
  95.2 5.2 %collective-permute-start.44 = (bf16[2,288,128]{2,1,0:T(8,128)(2,1)S(1)}, bf16[2,288,128]{2,1,0:T(8,128)(2,1)S(1)}, u32[]{:S(2)}, u32[]{:S(2)}) collective-permute-start(bf16[2,288,128]{2,1,0:T(8,128)(2,1)S(1)} %pad_maximum_fusion.12), channel_id=1, source_target_pairs={{0,2},{1,3},{2,0},{3,1},{4,6},{5,7},{6,4},{7,5},{8,10},{9,11},{10,... | collective-permute-start | bytes 442376 | tf_op jit(solution)/shard_map/ppermute | solution.py:548
  96.7 6.4 %collective-permute-start.41 = (bf16[2,2,256,128]{3,2,1,0:T(8,128)(2,1)S(1)}, bf16[2,2,256,128]{3,2,1,0:T(8,128)(2,1)S(1)}, u32[]{:S(2)}, u32[]{:S(2)}) collective-permute-start(bf16[2,2,256,128]{3,2,1,0:T(8,128)(2,1)S(1)} %get-tuple-element.655), channel_id=1, source_target_pairs={{0,1},{1,0},{2,3},{3,2},{4,5},{5,4},{6,7},{7,6},{8,9},{9,8},{10,11... | collective-permute-start | bytes 786440 | tf_op jit(solution)/shard_map/ppermute | solution.py:548
  100.4 7.0 %collective-permute-start.45 = (bf16[2,2,288,128]{3,2,1,0:T(8,128)(2,1)S(1)}, bf16[2,2,288,128]{3,2,1,0:T(8,128)(2,1)S(1)}, u32[]{:S(2)}, u32[]{:S(2)}) collective-permute-start(bf16[2,2,288,128]{3,2,1,0:T(8,128)(2,1)S(1)} %get-tuple-element.653), channel_id=1, source_target_pairs={{0,16},{1,17},{2,18},{3,19},{4,20},{5,21},{6,22},{7,23},{8,24},{9,... | collective-permute-start | bytes 884744 | tf_op jit(solution)/shard_map/ppermute | solution.py:548
  103.2 11.8 %copy-start.22 = (bf16[2,2,2,256,128]{4,3,2,1,0:T(8,128)(2,1)}, bf16[2,2,2,256,128]{4,3,2,1,0:T(8,128)(2,1)S(1)}, u32[]{:S(2)}) copy-start(bf16[2,2,2,256,128]{4,3,2,1,0:T(8,128)(2,1)S(1)} %pad_maximum_fusion.8) | copy-start | bytes 1572868
  103.2 7.5 %collective-permute-start.42 = (bf16[416,128]{1,0:T(8,128)(2,1)S(1)}, bf16[416,128]{1,0:T(8,128)(2,1)S(1)}, u32[]{:S(2)}, u32[]{:S(2)}) collective-permute-start(bf16[416,128]{1,0:T(8,128)(2,1)S(1)} %pad_maximum_fusion.17), channel_id=1, source_target_pairs={{0,4},{1,5},{2,6},{3,7},{4,0},{5,1},{6,2},{7,3},{8,12},{9,13},{10,... | collective-permute-start | bytes 319496 | tf_op jit(solution)/shard_map/ppermute | solution.py:548
  107.4 7.6 %copy-start.21 = (bf16[2,2,2,288,128]{4,3,2,1,0:T(8,128)(2,1)}, bf16[2,2,2,288,128]{4,3,2,1,0:T(8,128)(2,1)S(1)}, u32[]{:S(2)}) copy-start(bf16[2,2,2,288,128]{4,3,2,1,0:T(8,128)(2,1)S(1)} %pad_maximum_fusion.7) | copy-start | bytes 1769476
  107.4 7.5 %collective-permute-start.48 = (bf16[8,288,128]{2,1,0:T(8,128)(2,1)S(1)}, bf16[8,288,128]{2,1,0:T(8,128)(2,1)S(1)}, u32[]{:S(2)}, u32[]{:S(2)}) collective-permute-start(bf16[8,288,128]{2,1,0:T(8,128)(2,1)S(1)} %bitcast.489), channel_id=1, source_target_pairs={{0,8},{1,9},{2,10},{3,11},{4,12},{5,13},{6,14},{7,15},{8,0},{9,1},... | collective-permute-start | bytes 1769480 | tf_op jit(solution)/shard_map/ppermute | solution.py:548
  107.5 15.8 %collective-permute-start.46 = (bf16[2,2,2,288,128]{4,3,2,1,0:T(8,128)(2,1)S(1)}, bf16[2,2,2,288,128]{4,3,2,1,0:T(8,128)(2,1)}, u32[]{:S(2)}, u32[]{:S(2)}) collective-permute-start(bf16[2,2,2,288,128]{4,3,2,1,0:T(8,128)(2,1)S(1)} %pad_maximum_fusion.7), channel_id=1, source_target_pairs={{0,1},{1,0},{2,3},{3,2},{4,5},{5,4},{6,7},{7,6},{8,9},{9,8},{10,11... | collective-permute-start | bytes 1769480 | tf_op jit(solution)/shard_map/ppermute | solution.py:548
  108.7 14.3 %collective-permute-start.43 = (bf16[2,2,2,256,128]{4,3,2,1,0:T(8,128)(2,1)S(1)}, bf16[2,2,2,256,128]{4,3,2,1,0:T(8,128)(2,1)S(1)}, u32[]{:S(2)}, u32[]{:S(2)}) collective-permute-start(bf16[2,2,2,256,128]{4,3,2,1,0:T(8,128)(2,1)S(1)} %pad_maximum_fusion.8), channel_id=1, source_target_pairs={{0,16},{1,17},{2,18},{3,19},{4,20},{5,21},{6,22},{7,23},{8,24},{9,... | collective-permute-start | bytes 1572872 | tf_op jit(solution)/shard_map/ppermute | solution.py:548
  110.7 4.3 %collective-permute-start.47 = (bf16[8,256,128]{2,1,0:T(8,128)(2,1)S(1)}, bf16[8,256,128]{2,1,0:T(8,128)(2,1)S(1)}, u32[]{:S(2)}, u32[]{:S(2)}) collective-permute-start(bf16[8,256,128]{2,1,0:T(8,128)(2,1)S(1)} %bitcast.497), channel_id=1, source_target_pairs={{0,8},{1,9},{2,10},{3,11},{4,12},{5,13},{6,14},{7,15},{8,0},{9,1},... | collective-permute-start | bytes 1572872 | tf_op jit(solution)/shard_map/ppermute | solution.py:548
  115.0 0.8 copy-start.28
  115.8 0.8 copy-start.26
  123.0 0.8 copy-start.31
  123.8 3.7 %collective-permute-start.50 = (bf16[8,288,128]{2,1,0:T(8,128)(2,1)}, bf16[8,288,128]{2,1,0:T(8,128)(2,1)S(1)}, u32[]{:S(2)}, u32[]{:S(2)}) collective-permute-start(bf16[8,288,128]{2,1,0:T(8,128)(2,1)} %bitcast.83.refs_1_.refs_2_), channel_id=1, source_target_pairs={{0,8},{1,9},{2,10},{3,11},{4,12},{5,13},{6,14},{7,15},{8,0},{9,1},... | collective-permute-start | bytes 1769480 | tf_op jit(solution)/shard_map/ppermute | solution.py:548
  123.8 3.7 %collective-permute-start.49 = (bf16[8,256,128]{2,1,0:T(8,128)(2,1)}, bf16[8,256,128]{2,1,0:T(8,128)(2,1)S(1)}, u32[]{:S(2)}, u32[]{:S(2)}) collective-permute-start(bf16[8,256,128]{2,1,0:T(8,128)(2,1)} %bitcast.509), channel_id=1, source_target_pairs={{0,8},{1,9},{2,10},{3,11},{4,12},{5,13},{6,14},{7,15},{8,0},{9,1},... | collective-permute-start | bytes 1572872 | tf_op jit(solution)/shard_map/ppermute | solution.py:548
  124.3 4.2 %copy-start.33 = (f32[7,136,128]{2,1,0:T(8,128)S(1)}, f32[7,136,128]{2,1,0:T(8,128)}, u32[]{:S(2)}) copy-start(f32[7,136,128]{2,1,0:T(8,128)} %get-tuple-element.353.refs_4_) | copy-start | bytes 1462276
  124.3 4.2 %copy-start.43 = (bf16[32,128]{1,0:T(8,128)(2,1)S(1)}, bf16[32,128]{1,0:T(8,128)(2,1)}, u32[]{:S(2)}) copy-start(bf16[32,128]{1,0:T(8,128)(2,1)} %get-tuple-element.352.refs_3_) | copy-start | bytes 24580
  124.3 4.2 %copy-start.44 = (f32[40,128]{1,0:T(8,128)S(1)}, f32[40,128]{1,0:T(8,128)}, u32[]{:S(2)}) copy-start(f32[40,128]{1,0:T(8,128)} %get-tuple-element.354.refs_5_) | copy-start | bytes 61444
  127.5 0.8 copy-start.30
  127.5 1.0 copy-start.25
